TPU v7x, 1024 devices: a whole 8x8x8 slice. The times are simulated.
1024 devices in a mesh: row: 32 (over z_lo, x, core), col: 8 (over y), rep: 4 (over z_hi).
Axes of the slice: x: 8, y: 8, z: 8 (z_hi: 4, z_lo: 2; z = z_hi * 2 + z_lo), core: 2. Of those that a mesh axis runs over, the one named last changes fastest.
Arguments:
- tokens: bfloat16 [1024, 8192], P(('row', 'rep'), 'col'), may hold values from -6 to 6
- cotangent: bfloat16 [1024, 8192], P(('row', 'rep'), 'col'), may hold values from -0.59765625 to 0.59765625
- pad_mask: int32 [1024], P(('row', 'rep')), may hold values 0 or 1
- rewards: int32 [8, 8], replicated, may hold values from -4 to 4
- selected: int32 [8], replicated, may hold values from 0 to 7
- gate_weight: bfloat16 [8192, 16384], P('col', 'row'), may hold values from -0.0625 to 0.0625
- up_weight: bfloat16 [8192, 16384], P('col', 'row'), may hold values from -0.0625 to 0.0625
- down_weight: bfloat16 [16384, 8192], P('row', 'col'), may hold values from -0.046875 to 0.046875
Outputs:
- gate_grad: float32 [8192, 16384], P(('col', 'rep'), 'row')
- up_grad: float32 [8192, 16384], P(('col', 'rep'), 'row')
- down_grad: float32 [16384, 8192], P('row', ('col', 'rep'))
All inputs are finite; a program needn't handle non-finite values. No bound on the sum of `pad_mask` on one device may be relied on, other than what follows from the above.
Results may differ from a plain program's by a relative error of at most 0.0035.
Values may be sent and summed in bfloat16 or wider, within the bound.
No kernel may reach another device: no remote copies, remote signals or barrier semaphores. Data moves between devices by JAX's collectives and lax.ppermute only.
A program may use at most 32 MiB of HBM per device.

v0:
```python
import jax
import jax.numpy as jnp
from jax import lax
from jax.sharding import PartitionSpec as P

SAMPLES = 8
COMP_LEN = 16


def unit_values(summed, unit_width):
    gate_value = summed[:, :unit_width]
    up_value = summed[:, unit_width : 2 * unit_width]
    back_value = summed[:, 2 * unit_width :]
    sigmoid_gate = jax.nn.sigmoid(gate_value)
    active = gate_value * sigmoid_gate
    hidden = (active * up_value).astype(jnp.bfloat16)
    gate_back = (
        back_value * up_value * sigmoid_gate * (1.0 + gate_value * (1.0 - sigmoid_gate))
    ).astype(jnp.bfloat16)
    up_back = (back_value * active).astype(jnp.bfloat16)
    return jnp.concatenate([hidden, gate_back, up_back], axis=1)


def body(tokens, cotangent, pad_mask, rewards, selected, gate_weight, up_weight, down_weight):
    n_col = lax.axis_size("col")
    n_rep = lax.axis_size("rep")
    block_rows = tokens.shape[0]
    unit_width = gate_weight.shape[1]
    prompt_count = rewards.shape[0]
    block_index = lax.axis_index("row") * n_rep + lax.axis_index("rep")
    position = block_index * block_rows + jnp.arange(block_rows, dtype=jnp.int32)
    completion = position // COMP_LEN
    prompt_index = completion // SAMPLES
    sample_index = completion % SAMPLES
    slot_match = completion[:, None] == jnp.arange(prompt_count * SAMPLES, dtype=jnp.int32)[None, :]
    reward_flat = rewards.reshape(-1).astype(jnp.float32)
    reward_value = jnp.sum(jnp.where(slot_match, reward_flat[None, :], 0.0), axis=1)
    prompt_match = prompt_index[:, None] == jnp.arange(prompt_count, dtype=jnp.int32)[None, :]
    chosen_index = jnp.sum(jnp.where(prompt_match, selected[None, :], 0), axis=1)
    chosen_flag = (chosen_index == sample_index).astype(jnp.float32)
    weight = pad_mask.astype(jnp.float32) * (reward_value / 4.0 + chosen_flag)
    grads = (weight[:, None] * cotangent.astype(jnp.float32)).astype(jnp.bfloat16)
    stacked = jnp.stack([tokens, grads], axis=1)
    replica_rows = lax.all_gather(stacked, "row", axis=0, tiled=True)
    quarters = lax.all_to_all(replica_rows, "rep", split_axis=2, concat_axis=0, tiled=True)
    replica_tokens = replica_rows[:, 0]
    replica_grads = replica_rows[:, 1]
    total_rows = replica_rows.shape[0]
    share = total_rows // n_col
    gate_part = jnp.dot(replica_tokens, gate_weight, preferred_element_type=jnp.float32)
    up_part = jnp.dot(replica_tokens, up_weight, preferred_element_type=jnp.float32)
    back_part = lax.dot_general(
        replica_grads, down_weight, (((1,), (1,)), ((), ())), preferred_element_type=jnp.float32
    )
    summed = lax.psum_scatter(
        jnp.concatenate([gate_part, up_part, back_part], axis=1),
        "col",
        scatter_dimension=0,
        tiled=True,
    )
    every_unit = lax.all_gather(unit_values(summed, unit_width), ("col", "rep"), axis=0, tiled=True)
    unit_blocks = every_unit.reshape(n_col, n_rep, share, 3 * unit_width)
    unit_form = "cksf"
    quarter_width = quarters.shape[2]
    token_quarter = quarters[:, 0].reshape(n_rep, n_col, share, quarter_width)
    grad_quarter = quarters[:, 1].reshape(n_rep, n_col, share, quarter_width)
    hidden_all = unit_blocks[..., :unit_width]
    gate_back_all = unit_blocks[..., unit_width : 2 * unit_width]
    up_back_all = unit_blocks[..., 2 * unit_width :]
    gate_grad = jnp.einsum(
        "kcsq," + unit_form + "->qf",
        token_quarter,
        gate_back_all,
        preferred_element_type=jnp.float32,
    )
    up_grad = jnp.einsum(
        "kcsq," + unit_form + "->qf", token_quarter, up_back_all, preferred_element_type=jnp.float32
    )
    down_grad = jnp.einsum(
        unit_form + ",kcsq->fq", hidden_all, grad_quarter, preferred_element_type=jnp.float32
    )
    return (gate_grad, up_grad, down_grad)


def solution(mesh):
    placed = (
        P(("row", "rep"), "col"),
        P(("row", "rep"), "col"),
        P(("row", "rep")),
        P(),
        P(),
        P("col", "row"),
        P("col", "row"),
        P("row", "col"),
    )
    return jax.shard_map(
        body,
        mesh=mesh,
        in_specs=placed,
        out_specs=(P(("col", "rep"), "row"), P(("col", "rep"), "row"), P("row", ("col", "rep"))),
        check_vma=False,
    )
```

profile of v0, /device:TPU:14, one launch (start us, length us, event | category | flops | bytes accessed | tf_op | source)
XLA Modules:
  0.0 264.4 jit_solution(15898775783859924131)
XLA Ops:
  7.2 0.0 copy-start
  7.2 0.0 all-gather.3.cloned.1.call-start
  7.3 0.8 convert_element_type.32
  8.0 0.1 convert_element_type.33
  8.1 0.8 select_reduce_fusion
  8.9 0.2 select_reduce_fusion.1
  9.1 0.7 convert_multiply_fusion
  9.8 0.8 fusion.10
  10.6 0.7 pad_maximum_fusion.2
  11.3 0.6 copy.37
  12.0 0.0 all-gather.3.cloned.1.call-update
  12.0 0.0 copy-start.2
  12.0 0.0 reduce-scatter.2.cloned.1.call-start
  12.0 79.3 %all-gather.3.cloned.1.call-done = bf16[256,2,1024]{2,1,0:T(2,128)(2,1)} async-done(((bf16[8,2,1024]{2,1,0:T(2,128)(2,1)}), bf16[256,2,1024]{2,1,0:T(2,128)(2,1)}) %all-gather.3.cloned.1.call-update) | async-done | bytes 1048592 | tf_op jit(solution)/shard_map/all_gather | solution.py:44
  91.3 3.1 %fusion.13 = (bf16[256,1,1024]{2,1,0:T(2,128)(2,1)S(1)}, bf16[256,1,1024]{2,1,0:T(2,128)(2,1)S(1)}) fusion(bf16[256,2,1024]{2,1,0:T(2,128)(2,1)} %all-gather.3.cloned.1.call-done), kind=kLoop, calls=%fused_computation.41 | loop fusion | bytes 2097152 | tf_op jit(solution)/shard_map/slice | solution.py:46
  94.5 0.0 copy-start.3
  94.5 0.0 copy-done
  94.5 0.4 fusion.7
  95.0 0.0 copy-done.2
  95.0 0.4 fusion.8
  95.4 0.3 copy-done.3
  95.7 0.5 fusion.3
  96.2 0.0 copy-start.1
  96.2 1.3 pad_maximum_fusion
  97.5 0.0 reduce-scatter.2.cloned.1.call-update
  97.5 0.0 all-gather.5.cloned.1.call-start
  97.5 46.8 %reduce-scatter.2.cloned.1.call-done = f32[32,1536]{1,0:T(8,128)} async-done(((f32[256,1536]{1,0:T(8,128)}), f32[32,1536]{1,0:T(8,128)}) %reduce-scatter.2.cloned.1.call-update) | async-done | bytes 196624 | tf_op jit(solution)/shard_map/reduce_scatter | solution.py:55
  144.3 0.9 multiply_convert_fusion.2
  145.2 0.6 pad_maximum_fusion.1
  145.9 0.0 all-gather.5.cloned.1.call-update
  145.9 0.0 copy-done.1
  145.9 2.6 copy.38
  148.6 34.4 %all_to_all.18 = bf16[256,2,1024]{0,1,2:T(2,128)(2,1)S(1)} all-to-all(bf16[256,2,1024]{0,1,2:T(2,128)(2,1)S(1)} %copy.38), channel_id=1, replica_groups=mesh['row'=32,'col'=8,'rep'=4] {'rep'}, dimensions={2} | all-to-all | bytes 2097152 | tf_op jit(solution)/shard_map/all_to_all | solution.py:45
  182.9 0.1 copy.39
  183.1 0.5 copy.40
  183.6 0.1 fusion.12
  183.7 69.0 %all-gather.5.cloned.1.call-done = bf16[1024,1536]{1,0:T(8,128)(2,1)} async-done(((bf16[32,1536]{1,0:T(8,128)(2,1)}), bf16[1024,1536]{1,0:T(8,128)(2,1)}) %all-gather.5.cloned.1.call-update) | async-done | bytes 3145744 | tf_op jit(solution)/shard_map/all_gather | solution.py:61
  252.7 0.0 copy-start.4
  252.7 2.6 convolution_bitcast_fusion.1
  255.4 0.0 copy-done.4
  255.4 1.2 convolution_bitcast_fusion.2
  256.6 1.3 convolution_bitcast_fusion
  (1 shorter events, 0.0 us)
Async XLA Ops:
  7.2 87.3 %copy-start = (bf16[1024,512]{1,0:T(8,128)(2,1)S(1)}, bf16[1024,512]{1,0:T(8,128)(2,1)}, u32[]{:S(2)}) copy-start(bf16[1024,512]{1,0:T(8,128)(2,1)} %param.14) | copy-start | bytes 3145732
  7.2 84.2 %all-gather.3.cloned.1.call-start = ((), (), s32[]{:S(2)}) async-start(), calls=%async_computation.2 | async-start | bytes 1081344 | tf_op jit(solution)/shard_map/all_gather | solution.py:44
  12.0 83.0 %copy-start.2 = (bf16[1024,512]{1,0:T(8,128)(2,1)S(1)}, bf16[1024,512]{1,0:T(8,128)(2,1)}, u32[]{:S(2)}) copy-start(bf16[1024,512]{1,0:T(8,128)(2,1)} %param.13) | copy-start | bytes 3145732
  12.0 132.3 %reduce-scatter.2.cloned.1.call-start = ((), (), s32[]{:S(2)}) async-start(), calls=%async_computation.3 | async-start | bytes 1769472 | tf_op jit(solution)/shard_map/reduce_scatter | solution.py:55
  94.5 1.2 copy-start.3
  96.2 49.7 %copy-start.1 = (bf16[256,2,1024]{2,1,0:T(2,128)(2,1)S(1)}, bf16[256,2,1024]{2,1,0:T(2,128)(2,1)}, u32[]{:S(2)}) copy-start(bf16[256,2,1024]{2,1,0:T(2,128)(2,1)} %all-gather.3.cloned.1.call-done) | copy-start | bytes 3145732
  97.5 155.2 %all-gather.5.cloned.1.call-start = ((), (), s32[]{:S(2)}) async-start(), calls=%async_computation.4 | async-start | bytes 3244032 | tf_op jit(solution)/shard_map/all_gather | solution.py:61
  252.7 2.6 copy-start.4
Sparse Core Ops, SparseCore 0:
  12.1 79.1 all-gather.2
  97.6 46.6 reduce-scatter.1
  149.2 103.4 all-gather.4
where the time goes:
time: 265 us; the launch traced here: 264 us
  waiting for transfers between devices  195 us (74%)
  blocking collectives  34.4 us (13%)
  between operations  13.9 us (5%)
  local copies, waits for them, and re-layouts  7.55 us (3%)
  other arithmetic  6.84 us (3%)
  matrix products  6.51 us (2%)
    all_gather x1, waiting for transfers between devices, body(): replica_rows = lax.all_gather(stacked, 'row', axis=0, tiled=True)  79.3 us
    all_gather x1, waiting for transfers between devices, body(): lax.all_gather(unit_values(summed, unit_width), ('col', 'rep'), axis=0, t...  69 us
    reduce_scatter x1, waiting for transfers between devices, body(): lax.psum_scatter(jnp.concatenate([gate_part, up_part, back_part], axis=1)...  46.8 us
    all_to_all x1, blocking collectives, body(): lax.all_to_all(replica_rows, 'rep', split_axis=2, concat_axis=0, tiled=True)  34.4 us
  transfers between devices with their start and end apart: 3, of which 3 were waited for; matrix products, arithmetic and copies ran while one was open for 1% of the time, Pallas kernels for 0%

commit v1 on v0

v1 whole, which is shorter than its diff:
```python
import jax
import jax.numpy as jnp
from jax import lax
from jax.experimental import pallas as pl
from jax.experimental.pallas import tpu as pltpu
from jax.sharding import Mesh
from jax.sharding import PartitionSpec as P

SAMPLES = 8
COMP_LEN = 16
CORES = 2
Z_LO = 2
SCALE_UP = 128.0
SCALE_BACK = 1024.0
ROW = ("zlo", "x", "core")
bf16 = jnp.bfloat16
f32 = jnp.float32


def shift(value, axis, step):
    n = lax.axis_size(axis)
    return lax.ppermute(value, axis, [(i, (i + step) % n) for i in range(n)])


def prepare_kernel(block_ref, rewards_ref, selected_ref, pad_ref, tokens_ref, cotangent_ref, out_ref):
    rows, width = tokens_ref.shape
    completion = block_ref[0] * rows // COMP_LEN
    prompt = completion // SAMPLES
    sample = completion % SAMPLES
    reward = rewards_ref[prompt, sample].astype(f32)
    chosen = jnp.where(selected_ref[prompt] == sample, 1.0, 0.0)
    factor = reward / 4.0 + chosen
    weight = pad_ref[...].astype(f32) * factor
    grads = (weight * cotangent_ref[...].astype(f32)).astype(bf16)
    for copy in range(out_ref.shape[0]):
        out_ref[copy, :, :width] = tokens_ref[...]
        out_ref[copy, :, width:] = grads


def prepare(copies, block, rewards, selected, pad_mask, tokens, cotangent):
    rows, width = tokens.shape
    smem = pl.BlockSpec(memory_space=pltpu.SMEM)
    vmem = pl.BlockSpec(memory_space=pltpu.VMEM)
    return pl.pallas_call(
        prepare_kernel,
        out_shape=jax.ShapeDtypeStruct((copies, rows, 2 * width), bf16),
        in_specs=[smem, smem, smem, vmem, vmem, vmem],
        out_specs=vmem,
    )(block.reshape(1), rewards, selected, pad_mask.reshape(rows, 1), tokens, cotangent)


def unit_values(summed, unit_width):
    gate_value = summed[:, :unit_width] * (1.0 / SCALE_UP)
    up_value = summed[:, unit_width : 2 * unit_width] * (1.0 / SCALE_UP)
    back_value = summed[:, 2 * unit_width :] * (1.0 / SCALE_BACK)
    sigmoid_gate = jax.nn.sigmoid(gate_value)
    active = gate_value * sigmoid_gate
    hidden = (active * up_value).astype(bf16)
    gate_back = (
        back_value * up_value * sigmoid_gate * (1.0 + gate_value * (1.0 - sigmoid_gate))
    ).astype(bf16)
    up_back = (back_value * active).astype(bf16)
    return jnp.concatenate([hidden, gate_back, up_back], axis=1)


def body(tokens, cotangent, pad_mask, rewards, selected, gate_weight, up_weight, down_weight):
    n_y = lax.axis_size("y")
    n_k = lax.axis_size("zhi")
    y = lax.axis_index("y")
    k = lax.axis_index("zhi")
    rows, width = tokens.shape
    units = gate_weight.shape[1]
    block = lax.axis_index(ROW) * n_k + k
    copies = lax.axis_size(("zlo", "x"))
    spread = prepare(copies, block, rewards, selected, pad_mask, tokens, cotangent)
    mine = lax.all_to_all(spread, ("zlo", "x"), 0, 0)
    other = shift(mine, "core", 1)
    half = copies * rows
    part = half // n_y

    pieces = []
    halves = [mine.reshape(half, 2 * width), other.reshape(half, 2 * width)]
    for rows_in in halves:
        gate = jnp.dot(rows_in[:, :width], gate_weight, preferred_element_type=f32) * SCALE_UP
        up = jnp.dot(rows_in[:, :width], up_weight, preferred_element_type=f32) * SCALE_UP
        back = SCALE_BACK * lax.dot_general(
            rows_in[:, width:], down_weight, (((1,), (1,)), ((), ())), preferred_element_type=f32
        )
        whole = jnp.concatenate([gate, up, back], axis=1).astype(jnp.float16)
        pieces.append(whole.reshape(n_y, part, 3 * units))
    sums = lax.all_to_all(jnp.concatenate(pieces, axis=1), "y", 0, 0)
    values = unit_values(jnp.sum(sums.astype(f32), axis=0), units)
    share = 2 * part

    replicas = lax.all_to_all(
        jnp.broadcast_to(values[None], (n_k, share, 3 * units)), "zhi", 0, 0
    )

    chunks = []
    for c in range(2):
        held = replicas[c * n_k // 2 : (c + 1) * n_k // 2]
        right = left = held
        at = {0: held}
        for s in range(1, n_y // 2):
            right = shift(right, "y", 1)
            left = shift(left, "y", -1)
            at[n_y - s] = right
            at[s] = left
        top = shift(right[:1], "y", 1)
        low = shift(left[1:], "y", -1)
        at[n_y // 2] = jnp.concatenate([top, low], axis=0)
        chunks.append(jnp.stack([at[r] for r in range(n_y)], axis=0))
    every = jnp.concatenate(chunks, axis=1).reshape(n_y * n_k * share, 3 * units)

    quarter = width // n_k
    both = jnp.stack([h.reshape(n_y, part, 2, n_k, quarter) for h in halves], axis=1)
    got = []
    for t in range(n_k):
        owner = (k - t) % n_k
        cut = lax.dynamic_index_in_dim(both, owner, axis=4, keepdims=False)
        cut = cut.reshape(n_y, share, 2 * quarter)
        got.append(cut if t == 0 else shift(cut, "zhi", -t))
    near = jnp.stack(got + got[:-1], axis=1)
    near = lax.dynamic_slice_in_dim(near, (n_k - k) % n_k, n_k, axis=1)
    near = jnp.concatenate([near, near[:-1]], axis=0)
    near = lax.dynamic_slice_in_dim(near, y, n_y, axis=0)
    near = near.reshape(n_y * n_k * share, 2 * quarter)

    contract = (((0,), (0,)), ((), ()))
    gate_grad = lax.dot_general(
        near[:, :quarter], every[:, units : 2 * units], contract, preferred_element_type=f32
    )
    up_grad = lax.dot_general(
        near[:, :quarter], every[:, 2 * units :], contract, preferred_element_type=f32
    )
    down_grad = lax.dot_general(
        every[:, :units], near[:, quarter:], contract, preferred_element_type=f32
    )
    return (gate_grad, up_grad, down_grad)


def solution(mesh):
    n_row, n_col, n_rep = mesh.devices.shape
    fine = Mesh(
        mesh.devices.reshape(Z_LO, n_row // (Z_LO * CORES), CORES, n_col, n_rep),
        ("zlo", "x", "core", "y", "zhi"),
    )
    blocks = ROW + ("zhi",)
    placed = (
        P(blocks, "y"),
        P(blocks, "y"),
        P(blocks),
        P(),
        P(),
        P("y", ROW),
        P("y", ROW),
        P(ROW, "y"),
    )
    return jax.shard_map(
        body,
        mesh=fine,
        in_specs=placed,
        out_specs=(P(("y", "zhi"), ROW), P(("y", "zhi"), ROW), P(ROW, ("y", "zhi"))),
        check_vma=False,
    )
```

time: 265 us -> 184 us (0.69)
  waiting for transfers between devices: 195 us -> 39 us
  starting transfers between devices: 0.12 us -> 111 us
  blocking collectives: 34.4 us -> 0 us
  local copies, waits for them, and re-layouts: 7.55 us -> 21.3 us
  between operations: 13.9 us -> 1.21 us
  other arithmetic: 6.84 us -> 2 us
    all_gather x2 -> x0, waiting for transfers between devices: 148 us -> none  [the longest x1 79.3 us: body(): replica_rows = lax.all_gather(stacked, 'row', axis=0, tiled=True)]
    ppermute x0 -> x20, starting transfers between devices: none -> 79.8 us  [shift(): return lax.ppermute(value, axis, [(i, (i + step) % n) for i in range(n)])]
    reduce_scatter x1 -> x0, waiting for transfers between devices: 46.8 us -> none  [body(): lax.psum_scatter(jnp.concatenate([gate_part, up_part, back_part], axis=1)...]
    all_to_all x1 -> x0, blocking collectives: 34.4 us -> none  [body(): lax.all_to_all(replica_rows, 'rep', split_axis=2, concat_axis=0, tiled=True)]
    all_to_all x0 -> x3, starting transfers between devices: none -> 31.2 us  [the longest x1 16.4 us: body(): mine = lax.all_to_all(spread, ('zlo', 'x'), 0, 0)]
    all_to_all x0 -> x3, waiting for transfers between devices: none -> 21.2 us  [the longest x1 10.8 us: body(): mine = lax.all_to_all(spread, ('zlo', 'x'), 0, 0)]
    ppermute x0 -> x20, waiting for transfers between devices: none -> 17.9 us  [shift(): return lax.ppermute(value, axis, [(i, (i + step) % n) for i in range(n)])]
    unnamed x10 -> x28, local copies, waits for them, and re-layouts: 0.32 us -> 7.48 us
  transfers between devices with their start and end apart: 3 -> 23, of which waited for: 3 -> 7; matrix products, arithmetic and copies ran while one was open for 1% -> 11% of each run, Pallas kernels for 0% -> 0%
where the time goes in v1:
time: 184 us; the launch traced here: 182 us
  starting transfers between devices  111 us (60%)
  waiting for transfers between devices  39 us (21%)
  local copies, waits for them, and re-layouts  21.3 us (12%)
  matrix products  6.04 us (3%)
  other arithmetic  2 us (1%)
    ppermute x20, starting transfers between devices, shift(): return lax.ppermute(value, axis, [(i, (i + step) % n) for i in range(n)])  79.8 us
    ppermute x20, waiting for transfers between devices, shift(): return lax.ppermute(value, axis, [(i, (i + step) % n) for i in range(n)])  17.9 us
    all_to_all x1, starting transfers between devices, body(): mine = lax.all_to_all(spread, ('zlo', 'x'), 0, 0)  16.4 us
    all_to_all x1, waiting for transfers between devices, body(): mine = lax.all_to_all(spread, ('zlo', 'x'), 0, 0)  10.8 us
    all_to_all x1, waiting for transfers between devices, body(): lax.all_to_all(jnp.broadcast_to(values[None], (n_k, share, 3 * units)), '...  10.3 us
    all_to_all x1, starting transfers between devices, body(): lax.all_to_all(jnp.broadcast_to(values[None], (n_k, share, 3 * units)), '...  9.27 us
    unnamed x28, local copies, waits for them, and re-layouts  7.48 us
    all_to_all x1, starting transfers between devices, body(): sums = lax.all_to_all(jnp.concatenate(pieces, axis=1), 'y', 0, 0)  5.48 us
  transfers between devices with their start and end apart: 23, of which 7 were waited for; matrix products, arithmetic and copies ran while one was open for 11% of the time, Pallas kernels for 0%

profile of v1, /device:TPU:14, one launch (start us, length us, event | category | flops | bytes accessed | tf_op | source)
XLA Modules:
  0.0 182.2 jit_solution(3771235533585438012)
XLA Ops:
  0.7 1.4 copy.15.pad_ref
  2.1 1.8 shard_map.103
  3.8 16.4 %all-to-all-start = ((bf16[16,8,2048]{2,1,0:T(8,128)(2,1)}), bf16[16,8,2048]{2,1,0:T(8,128)(2,1)S(1)}, u32[]{:S(2)}, u32[]{:S(2)}) async-start(bf16[16,8,2048]{2,1,0:T(8,128)(2,1)} %shard_map.103), calls=%async_computation | async-start | bytes 1048576 | tf_op jit(solution)/shard_map/all_to_all | solution.py:76
  20.2 10.8 %all-to-all-done = bf16[16,8,2048]{2,1,0:T(8,128)(2,1)S(1)} async-done(((bf16[16,8,2048]{2,1,0:T(8,128)(2,1)}), bf16[16,8,2048]{2,1,0:T(8,128)(2,1)S(1)}, u32[]{:S(2)}, u32[]{:S(2)}) %all-to-all-start) | async-done | bytes 524320 | tf_op jit(solution)/shard_map/all_to_all | solution.py:76
  31.1 0.3 fusion
  31.4 1.9 %collective-permute-start = (bf16[16,8,2048]{2,1,0:T(8,128)(2,1)S(1)}, bf16[16,8,2048]{2,1,0:T(8,128)(2,1)S(1)}, u32[]{:S(2)}, u32[]{:S(2)}) collective-permute-start(bf16[16,8,2048]{2,1,0:T(8,128)(2,1)S(1)} %all-to-all-done), channel_id=1, source_target_pairs={{0,32},{32,0},{1,33},{33,1},{2,34},{34,2},{3,35},{35,3},{4,36},{36... | collective-permute-start | bytes 1572872 | tf_op jit(solution)/shard_map/ppermute | solution.py:22
  33.4 1.2 stack_reshape_reshape.6
  34.5 2.5 %copy_dynamic-update-slice_fusion.1 = bf16[8,2,16,2,4,256]{5,3,2,1,0,4:T(2,128)(2,1)} fusion(bf16[8,1,16,2,4,256]{5,4,3,2,0,1:T(4,128)(2,1)} %stack_reshape_reshape.6), kind=kLoop, calls=%fused_computation.26 | loop fusion | bytes 1048576
  37.0 0.3 fusion.1
  37.3 0.5 fusion.2
  37.9 0.3 fusion.3
  38.2 0.3 fusion.4
  38.5 0.5 fusion.5
  39.0 1.2 maximum_maximum_fusion
  40.2 5.5 %all-to-all-start.1 = ((f16[8,32,1536]{2,1,0:T(8,128)(2,1)}), f16[8,32,1536]{2,1,0:T(8,128)(2,1)S(1)}, u32[]{:S(2)}, u32[]{:S(2)}) async-start(f16[8,32,1536]{2,1,0:T(8,128)(2,1)} %maximum_maximum_fusion), calls=%async_computation.1 | async-start | bytes 1572864 | tf_op jit(solution)/shard_map/all_to_all | solution.py:91
  45.6 1.2 stack_reshape_reshape.7
  46.8 1.6 copy_dynamic-update-slice_fusion
  48.4 2.0 %constant_dynamic-slice_fusion.2 = (bf16[8,2,16,2,1,256]{5,3,2,1,0,4:T(2,128)(2,1)S(1)}, bf16[8,2,16,2,1,256]{5,3,2,1,0,4:T(2,128)(2,1)}, bf16[8,2,16,2,1,256]{5...) fusion(bf16[8,2,16,2,4,256]{5,3,2,1,0,4:T(2,128)(2,1)S(1)} %copy_dynamic-update-slice_fusion, s32[]{:T(128)S(6)} %select_n.49, ...), kind=kLoop, calls=%fused_computation.71 | loop fusion | bytes 2097168 | tf_op jit(solution)/shard_map/jit(dynamic_index_in_dim)/dynamic_slice | solution.py:120
  50.4 0.2 reshape.54
  50.6 15.5 %collective-permute-start.1 = (bf16[8,32,512]{2,1,0:T(8,128)(2,1)S(1)}, bf16[8,32,512]{2,1,0:T(8,128)(2,1)S(1)}, u32[]{:S(2)}, u32[]{:S(2)}) collective-permute-start(bf16[8,32,512]{2,1,0:T(8,128)(2,1)S(1)} %reshape.54), channel_id=1, source_target_pairs={{0,3},{1,0},{2,1},{3,2},{4,7},{5,4},{6,5},{7,6},{8,11},{9,8},{10,9... | collective-permute-start | bytes 786440 | tf_op jit(solution)/shard_map/ppermute | solution.py:22
  66.1 1.1 stack_reshape.4
  67.3 1.1 reshape.55
  68.4 1.9 %collective-permute-start.2 = (bf16[8,32,512]{2,1,0:T(8,128)(2,1)S(1)}, bf16[8,32,512]{2,1,0:T(8,128)(2,1)S(1)}, u32[]{:S(2)}, u32[]{:S(2)}) collective-permute-start(bf16[8,32,512]{2,1,0:T(8,128)(2,1)S(1)} %reshape.55), channel_id=1, source_target_pairs={{0,2},{1,3},{2,0},{3,1},{4,6},{5,7},{6,4},{7,5},{8,10},{9,11},{10,... | collective-permute-start | bytes 786440 | tf_op jit(solution)/shard_map/ppermute | solution.py:22
  70.3 0.7 constant_dynamic-update-slice_fusion.1
  71.0 0.9 reshape.56
  71.9 4.3 %collective-permute-start.3 = (bf16[8,32,512]{2,1,0:T(8,128)(2,1)}, bf16[8,32,512]{2,1,0:T(8,128)(2,1)S(1)}, u32[]{:S(2)}, u32[]{:S(2)}) collective-permute-start(bf16[8,32,512]{2,1,0:T(8,128)(2,1)} %reshape.56), channel_id=1, source_target_pairs={{0,1},{1,2},{2,3},{3,0},{4,5},{5,6},{6,7},{7,4},{8,9},{9,10},{10,1... | collective-permute-start | bytes 786440 | tf_op jit(solution)/shard_map/ppermute | solution.py:22
  76.2 12.7 %collective-permute-done.1 = bf16[8,32,512]{2,1,0:T(8,128)(2,1)S(1)} collective-permute-done((bf16[8,32,512]{2,1,0:T(8,128)(2,1)S(1)}, bf16[8,32,512]{2,1,0:T(8,128)(2,1)S(1)}, u32[]{:S(2)}, u32[]{:S(2)}) %collective-permute-start.1) | collective-permute-done | bytes 262176 | tf_op jit(solution)/shard_map/ppermute | solution.py:22
  88.9 0.7 bitcast_dynamic-update-slice_fusion.3
  89.6 0.7 bitcast_dynamic-update-slice_fusion.1
  90.4 1.3 collective-permute-done.3
  91.7 0.8 bitcast_dynamic-update-slice_fusion
  92.4 0.7 constant_dynamic-update-slice_fusion
  93.1 0.7 bitcast_dynamic-update-slice_fusion.4
  93.9 0.1 convert_reduce_fusion
  94.1 0.8 broadcast_in_dim.2
  94.8 9.3 %all-to-all-start.2 = ((bf16[4,32,1536]{2,1,0:T(8,128)(2,1)}), bf16[4,32,1536]{2,1,0:T(8,128)(2,1)S(1)}, u32[]{:S(2)}, u32[]{:S(2)}) async-start(bf16[4,32,1536]{2,1,0:T(8,128)(2,1)} %broadcast_in_dim.2), calls=%async_computation.2 | async-start | bytes 786432 | tf_op jit(solution)/shard_map/all_to_all | solution.py:95
  104.1 0.8 bitcast_dynamic-update-slice_fusion.2
  104.9 1.4 constant_dynamic-slice_fusion
  106.2 0.4 copy-done.3
  106.7 0.4 fusion.6
  107.2 10.3 %all-to-all-done.2 = bf16[4,32,1536]{2,1,0:T(8,128)(2,1)S(1)} async-done(((bf16[4,32,1536]{2,1,0:T(8,128)(2,1)}), bf16[4,32,1536]{2,1,0:T(8,128)(2,1)S(1)}, u32[]{:S(2)}, u32[]{:S(2)}) %all-to-all-start.2) | async-done | bytes 393248 | tf_op jit(solution)/shard_map/all_to_all | solution.py:95
  117.5 4.9 %collective-permute-start.4 = (bf16[2,32,1536]{2,1,0:T(8,128)(2,1)S(1)}, bf16[2,32,1536]{2,1,0:T(8,128)(2,1)S(1)}, u32[]{:S(2)}, u32[]{:S(2)}) collective-permute-start(bf16[2,32,1536]{2,1,0:T(8,128)(2,1)S(1)} %get-tuple-element.7), channel_id=1, source_target_pairs={{0,28},{4,0},{8,4},{12,8},{16,12},{20,16},{24,20},{28,24},{1,29},{... | collective-permute-start | bytes 589832 | tf_op jit(solution)/shard_map/ppermute | solution.py:22
  122.4 1.9 %collective-permute-start.7 = (bf16[2,32,1536]{2,1,0:T(8,128)(2,1)S(1)}, bf16[2,32,1536]{2,1,0:T(8,128)(2,1)S(1)}, u32[]{:S(2)}, u32[]{:S(2)}) collective-permute-start(bf16[2,32,1536]{2,1,0:T(8,128)(2,1)S(1)} %get-tuple-element.7), channel_id=1, source_target_pairs={{0,4},{4,8},{8,12},{12,16},{16,20},{20,24},{24,28},{28,0},{1,5},{5... | collective-permute-start | bytes 589832 | tf_op jit(solution)/shard_map/ppermute | solution.py:22
  124.3 5.1 %collective-permute-start.12 = (bf16[2,32,1536]{2,1,0:T(8,128)(2,1)S(1)}, bf16[2,32,1536]{2,1,0:T(8,128)(2,1)S(1)}, u32[]{:S(2)}, u32[]{:S(2)}) collective-permute-start(bf16[2,32,1536]{2,1,0:T(8,128)(2,1)S(1)} %get-tuple-element.8), channel_id=1, source_target_pairs={{0,28},{4,0},{8,4},{12,8},{16,12},{20,16},{24,20},{28,24},{1,29},{... | collective-permute-start | bytes 589832 | tf_op jit(solution)/shard_map/ppermute | solution.py:22
  129.5 1.9 %collective-permute-start.15 = (bf16[2,32,1536]{2,1,0:T(8,128)(2,1)S(1)}, bf16[2,32,1536]{2,1,0:T(8,128)(2,1)S(1)}, u32[]{:S(2)}, u32[]{:S(2)}) collective-permute-start(bf16[2,32,1536]{2,1,0:T(8,128)(2,1)S(1)} %get-tuple-element.8), channel_id=1, source_target_pairs={{0,4},{4,8},{8,12},{12,16},{16,20},{20,24},{24,28},{28,0},{1,5},{5... | collective-permute-start | bytes 589832 | tf_op jit(solution)/shard_map/ppermute | solution.py:22
  131.5 5.1 %collective-permute-start.5 = (bf16[2,32,1536]{2,1,0:T(8,128)(2,1)S(1)}, bf16[2,32,1536]{2,1,0:T(8,128)(2,1)S(1)}, u32[]{:S(2)}, u32[]{:S(2)}) collective-permute-start(bf16[2,32,1536]{2,1,0:T(8,128)(2,1)S(1)} %collective-permute-done.4), channel_id=1, source_target_pairs={{0,28},{4,0},{8,4},{12,8},{16,12},{20,16},{24,20},{28,24},{1,29},{... | collective-permute-start | bytes 589832 | tf_op jit(solution)/shard_map/ppermute | solution.py:22
  136.6 1.9 %collective-permute-start.8 = (bf16[2,32,1536]{2,1,0:T(8,128)(2,1)S(1)}, bf16[2,32,1536]{2,1,0:T(8,128)(2,1)S(1)}, u32[]{:S(2)}, u32[]{:S(2)}) collective-permute-start(bf16[2,32,1536]{2,1,0:T(8,128)(2,1)S(1)} %collective-permute-done.7), channel_id=1, source_target_pairs={{0,4},{4,8},{8,12},{12,16},{16,20},{20,24},{24,28},{28,0},{1,5},{5... | collective-permute-start | bytes 589832 | tf_op jit(solution)/shard_map/ppermute | solution.py:22
  138.6 5.1 %collective-permute-start.13 = (bf16[2,32,1536]{2,1,0:T(8,128)(2,1)S(1)}, bf16[2,32,1536]{2,1,0:T(8,128)(2,1)S(1)}, u32[]{:S(2)}, u32[]{:S(2)}) collective-permute-start(bf16[2,32,1536]{2,1,0:T(8,128)(2,1)S(1)} %collective-permute-done.12), channel_id=1, source_target_pairs={{0,28},{4,0},{8,4},{12,8},{16,12},{20,16},{24,20},{28,24},{1,29},{... | collective-permute-start | bytes 589832 | tf_op jit(solution)/shard_map/ppermute | solution.py:22
  143.7 1.9 %collective-permute-start.16 = (bf16[2,32,1536]{2,1,0:T(8,128)(2,1)S(1)}, bf16[2,32,1536]{2,1,0:T(8,128)(2,1)S(1)}, u32[]{:S(2)}, u32[]{:S(2)}) collective-permute-start(bf16[2,32,1536]{2,1,0:T(8,128)(2,1)S(1)} %collective-permute-done.15), channel_id=1, source_target_pairs={{0,4},{4,8},{8,12},{12,16},{16,20},{20,24},{24,28},{28,0},{1,5},{5... | collective-permute-start | bytes 589832 | tf_op jit(solution)/shard_map/ppermute | solution.py:22
  145.7 5.1 %collective-permute-start.6 = (bf16[2,32,1536]{2,1,0:T(8,128)(2,1)S(1)}, bf16[2,32,1536]{2,1,0:T(8,128)(2,1)S(1)}, u32[]{:S(2)}, u32[]{:S(2)}) collective-permute-start(bf16[2,32,1536]{2,1,0:T(8,128)(2,1)S(1)} %collective-permute-done.5), channel_id=1, source_target_pairs={{0,28},{4,0},{8,4},{12,8},{16,12},{20,16},{24,20},{28,24},{1,29},{... | collective-permute-start | bytes 589832 | tf_op jit(solution)/shard_map/ppermute | solution.py:22
  150.9 1.9 %collective-permute-start.9 = (bf16[2,32,1536]{2,1,0:T(8,128)(2,1)S(1)}, bf16[2,32,1536]{2,1,0:T(8,128)(2,1)S(1)}, u32[]{:S(2)}, u32[]{:S(2)}) collective-permute-start(bf16[2,32,1536]{2,1,0:T(8,128)(2,1)S(1)} %collective-permute-done.8), channel_id=1, source_target_pairs={{0,4},{4,8},{8,12},{12,16},{16,20},{20,24},{24,28},{28,0},{1,5},{5... | collective-permute-start | bytes 589832 | tf_op jit(solution)/shard_map/ppermute | solution.py:22
  152.8 5.1 %collective-permute-start.14 = (bf16[2,32,1536]{2,1,0:T(8,128)(2,1)S(1)}, bf16[2,32,1536]{2,1,0:T(8,128)(2,1)S(1)}, u32[]{:S(2)}, u32[]{:S(2)}) collective-permute-start(bf16[2,32,1536]{2,1,0:T(8,128)(2,1)S(1)} %collective-permute-done.13), channel_id=1, source_target_pairs={{0,28},{4,0},{8,4},{12,8},{16,12},{20,16},{24,20},{28,24},{1,29},{... | collective-permute-start | bytes 589832 | tf_op jit(solution)/shard_map/ppermute | solution.py:22
  157.9 1.9 %collective-permute-start.17 = (bf16[2,32,1536]{2,1,0:T(8,128)(2,1)S(1)}, bf16[2,32,1536]{2,1,0:T(8,128)(2,1)S(1)}, u32[]{:S(2)}, u32[]{:S(2)}) collective-permute-start(bf16[2,32,1536]{2,1,0:T(8,128)(2,1)S(1)} %collective-permute-done.16), channel_id=1, source_target_pairs={{0,4},{4,8},{8,12},{12,16},{16,20},{20,24},{24,28},{28,0},{1,5},{5... | collective-permute-start | bytes 589832 | tf_op jit(solution)/shard_map/ppermute | solution.py:22
  159.9 1.7 collective-permute-done.9
  161.7 1.9 %collective-permute-start.10 = (bf16[1,32,1536]{2,1,0:T(8,128)(2,1)S(1)}, bf16[1,32,1536]{2,1,0:T(8,128)(2,1)S(1)}, u32[]{:S(2)}, u32[]{:S(2)}) collective-permute-start(bf16[1,32,1536]{2,1,0:T(8,128)(2,1)S(1)} %slice.88), channel_id=1, source_target_pairs={{0,4},{4,8},{8,12},{12,16},{16,20},{20,24},{24,28},{28,0},{1,5},{5... | collective-permute-start | bytes 294920 | tf_op jit(solution)/shard_map/ppermute | solution.py:22
  163.6 5.1 %collective-permute-start.11 = (bf16[1,32,1536]{2,1,0:T(8,128)(2,1)S(1)}, bf16[1,32,1536]{2,1,0:T(8,128)(2,1)S(1)}, u32[]{:S(2)}, u32[]{:S(2)}) collective-permute-start(bf16[1,32,1536]{2,1,0:T(8,128)(2,1)S(1)} %slice.89), channel_id=1, source_target_pairs={{0,28},{4,0},{8,4},{12,8},{16,12},{20,16},{24,20},{28,24},{1,29},{... | collective-permute-start | bytes 294920 | tf_op jit(solution)/shard_map/ppermute | solution.py:22
  168.8 1.9 %collective-permute-start.18 = (bf16[1,32,1536]{2,1,0:T(8,128)(2,1)S(1)}, bf16[1,32,1536]{2,1,0:T(8,128)(2,1)S(1)}, u32[]{:S(2)}, u32[]{:S(2)}) collective-permute-start(bf16[1,32,1536]{2,1,0:T(8,128)(2,1)S(1)} %slice.91), channel_id=1, source_target_pairs={{0,4},{4,8},{8,12},{12,16},{16,20},{20,24},{24,28},{28,0},{1,5},{5... | collective-permute-start | bytes 294920 | tf_op jit(solution)/shard_map/ppermute | solution.py:22
  170.7 5.1 %collective-permute-start.19 = (bf16[1,32,1536]{2,1,0:T(8,128)(2,1)S(1)}, bf16[1,32,1536]{2,1,0:T(8,128)(2,1)S(1)}, u32[]{:S(2)}, u32[]{:S(2)}) collective-permute-start(bf16[1,32,1536]{2,1,0:T(8,128)(2,1)S(1)} %slice.92), channel_id=1, source_target_pairs={{0,28},{4,0},{8,4},{12,8},{16,12},{20,16},{24,20},{28,24},{1,29},{... | collective-permute-start | bytes 294920 | tf_op jit(solution)/shard_map/ppermute | solution.py:22
  176.0 0.5 collective-permute-done.18
  176.5 1.6 collective-permute-done.19
  178.1 0.3 pad_maximum_fusion
  178.4 1.3 fusion.7
  179.7 1.3 fusion.9
  181.0 1.3 fusion.11
  (49 shorter events, 0.6 us)
Async XLA Ops:
  0.6 30.5 %copy-start = (bf16[1024,512]{1,0:T(8,128)(2,1)S(1)}, bf16[1024,512]{1,0:T(8,128)(2,1)}, u32[]{:S(2)}) copy-start(bf16[1024,512]{1,0:T(8,128)(2,1)} %param.13) | copy-start | bytes 3145732
  3.8 27.3 %all-to-all-start = ((bf16[16,8,2048]{2,1,0:T(8,128)(2,1)}), bf16[16,8,2048]{2,1,0:T(8,128)(2,1)S(1)}, u32[]{:S(2)}, u32[]{:S(2)}) async-start(bf16[16,8,2048]{2,1,0:T(8,128)(2,1)} %shard_map.103), calls=%async_computation | async-start | bytes 1048576 | tf_op jit(solution)/shard_map/all_to_all | solution.py:76
  31.1 5.9 %copy-start.1 = (bf16[1024,512]{1,0:T(8,128)(2,1)S(1)}, bf16[1024,512]{1,0:T(8,128)(2,1)}, u32[]{:S(2)}) copy-start(bf16[1024,512]{1,0:T(8,128)(2,1)} %param.14) | copy-start | bytes 3145732
  31.4 6.4 %collective-permute-start = (bf16[16,8,2048]{2,1,0:T(8,128)(2,1)S(1)}, bf16[16,8,2048]{2,1,0:T(8,128)(2,1)S(1)}, u32[]{:S(2)}, u32[]{:S(2)}) collective-permute-start(bf16[16,8,2048]{2,1,0:T(8,128)(2,1)S(1)} %all-to-all-done), channel_id=1, source_target_pairs={{0,32},{32,0},{1,33},{33,1},{2,34},{34,2},{3,35},{35,3},{4,36},{36... | collective-permute-start | bytes 1572872 | tf_op jit(solution)/shard_map/ppermute | solution.py:22
  34.5 2.8 %copy-start.2 = (bf16[512,1024]{1,0:T(8,128)(2,1)S(1)}, bf16[512,1024]{1,0:T(8,128)(2,1)}, u32[]{:S(2)}) copy-start(bf16[512,1024]{1,0:T(8,128)(2,1)} %param.15) | copy-start | bytes 3145732
  40.1 6.7 %copy-start.4 = (bf16[8,2,16,2,4,256]{5,3,2,1,0,4:T(2,128)(2,1)S(1)}, bf16[8,2,16,2,4,256]{5,3,2,1,0,4:T(2,128)(2,1)}, u32[]{:S(2)}) copy-start(bf16[8,2,16,2,4,256]{5,3,2,1,0,4:T(2,128)(2,1)} %copy_dynamic-update-slice_fusion.1) | copy-start | bytes 3145732
  40.2 53.7 %all-to-all-start.1 = ((f16[8,32,1536]{2,1,0:T(8,128)(2,1)}), f16[8,32,1536]{2,1,0:T(8,128)(2,1)S(1)}, u32[]{:S(2)}, u32[]{:S(2)}) async-start(f16[8,32,1536]{2,1,0:T(8,128)(2,1)} %maximum_maximum_fusion), calls=%async_computation.1 | async-start | bytes 1572864 | tf_op jit(solution)/shard_map/all_to_all | solution.py:91
  50.6 38.3 %collective-permute-start.1 = (bf16[8,32,512]{2,1,0:T(8,128)(2,1)S(1)}, bf16[8,32,512]{2,1,0:T(8,128)(2,1)S(1)}, u32[]{:S(2)}, u32[]{:S(2)}) collective-permute-start(bf16[8,32,512]{2,1,0:T(8,128)(2,1)S(1)} %reshape.54), channel_id=1, source_target_pairs={{0,3},{1,0},{2,1},{3,2},{4,7},{5,4},{6,5},{7,6},{8,11},{9,8},{10,9... | collective-permute-start | bytes 786440 | tf_op jit(solution)/shard_map/ppermute | solution.py:22
  68.4 21.2 %collective-permute-start.2 = (bf16[8,32,512]{2,1,0:T(8,128)(2,1)S(1)}, bf16[8,32,512]{2,1,0:T(8,128)(2,1)S(1)}, u32[]{:S(2)}, u32[]{:S(2)}) collective-permute-start(bf16[8,32,512]{2,1,0:T(8,128)(2,1)S(1)} %reshape.55), channel_id=1, source_target_pairs={{0,2},{1,3},{2,0},{3,1},{4,6},{5,7},{6,4},{7,5},{8,10},{9,11},{10,... | collective-permute-start | bytes 786440 | tf_op jit(solution)/shard_map/ppermute | solution.py:22
  71.9 19.8 %collective-permute-start.3 = (bf16[8,32,512]{2,1,0:T(8,128)(2,1)}, bf16[8,32,512]{2,1,0:T(8,128)(2,1)S(1)}, u32[]{:S(2)}, u32[]{:S(2)}) collective-permute-start(bf16[8,32,512]{2,1,0:T(8,128)(2,1)} %reshape.56), channel_id=1, source_target_pairs={{0,1},{1,2},{2,3},{3,0},{4,5},{5,6},{6,7},{7,4},{8,9},{9,10},{10,1... | collective-permute-start | bytes 786440 | tf_op jit(solution)/shard_map/ppermute | solution.py:22
  94.8 22.7 %all-to-all-start.2 = ((bf16[4,32,1536]{2,1,0:T(8,128)(2,1)}), bf16[4,32,1536]{2,1,0:T(8,128)(2,1)S(1)}, u32[]{:S(2)}, u32[]{:S(2)}) async-start(bf16[4,32,1536]{2,1,0:T(8,128)(2,1)} %broadcast_in_dim.2), calls=%async_computation.2 | async-start | bytes 786432 | tf_op jit(solution)/shard_map/all_to_all | solution.py:95
  104.9 1.8 copy-start.3
  117.5 13.9 %collective-permute-start.4 = (bf16[2,32,1536]{2,1,0:T(8,128)(2,1)S(1)}, bf16[2,32,1536]{2,1,0:T(8,128)(2,1)S(1)}, u32[]{:S(2)}, u32[]{:S(2)}) collective-permute-start(bf16[2,32,1536]{2,1,0:T(8,128)(2,1)S(1)} %get-tuple-element.7), channel_id=1, source_target_pairs={{0,28},{4,0},{8,4},{12,8},{16,12},{20,16},{24,20},{28,24},{1,29},{... | collective-permute-start | bytes 589832 | tf_op jit(solution)/shard_map/ppermute | solution.py:22
  122.4 14.2 %collective-permute-start.7 = (bf16[2,32,1536]{2,1,0:T(8,128)(2,1)S(1)}, bf16[2,32,1536]{2,1,0:T(8,128)(2,1)S(1)}, u32[]{:S(2)}, u32[]{:S(2)}) collective-permute-start(bf16[2,32,1536]{2,1,0:T(8,128)(2,1)S(1)} %get-tuple-element.7), channel_id=1, source_target_pairs={{0,4},{4,8},{8,12},{12,16},{16,20},{20,24},{24,28},{28,0},{1,5},{5... | collective-permute-start | bytes 589832 | tf_op jit(solution)/shard_map/ppermute | solution.py:22
  124.3 14.2 %collective-permute-start.12 = (bf16[2,32,1536]{2,1,0:T(8,128)(2,1)S(1)}, bf16[2,32,1536]{2,1,0:T(8,128)(2,1)S(1)}, u32[]{:S(2)}, u32[]{:S(2)}) collective-permute-start(bf16[2,32,1536]{2,1,0:T(8,128)(2,1)S(1)} %get-tuple-element.8), channel_id=1, source_target_pairs={{0,28},{4,0},{8,4},{12,8},{16,12},{20,16},{24,20},{28,24},{1,29},{... | collective-permute-start | bytes 589832 | tf_op jit(solution)/shard_map/ppermute | solution.py:22
  129.5 14.3 %collective-permute-start.15 = (bf16[2,32,1536]{2,1,0:T(8,128)(2,1)S(1)}, bf16[2,32,1536]{2,1,0:T(8,128)(2,1)S(1)}, u32[]{:S(2)}, u32[]{:S(2)}) collective-permute-start(bf16[2,32,1536]{2,1,0:T(8,128)(2,1)S(1)} %get-tuple-element.8), channel_id=1, source_target_pairs={{0,4},{4,8},{8,12},{12,16},{16,20},{20,24},{24,28},{28,0},{1,5},{5... | collective-permute-start | bytes 589832 | tf_op jit(solution)/shard_map/ppermute | solution.py:22
  131.5 14.2 %collective-permute-start.5 = (bf16[2,32,1536]{2,1,0:T(8,128)(2,1)S(1)}, bf16[2,32,1536]{2,1,0:T(8,128)(2,1)S(1)}, u32[]{:S(2)}, u32[]{:S(2)}) collective-permute-start(bf16[2,32,1536]{2,1,0:T(8,128)(2,1)S(1)} %collective-permute-done.4), channel_id=1, source_target_pairs={{0,28},{4,0},{8,4},{12,8},{16,12},{20,16},{24,20},{28,24},{1,29},{... | collective-permute-start | bytes 589832 | tf_op jit(solution)/shard_map/ppermute | solution.py:22
  136.6 14.2 %collective-permute-start.8 = (bf16[2,32,1536]{2,1,0:T(8,128)(2,1)S(1)}, bf16[2,32,1536]{2,1,0:T(8,128)(2,1)S(1)}, u32[]{:S(2)}, u32[]{:S(2)}) collective-permute-start(bf16[2,32,1536]{2,1,0:T(8,128)(2,1)S(1)} %collective-permute-done.7), channel_id=1, source_target_pairs={{0,4},{4,8},{8,12},{12,16},{16,20},{20,24},{24,28},{28,0},{1,5},{5... | collective-permute-start | bytes 589832 | tf_op jit(solution)/shard_map/ppermute | solution.py:22
  138.6 14.2 %collective-permute-start.13 = (bf16[2,32,1536]{2,1,0:T(8,128)(2,1)S(1)}, bf16[2,32,1536]{2,1,0:T(8,128)(2,1)S(1)}, u32[]{:S(2)}, u32[]{:S(2)}) collective-permute-start(bf16[2,32,1536]{2,1,0:T(8,128)(2,1)S(1)} %collective-permute-done.12), channel_id=1, source_target_pairs={{0,28},{4,0},{8,4},{12,8},{16,12},{20,16},{24,20},{28,24},{1,29},{... | collective-permute-start | bytes 589832 | tf_op jit(solution)/shard_map/ppermute | solution.py:22
  143.7 14.2 %collective-permute-start.16 = (bf16[2,32,1536]{2,1,0:T(8,128)(2,1)S(1)}, bf16[2,32,1536]{2,1,0:T(8,128)(2,1)S(1)}, u32[]{:S(2)}, u32[]{:S(2)}) collective-permute-start(bf16[2,32,1536]{2,1,0:T(8,128)(2,1)S(1)} %collective-permute-done.15), channel_id=1, source_target_pairs={{0,4},{4,8},{8,12},{12,16},{16,20},{20,24},{24,28},{28,0},{1,5},{5... | collective-permute-start | bytes 589832 | tf_op jit(solution)/shard_map/ppermute | solution.py:22
  145.7 17.9 %collective-permute-start.6 = (bf16[2,32,1536]{2,1,0:T(8,128)(2,1)S(1)}, bf16[2,32,1536]{2,1,0:T(8,128)(2,1)S(1)}, u32[]{:S(2)}, u32[]{:S(2)}) collective-permute-start(bf16[2,32,1536]{2,1,0:T(8,128)(2,1)S(1)} %collective-permute-done.5), channel_id=1, source_target_pairs={{0,28},{4,0},{8,4},{12,8},{16,12},{20,16},{24,20},{28,24},{1,29},{... | collective-permute-start | bytes 589832 | tf_op jit(solution)/shard_map/ppermute | solution.py:22
  150.9 10.8 %collective-permute-start.9 = (bf16[2,32,1536]{2,1,0:T(8,128)(2,1)S(1)}, bf16[2,32,1536]{2,1,0:T(8,128)(2,1)S(1)}, u32[]{:S(2)}, u32[]{:S(2)}) collective-permute-start(bf16[2,32,1536]{2,1,0:T(8,128)(2,1)S(1)} %collective-permute-done.8), channel_id=1, source_target_pairs={{0,4},{4,8},{8,12},{12,16},{16,20},{20,24},{24,28},{28,0},{1,5},{5... | collective-permute-start | bytes 589832 | tf_op jit(solution)/shard_map/ppermute | solution.py:22
  152.8 17.9 %collective-permute-start.14 = (bf16[2,32,1536]{2,1,0:T(8,128)(2,1)S(1)}, bf16[2,32,1536]{2,1,0:T(8,128)(2,1)S(1)}, u32[]{:S(2)}, u32[]{:S(2)}) collective-permute-start(bf16[2,32,1536]{2,1,0:T(8,128)(2,1)S(1)} %collective-permute-done.13), channel_id=1, source_target_pairs={{0,28},{4,0},{8,4},{12,8},{16,12},{20,16},{24,20},{28,24},{1,29},{... | collective-permute-start | bytes 589832 | tf_op jit(solution)/shard_map/ppermute | solution.py:22
  157.9 10.8 %collective-permute-start.17 = (bf16[2,32,1536]{2,1,0:T(8,128)(2,1)S(1)}, bf16[2,32,1536]{2,1,0:T(8,128)(2,1)S(1)}, u32[]{:S(2)}, u32[]{:S(2)}) collective-permute-start(bf16[2,32,1536]{2,1,0:T(8,128)(2,1)S(1)} %collective-permute-done.16), channel_id=1, source_target_pairs={{0,4},{4,8},{8,12},{12,16},{16,20},{20,24},{24,28},{28,0},{1,5},{5... | collective-permute-start | bytes 589832 | tf_op jit(solution)/shard_map/ppermute | solution.py:22
  161.7 14.3 %collective-permute-start.10 = (bf16[1,32,1536]{2,1,0:T(8,128)(2,1)S(1)}, bf16[1,32,1536]{2,1,0:T(8,128)(2,1)S(1)}, u32[]{:S(2)}, u32[]{:S(2)}) collective-permute-start(bf16[1,32,1536]{2,1,0:T(8,128)(2,1)S(1)} %slice.88), channel_id=1, source_target_pairs={{0,4},{4,8},{8,12},{12,16},{16,20},{20,24},{24,28},{28,0},{1,5},{5... | collective-permute-start | bytes 294920 | tf_op jit(solution)/shard_map/ppermute | solution.py:22
  163.6 12.3 %collective-permute-start.11 = (bf16[1,32,1536]{2,1,0:T(8,128)(2,1)S(1)}, bf16[1,32,1536]{2,1,0:T(8,128)(2,1)S(1)}, u32[]{:S(2)}, u32[]{:S(2)}) collective-permute-start(bf16[1,32,1536]{2,1,0:T(8,128)(2,1)S(1)} %slice.89), channel_id=1, source_target_pairs={{0,28},{4,0},{8,4},{12,8},{16,12},{20,16},{24,20},{28,24},{1,29},{... | collective-permute-start | bytes 294920 | tf_op jit(solution)/shard_map/ppermute | solution.py:22
  168.8 7.7 %collective-permute-start.18 = (bf16[1,32,1536]{2,1,0:T(8,128)(2,1)S(1)}, bf16[1,32,1536]{2,1,0:T(8,128)(2,1)S(1)}, u32[]{:S(2)}, u32[]{:S(2)}) collective-permute-start(bf16[1,32,1536]{2,1,0:T(8,128)(2,1)S(1)} %slice.91), channel_id=1, source_target_pairs={{0,4},{4,8},{8,12},{12,16},{16,20},{20,24},{24,28},{28,0},{1,5},{5... | collective-permute-start | bytes 294920 | tf_op jit(solution)/shard_map/ppermute | solution.py:22
  170.7 7.3 %collective-permute-start.19 = (bf16[1,32,1536]{2,1,0:T(8,128)(2,1)S(1)}, bf16[1,32,1536]{2,1,0:T(8,128)(2,1)S(1)}, u32[]{:S(2)}, u32[]{:S(2)}) collective-permute-start(bf16[1,32,1536]{2,1,0:T(8,128)(2,1)S(1)} %slice.92), channel_id=1, source_target_pairs={{0,28},{4,0},{8,4},{12,8},{16,12},{20,16},{24,20},{28,24},{1,29},{... | collective-permute-start | bytes 294920 | tf_op jit(solution)/shard_map/ppermute | solution.py:22

commit v2 on v1

v2 whole, which is shorter than its diff:
```python
import functools

import jax
import jax.numpy as jnp
from jax import lax
from jax.experimental import pallas as pl
from jax.experimental.pallas import tpu as pltpu
from jax.sharding import Mesh
from jax.sharding import PartitionSpec as P

SAMPLES = 8
COMP_LEN = 16
CORES = 2
Z_LO = 2
SCALE_UP = 128.0
SCALE_BACK = 1024.0
ROW = ("zlo", "x", "core")
bf16 = jnp.bfloat16
f16 = jnp.float16
f32 = jnp.float32


def shift(value, axis, step):
    n = lax.axis_size(axis)
    return lax.ppermute(value, axis, [(i, (i + step) % n) for i in range(n)])


def prepare_kernel(block_ref, rewards_ref, selected_ref, pad_ref, tokens_ref, cotangent_ref, x_ref, g_ref):
    rows = tokens_ref.shape[0]
    completion = block_ref[0] * rows // COMP_LEN
    prompt = completion // SAMPLES
    sample = completion % SAMPLES
    reward = rewards_ref[prompt, sample].astype(f32)
    chosen = jnp.where(selected_ref[prompt] == sample, 1.0, 0.0)
    factor = reward / 4.0 + chosen
    row = lax.broadcasted_iota(jnp.int32, (rows, 1), 0)
    weight = jnp.zeros((rows, 1), f32)
    for n in range(rows):
        weight = jnp.where(row == n, pad_ref[n].astype(f32) * factor, weight)
    grads = (weight * cotangent_ref[...].astype(f32)).astype(bf16)
    for copy in range(x_ref.shape[0]):
        x_ref[copy] = tokens_ref[...]
        g_ref[copy] = grads


def prepare(copies, block, rewards, selected, pad_mask, tokens, cotangent):
    smem = pl.BlockSpec(memory_space=pltpu.SMEM)
    vmem = pl.BlockSpec(memory_space=pltpu.VMEM)
    out = jax.ShapeDtypeStruct((copies,) + tokens.shape, bf16)
    return pl.pallas_call(
        prepare_kernel,
        out_shape=(out, out),
        in_specs=[smem, smem, smem, smem, vmem, vmem],
        out_specs=(vmem, vmem),
    )(block.reshape(1), rewards, selected, pad_mask, tokens, cotangent)


def quarters_kernel(order, place_ref, x0_ref, x1_ref, g0_ref, g1_ref, *out_refs):
    n_k = len(out_refs)
    n_y = len(order)
    part = x0_ref.shape[0] // n_y
    quarter = x0_ref.shape[1] // n_k
    y = place_ref[0]
    k = place_ref[1]
    for t in range(n_k):
        owner = lax.rem(k + (n_k - t), n_k)
        lanes = pl.ds(pl.multiple_of(owner * quarter, quarter), quarter)
        for spot, r in enumerate(order):
            share = lax.rem(y + r, n_y)
            rows = pl.ds(pl.multiple_of(share * part, part), part)
            for c, (x_ref, g_ref) in enumerate(((x0_ref, g0_ref), (x1_ref, g1_ref))):
                to = slice((2 * spot + c) * part, (2 * spot + c + 1) * part)
                out_refs[t][to, :quarter] = x_ref[rows, lanes]
                out_refs[t][to, quarter:] = g_ref[rows, lanes]


def cut_quarters(order, n_k, place, x0, x1, g0, g1):
    rows, width = x0.shape
    vmem = pl.BlockSpec(memory_space=pltpu.VMEM)
    out = jax.ShapeDtypeStruct((2 * rows, 2 * width // n_k), bf16)
    return pl.pallas_call(
        functools.partial(quarters_kernel, order),
        out_shape=(out,) * n_k,
        in_specs=[pl.BlockSpec(memory_space=pltpu.SMEM)] + [vmem] * 4,
        out_specs=(vmem,) * n_k,
    )(place, x0, x1, g0, g1)


def unit_values(gate_value, up_value, back_value):
    sigmoid_gate = jax.nn.sigmoid(gate_value)
    active = gate_value * sigmoid_gate
    hidden = (active * up_value).astype(bf16)
    gate_back = (
        back_value * up_value * sigmoid_gate * (1.0 + gate_value * (1.0 - sigmoid_gate))
    ).astype(bf16)
    up_back = (back_value * active).astype(bf16)
    return jnp.concatenate([hidden, gate_back, up_back], axis=1)


def after(value, *others):
    return lax.optimization_barrier((value,) + others)[0]


def body(tokens, cotangent, pad_mask, rewards, selected, gate_weight, up_weight, down_weight):
    n_y = lax.axis_size("y")
    n_k = lax.axis_size("zhi")
    y = lax.axis_index("y")
    k = lax.axis_index("zhi")
    rows, width = tokens.shape
    units = gate_weight.shape[1]
    block = lax.axis_index(ROW) * n_k + k
    copies = lax.axis_size(("zlo", "x"))
    half = copies * rows
    part = half // n_y
    share = 2 * part
    quarter = width // n_k

    x_spread, g_spread = prepare(copies, block, rewards, selected, pad_mask, tokens, cotangent)
    x0 = lax.all_to_all(x_spread, ("zlo", "x"), 0, 0)
    g0 = lax.all_to_all(g_spread, ("zlo", "x"), 0, 0)
    x1 = shift(x0, "core", 1).reshape(half, width)
    g1 = shift(g0, "core", 1).reshape(half, width)
    x0 = x0.reshape(half, width)
    g0 = g0.reshape(half, width)

    forward = []
    backward = []
    for x in (x0, x1):
        gate = jnp.dot(x, gate_weight, preferred_element_type=f32) * SCALE_UP
        up = jnp.dot(x, up_weight, preferred_element_type=f32) * SCALE_UP
        both = jnp.concatenate([gate.astype(f16), up.astype(f16)], axis=1)
        forward.append(both.reshape(n_y, part, 2 * units))
    for g in (g0, g1):
        back = lax.dot_general(g, down_weight, (((1,), (1,)), ((), ())), preferred_element_type=f32)
        backward.append((back * SCALE_BACK).astype(f16).reshape(n_y, part, units))
    sums = lax.all_to_all(jnp.concatenate(forward, axis=1), "y", 0, 0)
    back_sums = lax.all_to_all(jnp.concatenate(backward, axis=1), "y", 0, 0)
    sums = jnp.sum(sums.astype(f32), axis=0) * (1.0 / SCALE_UP)
    back_sums = jnp.sum(back_sums.astype(f32), axis=0) * (1.0 / SCALE_BACK)
    values = unit_values(sums[:, :units], sums[:, units:], back_sums)

    replicas = lax.all_to_all(
        jnp.broadcast_to(values[None], (n_k, share, 3 * units)), "zhi", 0, 0
    )
    a_right = shift(values, "y", 1)
    a_left = shift(values, "y", -1)
    own = {0: values, n_y - 1: a_right, 1: a_left}

    turned = jnp.concatenate([replicas, replicas[:-1]], axis=0)
    near = lax.dynamic_slice_in_dim(turned, k + 1, n_k - 1, axis=0)
    near = near.reshape((n_k - 1) * share, 3 * units)
    rest = near.shape[0]
    far = {0: near}

    order = [0]
    for s in range(1, n_y // 2):
        order += [s, n_y - s]
    order.append(n_y // 2)
    pieces = cut_quarters(order, n_k, jnp.stack([y, k]), x0, x1, g0, after(g1, values))

    right = jnp.concatenate([near, a_right], axis=0)
    left = jnp.concatenate([near, a_left[part:], a_left[:part]], axis=0)
    got = [pieces[0]]
    for s in range(1, n_y // 2):
        if s == n_y // 2 - 1:
            right = right[: rest + part]
            left = left[: rest + part]
        right = shift(right, "y", 1)
        left = shift(left, "y", -1)
        far[n_y - s] = right[:rest]
        far[s] = left[:rest]
        if s == n_y // 2 - 1:
            own[n_y // 2] = jnp.concatenate([right[rest:], left[rest:]], axis=0)
        else:
            own[n_y - s - 1] = right[rest:]
            own[s + 1] = jnp.concatenate([left[rest + part :], left[rest : rest + part]], axis=0)
        if s < n_k:
            got.append(shift(after(pieces[s], right, left), "zhi", -s))
    top = shift(right[: rest // 2], "y", 1)
    low = shift(left[rest // 2 : rest], "y", -1)

    main = jnp.concatenate([v for r in order[:-1] for v in (own[r], far[r])], axis=0)
    last = jnp.concatenate([own[n_y // 2], top, low], axis=0)
    inputs = jnp.stack([v.reshape(n_y, share, 2 * quarter) for v in got], axis=1)
    inputs = inputs.reshape(n_y * n_k * share, 2 * quarter)
    cut = main.shape[0]
    contract = (((0,), (0,)), ((), ()))

    def product(a, b):
        return lax.dot_general(a, b, contract, preferred_element_type=f32)

    early = inputs[:cut]
    late = inputs[cut:]
    gate_grad = product(early[:, :quarter], main[:, units : 2 * units])
    up_grad = product(early[:, :quarter], main[:, 2 * units :])
    down_grad = product(main[:, :units], early[:, quarter:])
    gate_grad += product(late[:, :quarter], last[:, units : 2 * units])
    up_grad += product(late[:, :quarter], last[:, 2 * units :])
    down_grad += product(last[:, :units], late[:, quarter:])
    return (gate_grad, up_grad, down_grad)


def solution(mesh):
    n_row, n_col, n_rep = mesh.devices.shape
    fine = Mesh(
        mesh.devices.reshape(Z_LO, n_row // (Z_LO * CORES), CORES, n_col, n_rep),
        ("zlo", "x", "core", "y", "zhi"),
    )
    blocks = ROW + ("zhi",)
    placed = (
        P(blocks, "y"),
        P(blocks, "y"),
        P(blocks),
        P(),
        P(),
        P("y", ROW),
        P("y", ROW),
        P(ROW, "y"),
    )
    return jax.shard_map(
        body,
        mesh=fine,
        in_specs=placed,
        out_specs=(P(("y", "zhi"), ROW), P(("y", "zhi"), ROW), P(ROW, ("y", "zhi"))),
        check_vma=False,
    )
```

time: 184 us -> 186 us (1.011)
  starting transfers between devices: 111 us -> 79.9 us
  blocking collectives: 0 us -> 24.2 us
  local copies, waits for them, and re-layouts: 21.3 us -> 1.43 us
  waiting for transfers between devices: 39 us -> 54.6 us
  matrix products: 6.04 us -> 11.5 us
  other arithmetic: 2 us -> 6.23 us
  Pallas kernels: 1.77 us -> 4.02 us
    ppermute x20 -> x15, starting transfers between devices: 79.8 us -> 54.3 us  [shift(): return lax.ppermute(value, axis, [(i, (i + step) % n) for i in range(n)])]
    all_to_all x0 -> x1, blocking collectives: none -> 24.2 us  [body(): x0 = lax.all_to_all(x_spread, ('zlo', 'x'), 0, 0)]
    all_to_all x2 -> x3, waiting for transfers between devices: 10.9 us -> 30.7 us  [the longest x1 16.5 us: body(): sums = lax.all_to_all(jnp.concatenate(forward, axis=1), 'y', 0, 0)]
    all_to_all x2 -> x3, starting transfers between devices: 21.9 us -> 13 us  [the longest x1 5.4 us: body(): g0 = lax.all_to_all(g_spread, ('zlo', 'x'), 0, 0)]
    all_to_all x1, waiting for transfers between devices: 10.3 us -> 2.29 us  [body(): lax.all_to_all(jnp.broadcast_to(values[None], (n_k, share, 3 * units)), '...]
    unnamed x28 -> x36, local copies, waits for them, and re-layouts: 7.48 us -> 0.44 us
    another operation x7 -> x0, local copies, waits for them, and re-layouts: 5.88 us -> none  [the longest x3 3.97 us: body(): jnp.stack([h.reshape(n_y, part, 2, n_k, quarter) for h in halves], axis=1)]
    dot_general x9 -> x12, matrix products: 6.04 us -> 11.5 us  [the longest x6 4.51 us: product(): return lax.dot_general(a, b, contract, preferred_element_type=f32)]
  transfers between devices with their start and end apart: 23 -> 19, of which waited for: 7 -> 9; matrix products, arithmetic and copies ran while one was open for 11% -> 7% of each run, Pallas kernels for 0% -> 1%
where the time goes in v2:
time: 186 us; the launch traced here: 183 us
  starting transfers between devices  79.9 us (43%)
  waiting for transfers between devices  54.6 us (29%)
  blocking collectives  24.2 us (13%)
  matrix products  11.5 us (6%)
  other arithmetic  6.23 us (3%)
  Pallas kernels  4.02 us (2%)
    ppermute x15, starting transfers between devices, shift(): return lax.ppermute(value, axis, [(i, (i + step) % n) for i in range(n)])  54.3 us
    all_to_all x1, blocking collectives, body(): x0 = lax.all_to_all(x_spread, ('zlo', 'x'), 0, 0)  24.2 us
    ppermute x15, waiting for transfers between devices, shift(): return lax.ppermute(value, axis, [(i, (i + step) % n) for i in range(n)])  21.7 us
    all_to_all x1, waiting for transfers between devices, body(): sums = lax.all_to_all(jnp.concatenate(forward, axis=1), 'y', 0, 0)  16.5 us
    all_to_all x1, starting transfers between devices, body(): lax.all_to_all(jnp.broadcast_to(values[None], (n_k, share, 3 * units)), '...  12.7 us
    all_to_all x1, waiting for transfers between devices, body(): back_sums = lax.all_to_all(jnp.concatenate(backward, axis=1), 'y', 0, 0)  8.71 us
    all_to_all x1, waiting for transfers between devices, body(): g0 = lax.all_to_all(g_spread, ('zlo', 'x'), 0, 0)  5.41 us
    all_to_all x1, starting transfers between devices, body(): g0 = lax.all_to_all(g_spread, ('zlo', 'x'), 0, 0)  5.4 us
  transfers between devices with their start and end apart: 19, of which 9 were waited for; matrix products, arithmetic and copies ran while one was open for 7% of the time, Pallas kernels for 1%

profile of v2, /device:TPU:14, one launch (start us, length us, event | category | flops | bytes accessed | tf_op | source)
XLA Modules:
  0.0 183.2 jit_solution(11675427650039274879)
XLA Ops:
  0.6 0.0 copy-start
  0.7 1.7 shard_map.103
  2.4 24.2 %all_to_all.25 = bf16[16,8,1024]{2,1,0:T(8,128)(2,1)S(1)} all-to-all(bf16[16,8,1024]{2,1,0:T(8,128)(2,1)} %get-tuple-element.13), channel_id=1, replica_groups=mesh['zlo'=2,'x'=8,'core'=2,'y'=8,'zhi'=4] {'zlo','x'}, dimensions={0} | all-to-all | bytes 524288 | tf_op jit(solution)/shard_map/all_to_all | solution.py:119
  26.6 5.4 %all-to-all-start.1 = ((bf16[16,8,1024]{2,1,0:T(8,128)(2,1)}), bf16[16,8,1024]{2,1,0:T(8,128)(2,1)}, u32[]{:S(2)}, u32[]{:S(2)}) async-start(bf16[16,8,1024]{2,1,0:T(8,128)(2,1)} %get-tuple-element.14), calls=%async_computation.1 | async-start | bytes 524288 | tf_op jit(solution)/shard_map/all_to_all | solution.py:120
  32.0 1.5 fusion
  33.6 0.0 copy-start.1
  33.6 1.0 fusion.1
  34.5 5.4 %all-to-all-done.1 = bf16[16,8,1024]{2,1,0:T(8,128)(2,1)} async-done(((bf16[16,8,1024]{2,1,0:T(8,128)(2,1)}), bf16[16,8,1024]{2,1,0:T(8,128)(2,1)}, u32[]{:S(2)}, u32[]{:S(2)}) %all-to-all-start.1) | async-done | bytes 262176 | tf_op jit(solution)/shard_map/all_to_all | solution.py:120
  39.9 1.9 %collective-permute-start.1 = (bf16[16,8,1024]{2,1,0:T(8,128)(2,1)}, bf16[16,8,1024]{2,1,0:T(8,128)(2,1)S(1)}, u32[]{:S(2)}, u32[]{:S(2)}) collective-permute-start(bf16[16,8,1024]{2,1,0:T(8,128)(2,1)} %all-to-all-done.1), channel_id=1, source_target_pairs={{0,32},{32,0},{1,33},{33,1},{2,34},{34,2},{3,35},{35,3},{4,36},{36... | collective-permute-start | bytes 786440 | tf_op jit(solution)/shard_map/ppermute | solution.py:25
  41.9 1.7 pad_maximum_fusion.5
  43.5 2.4 %collective-permute-start = (bf16[16,8,1024]{2,1,0:T(8,128)(2,1)S(1)}, bf16[16,8,1024]{2,1,0:T(8,128)(2,1)}, u32[]{:S(2)}, u32[]{:S(2)}) collective-permute-start(bf16[16,8,1024]{2,1,0:T(8,128)(2,1)S(1)} %all_to_all.25), channel_id=1, source_target_pairs={{0,32},{32,0},{1,33},{33,1},{2,34},{34,2},{3,35},{35,3},{4,36},{36... | collective-permute-start | bytes 786440 | tf_op jit(solution)/shard_map/ppermute | solution.py:25
  45.9 1.4 fusion.4
  47.4 0.5 fusion.5
  47.9 0.2 copy-done.5
  48.1 0.8 pad_maximum_fusion.7
  48.9 4.1 %all-to-all-start.3 = ((f16[8,32,512]{2,1,0:T(8,128)(2,1)}), f16[8,32,512]{2,1,0:T(8,128)(2,1)}, u32[]{:S(2)}, u32[]{:S(2)}) async-start(f16[8,32,512]{2,1,0:T(8,128)(2,1)} %pad_maximum_fusion.7), calls=%async_computation.3 | async-start | bytes 524288 | tf_op jit(solution)/shard_map/all_to_all | solution.py:137
  52.9 0.0 copy-start.4
  53.0 0.0 collective-permute-done
  53.0 1.3 fusion.2
  54.3 1.3 fusion.3
  55.6 0.1 pad_maximum_fusion.6
  55.6 0.9 pad_maximum_fusion.1
  56.6 8.7 %all-to-all-done.3 = f16[8,32,512]{2,1,0:T(8,128)(2,1)} async-done(((f16[8,32,512]{2,1,0:T(8,128)(2,1)}), f16[8,32,512]{2,1,0:T(8,128)(2,1)}, u32[]{:S(2)}, u32[]{:S(2)}) %all-to-all-start.3) | async-done | bytes 262176 | tf_op jit(solution)/shard_map/all_to_all | solution.py:137
  65.3 3.5 %all-to-all-start.2 = ((f16[8,32,1024]{2,1,0:T(8,128)(2,1)}), f16[8,32,1024]{2,1,0:T(8,128)(2,1)S(1)}, u32[]{:S(2)}, u32[]{:S(2)}) async-start(f16[8,32,1024]{2,1,0:T(8,128)(2,1)} %pad_maximum_fusion.1), calls=%async_computation.2 | async-start | bytes 1048576 | tf_op jit(solution)/shard_map/all_to_all | solution.py:136
  68.8 1.0 convert_reduce_fusion.1
  69.8 16.5 %all-to-all-done.2 = f16[8,32,1024]{2,1,0:T(8,128)(2,1)S(1)} async-done(((f16[8,32,1024]{2,1,0:T(8,128)(2,1)}), f16[8,32,1024]{2,1,0:T(8,128)(2,1)S(1)}, u32[]{:S(2)}, u32[]{:S(2)}) %all-to-all-start.2) | async-done | bytes 524320 | tf_op jit(solution)/shard_map/all_to_all | solution.py:136
  86.3 0.1 convert_reduce_fusion
  86.4 0.1 multiply_convert_fusion.1
  86.5 0.7 constant_dynamic-update-slice_fusion.3
  87.1 0.8 broadcast_in_dim.2
  87.9 12.7 %all-to-all-start.4 = ((bf16[4,32,1536]{2,1,0:T(8,128)(2,1)}), bf16[4,32,1536]{2,1,0:T(8,128)(2,1)S(1)}, u32[]{:S(2)}, u32[]{:S(2)}) async-start(bf16[4,32,1536]{2,1,0:T(8,128)(2,1)} %broadcast_in_dim.2), calls=%async_computation.4 | async-start | bytes 786432 | tf_op jit(solution)/shard_map/all_to_all | solution.py:142
  100.6 1.9 %collective-permute-start.4 = (bf16[32,1536]{1,0:T(8,128)(2,1)S(1)}, bf16[32,1536]{1,0:T(8,128)(2,1)S(1)}, u32[]{:S(2)}, u32[]{:S(2)}) collective-permute-start(bf16[32,1536]{1,0:T(8,128)(2,1)S(1)} %get-tuple-element.29), channel_id=1, source_target_pairs={{0,28},{4,0},{8,4},{12,8},{16,12},{20,16},{24,20},{28,24},{1,29},{... | collective-permute-start | bytes 294920 | tf_op jit(solution)/shard_map/ppermute | solution.py:25
  102.5 0.6 pad_add_fusion.place_ref
  103.2 3.9 %collective-permute-start.2 = (bf16[32,1536]{1,0:T(8,128)(2,1)S(1)}, bf16[32,1536]{1,0:T(8,128)(2,1)S(1)}, u32[]{:S(2)}, u32[]{:S(2)}) collective-permute-start(bf16[32,1536]{1,0:T(8,128)(2,1)S(1)} %get-tuple-element.29), channel_id=1, source_target_pairs={{0,4},{4,8},{8,12},{12,16},{16,20},{20,24},{24,28},{28,0},{1,5},{5... | collective-permute-start | bytes 294920 | tf_op jit(solution)/shard_map/ppermute | solution.py:25
  107.1 2.3 %shard_map.104 = (bf16[256,512]{1,0:T(8,128)(2,1)}, bf16[256,512]{1,0:T(8,128)(2,1)}, bf16[256,512]{1,0:T(8,128)(2,1)}, bf16[256,512]{1,0:T(8,128)(2,1)}) custom-call(s32[2]{0:T(128)} %pad_add_fusion.place_ref, bf16[128,1024]{1,0:T(8,128)(2,1)} %bitcast.44, bf16[128,1024]{1,0:T(8,128)(2,1)} %bitcast.4.x1_ref, bf16[128,1024]{1,0:T(8,128)(2,1)} %bitcast.5.g0_ref, ...), custom_call_target="tpu_custom_call" | custom-call | tf_op jit(solution)/shard_map/pallas_call | solution.py:81
  109.4 2.3 %all-to-all-done.4 = bf16[4,32,1536]{2,1,0:T(8,128)(2,1)S(1)} async-done(((bf16[4,32,1536]{2,1,0:T(8,128)(2,1)}), bf16[4,32,1536]{2,1,0:T(8,128)(2,1)S(1)}, u32[]{:S(2)}, u32[]{:S(2)}) %all-to-all-start.4) | async-done | bytes 393248 | tf_op jit(solution)/shard_map/all_to_all | solution.py:142
  111.8 0.1 fusion.13
  111.9 0.0 collective-permute-done.2
  111.9 0.1 pad_maximum_fusion.3
  112.0 2.1 %collective-permute-start.3 = (bf16[128,1536]{1,0:T(8,128)(2,1)S(1)}, bf16[128,1536]{1,0:T(8,128)(2,1)S(1)}, u32[]{:S(2)}, u32[]{:S(2)}) collective-permute-start(bf16[128,1536]{1,0:T(8,128)(2,1)S(1)} %get-tuple-element.23), channel_id=1, source_target_pairs={{0,4},{4,8},{8,12},{12,16},{16,20},{20,24},{24,28},{28,0},{1,5},{5... | collective-permute-start | bytes 1179656 | tf_op jit(solution)/shard_map/ppermute | solution.py:25
  114.0 5.1 %collective-permute-start.5 = (bf16[128,1536]{1,0:T(8,128)(2,1)S(1)}, bf16[128,1536]{1,0:T(8,128)(2,1)S(1)}, u32[]{:S(2)}, u32[]{:S(2)}) collective-permute-start(bf16[128,1536]{1,0:T(8,128)(2,1)S(1)} %get-tuple-element.24), channel_id=1, source_target_pairs={{0,28},{4,0},{8,4},{12,8},{16,12},{20,16},{24,20},{28,24},{1,29},{... | collective-permute-start | bytes 1179656 | tf_op jit(solution)/shard_map/ppermute | solution.py:25
  119.2 3.7 %collective-permute-done.3 = bf16[128,1536]{1,0:T(8,128)(2,1)S(1)} collective-permute-done((bf16[128,1536]{1,0:T(8,128)(2,1)S(1)}, bf16[128,1536]{1,0:T(8,128)(2,1)S(1)}, u32[]{:S(2)}, u32[]{:S(2)}) %collective-permute-start.3) | collective-permute-done | bytes 393248 | tf_op jit(solution)/shard_map/ppermute | solution.py:25
  123.0 1.5 collective-permute-done.5
  124.5 4.9 %collective-permute-start.6 = (bf16[256,512]{1,0:T(8,128)(2,1)S(1)}, bf16[256,512]{1,0:T(8,128)(2,1)S(1)}, u32[]{:S(2)}, u32[]{:S(2)}) collective-permute-start(bf16[256,512]{1,0:T(8,128)(2,1)S(1)} %copy-done.10), channel_id=1, source_target_pairs={{0,3},{1,0},{2,1},{3,2},{4,7},{5,4},{6,5},{7,6},{8,11},{9,8},{10,9... | collective-permute-start | bytes 786440 | tf_op jit(solution)/shard_map/ppermute | solution.py:25
  129.4 2.5 %collective-permute-start.7 = (bf16[128,1536]{1,0:T(8,128)(2,1)S(1)}, bf16[128,1536]{1,0:T(8,128)(2,1)S(1)}, u32[]{:S(2)}, u32[]{:S(2)}) collective-permute-start(bf16[128,1536]{1,0:T(8,128)(2,1)S(1)} %collective-permute-done.3), channel_id=1, source_target_pairs={{0,4},{4,8},{8,12},{12,16},{16,20},{20,24},{24,28},{28,0},{1,5},{5... | collective-permute-start | bytes 1179656 | tf_op jit(solution)/shard_map/ppermute | solution.py:25
  131.9 5.0 %collective-permute-start.8 = (bf16[128,1536]{1,0:T(8,128)(2,1)S(1)}, bf16[128,1536]{1,0:T(8,128)(2,1)S(1)}, u32[]{:S(2)}, u32[]{:S(2)}) collective-permute-start(bf16[128,1536]{1,0:T(8,128)(2,1)S(1)} %collective-permute-done.5), channel_id=1, source_target_pairs={{0,28},{4,0},{8,4},{12,8},{16,12},{20,16},{24,20},{28,24},{1,29},{... | collective-permute-start | bytes 1179656 | tf_op jit(solution)/shard_map/ppermute | solution.py:25
  137.0 3.8 %collective-permute-done.7 = bf16[128,1536]{1,0:T(8,128)(2,1)S(1)} collective-permute-done((bf16[128,1536]{1,0:T(8,128)(2,1)S(1)}, bf16[128,1536]{1,0:T(8,128)(2,1)S(1)}, u32[]{:S(2)}, u32[]{:S(2)}) %collective-permute-start.7) | collective-permute-done | bytes 393248 | tf_op jit(solution)/shard_map/ppermute | solution.py:25
  140.8 0.0 copy-start.6
  140.8 2.1 %collective-permute-start.10 = (bf16[112,1536]{1,0:T(8,128)(2,1)S(1)}, bf16[112,1536]{1,0:T(8,128)(2,1)S(1)}, u32[]{:S(2)}, u32[]{:S(2)}) collective-permute-start(bf16[112,1536]{1,0:T(8,128)(2,1)S(1)} %slice.155), channel_id=1, source_target_pairs={{0,4},{4,8},{8,12},{12,16},{16,20},{20,24},{24,28},{28,0},{1,5},{5... | collective-permute-start | bytes 1032200 | tf_op jit(solution)/shard_map/ppermute | solution.py:25
  142.9 5.7 %collective-permute-start.9 = (bf16[256,512]{1,0:T(8,128)(2,1)S(1)}, bf16[256,512]{1,0:T(8,128)(2,1)S(1)}, u32[]{:S(2)}, u32[]{:S(2)}) collective-permute-start(bf16[256,512]{1,0:T(8,128)(2,1)S(1)} %copy-done.9), channel_id=1, source_target_pairs={{0,2},{1,3},{2,0},{3,1},{4,6},{5,7},{6,4},{7,5},{8,10},{9,11},{10,... | collective-permute-start | bytes 786440 | tf_op jit(solution)/shard_map/ppermute | solution.py:25
  148.6 5.6 %collective-permute-start.11 = (bf16[112,1536]{1,0:T(8,128)(2,1)S(1)}, bf16[112,1536]{1,0:T(8,128)(2,1)S(1)}, u32[]{:S(2)}, u32[]{:S(2)}) collective-permute-start(bf16[112,1536]{1,0:T(8,128)(2,1)S(1)} %slice.156), channel_id=1, source_target_pairs={{0,28},{4,0},{8,4},{12,8},{16,12},{20,16},{24,20},{28,24},{1,29},{... | collective-permute-start | bytes 1032200 | tf_op jit(solution)/shard_map/ppermute | solution.py:25
  154.3 1.9 %collective-permute-start.13 = (bf16[48,1536]{1,0:T(8,128)(2,1)S(1)}, bf16[48,1536]{1,0:T(8,128)(2,1)S(1)}, u32[]{:S(2)}, u32[]{:S(2)}) collective-permute-start(bf16[48,1536]{1,0:T(8,128)(2,1)S(1)} %slice.175), channel_id=1, source_target_pairs={{0,4},{4,8},{8,12},{12,16},{16,20},{20,24},{24,28},{28,0},{1,5},{5... | collective-permute-start | bytes 442376 | tf_op jit(solution)/shard_map/ppermute | solution.py:25
  156.3 3.7 %collective-permute-done.11 = bf16[112,1536]{1,0:T(8,128)(2,1)S(1)} collective-permute-done((bf16[112,1536]{1,0:T(8,128)(2,1)S(1)}, bf16[112,1536]{1,0:T(8,128)(2,1)S(1)}, u32[]{:S(2)}, u32[]{:S(2)}) %collective-permute-start.11) | collective-permute-done | bytes 344096 | tf_op jit(solution)/shard_map/ppermute | solution.py:25
  159.9 5.6 %collective-permute-start.14 = (bf16[48,1536]{1,0:T(8,128)(2,1)S(1)}, bf16[48,1536]{1,0:T(8,128)(2,1)S(1)}, u32[]{:S(2)}, u32[]{:S(2)}) collective-permute-start(bf16[48,1536]{1,0:T(8,128)(2,1)S(1)} %slice.176), channel_id=1, source_target_pairs={{0,28},{4,0},{8,4},{12,8},{16,12},{20,16},{24,20},{28,24},{1,29},{... | collective-permute-start | bytes 442376 | tf_op jit(solution)/shard_map/ppermute | solution.py:25
  165.5 3.8 %collective-permute-start.12 = (bf16[256,512]{1,0:T(8,128)(2,1)S(1)}, bf16[256,512]{1,0:T(8,128)(2,1)S(1)}, u32[]{:S(2)}, u32[]{:S(2)}) collective-permute-start(bf16[256,512]{1,0:T(8,128)(2,1)S(1)} %copy-done.8), channel_id=1, source_target_pairs={{0,1},{1,2},{2,3},{3,0},{4,5},{5,6},{6,7},{7,4},{8,9},{9,10},{10,1... | collective-permute-start | bytes 786440 | tf_op jit(solution)/shard_map/ppermute | solution.py:25
  169.5 9.0 %collective-permute-done.12 = bf16[256,512]{1,0:T(8,128)(2,1)S(1)} collective-permute-done((bf16[256,512]{1,0:T(8,128)(2,1)S(1)}, bf16[256,512]{1,0:T(8,128)(2,1)S(1)}, u32[]{:S(2)}, u32[]{:S(2)}) %collective-permute-start.12) | collective-permute-done | bytes 262176 | tf_op jit(solution)/shard_map/ppermute | solution.py:25
  178.5 0.1 pad_maximum_fusion
  178.6 0.2 fusion.16
  178.9 0.2 fusion.14
  179.1 0.2 fusion.18
  179.4 0.1 slice.157
  179.5 1.3 convolution_add_fusion.1
  180.7 1.3 convolution_add_fusion.2
  182.0 1.3 convolution_add_fusion
  (51 shorter events, 0.4 us)
Async XLA Ops:
  0.6 45.3 %copy-start = (bf16[512,1024]{1,0:T(8,128)(2,1)S(1)}, bf16[512,1024]{1,0:T(8,128)(2,1)}, u32[]{:S(2)}) copy-start(bf16[512,1024]{1,0:T(8,128)(2,1)} %param.15) | copy-start | bytes 3145732
  0.6 32.9 %copy-start.2 = (bf16[1024,512]{1,0:T(8,128)(2,1)S(1)}, bf16[1024,512]{1,0:T(8,128)(2,1)}, u32[]{:S(2)}) copy-start(bf16[1024,512]{1,0:T(8,128)(2,1)} %param.14) | copy-start | bytes 3145732
  26.6 21.3 %copy-start.3 = (bf16[16,8,1024]{2,1,0:T(8,128)(2,1)}, bf16[16,8,1024]{2,1,0:T(8,128)(2,1)S(1)}, u32[]{:S(2)}) copy-start(bf16[16,8,1024]{2,1,0:T(8,128)(2,1)S(1)} %all_to_all.25) | copy-start | bytes 786436
  26.6 13.3 %all-to-all-start.1 = ((bf16[16,8,1024]{2,1,0:T(8,128)(2,1)}), bf16[16,8,1024]{2,1,0:T(8,128)(2,1)}, u32[]{:S(2)}, u32[]{:S(2)}) async-start(bf16[16,8,1024]{2,1,0:T(8,128)(2,1)} %get-tuple-element.14), calls=%async_computation.1 | async-start | bytes 524288 | tf_op jit(solution)/shard_map/all_to_all | solution.py:120
  33.6 19.4 %copy-start.1 = (bf16[1024,512]{1,0:T(8,128)(2,1)S(1)}, bf16[1024,512]{1,0:T(8,128)(2,1)}, u32[]{:S(2)}) copy-start(bf16[1024,512]{1,0:T(8,128)(2,1)} %param.13) | copy-start | bytes 3145732
  39.9 7.4 %collective-permute-start.1 = (bf16[16,8,1024]{2,1,0:T(8,128)(2,1)}, bf16[16,8,1024]{2,1,0:T(8,128)(2,1)S(1)}, u32[]{:S(2)}, u32[]{:S(2)}) collective-permute-start(bf16[16,8,1024]{2,1,0:T(8,128)(2,1)} %all-to-all-done.1), channel_id=1, source_target_pairs={{0,32},{32,0},{1,33},{33,1},{2,34},{34,2},{3,35},{35,3},{4,36},{36... | collective-permute-start | bytes 786440 | tf_op jit(solution)/shard_map/ppermute | solution.py:25
  43.5 9.4 %collective-permute-start = (bf16[16,8,1024]{2,1,0:T(8,128)(2,1)S(1)}, bf16[16,8,1024]{2,1,0:T(8,128)(2,1)}, u32[]{:S(2)}, u32[]{:S(2)}) collective-permute-start(bf16[16,8,1024]{2,1,0:T(8,128)(2,1)S(1)} %all_to_all.25), channel_id=1, source_target_pairs={{0,32},{32,0},{1,33},{33,1},{2,34},{34,2},{3,35},{35,3},{4,36},{36... | collective-permute-start | bytes 786440 | tf_op jit(solution)/shard_map/ppermute | solution.py:25
  47.4 0.7 copy-start.5
  48.9 16.4 %all-to-all-start.3 = ((f16[8,32,512]{2,1,0:T(8,128)(2,1)}), f16[8,32,512]{2,1,0:T(8,128)(2,1)}, u32[]{:S(2)}, u32[]{:S(2)}) async-start(f16[8,32,512]{2,1,0:T(8,128)(2,1)} %pad_maximum_fusion.7), calls=%async_computation.3 | async-start | bytes 524288 | tf_op jit(solution)/shard_map/all_to_all | solution.py:137
  52.9 2.7 %copy-start.4 = (f16[128,1024]{1,0:T(8,128)(2,1)S(1)}, f16[128,1024]{1,0:T(8,128)(2,1)}, u32[]{:S(2)}) copy-start(f16[128,1024]{1,0:T(8,128)(2,1)} %pad_maximum_fusion.5) | copy-start | bytes 786436
  65.3 21.0 %all-to-all-start.2 = ((f16[8,32,1024]{2,1,0:T(8,128)(2,1)}), f16[8,32,1024]{2,1,0:T(8,128)(2,1)S(1)}, u32[]{:S(2)}, u32[]{:S(2)}) async-start(f16[8,32,1024]{2,1,0:T(8,128)(2,1)} %pad_maximum_fusion.1), calls=%async_computation.2 | async-start | bytes 1048576 | tf_op jit(solution)/shard_map/all_to_all | solution.py:136
  87.9 23.8 %all-to-all-start.4 = ((bf16[4,32,1536]{2,1,0:T(8,128)(2,1)}), bf16[4,32,1536]{2,1,0:T(8,128)(2,1)S(1)}, u32[]{:S(2)}, u32[]{:S(2)}) async-start(bf16[4,32,1536]{2,1,0:T(8,128)(2,1)} %broadcast_in_dim.2), calls=%async_computation.4 | async-start | bytes 786432 | tf_op jit(solution)/shard_map/all_to_all | solution.py:142
  100.6 8.8 %collective-permute-start.4 = (bf16[32,1536]{1,0:T(8,128)(2,1)S(1)}, bf16[32,1536]{1,0:T(8,128)(2,1)S(1)}, u32[]{:S(2)}, u32[]{:S(2)}) collective-permute-start(bf16[32,1536]{1,0:T(8,128)(2,1)S(1)} %get-tuple-element.29), channel_id=1, source_target_pairs={{0,28},{4,0},{8,4},{12,8},{16,12},{20,16},{24,20},{28,24},{1,29},{... | collective-permute-start | bytes 294920 | tf_op jit(solution)/shard_map/ppermute | solution.py:25
  103.2 8.7 %collective-permute-start.2 = (bf16[32,1536]{1,0:T(8,128)(2,1)S(1)}, bf16[32,1536]{1,0:T(8,128)(2,1)S(1)}, u32[]{:S(2)}, u32[]{:S(2)}) collective-permute-start(bf16[32,1536]{1,0:T(8,128)(2,1)S(1)} %get-tuple-element.29), channel_id=1, source_target_pairs={{0,4},{4,8},{8,12},{12,16},{16,20},{20,24},{24,28},{28,0},{1,5},{5... | collective-permute-start | bytes 294920 | tf_op jit(solution)/shard_map/ppermute | solution.py:25
  109.4 15.0 %copy-start.10 = (bf16[256,512]{1,0:T(8,128)(2,1)S(1)}, bf16[256,512]{1,0:T(8,128)(2,1)}, u32[]{:S(2)}) copy-start(bf16[256,512]{1,0:T(8,128)(2,1)} %get-tuple-element.18) | copy-start | bytes 786436
  111.7 7.4 %copy-start.7 = (bf16[896,1536]{1,0:T(8,128)(2,1)S(1)}, bf16[896,1536]{1,0:T(8,128)(2,1)}, u32[]{:S(2)}) copy-start(bf16[896,1536]{1,0:T(8,128)(2,1)} %get-tuple-element.28) | copy-start | bytes 8257540
  111.8 31.1 %copy-start.9 = (bf16[256,512]{1,0:T(8,128)(2,1)S(1)}, bf16[256,512]{1,0:T(8,128)(2,1)}, u32[]{:S(2)}) copy-start(bf16[256,512]{1,0:T(8,128)(2,1)} %get-tuple-element.20) | copy-start | bytes 786436
  112.0 11.0 %collective-permute-start.3 = (bf16[128,1536]{1,0:T(8,128)(2,1)S(1)}, bf16[128,1536]{1,0:T(8,128)(2,1)S(1)}, u32[]{:S(2)}, u32[]{:S(2)}) collective-permute-start(bf16[128,1536]{1,0:T(8,128)(2,1)S(1)} %get-tuple-element.23), channel_id=1, source_target_pairs={{0,4},{4,8},{8,12},{12,16},{16,20},{20,24},{24,28},{28,0},{1,5},{5... | collective-permute-start | bytes 1179656 | tf_op jit(solution)/shard_map/ppermute | solution.py:25
  114.0 10.4 %collective-permute-start.5 = (bf16[128,1536]{1,0:T(8,128)(2,1)S(1)}, bf16[128,1536]{1,0:T(8,128)(2,1)S(1)}, u32[]{:S(2)}, u32[]{:S(2)}) collective-permute-start(bf16[128,1536]{1,0:T(8,128)(2,1)S(1)} %get-tuple-element.24), channel_id=1, source_target_pairs={{0,28},{4,0},{8,4},{12,8},{16,12},{20,16},{24,20},{28,24},{1,29},{... | collective-permute-start | bytes 1179656 | tf_op jit(solution)/shard_map/ppermute | solution.py:25
  119.2 46.3 %copy-start.8 = (bf16[256,512]{1,0:T(8,128)(2,1)S(1)}, bf16[256,512]{1,0:T(8,128)(2,1)}, u32[]{:S(2)}) copy-start(bf16[256,512]{1,0:T(8,128)(2,1)} %get-tuple-element.22) | copy-start | bytes 786436
  124.5 45.0 %collective-permute-start.6 = (bf16[256,512]{1,0:T(8,128)(2,1)S(1)}, bf16[256,512]{1,0:T(8,128)(2,1)S(1)}, u32[]{:S(2)}, u32[]{:S(2)}) collective-permute-start(bf16[256,512]{1,0:T(8,128)(2,1)S(1)} %copy-done.10), channel_id=1, source_target_pairs={{0,3},{1,0},{2,1},{3,2},{4,7},{5,4},{6,5},{7,6},{8,11},{9,8},{10,9... | collective-permute-start | bytes 786440 | tf_op jit(solution)/shard_map/ppermute | solution.py:25
  129.4 11.4 %collective-permute-start.7 = (bf16[128,1536]{1,0:T(8,128)(2,1)S(1)}, bf16[128,1536]{1,0:T(8,128)(2,1)S(1)}, u32[]{:S(2)}, u32[]{:S(2)}) collective-permute-start(bf16[128,1536]{1,0:T(8,128)(2,1)S(1)} %collective-permute-done.3), channel_id=1, source_target_pairs={{0,4},{4,8},{8,12},{12,16},{16,20},{20,24},{24,28},{28,0},{1,5},{5... | collective-permute-start | bytes 1179656 | tf_op jit(solution)/shard_map/ppermute | solution.py:25
  131.9 11.0 %collective-permute-start.8 = (bf16[128,1536]{1,0:T(8,128)(2,1)S(1)}, bf16[128,1536]{1,0:T(8,128)(2,1)S(1)}, u32[]{:S(2)}, u32[]{:S(2)}) collective-permute-start(bf16[128,1536]{1,0:T(8,128)(2,1)S(1)} %collective-permute-done.5), channel_id=1, source_target_pairs={{0,28},{4,0},{8,4},{12,8},{16,12},{20,16},{24,20},{28,24},{1,29},{... | collective-permute-start | bytes 1179656 | tf_op jit(solution)/shard_map/ppermute | solution.py:25
  140.8 37.6 %copy-start.6 = (bf16[256,512]{1,0:T(8,128)(2,1)S(1)}, bf16[256,512]{1,0:T(8,128)(2,1)}, u32[]{:S(2)}) copy-start(bf16[256,512]{1,0:T(8,128)(2,1)} %get-tuple-element.16) | copy-start | bytes 786436
  140.8 13.5 %collective-permute-start.10 = (bf16[112,1536]{1,0:T(8,128)(2,1)S(1)}, bf16[112,1536]{1,0:T(8,128)(2,1)S(1)}, u32[]{:S(2)}, u32[]{:S(2)}) collective-permute-start(bf16[112,1536]{1,0:T(8,128)(2,1)S(1)} %slice.155), channel_id=1, source_target_pairs={{0,4},{4,8},{8,12},{12,16},{16,20},{20,24},{24,28},{28,0},{1,5},{5... | collective-permute-start | bytes 1032200 | tf_op jit(solution)/shard_map/ppermute | solution.py:25
  142.9 26.6 %collective-permute-start.9 = (bf16[256,512]{1,0:T(8,128)(2,1)S(1)}, bf16[256,512]{1,0:T(8,128)(2,1)S(1)}, u32[]{:S(2)}, u32[]{:S(2)}) collective-permute-start(bf16[256,512]{1,0:T(8,128)(2,1)S(1)} %copy-done.9), channel_id=1, source_target_pairs={{0,2},{1,3},{2,0},{3,1},{4,6},{5,7},{6,4},{7,5},{8,10},{9,11},{10,... | collective-permute-start | bytes 786440 | tf_op jit(solution)/shard_map/ppermute | solution.py:25
  148.6 11.3 %collective-permute-start.11 = (bf16[112,1536]{1,0:T(8,128)(2,1)S(1)}, bf16[112,1536]{1,0:T(8,128)(2,1)S(1)}, u32[]{:S(2)}, u32[]{:S(2)}) collective-permute-start(bf16[112,1536]{1,0:T(8,128)(2,1)S(1)} %slice.156), channel_id=1, source_target_pairs={{0,28},{4,0},{8,4},{12,8},{16,12},{20,16},{24,20},{28,24},{1,29},{... | collective-permute-start | bytes 1032200 | tf_op jit(solution)/shard_map/ppermute | solution.py:25
  154.3 15.1 %collective-permute-start.13 = (bf16[48,1536]{1,0:T(8,128)(2,1)S(1)}, bf16[48,1536]{1,0:T(8,128)(2,1)S(1)}, u32[]{:S(2)}, u32[]{:S(2)}) collective-permute-start(bf16[48,1536]{1,0:T(8,128)(2,1)S(1)} %slice.175), channel_id=1, source_target_pairs={{0,4},{4,8},{8,12},{12,16},{16,20},{20,24},{24,28},{28,0},{1,5},{5... | collective-permute-start | bytes 442376 | tf_op jit(solution)/shard_map/ppermute | solution.py:25
  159.9 9.5 %collective-permute-start.14 = (bf16[48,1536]{1,0:T(8,128)(2,1)S(1)}, bf16[48,1536]{1,0:T(8,128)(2,1)S(1)}, u32[]{:S(2)}, u32[]{:S(2)}) collective-permute-start(bf16[48,1536]{1,0:T(8,128)(2,1)S(1)} %slice.176), channel_id=1, source_target_pairs={{0,28},{4,0},{8,4},{12,8},{16,12},{20,16},{24,20},{28,24},{1,29},{... | collective-permute-start | bytes 442376 | tf_op jit(solution)/shard_map/ppermute | solution.py:25
  165.5 12.9 %collective-permute-start.12 = (bf16[256,512]{1,0:T(8,128)(2,1)S(1)}, bf16[256,512]{1,0:T(8,128)(2,1)S(1)}, u32[]{:S(2)}, u32[]{:S(2)}) collective-permute-start(bf16[256,512]{1,0:T(8,128)(2,1)S(1)} %copy-done.8), channel_id=1, source_target_pairs={{0,1},{1,2},{2,3},{3,0},{4,5},{5,6},{6,7},{7,4},{8,9},{9,10},{10,1... | collective-permute-start | bytes 786440 | tf_op jit(solution)/shard_map/ppermute | solution.py:25

commit v3 on v1

v3 whole, which is shorter than its diff:
```python
import functools

import jax
import jax.numpy as jnp
from jax import lax
from jax.experimental import pallas as pl
from jax.experimental.pallas import tpu as pltpu
from jax.sharding import Mesh
from jax.sharding import PartitionSpec as P

SAMPLES = 8
COMP_LEN = 16
CORES = 2
Z_LO = 2
SCALE_UP = 128.0
SCALE_BACK = 1024.0
ROW = ("zlo", "x", "core")
bf16 = jnp.bfloat16
f16 = jnp.float16
f32 = jnp.float32


def shift(value, axis, step):
    n = lax.axis_size(axis)
    return lax.ppermute(value, axis, [(i, (i + step) % n) for i in range(n)])


def prepare_kernel(block_ref, rewards_ref, selected_ref, pad_ref, tokens_ref, cotangent_ref, all_ref, cut_ref):
    rows, width = tokens_ref.shape
    quarter = cut_ref.shape[2] // 2
    n_k = width // quarter
    completion = block_ref[0] * rows // COMP_LEN
    prompt = completion // SAMPLES
    sample = completion % SAMPLES
    reward = rewards_ref[prompt, sample].astype(f32)
    chosen = jnp.where(selected_ref[prompt] == sample, 1.0, 0.0)
    factor = reward / 4.0 + chosen
    row = lax.broadcasted_iota(jnp.int32, (rows, 1), 0)
    weight = jnp.zeros((rows, 1), f32)
    for n in range(rows):
        weight = jnp.where(row == n, pad_ref[n].astype(f32) * factor, weight)
    grads = (weight * cotangent_ref[...].astype(f32)).astype(bf16)
    for copy in range(all_ref.shape[0]):
        all_ref[copy, :, :width] = tokens_ref[...]
        all_ref[copy, :, width:] = grads
    for t in range(n_k):
        lanes = slice(t * quarter, (t + 1) * quarter)
        cut_ref[t, :, :quarter] = tokens_ref[:, lanes]
        cut_ref[t, :, quarter:] = grads[:, lanes]


def prepare(copies, n_k, block, rewards, selected, pad_mask, tokens, cotangent):
    rows, width = tokens.shape
    smem = pl.BlockSpec(memory_space=pltpu.SMEM)
    vmem = pl.BlockSpec(memory_space=pltpu.VMEM)
    return pl.pallas_call(
        prepare_kernel,
        out_shape=(
            jax.ShapeDtypeStruct((copies, rows, 2 * width), bf16),
            jax.ShapeDtypeStruct((n_k, rows, 2 * width // n_k), bf16),
        ),
        in_specs=[smem, smem, smem, smem, vmem, vmem],
        out_specs=(vmem, vmem),
    )(block.reshape(1), rewards, selected, pad_mask, tokens, cotangent)


def order_kernel(order, n_k, place_ref, pieces_ref, turned_ref):
    n_y = len(order)
    per = pieces_ref.shape[0] // (n_y * n_k * CORES)
    y = place_ref[0]
    k = place_ref[1]
    core = place_ref[2]

    def source(share, e, c, t):
        row = (share * per + e) * CORES + lax.rem(core + c, CORES)
        return row * n_k + lax.rem(t + n_k - k, n_k)

    spots = [(c, e) for c in range(CORES) for e in range(per)]
    at = 0
    for r in order:
        share = lax.rem(y + r, n_y)
        for t in range(n_k):
            for c, e in spots:
                turned_ref[at] = pieces_ref[source(share, e, c, t)]
                at += 1


def put_in_order(order, n_k, place, pieces):
    blocks, rows, both = pieces.shape
    vmem = pl.BlockSpec(memory_space=pltpu.VMEM)
    turned = pl.pallas_call(
        functools.partial(order_kernel, order, n_k),
        out_shape=jax.ShapeDtypeStruct((blocks, rows, both), bf16),
        in_specs=[pl.BlockSpec(memory_space=pltpu.SMEM), vmem],
        out_specs=vmem,
    )(place, pieces)
    return turned.reshape(blocks * rows, both)


def after(value, *others):
    return lax.optimization_barrier((value,) + others)[0]


def copies_to(value, axis):
    spread = jnp.broadcast_to(value[None], (lax.axis_size(axis),) + value.shape)
    return lax.all_to_all(spread, axis, 0, 0)


def body(tokens, cotangent, pad_mask, rewards, selected, gate_weight, up_weight, down_weight):
    n_y = lax.axis_size("y")
    n_k = lax.axis_size("zhi")
    y = lax.axis_index("y")
    rows, width = tokens.shape
    units = gate_weight.shape[1]
    k = lax.axis_index("zhi")
    block = lax.axis_index(ROW) * n_k + k
    copies = lax.axis_size(("zlo", "x"))
    half = copies * rows
    part = half // n_y
    share = 2 * part
    quarter = width // n_k

    spread, cut_spread = prepare(copies, n_k, block, rewards, selected, pad_mask, tokens, cotangent)
    mine = lax.all_to_all(spread, ("zlo", "x"), 0, 0)
    cuts = []
    for t in range(n_k):
        piece = lax.dynamic_index_in_dim(cut_spread, (k + n_k - t) % n_k, axis=0, keepdims=False)
        cuts.append(piece if t == 0 else shift(piece, "zhi", -t))
    cuts = jnp.stack(cuts, axis=0)
    mine, cuts = lax.optimization_barrier((mine, cuts))
    cuts = lax.all_gather(cuts, ROW, axis=0, tiled=True)
    other = shift(mine, "core", 1)

    pieces = []
    for rows_in in (mine.reshape(half, 2 * width), other.reshape(half, 2 * width)):
        gate = jnp.dot(rows_in[:, :width], gate_weight, preferred_element_type=f32) * SCALE_UP
        up = jnp.dot(rows_in[:, :width], up_weight, preferred_element_type=f32) * SCALE_UP
        back = SCALE_BACK * lax.dot_general(
            rows_in[:, width:], down_weight, (((1,), (1,)), ((), ())), preferred_element_type=f32
        )
        whole = jnp.concatenate([gate, up, back], axis=1).astype(f16)
        pieces.append(whole.reshape(n_y, part, 3 * units))
    partial_sums = jnp.concatenate(pieces, axis=1)
    sums = lax.all_to_all(partial_sums, "y", 0, 0)

    sums = jnp.sum(sums.astype(f32), axis=0)
    gate_value = sums[:, :units] * (1.0 / SCALE_UP)
    up_value = sums[:, units : 2 * units] * (1.0 / SCALE_UP)
    back_value = sums[:, 2 * units :] * (1.0 / SCALE_BACK)
    sigmoid_gate = jax.nn.sigmoid(gate_value)
    active = gate_value * sigmoid_gate
    hidden = (active * up_value).astype(bf16)
    gate_back = (
        back_value * up_value * sigmoid_gate * (1.0 + gate_value * (1.0 - sigmoid_gate))
    ).astype(bf16)
    up_back = (back_value * active).astype(bf16)

    values = jnp.concatenate([hidden, gate_back, up_back], axis=1)
    near = copies_to(values, "zhi").reshape(n_k * share, 3 * units)

    order = [0]
    for s in range(1, n_y // 2):
        order += [s, n_y - s]
    order.append(n_y // 2)
    place = jnp.stack([y, k, lax.axis_index("core")])

    right = left = near
    held = {0: near}
    for s in range(1, n_y // 2):
        right = shift(right, "y", 1)
        left = shift(left, "y", -1)
        held[n_y - s] = right
        held[s] = left
    middle = near.shape[0] // 2
    top = shift(right[:middle], "y", 1)
    low = shift(left[middle:], "y", -1)

    turned = put_in_order(order, n_k, place, after(cuts, top))

    contract = (((0,), (0,)), ((), ()))

    def product(a, b):
        return lax.dot_general(a, b, contract, preferred_element_type=f32)

    held[n_y // 2] = jnp.concatenate([top, low], axis=0)
    every = jnp.concatenate([held[r] for r in order], axis=0)
    gate_grad = product(turned[:, :quarter], every[:, units : 2 * units])
    up_grad = product(turned[:, :quarter], every[:, 2 * units :])
    down_grad = product(every[:, :units], turned[:, quarter:])
    return (gate_grad, up_grad, down_grad)


def solution(mesh):
    n_row, n_col, n_rep = mesh.devices.shape
    fine = Mesh(
        mesh.devices.reshape(Z_LO, n_row // (Z_LO * CORES), CORES, n_col, n_rep),
        ("zlo", "x", "core", "y", "zhi"),
    )
    blocks = ROW + ("zhi",)
    placed = (
        P(blocks, "y"),
        P(blocks, "y"),
        P(blocks),
        P(),
        P(),
        P("y", ROW),
        P("y", ROW),
        P(ROW, "y"),
    )
    return jax.shard_map(
        body,
        mesh=fine,
        in_specs=placed,
        out_specs=(P(("y", "zhi"), ROW), P(("y", "zhi"), ROW), P(ROW, ("y", "zhi"))),
        check_vma=False,
    )
```

time: 184 us -> 182 us (0.989)
  starting transfers between devices: 111 us -> 65 us
  blocking collectives: 0 us -> 31.1 us
  between operations: 1.21 us -> 14.4 us
  local copies, waits for them, and re-layouts: 21.3 us -> 8.5 us
  matrix products: 6.04 us -> 13 us
  Pallas kernels: 1.77 us -> 4.05 us
  waiting for transfers between devices: 39 us -> 41.1 us
    ppermute x20 -> x12, starting transfers between devices: 79.8 us -> 40.9 us  [shift(): return lax.ppermute(value, axis, [(i, (i + step) % n) for i in range(n)])]
    all_to_all x0 -> x1, blocking collectives: none -> 31.1 us  [body(): sums = lax.all_to_all(partial_sums, 'y', 0, 0)]
    all_to_all x1, waiting for transfers between devices: 10.8 us -> 0.01 us  [body(): mine = lax.all_to_all(spread, ('zlo', 'x'), 0, 0)]
    all_gather x0 -> x1, waiting for transfers between devices: none -> 10.5 us  [body(): cuts = lax.all_gather(cuts, ROW, axis=0, tiled=True)]
    all_to_all x2 -> x1, starting transfers between devices: 14.8 us -> 7.1 us  [copies_to(): return lax.all_to_all(spread, axis, 0, 0)]
    another operation x7 -> x0, local copies, waits for them, and re-layouts: 5.88 us -> none  [the longest x3 3.97 us: body(): jnp.stack([h.reshape(n_y, part, 2, n_k, quarter) for h in halves], axis=1)]
    dot_general x3, matrix products: 3.81 us -> 7.58 us  [product(): return lax.dot_general(a, b, contract, preferred_element_type=f32)]
    reshape x4 -> x0, local copies, waits for them, and re-layouts: 3.57 us -> none  [the longest x3 2.16 us: body(): cut = cut.reshape(n_y, share, 2 * quarter)]
  transfers between devices with their start and end apart: 23 -> 15, of which waited for: 7 -> 8; matrix products, arithmetic and copies ran while one was open for 11% -> 7% of each run, Pallas kernels for 0% -> 1%
where the time goes in v3:
time: 182 us; the launch traced here: 179 us
  starting transfers between devices  65 us (36%)
  waiting for transfers between devices  41.1 us (23%)
  blocking collectives  31.1 us (17%)
  between operations  14.4 us (8%)
  matrix products  13 us (7%)
  local copies, waits for them, and re-layouts  8.5 us (5%)
  Pallas kernels  4.05 us (2%)
    ppermute x12, starting transfers between devices, shift(): return lax.ppermute(value, axis, [(i, (i + step) % n) for i in range(n)])  40.9 us
    all_to_all x1, blocking collectives, body(): sums = lax.all_to_all(partial_sums, 'y', 0, 0)  31.1 us
    ppermute x12, waiting for transfers between devices, shift(): return lax.ppermute(value, axis, [(i, (i + step) % n) for i in range(n)])  17.2 us
    all_to_all x1, starting transfers between devices, body(): mine = lax.all_to_all(spread, ('zlo', 'x'), 0, 0)  17 us
    all_to_all x1, waiting for transfers between devices, copies_to(): return lax.all_to_all(spread, axis, 0, 0)  12.7 us
    all_gather x1, waiting for transfers between devices, body(): cuts = lax.all_gather(cuts, ROW, axis=0, tiled=True)  10.5 us
    dot_general x3, matrix products, product(): return lax.dot_general(a, b, contract, preferred_element_type=f32)  7.58 us
    all_to_all x1, starting transfers between devices, copies_to(): return lax.all_to_all(spread, axis, 0, 0)  7.1 us
  transfers between devices with their start and end apart: 15, of which 8 were waited for; matrix products, arithmetic and copies ran while one was open for 7% of the time, Pallas kernels for 1%

profile of v3, /device:TPU:14, one launch (start us, length us, event | category | flops | bytes accessed | tf_op | source)
XLA Modules:
  0.0 178.9 jit_solution(12417685941054060459)
XLA Ops:
  7.2 0.0 copy-start
  7.2 0.0 copy-start.2
  7.2 1.7 shard_map.103
  8.9 17.0 %all-to-all-start = ((bf16[16,8,2048]{2,1,0:T(8,128)(2,1)}), bf16[16,8,2048]{2,1,0:T(8,128)(2,1)}, u32[]{:S(2)}, u32[]{:S(2)}) async-start(bf16[16,8,2048]{2,1,0:T(8,128)(2,1)} %get-tuple-element.8), calls=%async_computation | async-start | bytes 1048576 | tf_op jit(solution)/shard_map/all_to_all | solution.py:124
  26.0 0.8 constant_dynamic-slice_fusion
  26.9 8.3 %collective-permute-start = (bf16[8,512]{1,0:T(8,128)(2,1)S(1)}, bf16[8,512]{1,0:T(8,128)(2,1)S(1)}, u32[]{:S(2)}, u32[]{:S(2)}) collective-permute-start(bf16[8,512]{1,0:T(8,128)(2,1)S(1)} %get-tuple-element.19), channel_id=1, source_target_pairs={{0,3},{1,0},{2,1},{3,2},{4,7},{5,4},{6,5},{7,6},{8,11},{9,8},{10,9... | collective-permute-start | bytes 24584 | tf_op jit(solution)/shard_map/ppermute | solution.py:25
  35.2 1.9 %collective-permute-start.1 = (bf16[8,512]{1,0:T(8,128)(2,1)S(1)}, bf16[8,512]{1,0:T(8,128)(2,1)S(1)}, u32[]{:S(2)}, u32[]{:S(2)}) collective-permute-start(bf16[8,512]{1,0:T(8,128)(2,1)S(1)} %get-tuple-element.18), channel_id=1, source_target_pairs={{0,2},{1,3},{2,0},{3,1},{4,6},{5,7},{6,4},{7,5},{8,10},{9,11},{10,... | collective-permute-start | bytes 24584 | tf_op jit(solution)/shard_map/ppermute | solution.py:25
  37.1 4.3 %collective-permute-start.2 = (bf16[8,512]{1,0:T(8,128)(2,1)S(1)}, bf16[8,512]{1,0:T(8,128)(2,1)S(1)}, u32[]{:S(2)}, u32[]{:S(2)}) collective-permute-start(bf16[8,512]{1,0:T(8,128)(2,1)S(1)} %get-tuple-element.17), channel_id=1, source_target_pairs={{0,1},{1,2},{2,3},{3,0},{4,5},{5,6},{6,7},{7,4},{8,9},{9,10},{10,1... | collective-permute-start | bytes 24584 | tf_op jit(solution)/shard_map/ppermute | solution.py:25
  41.4 0.0 collective-permute-done
  41.4 3.3 %collective-permute-done.1 = bf16[8,512]{1,0:T(8,128)(2,1)S(1)} collective-permute-done((bf16[8,512]{1,0:T(8,128)(2,1)S(1)}, bf16[8,512]{1,0:T(8,128)(2,1)S(1)}, u32[]{:S(2)}, u32[]{:S(2)}) %collective-permute-start.1) | collective-permute-done | bytes 8224 | tf_op jit(solution)/shard_map/ppermute | solution.py:25
  44.7 0.2 collective-permute-done.2
  44.9 0.6 pad_maximum_fusion.1
  45.5 0.0 all-to-all-done
  45.5 1.9 %collective-permute-start.3 = (bf16[16,8,2048]{2,1,0:T(8,128)(2,1)}, bf16[16,8,2048]{2,1,0:T(8,128)(2,1)S(1)}, u32[]{:S(2)}, u32[]{:S(2)}) collective-permute-start(bf16[16,8,2048]{2,1,0:T(8,128)(2,1)} %all-to-all-done), channel_id=1, source_target_pairs={{0,32},{32,0},{1,33},{33,1},{2,34},{34,2},{3,35},{35,3},{4,36},{36... | collective-permute-start | bytes 1572872 | tf_op jit(solution)/shard_map/ppermute | solution.py:25
  47.4 0.0 copy-done
  47.4 1.3 fusion
  48.7 1.6 fusion.1
  50.3 0.0 copy-done.2
  50.3 1.4 fusion.2
  51.8 0.0 collective-permute-done.3
  51.8 0.3 fusion.3
  52.1 0.0 copy-done.1
  52.1 0.3 fusion.4
  52.4 0.5 fusion.5
  52.9 0.3 maximum_maximum_fusion
  53.2 31.1 %all_to_all.15 = f16[8,32,1536]{2,1,0:T(8,128)(2,1)S(1)} all-to-all(f16[8,32,1536]{2,1,0:T(8,128)(2,1)S(1)} %maximum_maximum_fusion), channel_id=1, replica_groups=mesh['zlo'=2,'x'=8,'core'=2,'y'=8,'zhi'=4] {'y'}, dimensions={0} | all-to-all | bytes 1572864 | tf_op jit(solution)/shard_map/all_to_all | solution.py:144
  84.3 0.1 convert_reduce_fusion
  84.4 0.1 multiply_convert_fusion.2
  84.5 0.8 broadcast_in_dim.2
  85.3 7.1 %all-to-all-start.2 = ((bf16[4,32,1536]{2,1,0:T(8,128)(2,1)}), bf16[4,32,1536]{2,1,0:T(8,128)(2,1)S(1)}, u32[]{:S(2)}, u32[]{:S(2)}) async-start(bf16[4,32,1536]{2,1,0:T(8,128)(2,1)} %broadcast_in_dim.2), calls=%async_computation.2 | async-start | bytes 786432 | tf_op jit(solution)/shard_map/all_to_all | solution.py:106
  92.4 0.0 all-gather.2.cloned.1.call-start
  92.4 0.7 all-gather.2.cloned.1.call-update
  93.1 12.7 %all-to-all-done.2 = bf16[4,32,1536]{2,1,0:T(8,128)(2,1)S(1)} async-done(((bf16[4,32,1536]{2,1,0:T(8,128)(2,1)}), bf16[4,32,1536]{2,1,0:T(8,128)(2,1)S(1)}, u32[]{:S(2)}, u32[]{:S(2)}) %all-to-all-start.2) | async-done | bytes 393248 | tf_op jit(solution)/shard_map/all_to_all | solution.py:106
  105.8 1.9 %collective-permute-start.8 = (bf16[128,1536]{1,0:T(8,128)(2,1)S(1)}, bf16[128,1536]{1,0:T(8,128)(2,1)S(1)}, u32[]{:S(2)}, u32[]{:S(2)}) collective-permute-start(bf16[128,1536]{1,0:T(8,128)(2,1)S(1)} %bitcast.29), channel_id=1, source_target_pairs={{0,28},{4,0},{8,4},{12,8},{16,12},{20,16},{24,20},{28,24},{1,29},{... | collective-permute-start | bytes 1179656 | tf_op jit(solution)/shard_map/ppermute | solution.py:25
  107.7 3.9 %collective-permute-start.4 = (bf16[128,1536]{1,0:T(8,128)(2,1)S(1)}, bf16[128,1536]{1,0:T(8,128)(2,1)S(1)}, u32[]{:S(2)}, u32[]{:S(2)}) collective-permute-start(bf16[128,1536]{1,0:T(8,128)(2,1)S(1)} %bitcast.30), channel_id=1, source_target_pairs={{0,4},{4,8},{8,12},{12,16},{16,20},{20,24},{24,28},{28,0},{1,5},{5... | collective-permute-start | bytes 1179656 | tf_op jit(solution)/shard_map/ppermute | solution.py:25
  111.6 0.7 pad_add_fusion.place_ref
  112.3 0.8 constant_dynamic-update-slice_fusion.8
  113.1 2.4 %collective-permute-done.8 = bf16[128,1536]{1,0:T(8,128)(2,1)S(1)} collective-permute-done((bf16[128,1536]{1,0:T(8,128)(2,1)S(1)}, bf16[128,1536]{1,0:T(8,128)(2,1)S(1)}, u32[]{:S(2)}, u32[]{:S(2)}) %collective-permute-start.8) | collective-permute-done | bytes 393248 | tf_op jit(solution)/shard_map/ppermute | solution.py:25
  115.5 3.1 %collective-permute-start.9 = (bf16[128,1536]{1,0:T(8,128)(2,1)S(1)}, bf16[128,1536]{1,0:T(8,128)(2,1)S(1)}, u32[]{:S(2)}, u32[]{:S(2)}) collective-permute-start(bf16[128,1536]{1,0:T(8,128)(2,1)S(1)} %collective-permute-done.8), channel_id=1, source_target_pairs={{0,28},{4,0},{8,4},{12,8},{16,12},{20,16},{24,20},{28,24},{1,29},{... | collective-permute-start | bytes 1179656 | tf_op jit(solution)/shard_map/ppermute | solution.py:25
  118.6 0.0 collective-permute-done.4
  118.6 2.7 %collective-permute-start.5 = (bf16[128,1536]{1,0:T(8,128)(2,1)S(1)}, bf16[128,1536]{1,0:T(8,128)(2,1)S(1)}, u32[]{:S(2)}, u32[]{:S(2)}) collective-permute-start(bf16[128,1536]{1,0:T(8,128)(2,1)S(1)} %collective-permute-done.4), channel_id=1, source_target_pairs={{0,4},{4,8},{8,12},{12,16},{16,20},{20,24},{24,28},{28,0},{1,5},{5... | collective-permute-start | bytes 1179656 | tf_op jit(solution)/shard_map/ppermute | solution.py:25
  121.4 0.8 constant_dynamic-update-slice_fusion.7
  122.1 0.8 constant_dynamic-update-slice_fusion.6
  122.9 3.0 %collective-permute-done.9 = bf16[128,1536]{1,0:T(8,128)(2,1)S(1)} collective-permute-done((bf16[128,1536]{1,0:T(8,128)(2,1)S(1)}, bf16[128,1536]{1,0:T(8,128)(2,1)S(1)}, u32[]{:S(2)}, u32[]{:S(2)}) %collective-permute-start.9) | collective-permute-done | bytes 393248 | tf_op jit(solution)/shard_map/ppermute | solution.py:25
  126.0 3.5 %collective-permute-start.10 = (bf16[128,1536]{1,0:T(8,128)(2,1)S(1)}, bf16[128,1536]{1,0:T(8,128)(2,1)S(1)}, u32[]{:S(2)}, u32[]{:S(2)}) collective-permute-start(bf16[128,1536]{1,0:T(8,128)(2,1)S(1)} %collective-permute-done.9), channel_id=1, source_target_pairs={{0,28},{4,0},{8,4},{12,8},{16,12},{20,16},{24,20},{28,24},{1,29},{... | collective-permute-start | bytes 1179656 | tf_op jit(solution)/shard_map/ppermute | solution.py:25
  129.5 0.1 collective-permute-done.5
  129.6 2.2 %collective-permute-start.6 = (bf16[128,1536]{1,0:T(8,128)(2,1)S(1)}, bf16[128,1536]{1,0:T(8,128)(2,1)S(1)}, u32[]{:S(2)}, u32[]{:S(2)}) collective-permute-start(bf16[128,1536]{1,0:T(8,128)(2,1)S(1)} %collective-permute-done.5), channel_id=1, source_target_pairs={{0,4},{4,8},{8,12},{12,16},{16,20},{20,24},{24,28},{28,0},{1,5},{5... | collective-permute-start | bytes 1179656 | tf_op jit(solution)/shard_map/ppermute | solution.py:25
  131.8 0.8 constant_dynamic-update-slice_fusion.5
  132.6 0.8 constant_dynamic-update-slice_fusion.4
  133.4 8.2 %collective-permute-done.6 = bf16[128,1536]{1,0:T(8,128)(2,1)S(1)} collective-permute-done((bf16[128,1536]{1,0:T(8,128)(2,1)S(1)}, bf16[128,1536]{1,0:T(8,128)(2,1)S(1)}, u32[]{:S(2)}, u32[]{:S(2)}) %collective-permute-start.6) | collective-permute-done | bytes 393248 | tf_op jit(solution)/shard_map/ppermute | solution.py:25
  141.6 1.9 %collective-permute-start.7 = (bf16[64,1536]{1,0:T(8,128)(2,1)S(1)}, bf16[64,1536]{1,0:T(8,128)(2,1)S(1)}, u32[]{:S(2)}, u32[]{:S(2)}) collective-permute-start(bf16[64,1536]{1,0:T(8,128)(2,1)S(1)} %slice.66), channel_id=1, source_target_pairs={{0,4},{4,8},{8,12},{12,16},{16,20},{20,24},{24,28},{28,0},{1,5},{5... | collective-permute-start | bytes 589832 | tf_op jit(solution)/shard_map/ppermute | solution.py:25
  143.5 0.0 collective-permute-done.10
  143.6 5.1 %collective-permute-start.11 = (bf16[64,1536]{1,0:T(8,128)(2,1)S(1)}, bf16[64,1536]{1,0:T(8,128)(2,1)S(1)}, u32[]{:S(2)}, u32[]{:S(2)}) collective-permute-start(bf16[64,1536]{1,0:T(8,128)(2,1)S(1)} %slice.68), channel_id=1, source_target_pairs={{0,28},{4,0},{8,4},{12,8},{16,12},{20,16},{24,20},{28,24},{1,29},{... | collective-permute-start | bytes 589832 | tf_op jit(solution)/shard_map/ppermute | solution.py:25
  148.7 0.8 constant_dynamic-update-slice_fusion.3
  149.5 0.8 constant_dynamic-update-slice_fusion.2
  150.2 10.5 %all-gather.2.cloned.1.call-done.pieces_ref = bf16[128,8,512]{2,1,0:T(8,128)(2,1)} async-done(((bf16[4,8,512]{2,1,0:T(8,128)(2,1)}), bf16[128,8,512]{2,1,0:T(8,128)(2,1)}) %all-gather.2.cloned.1.call-update) | async-done | bytes 1048592 | tf_op jit(solution)/shard_map/all_gather | solution.py:131
  160.7 0.0 collective-permute-done.7
  160.7 2.3 %shard_map.104 = bf16[128,8,512]{2,1,0:T(8,128)(2,1)} custom-call(s32[3]{0:T(128)} %pad_add_fusion.place_ref, bf16[128,8,512]{2,1,0:T(8,128)(2,1)} %all-gather.2.cloned.1.call-done.pieces_ref), custom_call_target="tpu_custom_call" | custom-call | tf_op jit(solution)/shard_map/pallas_call | solution.py:91
  163.1 0.7 constant_dynamic-update-slice_fusion.1
  163.8 0.0 collective-permute-done.11
  163.8 0.7 constant_dynamic-update-slice_fusion
  164.4 2.6 %fusion.6 = f32[512,256]{1,0:T(8,128)} fusion(bf16[1024,1536]{1,0:T(8,128)(2,1)} %constant_dynamic-update-slice_fusion, bf16[1024,512]{1,0:T(8,128)(2,1)} %bitcast.35), kind=kOutput, calls=%fused_computation.13 | convolution fusion | flops 268435456 | bytes 2097152 | tf_op jit(solution)/shard_map/dot_general | solution.py:183
  167.1 2.5 %fusion.8 = f32[256,512]{1,0:T(8,128)} fusion(bf16[1024,1536]{1,0:T(8,128)(2,1)} %constant_dynamic-update-slice_fusion, bf16[1024,512]{1,0:T(8,128)(2,1)S(1)} %bitcast.36), kind=kOutput, calls=%fused_computation.15 | convolution fusion | flops 268435456 | bytes 2097152 | tf_op jit(solution)/shard_map/dot_general | solution.py:183
  169.6 2.5 %fusion.10 = f32[256,512]{1,0:T(8,128)} fusion(bf16[1024,1536]{1,0:T(8,128)(2,1)} %constant_dynamic-update-slice_fusion, bf16[1024,512]{1,0:T(8,128)(2,1)S(1)} %bitcast.37), kind=kOutput, calls=%fused_computation.17 | convolution fusion | flops 268435456 | bytes 2097152 | tf_op jit(solution)/shard_map/dot_general | solution.py:183
  (6 shorter events, 0.0 us)
Async XLA Ops:
  7.2 40.3 %copy-start = (bf16[1024,512]{1,0:T(8,128)(2,1)S(1)}, bf16[1024,512]{1,0:T(8,128)(2,1)}, u32[]{:S(2)}) copy-start(bf16[1024,512]{1,0:T(8,128)(2,1)} %param.13) | copy-start | bytes 3145732
  7.2 43.2 %copy-start.2 = (bf16[512,1024]{1,0:T(8,128)(2,1)S(1)}, bf16[512,1024]{1,0:T(8,128)(2,1)}, u32[]{:S(2)}) copy-start(bf16[512,1024]{1,0:T(8,128)(2,1)} %param.15) | copy-start | bytes 3145732
  8.9 36.6 %all-to-all-start = ((bf16[16,8,2048]{2,1,0:T(8,128)(2,1)}), bf16[16,8,2048]{2,1,0:T(8,128)(2,1)}, u32[]{:S(2)}, u32[]{:S(2)}) async-start(bf16[16,8,2048]{2,1,0:T(8,128)(2,1)} %get-tuple-element.8), calls=%async_computation | async-start | bytes 1048576 | tf_op jit(solution)/shard_map/all_to_all | solution.py:124
  26.0 26.2 %copy-start.1 = (bf16[1024,512]{1,0:T(8,128)(2,1)S(1)}, bf16[1024,512]{1,0:T(8,128)(2,1)}, u32[]{:S(2)}) copy-start(bf16[1024,512]{1,0:T(8,128)(2,1)} %param.14) | copy-start | bytes 3145732
  26.9 14.5 %collective-permute-start = (bf16[8,512]{1,0:T(8,128)(2,1)S(1)}, bf16[8,512]{1,0:T(8,128)(2,1)S(1)}, u32[]{:S(2)}, u32[]{:S(2)}) collective-permute-start(bf16[8,512]{1,0:T(8,128)(2,1)S(1)} %get-tuple-element.19), channel_id=1, source_target_pairs={{0,3},{1,0},{2,1},{3,2},{4,7},{5,4},{6,5},{7,6},{8,11},{9,8},{10,9... | collective-permute-start | bytes 24584 | tf_op jit(solution)/shard_map/ppermute | solution.py:25
  35.2 9.5 %collective-permute-start.1 = (bf16[8,512]{1,0:T(8,128)(2,1)S(1)}, bf16[8,512]{1,0:T(8,128)(2,1)S(1)}, u32[]{:S(2)}, u32[]{:S(2)}) collective-permute-start(bf16[8,512]{1,0:T(8,128)(2,1)S(1)} %get-tuple-element.18), channel_id=1, source_target_pairs={{0,2},{1,3},{2,0},{3,1},{4,6},{5,7},{6,4},{7,5},{8,10},{9,11},{10,... | collective-permute-start | bytes 24584 | tf_op jit(solution)/shard_map/ppermute | solution.py:25
  37.1 7.8 %collective-permute-start.2 = (bf16[8,512]{1,0:T(8,128)(2,1)S(1)}, bf16[8,512]{1,0:T(8,128)(2,1)S(1)}, u32[]{:S(2)}, u32[]{:S(2)}) collective-permute-start(bf16[8,512]{1,0:T(8,128)(2,1)S(1)} %get-tuple-element.17), channel_id=1, source_target_pairs={{0,1},{1,2},{2,3},{3,0},{4,5},{5,6},{6,7},{7,4},{8,9},{9,10},{10,1... | collective-permute-start | bytes 24584 | tf_op jit(solution)/shard_map/ppermute | solution.py:25
  45.5 6.3 %collective-permute-start.3 = (bf16[16,8,2048]{2,1,0:T(8,128)(2,1)}, bf16[16,8,2048]{2,1,0:T(8,128)(2,1)S(1)}, u32[]{:S(2)}, u32[]{:S(2)}) collective-permute-start(bf16[16,8,2048]{2,1,0:T(8,128)(2,1)} %all-to-all-done), channel_id=1, source_target_pairs={{0,32},{32,0},{1,33},{33,1},{2,34},{34,2},{3,35},{35,3},{4,36},{36... | collective-permute-start | bytes 1572872 | tf_op jit(solution)/shard_map/ppermute | solution.py:25
  85.3 20.5 %all-to-all-start.2 = ((bf16[4,32,1536]{2,1,0:T(8,128)(2,1)}), bf16[4,32,1536]{2,1,0:T(8,128)(2,1)S(1)}, u32[]{:S(2)}, u32[]{:S(2)}) async-start(bf16[4,32,1536]{2,1,0:T(8,128)(2,1)} %broadcast_in_dim.2), calls=%async_computation.2 | async-start | bytes 786432 | tf_op jit(solution)/shard_map/all_to_all | solution.py:106
  92.4 68.4 %all-gather.2.cloned.1.call-start = ((), (), s32[]{:S(2)}) async-start(), calls=%async_computation.3 | async-start | bytes 1081344 | tf_op jit(solution)/shard_map/all_gather | solution.py:131
  105.8 9.7 %collective-permute-start.8 = (bf16[128,1536]{1,0:T(8,128)(2,1)S(1)}, bf16[128,1536]{1,0:T(8,128)(2,1)S(1)}, u32[]{:S(2)}, u32[]{:S(2)}) collective-permute-start(bf16[128,1536]{1,0:T(8,128)(2,1)S(1)} %bitcast.29), channel_id=1, source_target_pairs={{0,28},{4,0},{8,4},{12,8},{16,12},{20,16},{24,20},{28,24},{1,29},{... | collective-permute-start | bytes 1179656 | tf_op jit(solution)/shard_map/ppermute | solution.py:25
  107.7 10.9 %collective-permute-start.4 = (bf16[128,1536]{1,0:T(8,128)(2,1)S(1)}, bf16[128,1536]{1,0:T(8,128)(2,1)S(1)}, u32[]{:S(2)}, u32[]{:S(2)}) collective-permute-start(bf16[128,1536]{1,0:T(8,128)(2,1)S(1)} %bitcast.30), channel_id=1, source_target_pairs={{0,4},{4,8},{8,12},{12,16},{16,20},{20,24},{24,28},{28,0},{1,5},{5... | collective-permute-start | bytes 1179656 | tf_op jit(solution)/shard_map/ppermute | solution.py:25
  115.5 10.5 %collective-permute-start.9 = (bf16[128,1536]{1,0:T(8,128)(2,1)S(1)}, bf16[128,1536]{1,0:T(8,128)(2,1)S(1)}, u32[]{:S(2)}, u32[]{:S(2)}) collective-permute-start(bf16[128,1536]{1,0:T(8,128)(2,1)S(1)} %collective-permute-done.8), channel_id=1, source_target_pairs={{0,28},{4,0},{8,4},{12,8},{16,12},{20,16},{24,20},{28,24},{1,29},{... | collective-permute-start | bytes 1179656 | tf_op jit(solution)/shard_map/ppermute | solution.py:25
  118.6 10.9 %collective-permute-start.5 = (bf16[128,1536]{1,0:T(8,128)(2,1)S(1)}, bf16[128,1536]{1,0:T(8,128)(2,1)S(1)}, u32[]{:S(2)}, u32[]{:S(2)}) collective-permute-start(bf16[128,1536]{1,0:T(8,128)(2,1)S(1)} %collective-permute-done.4), channel_id=1, source_target_pairs={{0,4},{4,8},{8,12},{12,16},{16,20},{20,24},{24,28},{28,0},{1,5},{5... | collective-permute-start | bytes 1179656 | tf_op jit(solution)/shard_map/ppermute | solution.py:25
  126.0 17.6 %collective-permute-start.10 = (bf16[128,1536]{1,0:T(8,128)(2,1)S(1)}, bf16[128,1536]{1,0:T(8,128)(2,1)S(1)}, u32[]{:S(2)}, u32[]{:S(2)}) collective-permute-start(bf16[128,1536]{1,0:T(8,128)(2,1)S(1)} %collective-permute-done.9), channel_id=1, source_target_pairs={{0,28},{4,0},{8,4},{12,8},{16,12},{20,16},{24,20},{28,24},{1,29},{... | collective-permute-start | bytes 1179656 | tf_op jit(solution)/shard_map/ppermute | solution.py:25
  129.6 12.0 %collective-permute-start.6 = (bf16[128,1536]{1,0:T(8,128)(2,1)S(1)}, bf16[128,1536]{1,0:T(8,128)(2,1)S(1)}, u32[]{:S(2)}, u32[]{:S(2)}) collective-permute-start(bf16[128,1536]{1,0:T(8,128)(2,1)S(1)} %collective-permute-done.5), channel_id=1, source_target_pairs={{0,4},{4,8},{8,12},{12,16},{16,20},{20,24},{24,28},{28,0},{1,5},{5... | collective-permute-start | bytes 1179656 | tf_op jit(solution)/shard_map/ppermute | solution.py:25
  141.6 19.2 %collective-permute-start.7 = (bf16[64,1536]{1,0:T(8,128)(2,1)S(1)}, bf16[64,1536]{1,0:T(8,128)(2,1)S(1)}, u32[]{:S(2)}, u32[]{:S(2)}) collective-permute-start(bf16[64,1536]{1,0:T(8,128)(2,1)S(1)} %slice.66), channel_id=1, source_target_pairs={{0,4},{4,8},{8,12},{12,16},{16,20},{20,24},{24,28},{28,0},{1,5},{5... | collective-permute-start | bytes 589832 | tf_op jit(solution)/shard_map/ppermute | solution.py:25
  143.6 20.2 %collective-permute-start.11 = (bf16[64,1536]{1,0:T(8,128)(2,1)S(1)}, bf16[64,1536]{1,0:T(8,128)(2,1)S(1)}, u32[]{:S(2)}, u32[]{:S(2)}) collective-permute-start(bf16[64,1536]{1,0:T(8,128)(2,1)S(1)} %slice.68), channel_id=1, source_target_pairs={{0,28},{4,0},{8,4},{12,8},{16,12},{20,16},{24,20},{28,24},{1,29},{... | collective-permute-start | bytes 589832 | tf_op jit(solution)/shard_map/ppermute | solution.py:25
  163.1 4.0 %copy-start.3 = (bf16[128,8,512]{2,1,0:T(8,128)(2,1)S(1)}, bf16[128,8,512]{2,1,0:T(8,128)(2,1)}, u32[]{:S(2)}) copy-start(bf16[128,8,512]{2,1,0:T(8,128)(2,1)} %shard_map.104) | copy-start | bytes 3145732
Sparse Core Ops, SparseCore 0:
  96.5 64.1 all-gather.1

commit v4 on v3

v4 whole, which is shorter than its diff:
```python
import functools

import jax
import jax.numpy as jnp
from jax import lax
from jax.experimental import pallas as pl
from jax.experimental.pallas import tpu as pltpu
from jax.sharding import Mesh
from jax.sharding import PartitionSpec as P

SAMPLES = 8
COMP_LEN = 16
CORES = 2
Z_LO = 2
SCALE_UP = 128.0
SCALE_BACK = 1024.0
ROW = ("zlo", "x", "core")
bf16 = jnp.bfloat16
f16 = jnp.float16
f32 = jnp.float32


def shift(value, axis, step):
    n = lax.axis_size(axis)
    return lax.ppermute(value, axis, [(i, (i + step) % n) for i in range(n)])


def prepare_kernel(block_ref, rewards_ref, selected_ref, pad_ref, tokens_ref, cotangent_ref, all_ref):
    rows, width = tokens_ref.shape
    completion = block_ref[0] * rows // COMP_LEN
    prompt = completion // SAMPLES
    sample = completion % SAMPLES
    reward = rewards_ref[prompt, sample].astype(f32)
    chosen = jnp.where(selected_ref[prompt] == sample, 1.0, 0.0)
    factor = reward / 4.0 + chosen
    row = lax.broadcasted_iota(jnp.int32, (rows, 1), 0)
    weight = jnp.zeros((rows, 1), f32)
    for n in range(rows):
        weight = jnp.where(row == n, pad_ref[n].astype(f32) * factor, weight)
    grads = (weight * cotangent_ref[...].astype(f32)).astype(bf16)
    for copy in range(all_ref.shape[0]):
        all_ref[copy, :, :width] = tokens_ref[...]
        all_ref[copy, :, width:] = grads


def in_vmem():
    return pl.BlockSpec(memory_space=pltpu.VMEM)


def in_smem():
    return pl.BlockSpec(memory_space=pltpu.SMEM)


def prepare(copies, block, rewards, selected, pad_mask, tokens, cotangent):
    rows, width = tokens.shape
    return pl.pallas_call(
        prepare_kernel,
        out_shape=jax.ShapeDtypeStruct((copies, rows, 2 * width), bf16),
        in_specs=[in_smem()] * 4 + [in_vmem()] * 2,
        out_specs=in_vmem(),
    )(block.reshape(1), rewards, selected, pad_mask, tokens, cotangent)


def cut_kernel(rows_ref, out_ref):
    n_k = out_ref.shape[0]
    width = rows_ref.shape[1] // 2
    quarter = width // n_k
    for t in range(n_k):
        out_ref[t, :, :quarter] = rows_ref[:, t * quarter : (t + 1) * quarter]
        out_ref[t, :, quarter:] = rows_ref[:, width + t * quarter : width + (t + 1) * quarter]


def cut_quarters(n_k, rows):
    return pl.pallas_call(
        cut_kernel,
        out_shape=jax.ShapeDtypeStruct((n_k, rows.shape[0], rows.shape[1] // n_k), bf16),
        in_specs=[in_vmem()],
        out_specs=in_vmem(),
    )(rows)


def order_kernel(order, place_ref, own_ref, other_ref, out_ref):
    n_k, rows, _ = own_ref.shape
    n_y = len(order)
    part = rows // n_y
    y = place_ref[0]
    at = 0
    for r in order:
        share = lax.rem(y + r, n_y)
        spot = pl.ds(pl.multiple_of(share * part, part), part)
        for t in range(n_k):
            for ref in (own_ref, other_ref):
                out_ref[at : at + part, :] = ref[t, spot, :]
                at += part


def put_in_order(order, y, own, other):
    n_k, rows, both = own.shape
    return pl.pallas_call(
        functools.partial(order_kernel, order),
        out_shape=jax.ShapeDtypeStruct((2 * n_k * rows, both), bf16),
        in_specs=[in_smem(), in_vmem(), in_vmem()],
        out_specs=in_vmem(),
    )(y.reshape(1), own, other)


def product(a, b):
    return lax.dot_general(a, b, (((0,), (0,)), ((), ())), preferred_element_type=f32)


def products_kernel(n, inputs_ref, *refs):
    value_refs = refs[:n]
    gate_ref, up_ref, down_ref, every_ref = refs[n:]
    at = 0
    for ref in value_refs:
        rows = ref.shape[0]
        every_ref[at : at + rows, :] = ref[...]
        at += rows
    units = gate_ref.shape[1]
    quarter = gate_ref.shape[0]
    tokens = inputs_ref[:, :quarter]
    down_ref[...] = product(every_ref[:, :units], inputs_ref[:, quarter:])
    gate_ref[...] = product(tokens, every_ref[:, units : 2 * units])
    up_ref[...] = product(tokens, every_ref[:, 2 * units :])


def products(inputs, values):
    rows, both = inputs.shape
    quarter = both // 2
    width = values[0].shape[1]
    units = width // 3
    wide = jax.ShapeDtypeStruct((quarter, units), f32)
    return pl.pallas_call(
        functools.partial(products_kernel, len(values)),
        out_shape=(wide, wide, jax.ShapeDtypeStruct((units, quarter), f32)),
        in_specs=[in_vmem()] * (1 + len(values)),
        out_specs=(in_vmem(),) * 3,
        scratch_shapes=[pltpu.VMEM((rows, width), bf16)],
        compiler_params=pltpu.CompilerParams(vmem_limit_bytes=40 * 1024 * 1024),
    )(inputs, *values)


def after(value, *others):
    return lax.optimization_barrier((value,) + others)[0]


def copies_to(value, axis):
    spread = jnp.broadcast_to(value[None], (lax.axis_size(axis),) + value.shape)
    return lax.all_to_all(spread, axis, 0, 0)


def body(tokens, cotangent, pad_mask, rewards, selected, gate_weight, up_weight, down_weight):
    n_y = lax.axis_size("y")
    n_k = lax.axis_size("zhi")
    y = lax.axis_index("y")
    rows, width = tokens.shape
    units = gate_weight.shape[1]
    block = lax.axis_index(ROW) * n_k + lax.axis_index("zhi")
    copies = lax.axis_size(("zlo", "x"))
    half = copies * rows
    part = half // n_y
    share = 2 * part
    quarter = width // n_k

    spread = prepare(copies, block, rewards, selected, pad_mask, tokens, cotangent)
    mine = lax.all_to_all(spread, ("zlo", "x"), 0, 0)
    other = shift(mine, "core", 1).reshape(half, 2 * width)
    mine = mine.reshape(half, 2 * width)
    own_cuts = lax.all_to_all(cut_quarters(n_k, mine), "zhi", 0, 0)

    pieces = []
    for rows_in in (mine, other):
        gate = jnp.dot(rows_in[:, :width], gate_weight, preferred_element_type=f32) * SCALE_UP
        up = jnp.dot(rows_in[:, :width], up_weight, preferred_element_type=f32) * SCALE_UP
        back = SCALE_BACK * lax.dot_general(
            rows_in[:, width:], down_weight, (((1,), (1,)), ((), ())), preferred_element_type=f32
        )
        whole = jnp.concatenate([gate, up, back], axis=1).astype(f16)
        pieces.append(whole.reshape(n_y, part, 3 * units))
    partial_sums = after(jnp.concatenate(pieces, axis=1), own_cuts)
    sums = jnp.sum(lax.all_to_all(partial_sums, "y", 0, 0).astype(f32), axis=0)

    gate_value = sums[:, :units] * (1.0 / SCALE_UP)
    up_value = sums[:, units : 2 * units] * (1.0 / SCALE_UP)
    back_value = sums[:, 2 * units :] * (1.0 / SCALE_BACK)
    sigmoid_gate = jax.nn.sigmoid(gate_value)
    active = gate_value * sigmoid_gate
    hidden = (active * up_value).astype(bf16)
    gate_back = (
        back_value * up_value * sigmoid_gate * (1.0 + gate_value * (1.0 - sigmoid_gate))
    ).astype(bf16)
    up_back = (back_value * active).astype(bf16)
    values = jnp.concatenate([hidden, gate_back, up_back], axis=1)
    near = copies_to(values, "zhi").reshape(n_k * share, 3 * units)

    order = [0]
    for s in range(1, n_y // 2):
        order += [s, n_y - s]
    order.append(n_y // 2)
    other_cuts = shift(own_cuts, "core", 1)
    right = left = near
    held = {0: near}
    for s in range(1, n_y // 2):
        right = shift(right, "y", 1)
        left = shift(left, "y", -1)
        held[n_y - s] = right
        held[s] = left
        if s == 1:
            inputs = put_in_order(order, y, own_cuts, after(other_cuts, right, left))
    middle = near.shape[0] // 2
    top = shift(right[:middle], "y", 1)
    low = shift(left[middle:], "y", -1)
    return products(inputs, [held[r] for r in order[:-1]] + [top, low])


def solution(mesh):
    n_row, n_col, n_rep = mesh.devices.shape
    fine = Mesh(
        mesh.devices.reshape(Z_LO, n_row // (Z_LO * CORES), CORES, n_col, n_rep),
        ("zlo", "x", "core", "y", "zhi"),
    )
    blocks = ROW + ("zhi",)
    placed = (
        P(blocks, "y"),
        P(blocks, "y"),
        P(blocks),
        P(),
        P(),
        P("y", ROW),
        P("y", ROW),
        P(ROW, "y"),
    )
    return jax.shard_map(
        body,
        mesh=fine,
        in_specs=placed,
        out_specs=(P(("y", "zhi"), ROW), P(("y", "zhi"), ROW), P(ROW, ("y", "zhi"))),
        check_vma=False,
    )
```

time: 182 us -> 162 us (0.89)
  blocking collectives: 31.1 us -> 73.3 us
  starting transfers between devices: 65 us -> 39.7 us
  waiting for transfers between devices: 41.1 us -> 24.9 us
  between operations: 14.4 us -> 0.87 us
  matrix products: 13 us -> 7.93 us
  Pallas kernels: 4.05 us -> 8.94 us
  local copies, waits for them, and re-layouts: 8.5 us -> 3.65 us
    all_to_all x1 -> x3, blocking collectives: 31.1 us -> 73.3 us  [the longest x1 29 us: body(): sums = jnp.sum(lax.all_to_all(partial_sums, 'y', 0, 0).astype(f32), axis=0)]
    ppermute x12 -> x10, starting transfers between devices: 40.9 us -> 27.5 us  [shift(): return lax.ppermute(value, axis, [(i, (i + step) % n) for i in range(n)])]
    all_to_all x2 -> x1, starting transfers between devices: 24.1 us -> 12.2 us  [body(): own_cuts = lax.all_to_all(cut_quarters(n_k, mine), 'zhi', 0, 0)]
    all_gather x1 -> x0, waiting for transfers between devices: 10.5 us -> none  [body(): cuts = lax.all_gather(cuts, ROW, axis=0, tiled=True)]
    dot_general x3 -> x0, matrix products: 7.58 us -> none  [product(): return lax.dot_general(a, b, contract, preferred_element_type=f32)]
    pallas_call x2 -> x4, Pallas kernels: 4.05 us -> 8.94 us  [the longest x1 3.01 us: products(): pl.pallas_call(functools.partial(products_kernel, len(values)), out_shape...]
    unnamed x16 -> x12, local copies, waits for them, and re-layouts: 6.17 us -> 2.24 us
    all_to_all x2 -> x1, waiting for transfers between devices: 12.7 us -> 9.07 us  [body(): own_cuts = lax.all_to_all(cut_quarters(n_k, mine), 'zhi', 0, 0)]
  transfers between devices with their start and end apart: 15 -> 11, of which waited for: 8 -> 7; matrix products, arithmetic and copies ran while one was open for 7% -> 6% of each run, Pallas kernels for 1% -> 3%
where the time goes in v4:
time: 162 us; the launch traced here: 160 us
  blocking collectives  73.3 us (45%)
  starting transfers between devices  39.7 us (25%)
  waiting for transfers between devices  24.9 us (15%)
  Pallas kernels  8.94 us (6%)
  matrix products  7.93 us (5%)
  local copies, waits for them, and re-layouts  3.65 us (2%)
    all_to_all x1, blocking collectives, body(): sums = jnp.sum(lax.all_to_all(partial_sums, 'y', 0, 0).astype(f32), axis=0)  29 us
    all_to_all x1, blocking collectives, body(): mine = lax.all_to_all(spread, ('zlo', 'x'), 0, 0)  28 us
    ppermute x10, starting transfers between devices, shift(): return lax.ppermute(value, axis, [(i, (i + step) % n) for i in range(n)])  27.5 us
    all_to_all x1, blocking collectives, copies_to(): return lax.all_to_all(spread, axis, 0, 0)  16.3 us
    ppermute x10, waiting for transfers between devices, shift(): return lax.ppermute(value, axis, [(i, (i + step) % n) for i in range(n)])  15.8 us
    all_to_all x1, starting transfers between devices, body(): own_cuts = lax.all_to_all(cut_quarters(n_k, mine), 'zhi', 0, 0)  12.2 us
    all_to_all x1, waiting for transfers between devices, body(): own_cuts = lax.all_to_all(cut_quarters(n_k, mine), 'zhi', 0, 0)  9.07 us
  transfers between devices with their start and end apart: 11, of which 7 were waited for; matrix products, arithmetic and copies ran while one was open for 6% of the time, Pallas kernels for 3%

profile of v4, /device:TPU:14, one launch (start us, length us, event | category | flops | bytes accessed | tf_op | source)
XLA Modules:
  0.0 159.7 jit_solution(10162260837527889907)
XLA Ops:
  0.6 0.0 copy-start
  0.7 1.7 %shard_map.103 = bf16[16,8,2048]{2,1,0:T(8,128)(2,1)} custom-call(s32[1]{0:T(128)} %bitcast.1.block_ref, s32[8,8]{1,0:T(8,128)} %rewards_ref.1, s32[8]{0:T(128)} %selected_ref.1, s32[8]{0:T(128)} %pad_ref.1, bf16[8,1024]{1,0:T(8,128)(2,1)} %tokens_ref.1, bf16[8,1024]{1,0:T(8,128)(2,1)} %cotangent_ref.1), custom_call_target="tpu_custom_call" | custom-call | tf_op jit(solution)/shard_map/pallas_call | solution.py:56
  2.4 28.0 %all_to_all.20 = bf16[16,8,2048]{2,1,0:T(8,128)(2,1)} all-to-all(bf16[16,8,2048]{2,1,0:T(8,128)(2,1)} %shard_map.103), channel_id=1, replica_groups=mesh['zlo'=2,'x'=8,'core'=2,'y'=8,'zhi'=4] {'zlo','x'}, dimensions={0} | all-to-all | bytes 1048576 | tf_op jit(solution)/shard_map/all_to_all | solution.py:166
  30.3 1.9 %collective-permute-start.1 = (bf16[16,8,2048]{2,1,0:T(8,128)(2,1)}, bf16[16,8,2048]{2,1,0:T(8,128)(2,1)}, u32[]{:S(2)}, u32[]{:S(2)}) collective-permute-start(bf16[16,8,2048]{2,1,0:T(8,128)(2,1)} %all_to_all.20), channel_id=1, source_target_pairs={{0,32},{32,0},{1,33},{33,1},{2,34},{34,2},{3,35},{35,3},{4,36},{36... | collective-permute-start | bytes 1572872 | tf_op jit(solution)/shard_map/ppermute | solution.py:25
  32.3 0.0 copy-done
  32.3 1.3 fusion.1
  33.5 0.0 copy-start.4
  33.6 2.0 %shard_map.104 = bf16[4,128,512]{2,1,0:T(8,128)(2,1)} custom-call(bf16[128,2048]{1,0:T(8,128)(2,1)} %bitcast.2.rows_ref), custom_call_target="tpu_custom_call" | custom-call | tf_op jit(solution)/shard_map/pallas_call | solution.py:74
  35.5 0.0 copy-start.5
  35.5 12.2 %all-to-all-start.1 = ((bf16[4,128,512]{2,1,0:T(8,128)(2,1)}), bf16[4,128,512]{2,1,0:T(8,128)(2,1)}, u32[]{:S(2)}, u32[]{:S(2)}) async-start(bf16[4,128,512]{2,1,0:T(8,128)(2,1)} %shard_map.104), calls=%async_computation.1 | async-start | bytes 1048576 | tf_op jit(solution)/shard_map/all_to_all | solution.py:169
  47.7 0.0 copy-done.4
  47.7 1.4 fusion.2
  49.1 0.0 copy-done.5
  49.2 1.3 fusion
  50.4 0.0 collective-permute-done.1
  50.4 1.3 fusion.4
  51.7 1.4 fusion.5
  53.1 1.3 fusion.3
  54.4 0.3 maximum_maximum_fusion
  54.7 9.1 %all-to-all-done.1.own_ref = bf16[4,128,512]{2,1,0:T(8,128)(2,1)} async-done(((bf16[4,128,512]{2,1,0:T(8,128)(2,1)}), bf16[4,128,512]{2,1,0:T(8,128)(2,1)}, u32[]{:S(2)}, u32[]{:S(2)}) %all-to-all-start.1) | async-done | bytes 524320 | tf_op jit(solution)/shard_map/all_to_all | solution.py:169
  63.8 29.0 %all_to_all.21 = f16[8,32,1536]{2,1,0:T(8,128)(2,1)S(1)} all-to-all(f16[8,32,1536]{2,1,0:T(8,128)(2,1)S(1)} %maximum_maximum_fusion), channel_id=1, replica_groups=mesh['zlo'=2,'x'=8,'core'=2,'y'=8,'zhi'=4] {'y'}, dimensions={0} | all-to-all | bytes 1572864 | tf_op jit(solution)/shard_map/all_to_all | solution.py:181
  92.8 0.1 convert_reduce_fusion
  92.9 0.1 multiply_convert_fusion.2
  93.0 16.3 %all_to_all.22 = bf16[4,32,1536]{2,1,0:T(8,128)(2,1)S(1)} all-to-all(bf16[4,32,1536]{2,1,0:T(8,128)(2,1)S(1)} %broadcast_in_dim.2), channel_id=1, replica_groups=mesh['zlo'=2,'x'=8,'core'=2,'y'=8,'zhi'=4] {'zhi'}, dimensions={0} | all-to-all | bytes 786432 | tf_op jit(solution)/shard_map/all_to_all | solution.py:149
  109.3 1.9 %collective-permute-start.3 = (bf16[128,1536]{1,0:T(8,128)(2,1)S(1)}, bf16[128,1536]{1,0:T(8,128)(2,1)S(1)}, u32[]{:S(2)}, u32[]{:S(2)}) collective-permute-start(bf16[128,1536]{1,0:T(8,128)(2,1)S(1)} %bitcast.17), channel_id=1, source_target_pairs={{0,28},{4,0},{8,4},{12,8},{16,12},{20,16},{24,20},{28,24},{1,29},{... | collective-permute-start | bytes 1179656 | tf_op jit(solution)/shard_map/ppermute | solution.py:25
  111.2 3.9 %collective-permute-start.2 = (bf16[128,1536]{1,0:T(8,128)(2,1)S(1)}, bf16[128,1536]{1,0:T(8,128)(2,1)S(1)}, u32[]{:S(2)}, u32[]{:S(2)}) collective-permute-start(bf16[128,1536]{1,0:T(8,128)(2,1)S(1)} %bitcast.18), channel_id=1, source_target_pairs={{0,4},{4,8},{8,12},{12,16},{16,20},{20,24},{24,28},{28,0},{1,5},{5... | collective-permute-start | bytes 1179656 | tf_op jit(solution)/shard_map/ppermute | solution.py:25
  115.1 4.0 %collective-permute-done.3.refs_1_ = bf16[128,1536]{1,0:T(8,128)(2,1)S(1)} collective-permute-done((bf16[128,1536]{1,0:T(8,128)(2,1)S(1)}, bf16[128,1536]{1,0:T(8,128)(2,1)S(1)}, u32[]{:S(2)}, u32[]{:S(2)}) %collective-permute-start.3) | collective-permute-done | bytes 393248 | tf_op jit(solution)/shard_map/ppermute | solution.py:25
  119.1 2.9 %collective-permute-start.4 = (bf16[128,1536]{1,0:T(8,128)(2,1)S(1)}, bf16[128,1536]{1,0:T(8,128)(2,1)S(1)}, u32[]{:S(2)}, u32[]{:S(2)}) collective-permute-start(bf16[128,1536]{1,0:T(8,128)(2,1)S(1)} %collective-permute-done.3.refs_1_), channel_id=1, source_target_pairs={{0,28},{4,0},{8,4},{12,8},{16,12},{20,16},{24,20},{28,24},{1,29},{... | collective-permute-start | bytes 1179656 | tf_op jit(solution)/shard_map/ppermute | solution.py:25
  122.1 0.3 collective-permute-done.2.refs_2_
  122.3 2.7 %collective-permute-start.5 = (bf16[128,1536]{1,0:T(8,128)(2,1)S(1)}, bf16[128,1536]{1,0:T(8,128)(2,1)S(1)}, u32[]{:S(2)}, u32[]{:S(2)}) collective-permute-start(bf16[128,1536]{1,0:T(8,128)(2,1)S(1)} %collective-permute-done.2.refs_2_), channel_id=1, source_target_pairs={{0,4},{4,8},{8,12},{12,16},{16,20},{20,24},{24,28},{28,0},{1,5},{5... | collective-permute-start | bytes 1179656 | tf_op jit(solution)/shard_map/ppermute | solution.py:25
  125.0 4.7 %collective-permute-done.4.refs_3_ = bf16[128,1536]{1,0:T(8,128)(2,1)S(1)} collective-permute-done((bf16[128,1536]{1,0:T(8,128)(2,1)S(1)}, bf16[128,1536]{1,0:T(8,128)(2,1)S(1)}, u32[]{:S(2)}, u32[]{:S(2)}) %collective-permute-start.4) | collective-permute-done | bytes 393248 | tf_op jit(solution)/shard_map/ppermute | solution.py:25
  129.6 3.4 %collective-permute-start.6 = (bf16[128,1536]{1,0:T(8,128)(2,1)S(1)}, bf16[128,1536]{1,0:T(8,128)(2,1)S(1)}, u32[]{:S(2)}, u32[]{:S(2)}) collective-permute-start(bf16[128,1536]{1,0:T(8,128)(2,1)S(1)} %collective-permute-done.4.refs_3_), channel_id=1, source_target_pairs={{0,28},{4,0},{8,4},{12,8},{16,12},{20,16},{24,20},{28,24},{1,29},{... | collective-permute-start | bytes 1179656 | tf_op jit(solution)/shard_map/ppermute | solution.py:25
  133.1 0.1 collective-permute-done.5.refs_4_
  133.2 0.0 copy-start.2
  133.2 2.3 %collective-permute-start.7 = (bf16[128,1536]{1,0:T(8,128)(2,1)S(1)}, bf16[128,1536]{1,0:T(8,128)(2,1)S(1)}, u32[]{:S(2)}, u32[]{:S(2)}) collective-permute-start(bf16[128,1536]{1,0:T(8,128)(2,1)S(1)} %collective-permute-done.5.refs_4_), channel_id=1, source_target_pairs={{0,4},{4,8},{8,12},{12,16},{16,20},{20,24},{24,28},{28,0},{1,5},{5... | collective-permute-start | bytes 1179656 | tf_op jit(solution)/shard_map/ppermute | solution.py:25
  135.5 1.9 %collective-permute-start = (bf16[4,128,512]{2,1,0:T(8,128)(2,1)}, bf16[4,128,512]{2,1,0:T(8,128)(2,1)}, u32[]{:S(2)}, u32[]{:S(2)}) collective-permute-start(bf16[4,128,512]{2,1,0:T(8,128)(2,1)} %all-to-all-done.1.own_ref), channel_id=1, source_target_pairs={{0,32},{32,0},{1,33},{33,1},{2,34},{34,2},{3,35},{35,3},{4,36},{36... | collective-permute-start | bytes 1572872 | tf_op jit(solution)/shard_map/ppermute | solution.py:25
  137.4 1.9 %collective-permute-done.6.refs_5_ = bf16[128,1536]{1,0:T(8,128)(2,1)S(1)} collective-permute-done((bf16[128,1536]{1,0:T(8,128)(2,1)S(1)}, bf16[128,1536]{1,0:T(8,128)(2,1)S(1)}, u32[]{:S(2)}, u32[]{:S(2)}) %collective-permute-start.6) | collective-permute-done | bytes 393248 | tf_op jit(solution)/shard_map/ppermute | solution.py:25
  139.3 0.7 slice.46
  140.0 4.6 %collective-permute-start.9 = (bf16[64,1536]{1,0:T(8,128)(2,1)}, bf16[64,1536]{1,0:T(8,128)(2,1)}, u32[]{:S(2)}, u32[]{:S(2)}) collective-permute-start(bf16[64,1536]{1,0:T(8,128)(2,1)} %slice.46), channel_id=1, source_target_pairs={{0,28},{4,0},{8,4},{12,8},{16,12},{20,16},{24,20},{28,24},{1,29},{... | collective-permute-start | bytes 589832 | tf_op jit(solution)/shard_map/ppermute | solution.py:25
  144.6 0.0 collective-permute-done.7.refs_6_
  144.7 0.0 copy-done.2
  144.7 0.7 slice.45
  145.4 1.9 %collective-permute-start.8 = (bf16[64,1536]{1,0:T(8,128)(2,1)}, bf16[64,1536]{1,0:T(8,128)(2,1)}, u32[]{:S(2)}, u32[]{:S(2)}) collective-permute-start(bf16[64,1536]{1,0:T(8,128)(2,1)} %slice.45), channel_id=1, source_target_pairs={{0,4},{4,8},{8,12},{12,16},{16,20},{20,24},{24,28},{28,0},{1,5},{5... | collective-permute-start | bytes 589832 | tf_op jit(solution)/shard_map/ppermute | solution.py:25
  147.3 0.0 collective-permute-done.other_ref
  147.3 2.2 %shard_map.105.inputs_ref = bf16[1024,512]{1,0:T(8,128)(2,1)} custom-call(s32[1]{0:T(128)} %bitcast.place_ref, bf16[4,128,512]{2,1,0:T(8,128)(2,1)} %all-to-all-done.1.own_ref, bf16[4,128,512]{2,1,0:T(8,128)(2,1)} %collective-permute-done.other_ref), custom_call_target="tpu_custom_call" | custom-call | tf_op jit(solution)/shard_map/pallas_call | solution.py:99
  149.5 0.0 collective-permute-done.9.refs_8_
  149.5 4.9 %collective-permute-done.8.refs_7_ = bf16[64,1536]{1,0:T(8,128)(2,1)} collective-permute-done((bf16[64,1536]{1,0:T(8,128)(2,1)}, bf16[64,1536]{1,0:T(8,128)(2,1)}, u32[]{:S(2)}, u32[]{:S(2)}) %collective-permute-start.8) | collective-permute-done | bytes 196640 | tf_op jit(solution)/shard_map/ppermute | solution.py:25
  154.4 0.0 copy-start.1
  154.4 1.2 copy-done.1
  155.7 0.0 copy-start.3
  155.7 1.0 copy-done.3
  156.7 3.0 %shard_map.106 = (f32[256,512]{1,0:T(8,128)}, f32[256,512]{1,0:T(8,128)}, f32[512,256]{1,0:T(8,128)}) custom-call(bf16[1024,512]{1,0:T(8,128)(2,1)S(1)} %copy-done.1, bf16[128,1536]{1,0:T(8,128)(2,1)S(1)} %bitcast.19, bf16[128,1536]{1,0:T(8,128)(2,1)S(1)} %collective-permute-done.3.refs_1_, bf16[128,1536]{1,0:T(8,128)(2,1)S(1)} %collective-permute-done.2.refs_2_, ...), custom_call_target="tpu_custom_call" | custom-call | tf_op jit(solution)/shard_map/pallas_call | solution.py:133
  (2 shorter events, 0.0 us)
Async XLA Ops:
  0.6 31.6 %copy-start = (bf16[1024,512]{1,0:T(8,128)(2,1)S(1)}, bf16[1024,512]{1,0:T(8,128)(2,1)}, u32[]{:S(2)}) copy-start(bf16[1024,512]{1,0:T(8,128)(2,1)} %param.14) | copy-start | bytes 3145732
  30.3 20.1 %collective-permute-start.1 = (bf16[16,8,2048]{2,1,0:T(8,128)(2,1)}, bf16[16,8,2048]{2,1,0:T(8,128)(2,1)}, u32[]{:S(2)}, u32[]{:S(2)}) collective-permute-start(bf16[16,8,2048]{2,1,0:T(8,128)(2,1)} %all_to_all.20), channel_id=1, source_target_pairs={{0,32},{32,0},{1,33},{33,1},{2,34},{34,2},{3,35},{35,3},{4,36},{36... | collective-permute-start | bytes 1572872 | tf_op jit(solution)/shard_map/ppermute | solution.py:25
  33.5 14.2 %copy-start.4 = (bf16[512,1024]{1,0:T(8,128)(2,1)S(1)}, bf16[512,1024]{1,0:T(8,128)(2,1)}, u32[]{:S(2)}) copy-start(bf16[512,1024]{1,0:T(8,128)(2,1)} %param.15) | copy-start | bytes 3145732
  35.5 13.6 %copy-start.5 = (bf16[1024,512]{1,0:T(8,128)(2,1)S(1)}, bf16[1024,512]{1,0:T(8,128)(2,1)}, u32[]{:S(2)}) copy-start(bf16[1024,512]{1,0:T(8,128)(2,1)} %param.13) | copy-start | bytes 3145732
  35.5 28.2 %all-to-all-start.1 = ((bf16[4,128,512]{2,1,0:T(8,128)(2,1)}), bf16[4,128,512]{2,1,0:T(8,128)(2,1)}, u32[]{:S(2)}, u32[]{:S(2)}) async-start(bf16[4,128,512]{2,1,0:T(8,128)(2,1)} %shard_map.104), calls=%async_computation.1 | async-start | bytes 1048576 | tf_op jit(solution)/shard_map/all_to_all | solution.py:169
  109.3 9.9 %collective-permute-start.3 = (bf16[128,1536]{1,0:T(8,128)(2,1)S(1)}, bf16[128,1536]{1,0:T(8,128)(2,1)S(1)}, u32[]{:S(2)}, u32[]{:S(2)}) collective-permute-start(bf16[128,1536]{1,0:T(8,128)(2,1)S(1)} %bitcast.17), channel_id=1, source_target_pairs={{0,28},{4,0},{8,4},{12,8},{16,12},{20,16},{24,20},{28,24},{1,29},{... | collective-permute-start | bytes 1179656 | tf_op jit(solution)/shard_map/ppermute | solution.py:25
  111.2 11.1 %collective-permute-start.2 = (bf16[128,1536]{1,0:T(8,128)(2,1)S(1)}, bf16[128,1536]{1,0:T(8,128)(2,1)S(1)}, u32[]{:S(2)}, u32[]{:S(2)}) collective-permute-start(bf16[128,1536]{1,0:T(8,128)(2,1)S(1)} %bitcast.18), channel_id=1, source_target_pairs={{0,4},{4,8},{8,12},{12,16},{16,20},{20,24},{24,28},{28,0},{1,5},{5... | collective-permute-start | bytes 1179656 | tf_op jit(solution)/shard_map/ppermute | solution.py:25
  119.1 10.5 %collective-permute-start.4 = (bf16[128,1536]{1,0:T(8,128)(2,1)S(1)}, bf16[128,1536]{1,0:T(8,128)(2,1)S(1)}, u32[]{:S(2)}, u32[]{:S(2)}) collective-permute-start(bf16[128,1536]{1,0:T(8,128)(2,1)S(1)} %collective-permute-done.3.refs_1_), channel_id=1, source_target_pairs={{0,28},{4,0},{8,4},{12,8},{16,12},{20,16},{24,20},{28,24},{1,29},{... | collective-permute-start | bytes 1179656 | tf_op jit(solution)/shard_map/ppermute | solution.py:25
  122.3 10.9 %collective-permute-start.5 = (bf16[128,1536]{1,0:T(8,128)(2,1)S(1)}, bf16[128,1536]{1,0:T(8,128)(2,1)S(1)}, u32[]{:S(2)}, u32[]{:S(2)}) collective-permute-start(bf16[128,1536]{1,0:T(8,128)(2,1)S(1)} %collective-permute-done.2.refs_2_), channel_id=1, source_target_pairs={{0,4},{4,8},{8,12},{12,16},{16,20},{20,24},{24,28},{28,0},{1,5},{5... | collective-permute-start | bytes 1179656 | tf_op jit(solution)/shard_map/ppermute | solution.py:25
  129.6 9.7 %collective-permute-start.6 = (bf16[128,1536]{1,0:T(8,128)(2,1)S(1)}, bf16[128,1536]{1,0:T(8,128)(2,1)S(1)}, u32[]{:S(2)}, u32[]{:S(2)}) collective-permute-start(bf16[128,1536]{1,0:T(8,128)(2,1)S(1)} %collective-permute-done.4.refs_3_), channel_id=1, source_target_pairs={{0,28},{4,0},{8,4},{12,8},{16,12},{20,16},{24,20},{28,24},{1,29},{... | collective-permute-start | bytes 1179656 | tf_op jit(solution)/shard_map/ppermute | solution.py:25
  133.2 11.5 %copy-start.2 = (bf16[128,1536]{1,0:T(8,128)(2,1)}, bf16[128,1536]{1,0:T(8,128)(2,1)S(1)}, u32[]{:S(2)}) copy-start(bf16[128,1536]{1,0:T(8,128)(2,1)S(1)} %collective-permute-done.5.refs_4_) | copy-start | bytes 1179652
  133.2 11.5 %collective-permute-start.7 = (bf16[128,1536]{1,0:T(8,128)(2,1)S(1)}, bf16[128,1536]{1,0:T(8,128)(2,1)S(1)}, u32[]{:S(2)}, u32[]{:S(2)}) collective-permute-start(bf16[128,1536]{1,0:T(8,128)(2,1)S(1)} %collective-permute-done.5.refs_4_), channel_id=1, source_target_pairs={{0,4},{4,8},{8,12},{12,16},{16,20},{20,24},{24,28},{28,0},{1,5},{5... | collective-permute-start | bytes 1179656 | tf_op jit(solution)/shard_map/ppermute | solution.py:25
  135.5 11.8 %collective-permute-start = (bf16[4,128,512]{2,1,0:T(8,128)(2,1)}, bf16[4,128,512]{2,1,0:T(8,128)(2,1)}, u32[]{:S(2)}, u32[]{:S(2)}) collective-permute-start(bf16[4,128,512]{2,1,0:T(8,128)(2,1)} %all-to-all-done.1.own_ref), channel_id=1, source_target_pairs={{0,32},{32,0},{1,33},{33,1},{2,34},{34,2},{3,35},{35,3},{4,36},{36... | collective-permute-start | bytes 1572872 | tf_op jit(solution)/shard_map/ppermute | solution.py:25
  140.0 9.5 %collective-permute-start.9 = (bf16[64,1536]{1,0:T(8,128)(2,1)}, bf16[64,1536]{1,0:T(8,128)(2,1)}, u32[]{:S(2)}, u32[]{:S(2)}) collective-permute-start(bf16[64,1536]{1,0:T(8,128)(2,1)} %slice.46), channel_id=1, source_target_pairs={{0,28},{4,0},{8,4},{12,8},{16,12},{20,16},{24,20},{28,24},{1,29},{... | collective-permute-start | bytes 589832 | tf_op jit(solution)/shard_map/ppermute | solution.py:25
  145.4 9.1 %collective-permute-start.8 = (bf16[64,1536]{1,0:T(8,128)(2,1)}, bf16[64,1536]{1,0:T(8,128)(2,1)}, u32[]{:S(2)}, u32[]{:S(2)}) collective-permute-start(bf16[64,1536]{1,0:T(8,128)(2,1)} %slice.45), channel_id=1, source_target_pairs={{0,4},{4,8},{8,12},{12,16},{16,20},{20,24},{24,28},{28,0},{1,5},{5... | collective-permute-start | bytes 589832 | tf_op jit(solution)/shard_map/ppermute | solution.py:25
  154.4 1.2 copy-start.1
  155.7 1.0 copy-start.3

commit v5 on v4

--- a/solution.py
+++ b/solution.py
@@ -51,6 +51,10 @@
     return pl.BlockSpec(memory_space=pltpu.SMEM)
 
 
+def limit(mebibytes):
+    return pltpu.CompilerParams(vmem_limit_bytes=mebibytes * 1024 * 1024)
+
+
 def prepare(copies, block, rewards, selected, pad_mask, tokens, cotangent):
     rows, width = tokens.shape
     return pl.pallas_call(
@@ -76,18 +80,18 @@
         out_shape=jax.ShapeDtypeStruct((n_k, rows.shape[0], rows.shape[1] // n_k), bf16),
         in_specs=[in_vmem()],
         out_specs=in_vmem(),
+        compiler_params=limit(4),
     )(rows)
 
 
-def order_kernel(order, place_ref, own_ref, other_ref, out_ref):
+def order_kernel(order, y_ref, own_ref, other_ref, *out_refs):
     n_k, rows, _ = own_ref.shape
     n_y = len(order)
     part = rows // n_y
-    y = place_ref[0]
-    at = 0
-    for r in order:
-        share = lax.rem(y + r, n_y)
+    for r, out_ref in zip(order, out_refs):
+        share = lax.rem(y_ref[0] + r, n_y)
         spot = pl.ds(pl.multiple_of(share * part, part), part)
+        at = 0
         for t in range(n_k):
             for ref in (own_ref, other_ref):
                 out_ref[at : at + part, :] = ref[t, spot, :]
@@ -96,48 +100,62 @@
 
 def put_in_order(order, y, own, other):
     n_k, rows, both = own.shape
-    return pl.pallas_call(
+    n_y = len(order)
+    out = jax.ShapeDtypeStruct((2 * n_k * rows // n_y, both), bf16)
+    pieces = pl.pallas_call(
         functools.partial(order_kernel, order),
-        out_shape=jax.ShapeDtypeStruct((2 * n_k * rows, both), bf16),
+        out_shape=(out,) * n_y,
         in_specs=[in_smem(), in_vmem(), in_vmem()],
-        out_specs=in_vmem(),
+        out_specs=(in_vmem(),) * n_y,
+        compiler_params=limit(8),
     )(y.reshape(1), own, other)
+    return dict(zip(order, pieces))
 
 
 def product(a, b):
     return lax.dot_general(a, b, (((0,), (0,)), ((), ())), preferred_element_type=f32)
 
 
-def products_kernel(n, inputs_ref, *refs):
-    value_refs = refs[:n]
-    gate_ref, up_ref, down_ref, every_ref = refs[n:]
-    at = 0
-    for ref in value_refs:
-        rows = ref.shape[0]
-        every_ref[at : at + rows, :] = ref[...]
-        at += rows
-    units = gate_ref.shape[1]
-    quarter = gate_ref.shape[0]
-    tokens = inputs_ref[:, :quarter]
-    down_ref[...] = product(every_ref[:, :units], inputs_ref[:, quarter:])
-    gate_ref[...] = product(tokens, every_ref[:, units : 2 * units])
-    up_ref[...] = product(tokens, every_ref[:, 2 * units :])
-
-
-def products(inputs, values):
-    rows, both = inputs.shape
-    quarter = both // 2
-    width = values[0].shape[1]
+def add_kernel(blocks, *refs):
+    down_ref, gate_ref, up_ref = refs[-3:]
+    earlier = refs[2 * blocks : -3]
+    quarter, units = gate_ref.shape
+    sums = [ref[...] for ref in earlier]
+    for n in range(blocks):
+        inputs_ref = refs[n]
+        values_ref = refs[blocks + n]
+        tokens = inputs_ref[:, :quarter]
+        terms = (
+            product(values_ref[:, :units], inputs_ref[:, quarter:]),
+            product(tokens, values_ref[:, units : 2 * units]),
+            product(tokens, values_ref[:, 2 * units :]),
+        )
+        sums = [a + b for a, b in zip(sums, terms)] if sums else terms
+    down_ref[...], gate_ref[...], up_ref[...] = sums
+
+
+def add_products(sums, inputs, values):
+    blocks = len(values)
+    quarter = inputs[0].shape[1] // 2
+    rows, width = values[0].shape
     units = width // 3
     wide = jax.ShapeDtypeStruct((quarter, units), f32)
+    tall = jax.ShapeDtypeStruct((units, quarter), f32)
+    operands = tuple(inputs) + tuple(values) + tuple(sums)
+    first = 2 * blocks
     return pl.pallas_call(
-        functools.partial(products_kernel, len(values)),
-        out_shape=(wide, wide, jax.ShapeDtypeStruct((units, quarter), f32)),
-        in_specs=[in_vmem()] * (1 + len(values)),
+        functools.partial(add_kernel, blocks),
+        out_shape=(tall, wide, wide),
+        in_specs=[in_vmem()] * len(operands),
         out_specs=(in_vmem(),) * 3,
-        scratch_shapes=[pltpu.VMEM((rows, width), bf16)],
-        compiler_params=pltpu.CompilerParams(vmem_limit_bytes=40 * 1024 * 1024),
-    )(inputs, *values)
+        input_output_aliases={first + n: n for n in range(len(sums))},
+        compiler_params=limit(12),
+        cost_estimate=pl.CostEstimate(
+            flops=6 * blocks * rows * quarter * units,
+            bytes_accessed=2 * blocks * rows * width,
+            transcendentals=0,
+        ),
+    )(*operands)
 
 
 def after(value, *others):
@@ -197,20 +215,24 @@
     for s in range(1, n_y // 2):
         order += [s, n_y - s]
     order.append(n_y // 2)
-    other_cuts = shift(own_cuts, "core", 1)
+    inputs = put_in_order(order, y, own_cuts, shift(own_cuts, "core", 1))
     right = left = near
-    held = {0: near}
+    sums = ()
     for s in range(1, n_y // 2):
         right = shift(right, "y", 1)
         left = shift(left, "y", -1)
-        held[n_y - s] = right
-        held[s] = left
+        rows_in = [inputs[n_y - s], inputs[s]]
+        blocks = [right, left]
         if s == 1:
-            inputs = put_in_order(order, y, own_cuts, after(other_cuts, right, left))
+            rows_in.append(inputs[0])
+            blocks.append(near)
+        sums = add_products(sums, rows_in, blocks)
     middle = near.shape[0] // 2
     top = shift(right[:middle], "y", 1)
     low = shift(left[middle:], "y", -1)
-    return products(inputs, [held[r] for r in order[:-1]] + [top, low])
+    at = inputs[n_y // 2]
+    down_grad, gate_grad, up_grad = add_products(sums, [at[:middle], at[middle:]], [top, low])
+    return (gate_grad, up_grad, down_grad)
 
 
 def solution(mesh):

time: 162 us -> 163 us (level)
  starting transfers between devices: 39.7 us -> 45.2 us
  Pallas kernels: 8.94 us -> 13.8 us
  waiting for transfers between devices: 24.9 us -> 20.9 us
  matrix products: 7.93 us -> 5.07 us
    pallas_call x2 -> x5, Pallas kernels: 5.26 us -> 11.2 us  [the longest x4 11.2 us: add_products(): pl.pallas_call(functools.partial(add_kernel, blocks), out_shape=(tall, wi...]
    ppermute x10, starting transfers between devices: 27.5 us -> 32.5 us  [shift(): return lax.ppermute(value, axis, [(i, (i + step) % n) for i in range(n)])]
    ppermute x10, waiting for transfers between devices: 15.8 us -> 10.9 us  [shift(): return lax.ppermute(value, axis, [(i, (i + step) % n) for i in range(n)])]
  transfers between devices with their start and end apart: 11 -> 11, of which waited for: 7 -> 5; matrix products, arithmetic and copies ran while one was open for 6% -> 3% of each run, Pallas kernels for 3% -> 6%
where the time goes in v5:
time: 163 us; the launch traced here: 161 us
  blocking collectives  72.5 us (44%)
  starting transfers between devices  45.2 us (28%)
  waiting for transfers between devices  20.9 us (13%)
  Pallas kernels  13.8 us (8%)
  matrix products  5.07 us (3%)
  local copies, waits for them, and re-layouts  2.48 us (2%)
    ppermute x10, starting transfers between devices, shift(): return lax.ppermute(value, axis, [(i, (i + step) % n) for i in range(n)])  32.5 us
    all_to_all x1, blocking collectives, body(): sums = jnp.sum(lax.all_to_all(partial_sums, 'y', 0, 0).astype(f32), axis=0)  29 us
    all_to_all x1, blocking collectives, body(): mine = lax.all_to_all(spread, ('zlo', 'x'), 0, 0)  27.2 us
    all_to_all x1, blocking collectives, copies_to(): return lax.all_to_all(spread, axis, 0, 0)  16.3 us
    all_to_all x1, starting transfers between devices, body(): own_cuts = lax.all_to_all(cut_quarters(n_k, mine), 'zhi', 0, 0)  12.7 us
    pallas_call x4, Pallas kernels, add_products(): pl.pallas_call(functools.partial(add_kernel, blocks), out_shape=(tall, wi...  11.2 us
    ppermute x10, waiting for transfers between devices, shift(): return lax.ppermute(value, axis, [(i, (i + step) % n) for i in range(n)])  10.9 us
    all_to_all x1, waiting for transfers between devices, body(): own_cuts = lax.all_to_all(cut_quarters(n_k, mine), 'zhi', 0, 0)  9.98 us
  transfers between devices with their start and end apart: 11, of which 5 were waited for; matrix products, arithmetic and copies ran while one was open for 3% of the time, Pallas kernels for 6%

profile of v5, /device:TPU:14, one launch (start us, length us, event | category | flops | bytes accessed | tf_op | source)
XLA Modules:
  0.0 161.3 jit_solution(15380546812683332256)
XLA Ops:
  0.6 0.0 copy-start
  0.7 1.7 %shard_map.103 = bf16[16,8,2048]{2,1,0:T(8,128)(2,1)} custom-call(s32[1]{0:T(128)} %bitcast.1.block_ref, s32[8,8]{1,0:T(8,128)} %rewards_ref.1, s32[8]{0:T(128)} %selected_ref.1, s32[8]{0:T(128)} %pad_ref.1, bf16[8,1024]{1,0:T(8,128)(2,1)} %tokens_ref.1, bf16[8,1024]{1,0:T(8,128)(2,1)} %cotangent_ref.1), custom_call_target="tpu_custom_call" | custom-call | tf_op jit(solution)/shard_map/pallas_call | solution.py:60
  2.4 27.2 %all_to_all.20 = bf16[16,8,2048]{2,1,0:T(8,128)(2,1)S(1)} all-to-all(bf16[16,8,2048]{2,1,0:T(8,128)(2,1)} %shard_map.103), channel_id=1, replica_groups=mesh['zlo'=2,'x'=8,'core'=2,'y'=8,'zhi'=4] {'zlo','x'}, dimensions={0} | all-to-all | bytes 1048576 | tf_op jit(solution)/shard_map/all_to_all | solution.py:184
  29.6 1.9 %collective-permute-start.1 = (bf16[16,8,2048]{2,1,0:T(8,128)(2,1)S(1)}, bf16[16,8,2048]{2,1,0:T(8,128)(2,1)}, u32[]{:S(2)}, u32[]{:S(2)}) collective-permute-start(bf16[16,8,2048]{2,1,0:T(8,128)(2,1)S(1)} %all_to_all.20), channel_id=1, source_target_pairs={{0,32},{32,0},{1,33},{33,1},{2,34},{34,2},{3,35},{35,3},{4,36},{36... | collective-permute-start | bytes 1572872 | tf_op jit(solution)/shard_map/ppermute | solution.py:25
  31.5 0.0 copy-done
  31.6 0.3 fusion
  31.9 0.0 copy-start.5
  31.9 0.8 shard_map.104
  32.7 12.7 %all-to-all-start.1 = ((bf16[4,128,512]{2,1,0:T(8,128)(2,1)}), bf16[4,128,512]{2,1,0:T(8,128)(2,1)S(1)}, u32[]{:S(2)}, u32[]{:S(2)}) async-start(bf16[4,128,512]{2,1,0:T(8,128)(2,1)} %shard_map.104), calls=%async_computation.1 | async-start | bytes 1048576 | tf_op jit(solution)/shard_map/all_to_all | solution.py:187
  45.4 0.0 copy-done.5
  45.4 0.0 copy-start.6
  45.4 0.3 fusion.1
  45.7 0.9 copy-done.6
  46.6 0.5 fusion.2
  47.1 0.0 collective-permute-done.1
  47.1 1.3 fusion.3
  48.4 1.3 fusion.4
  49.7 1.4 fusion.5
  51.1 0.3 maximum_maximum_fusion
  51.4 10.0 %all-to-all-done.1.own_ref = bf16[4,128,512]{2,1,0:T(8,128)(2,1)S(1)} async-done(((bf16[4,128,512]{2,1,0:T(8,128)(2,1)}), bf16[4,128,512]{2,1,0:T(8,128)(2,1)S(1)}, u32[]{:S(2)}, u32[]{:S(2)}) %all-to-all-start.1) | async-done | bytes 524320 | tf_op jit(solution)/shard_map/all_to_all | solution.py:187
  61.4 29.0 %all_to_all.21 = f16[8,32,1536]{2,1,0:T(8,128)(2,1)S(1)} all-to-all(f16[8,32,1536]{2,1,0:T(8,128)(2,1)S(1)} %maximum_maximum_fusion), channel_id=1, replica_groups=mesh['zlo'=2,'x'=8,'core'=2,'y'=8,'zhi'=4] {'y'}, dimensions={0} | all-to-all | bytes 1572864 | tf_op jit(solution)/shard_map/all_to_all | solution.py:199
  90.3 0.1 convert_reduce_fusion
  90.5 0.1 multiply_convert_fusion.2
  90.6 16.3 %all_to_all.22 = bf16[4,32,1536]{2,1,0:T(8,128)(2,1)S(1)} all-to-all(bf16[4,32,1536]{2,1,0:T(8,128)(2,1)S(1)} %broadcast_in_dim.2), channel_id=1, replica_groups=mesh['zlo'=2,'x'=8,'core'=2,'y'=8,'zhi'=4] {'zhi'}, dimensions={0} | all-to-all | bytes 786432 | tf_op jit(solution)/shard_map/all_to_all | solution.py:167
  106.8 2.6 %collective-permute-start.2 = (bf16[128,1536]{1,0:T(8,128)(2,1)S(1)}, bf16[128,1536]{1,0:T(8,128)(2,1)S(1)}, u32[]{:S(2)}, u32[]{:S(2)}) collective-permute-start(bf16[128,1536]{1,0:T(8,128)(2,1)S(1)} %bitcast.21), channel_id=1, source_target_pairs={{0,4},{4,8},{8,12},{12,16},{16,20},{20,24},{24,28},{28,0},{1,5},{5... | collective-permute-start | bytes 1179656 | tf_op jit(solution)/shard_map/ppermute | solution.py:25
  109.4 4.5 %collective-permute-start.6 = (bf16[128,1536]{1,0:T(8,128)(2,1)S(1)}, bf16[128,1536]{1,0:T(8,128)(2,1)S(1)}, u32[]{:S(2)}, u32[]{:S(2)}) collective-permute-start(bf16[128,1536]{1,0:T(8,128)(2,1)S(1)} %bitcast.22), channel_id=1, source_target_pairs={{0,28},{4,0},{8,4},{12,8},{16,12},{20,16},{24,20},{28,24},{1,29},{... | collective-permute-start | bytes 1179656 | tf_op jit(solution)/shard_map/ppermute | solution.py:25
  113.9 3.8 %collective-permute-done.2.refs_3_ = bf16[128,1536]{1,0:T(8,128)(2,1)S(1)} collective-permute-done((bf16[128,1536]{1,0:T(8,128)(2,1)S(1)}, bf16[128,1536]{1,0:T(8,128)(2,1)S(1)}, u32[]{:S(2)}, u32[]{:S(2)}) %collective-permute-start.2) | collective-permute-done | bytes 393248 | tf_op jit(solution)/shard_map/ppermute | solution.py:25
  117.7 1.9 %collective-permute-start.3 = (bf16[128,1536]{1,0:T(8,128)(2,1)S(1)}, bf16[128,1536]{1,0:T(8,128)(2,1)}, u32[]{:S(2)}, u32[]{:S(2)}) collective-permute-start(bf16[128,1536]{1,0:T(8,128)(2,1)S(1)} %collective-permute-done.2.refs_3_), channel_id=1, source_target_pairs={{0,4},{4,8},{8,12},{12,16},{16,20},{20,24},{24,28},{28,0},{1,5},{5... | collective-permute-start | bytes 1179656 | tf_op jit(solution)/shard_map/ppermute | solution.py:25
  119.6 0.0 copy-start.1
  119.6 0.7 copy-done.1
  120.4 0.0 collective-permute-done.6.refs_4_
  120.4 5.1 %collective-permute-start.7 = (bf16[128,1536]{1,0:T(8,128)(2,1)S(1)}, bf16[128,1536]{1,0:T(8,128)(2,1)}, u32[]{:S(2)}, u32[]{:S(2)}) collective-permute-start(bf16[128,1536]{1,0:T(8,128)(2,1)S(1)} %collective-permute-done.6.refs_4_), channel_id=1, source_target_pairs={{0,28},{4,0},{8,4},{12,8},{16,12},{20,16},{24,20},{28,24},{1,29},{... | collective-permute-start | bytes 1179656 | tf_op jit(solution)/shard_map/ppermute | solution.py:25
  125.5 0.0 copy-start.3
  125.5 0.7 copy-done.3
  126.3 1.9 %collective-permute-start = (bf16[4,128,512]{2,1,0:T(8,128)(2,1)S(1)}, bf16[4,128,512]{2,1,0:T(8,128)(2,1)S(1)}, u32[]{:S(2)}, u32[]{:S(2)}) collective-permute-start(bf16[4,128,512]{2,1,0:T(8,128)(2,1)S(1)} %all-to-all-done.1.own_ref), channel_id=1, source_target_pairs={{0,32},{32,0},{1,33},{33,1},{2,34},{34,2},{3,35},{35,3},{4,36},{36... | collective-permute-start | bytes 1572872 | tf_op jit(solution)/shard_map/ppermute | solution.py:25
  128.2 0.5 collective-permute-done.3.refs_2_
  128.7 1.9 %collective-permute-start.4 = (bf16[128,1536]{1,0:T(8,128)(2,1)}, bf16[128,1536]{1,0:T(8,128)(2,1)S(1)}, u32[]{:S(2)}, u32[]{:S(2)}) collective-permute-start(bf16[128,1536]{1,0:T(8,128)(2,1)} %collective-permute-done.3.refs_2_), channel_id=1, source_target_pairs={{0,4},{4,8},{8,12},{12,16},{16,20},{20,24},{24,28},{28,0},{1,5},{5... | collective-permute-start | bytes 1179656 | tf_op jit(solution)/shard_map/ppermute | solution.py:25
  130.6 0.2 collective-permute-done.7.refs_3_
  130.8 5.7 %collective-permute-start.8 = (bf16[128,1536]{1,0:T(8,128)(2,1)}, bf16[128,1536]{1,0:T(8,128)(2,1)S(1)}, u32[]{:S(2)}, u32[]{:S(2)}) collective-permute-start(bf16[128,1536]{1,0:T(8,128)(2,1)} %collective-permute-done.7.refs_3_), channel_id=1, source_target_pairs={{0,28},{4,0},{8,4},{12,8},{16,12},{20,16},{24,20},{28,24},{1,29},{... | collective-permute-start | bytes 1179656 | tf_op jit(solution)/shard_map/ppermute | solution.py:25
  136.5 0.0 collective-permute-done.other_ref
  136.5 0.0 copy-start.2
  136.5 0.0 copy-start.4
  136.5 0.1 shard_map.105
  136.6 6.4 %collective-permute-done.4.refs_2_ = bf16[128,1536]{1,0:T(8,128)(2,1)S(1)} collective-permute-done((bf16[128,1536]{1,0:T(8,128)(2,1)}, bf16[128,1536]{1,0:T(8,128)(2,1)S(1)}, u32[]{:S(2)}, u32[]{:S(2)}) %collective-permute-start.4) | collective-permute-done | bytes 393248 | tf_op jit(solution)/shard_map/ppermute | solution.py:25
  143.0 1.9 %collective-permute-start.5 = (bf16[64,1536]{1,0:T(8,128)(2,1)S(1)}, bf16[64,1536]{1,0:T(8,128)(2,1)S(1)}, u32[]{:S(2)}, u32[]{:S(2)}) collective-permute-start(bf16[64,1536]{1,0:T(8,128)(2,1)S(1)} %slice.53), channel_id=1, source_target_pairs={{0,4},{4,8},{8,12},{12,16},{16,20},{20,24},{24,28},{28,0},{1,5},{5... | collective-permute-start | bytes 589832 | tf_op jit(solution)/shard_map/ppermute | solution.py:25
  145.0 0.0 collective-permute-done.8.refs_3_
  145.0 5.1 %collective-permute-start.9 = (bf16[64,1536]{1,0:T(8,128)(2,1)S(1)}, bf16[64,1536]{1,0:T(8,128)(2,1)S(1)}, u32[]{:S(2)}, u32[]{:S(2)}) collective-permute-start(bf16[64,1536]{1,0:T(8,128)(2,1)S(1)} %slice.54), channel_id=1, source_target_pairs={{0,28},{4,0},{8,4},{12,8},{16,12},{20,16},{24,20},{28,24},{1,29},{... | collective-permute-start | bytes 589832 | tf_op jit(solution)/shard_map/ppermute | solution.py:25
  150.2 0.0 copy-done.2
  150.2 0.0 copy-done.4
  150.2 1.9 %shard_map.106 = (f32[512,256]{1,0:T(8,128)}, f32[256,512]{1,0:T(8,128)}, f32[256,512]{1,0:T(8,128)}) custom-call(bf16[128,512]{1,0:T(8,128)(2,1)S(1)} %get-tuple-element.30.refs_0_, bf16[128,512]{1,0:T(8,128)(2,1)S(1)} %get-tuple-element.31.refs_1_, bf16[128,512]{1,0:T(8,128)(2,1)S(1)} %get-tuple-element.32.refs_2_, bf16[128,1536]{1,0:T(8,128)(2,1)S(1)} %copy-done.2, ...), custom_call_target="tpu_custom_call" | custom-call | flops 301989888 | bytes 1179648 | tf_op jit(solution)/shard_map/pallas_call | solution.py:146
  152.0 3.3 %shard_map.107 = (f32[512,256]{1,0:T(8,128)}, f32[256,512]{1,0:T(8,128)}, f32[256,512]{1,0:T(8,128)}) custom-call(bf16[128,512]{1,0:T(8,128)(2,1)S(1)} %get-tuple-element.28.refs_0_, bf16[128,512]{1,0:T(8,128)(2,1)S(1)} %get-tuple-element.29.refs_1_, ...), custom_call_target="tpu_custom_call", output_to_operand_aliasing={{0}: (4, {}), {1}: (5, {}), {2}: (6, {})} | custom-call | flops 201326592 | bytes 786432 | tf_op jit(solution)/shard_map/pallas_call | solution.py:146
  155.3 3.0 %shard_map.108 = (f32[512,256]{1,0:T(8,128)}, f32[256,512]{1,0:T(8,128)}, f32[256,512]{1,0:T(8,128)}) custom-call(bf16[128,512]{1,0:T(8,128)(2,1)S(1)} %get-tuple-element.26.refs_0_, bf16[128,512]{1,0:T(8,128)(2,1)S(1)} %get-tuple-element.27.refs_1_, ...), custom_call_target="tpu_custom_call", output_to_operand_aliasing={{0}: (4, {}), {1}: (5, {}), {2}: (6, {})} | custom-call | flops 201326592 | bytes 786432 | tf_op jit(solution)/shard_map/pallas_call | solution.py:146
  158.3 0.0 collective-permute-done.5.refs_2_
  158.3 0.0 collective-permute-done.9.refs_3_
  158.3 3.0 %shard_map.109 = (f32[512,256]{1,0:T(8,128)}, f32[256,512]{1,0:T(8,128)}, f32[256,512]{1,0:T(8,128)}) custom-call(bf16[64,512]{1,0:T(8,128)(2,1)S(1)} %get-tuple-element.49.refs_0_, bf16[64,512]{1,0:T(8,128)(2,1)S(1)} %get-tuple-element.48.refs_1_, ...), custom_call_target="tpu_custom_call", output_to_operand_aliasing={{0}: (4, {}), {1}: (5, {}), {2}: (6, {})} | custom-call | flops 100663296 | bytes 393216 | tf_op jit(solution)/shard_map/pallas_call | solution.py:146
  (5 shorter events, 0.1 us)
Async XLA Ops:
  0.6 30.9 %copy-start = (bf16[1024,512]{1,0:T(8,128)(2,1)S(1)}, bf16[1024,512]{1,0:T(8,128)(2,1)}, u32[]{:S(2)}) copy-start(bf16[1024,512]{1,0:T(8,128)(2,1)} %param.13) | copy-start | bytes 3145732
  29.6 17.5 %collective-permute-start.1 = (bf16[16,8,2048]{2,1,0:T(8,128)(2,1)S(1)}, bf16[16,8,2048]{2,1,0:T(8,128)(2,1)}, u32[]{:S(2)}, u32[]{:S(2)}) collective-permute-start(bf16[16,8,2048]{2,1,0:T(8,128)(2,1)S(1)} %all_to_all.20), channel_id=1, source_target_pairs={{0,32},{32,0},{1,33},{33,1},{2,34},{34,2},{3,35},{35,3},{4,36},{36... | collective-permute-start | bytes 1572872 | tf_op jit(solution)/shard_map/ppermute | solution.py:25
  31.9 13.5 %copy-start.5 = (bf16[1024,512]{1,0:T(8,128)(2,1)S(1)}, bf16[1024,512]{1,0:T(8,128)(2,1)}, u32[]{:S(2)}) copy-start(bf16[1024,512]{1,0:T(8,128)(2,1)} %param.14) | copy-start | bytes 3145732
  32.7 28.6 %all-to-all-start.1 = ((bf16[4,128,512]{2,1,0:T(8,128)(2,1)}), bf16[4,128,512]{2,1,0:T(8,128)(2,1)S(1)}, u32[]{:S(2)}, u32[]{:S(2)}) async-start(bf16[4,128,512]{2,1,0:T(8,128)(2,1)} %shard_map.104), calls=%async_computation.1 | async-start | bytes 1048576 | tf_op jit(solution)/shard_map/all_to_all | solution.py:187
  45.4 1.2 copy-start.6
  106.8 10.9 %collective-permute-start.2 = (bf16[128,1536]{1,0:T(8,128)(2,1)S(1)}, bf16[128,1536]{1,0:T(8,128)(2,1)S(1)}, u32[]{:S(2)}, u32[]{:S(2)}) collective-permute-start(bf16[128,1536]{1,0:T(8,128)(2,1)S(1)} %bitcast.21), channel_id=1, source_target_pairs={{0,4},{4,8},{8,12},{12,16},{16,20},{20,24},{24,28},{28,0},{1,5},{5... | collective-permute-start | bytes 1179656 | tf_op jit(solution)/shard_map/ppermute | solution.py:25
  109.4 11.0 %collective-permute-start.6 = (bf16[128,1536]{1,0:T(8,128)(2,1)S(1)}, bf16[128,1536]{1,0:T(8,128)(2,1)S(1)}, u32[]{:S(2)}, u32[]{:S(2)}) collective-permute-start(bf16[128,1536]{1,0:T(8,128)(2,1)S(1)} %bitcast.22), channel_id=1, source_target_pairs={{0,28},{4,0},{8,4},{12,8},{16,12},{20,16},{24,20},{28,24},{1,29},{... | collective-permute-start | bytes 1179656 | tf_op jit(solution)/shard_map/ppermute | solution.py:25
  117.7 11.0 %collective-permute-start.3 = (bf16[128,1536]{1,0:T(8,128)(2,1)S(1)}, bf16[128,1536]{1,0:T(8,128)(2,1)}, u32[]{:S(2)}, u32[]{:S(2)}) collective-permute-start(bf16[128,1536]{1,0:T(8,128)(2,1)S(1)} %collective-permute-done.2.refs_3_), channel_id=1, source_target_pairs={{0,4},{4,8},{8,12},{12,16},{16,20},{20,24},{24,28},{28,0},{1,5},{5... | collective-permute-start | bytes 1179656 | tf_op jit(solution)/shard_map/ppermute | solution.py:25
  119.6 0.7 copy-start.1
  120.4 10.4 %collective-permute-start.7 = (bf16[128,1536]{1,0:T(8,128)(2,1)S(1)}, bf16[128,1536]{1,0:T(8,128)(2,1)}, u32[]{:S(2)}, u32[]{:S(2)}) collective-permute-start(bf16[128,1536]{1,0:T(8,128)(2,1)S(1)} %collective-permute-done.6.refs_4_), channel_id=1, source_target_pairs={{0,28},{4,0},{8,4},{12,8},{16,12},{20,16},{24,20},{28,24},{1,29},{... | collective-permute-start | bytes 1179656 | tf_op jit(solution)/shard_map/ppermute | solution.py:25
  125.5 0.7 copy-start.3
  126.3 10.2 %collective-permute-start = (bf16[4,128,512]{2,1,0:T(8,128)(2,1)S(1)}, bf16[4,128,512]{2,1,0:T(8,128)(2,1)S(1)}, u32[]{:S(2)}, u32[]{:S(2)}) collective-permute-start(bf16[4,128,512]{2,1,0:T(8,128)(2,1)S(1)} %all-to-all-done.1.own_ref), channel_id=1, source_target_pairs={{0,32},{32,0},{1,33},{33,1},{2,34},{34,2},{3,35},{35,3},{4,36},{36... | collective-permute-start | bytes 1572872 | tf_op jit(solution)/shard_map/ppermute | solution.py:25
  128.7 14.3 %collective-permute-start.4 = (bf16[128,1536]{1,0:T(8,128)(2,1)}, bf16[128,1536]{1,0:T(8,128)(2,1)S(1)}, u32[]{:S(2)}, u32[]{:S(2)}) collective-permute-start(bf16[128,1536]{1,0:T(8,128)(2,1)} %collective-permute-done.3.refs_2_), channel_id=1, source_target_pairs={{0,4},{4,8},{8,12},{12,16},{16,20},{20,24},{24,28},{28,0},{1,5},{5... | collective-permute-start | bytes 1179656 | tf_op jit(solution)/shard_map/ppermute | solution.py:25
  130.8 14.2 %collective-permute-start.8 = (bf16[128,1536]{1,0:T(8,128)(2,1)}, bf16[128,1536]{1,0:T(8,128)(2,1)S(1)}, u32[]{:S(2)}, u32[]{:S(2)}) collective-permute-start(bf16[128,1536]{1,0:T(8,128)(2,1)} %collective-permute-done.7.refs_3_), channel_id=1, source_target_pairs={{0,28},{4,0},{8,4},{12,8},{16,12},{20,16},{24,20},{28,24},{1,29},{... | collective-permute-start | bytes 1179656 | tf_op jit(solution)/shard_map/ppermute | solution.py:25
  136.5 13.7 %copy-start.2 = (bf16[128,1536]{1,0:T(8,128)(2,1)S(1)}, bf16[128,1536]{1,0:T(8,128)(2,1)}, u32[]{:S(2)}) copy-start(bf16[128,1536]{1,0:T(8,128)(2,1)} %copy-done.1) | copy-start | bytes 1179652
  136.5 13.7 %copy-start.4 = (bf16[128,1536]{1,0:T(8,128)(2,1)S(1)}, bf16[128,1536]{1,0:T(8,128)(2,1)}, u32[]{:S(2)}) copy-start(bf16[128,1536]{1,0:T(8,128)(2,1)} %copy-done.3) | copy-start | bytes 1179652
  143.0 15.3 %collective-permute-start.5 = (bf16[64,1536]{1,0:T(8,128)(2,1)S(1)}, bf16[64,1536]{1,0:T(8,128)(2,1)S(1)}, u32[]{:S(2)}, u32[]{:S(2)}) collective-permute-start(bf16[64,1536]{1,0:T(8,128)(2,1)S(1)} %slice.53), channel_id=1, source_target_pairs={{0,4},{4,8},{8,12},{12,16},{16,20},{20,24},{24,28},{28,0},{1,5},{5... | collective-permute-start | bytes 589832 | tf_op jit(solution)/shard_map/ppermute | solution.py:25
  145.0 13.3 %collective-permute-start.9 = (bf16[64,1536]{1,0:T(8,128)(2,1)S(1)}, bf16[64,1536]{1,0:T(8,128)(2,1)S(1)}, u32[]{:S(2)}, u32[]{:S(2)}) collective-permute-start(bf16[64,1536]{1,0:T(8,128)(2,1)S(1)} %slice.54), channel_id=1, source_target_pairs={{0,28},{4,0},{8,4},{12,8},{16,12},{20,16},{24,20},{28,24},{1,29},{... | collective-permute-start | bytes 589832 | tf_op jit(solution)/shard_map/ppermute | solution.py:25

commit v6 on v5

--- a/solution.py
+++ b/solution.py
@@ -116,46 +116,15 @@
     return lax.dot_general(a, b, (((0,), (0,)), ((), ())), preferred_element_type=f32)
 
 
-def add_kernel(blocks, *refs):
-    down_ref, gate_ref, up_ref = refs[-3:]
-    earlier = refs[2 * blocks : -3]
-    quarter, units = gate_ref.shape
-    sums = [ref[...] for ref in earlier]
-    for n in range(blocks):
-        inputs_ref = refs[n]
-        values_ref = refs[blocks + n]
-        tokens = inputs_ref[:, :quarter]
-        terms = (
-            product(values_ref[:, :units], inputs_ref[:, quarter:]),
-            product(tokens, values_ref[:, units : 2 * units]),
-            product(tokens, values_ref[:, 2 * units :]),
-        )
-        sums = [a + b for a, b in zip(sums, terms)] if sums else terms
-    down_ref[...], gate_ref[...], up_ref[...] = sums
-
-
 def add_products(sums, inputs, values):
-    blocks = len(values)
-    quarter = inputs[0].shape[1] // 2
-    rows, width = values[0].shape
-    units = width // 3
-    wide = jax.ShapeDtypeStruct((quarter, units), f32)
-    tall = jax.ShapeDtypeStruct((units, quarter), f32)
-    operands = tuple(inputs) + tuple(values) + tuple(sums)
-    first = 2 * blocks
-    return pl.pallas_call(
-        functools.partial(add_kernel, blocks),
-        out_shape=(tall, wide, wide),
-        in_specs=[in_vmem()] * len(operands),
-        out_specs=(in_vmem(),) * 3,
-        input_output_aliases={first + n: n for n in range(len(sums))},
-        compiler_params=limit(12),
-        cost_estimate=pl.CostEstimate(
-            flops=6 * blocks * rows * quarter * units,
-            bytes_accessed=2 * blocks * rows * width,
-            transcendentals=0,
-        ),
-    )(*operands)
+    quarter = inputs.shape[1] // 2
+    units = values.shape[1] // 3
+    terms = (
+        product(inputs[:, :quarter], values[:, units : 2 * units]),
+        product(inputs[:, :quarter], values[:, 2 * units :]),
+        product(values[:, :units], inputs[:, quarter:]),
+    )
+    return terms if sums is None else tuple(a + b for a, b in zip(sums, terms))
 
 
 def after(value, *others):
@@ -217,22 +186,21 @@
     order.append(n_y // 2)
     inputs = put_in_order(order, y, own_cuts, shift(own_cuts, "core", 1))
     right = left = near
-    sums = ()
+    sums = None
+    waiting = [(inputs[0], near)]
     for s in range(1, n_y // 2):
         right = shift(right, "y", 1)
         left = shift(left, "y", -1)
-        rows_in = [inputs[n_y - s], inputs[s]]
-        blocks = [right, left]
-        if s == 1:
-            rows_in.append(inputs[0])
-            blocks.append(near)
-        sums = add_products(sums, rows_in, blocks)
+        rows_in, blocks = zip(*waiting)
+        blocks = jnp.concatenate([after(v, right) for v in blocks], axis=0)
+        sums = add_products(sums, jnp.concatenate(rows_in, axis=0), blocks)
+        waiting = [(inputs[n_y - s], right), (inputs[s], left)]
     middle = near.shape[0] // 2
     top = shift(right[:middle], "y", 1)
     low = shift(left[middle:], "y", -1)
-    at = inputs[n_y // 2]
-    down_grad, gate_grad, up_grad = add_products(sums, [at[:middle], at[middle:]], [top, low])
-    return (gate_grad, up_grad, down_grad)
+    for rows_in, block_in in waiting:
+        sums = add_products(sums, rows_in, block_in)
+    return add_products(sums, inputs[n_y // 2], jnp.concatenate([top, low], axis=0))
 
 
 def solution(mesh):

time: 163 us -> 160 us (0.982)
  blocking collectives: 72.5 us -> 56.2 us
  waiting for transfers between devices: 20.9 us -> 32.7 us
  Pallas kernels: 13.8 us -> 2.64 us
  matrix products: 5.07 us -> 11.9 us
  starting transfers between devices: 45.2 us -> 49.9 us
    all_to_all x1 -> x0, blocking collectives: 16.3 us -> none  [copies_to(): return lax.all_to_all(spread, axis, 0, 0)]
    pallas_call x4 -> x0, Pallas kernels: 11.2 us -> none  [add_products(): pl.pallas_call(functools.partial(add_kernel, blocks), out_shape=(tall, wi...]
    all_to_all x0 -> x1, waiting for transfers between devices: none -> 9.01 us  [copies_to(): return lax.all_to_all(spread, axis, 0, 0)]
    dot_general x0 -> x18, matrix products: none -> 6.86 us  [product(): lax.dot_general(a, b, (((0,), (0,)), ((), ())), preferred_element_type=f32)]
    all_to_all x0 -> x1, starting transfers between devices: none -> 5.27 us  [copies_to(): return lax.all_to_all(spread, axis, 0, 0)]
    ppermute x10, waiting for transfers between devices: 10.9 us -> 13.7 us  [shift(): return lax.ppermute(value, axis, [(i, (i + step) % n) for i in range(n)])]
  transfers between devices with their start and end apart: 11 -> 12, of which waited for: 5 -> 6; matrix products, arithmetic and copies ran while one was open for 3% -> 6% of each run, Pallas kernels for 6% -> 1%
where the time goes in v6:
time: 160 us; the launch traced here: 158 us
  blocking collectives  56.2 us (35%)
  starting transfers between devices  49.9 us (31%)
  waiting for transfers between devices  32.7 us (20%)
  matrix products  11.9 us (7%)
  local copies, waits for them, and re-layouts  2.9 us (2%)
  Pallas kernels  2.64 us (2%)
    ppermute x10, starting transfers between devices, shift(): return lax.ppermute(value, axis, [(i, (i + step) % n) for i in range(n)])  32 us
    all_to_all x1, blocking collectives, body(): sums = jnp.sum(lax.all_to_all(partial_sums, 'y', 0, 0).astype(f32), axis=0)  29 us
    all_to_all x1, blocking collectives, body(): mine = lax.all_to_all(spread, ('zlo', 'x'), 0, 0)  27.2 us
    ppermute x10, waiting for transfers between devices, shift(): return lax.ppermute(value, axis, [(i, (i + step) % n) for i in range(n)])  13.7 us
    all_to_all x1, starting transfers between devices, body(): own_cuts = lax.all_to_all(cut_quarters(n_k, mine), 'zhi', 0, 0)  12.7 us
    all_to_all x1, waiting for transfers between devices, body(): own_cuts = lax.all_to_all(cut_quarters(n_k, mine), 'zhi', 0, 0)  9.98 us
    all_to_all x1, waiting for transfers between devices, copies_to(): return lax.all_to_all(spread, axis, 0, 0)  9.01 us
    dot_general x18, matrix products, product(): lax.dot_general(a, b, (((0,), (0,)), ((), ())), preferred_element_type=f32)  6.86 us
  transfers between devices with their start and end apart: 12, of which 6 were waited for; matrix products, arithmetic and copies ran while one was open for 6% of the time, Pallas kernels for 1%

profile of v6, /device:TPU:14, one launch (start us, length us, event | category | flops | bytes accessed | tf_op | source)
XLA Modules:
  0.0 157.8 jit_solution(12478786410942291148)
XLA Ops:
  0.6 0.0 copy-start
  0.7 1.7 %shard_map.103 = bf16[16,8,2048]{2,1,0:T(8,128)(2,1)} custom-call(s32[1]{0:T(128)} %bitcast.1.block_ref, s32[8,8]{1,0:T(8,128)} %rewards_ref.1, s32[8]{0:T(128)} %selected_ref.1, s32[8]{0:T(128)} %pad_ref.1, bf16[8,1024]{1,0:T(8,128)(2,1)} %tokens_ref.1, bf16[8,1024]{1,0:T(8,128)(2,1)} %cotangent_ref.1), custom_call_target="tpu_custom_call" | custom-call | tf_op jit(solution)/shard_map/pallas_call | solution.py:60
  2.4 27.2 %all_to_all.20 = bf16[16,8,2048]{2,1,0:T(8,128)(2,1)S(1)} all-to-all(bf16[16,8,2048]{2,1,0:T(8,128)(2,1)} %shard_map.103), channel_id=1, replica_groups=mesh['zlo'=2,'x'=8,'core'=2,'y'=8,'zhi'=4] {'zlo','x'}, dimensions={0} | all-to-all | bytes 1048576 | tf_op jit(solution)/shard_map/all_to_all | solution.py:153
  29.6 1.9 %collective-permute-start.1 = (bf16[16,8,2048]{2,1,0:T(8,128)(2,1)S(1)}, bf16[16,8,2048]{2,1,0:T(8,128)(2,1)}, u32[]{:S(2)}, u32[]{:S(2)}) collective-permute-start(bf16[16,8,2048]{2,1,0:T(8,128)(2,1)S(1)} %all_to_all.20), channel_id=1, source_target_pairs={{0,32},{32,0},{1,33},{33,1},{2,34},{34,2},{3,35},{35,3},{4,36},{36... | collective-permute-start | bytes 1572872 | tf_op jit(solution)/shard_map/ppermute | solution.py:25
  31.5 0.0 copy-done
  31.6 0.3 fusion.9
  31.9 0.0 copy-start.1
  31.9 0.8 shard_map.104
  32.7 12.7 %all-to-all-start.1 = ((bf16[4,128,512]{2,1,0:T(8,128)(2,1)}), bf16[4,128,512]{2,1,0:T(8,128)(2,1)S(1)}, u32[]{:S(2)}, u32[]{:S(2)}) async-start(bf16[4,128,512]{2,1,0:T(8,128)(2,1)} %shard_map.104), calls=%async_computation.1 | async-start | bytes 1048576 | tf_op jit(solution)/shard_map/all_to_all | solution.py:156
  45.4 0.0 copy-done.1
  45.4 0.0 copy-start.2
  45.4 0.3 fusion.10
  45.7 0.9 copy-done.2
  46.6 0.5 fusion.11
  47.1 0.0 collective-permute-done.1
  47.1 1.3 fusion.12
  48.4 1.3 fusion.13
  49.7 1.4 fusion.14
  51.1 0.3 maximum_maximum_fusion
  51.4 10.0 %all-to-all-done.1.own_ref = bf16[4,128,512]{2,1,0:T(8,128)(2,1)S(1)} async-done(((bf16[4,128,512]{2,1,0:T(8,128)(2,1)}), bf16[4,128,512]{2,1,0:T(8,128)(2,1)S(1)}, u32[]{:S(2)}, u32[]{:S(2)}) %all-to-all-start.1) | async-done | bytes 524320 | tf_op jit(solution)/shard_map/all_to_all | solution.py:156
  61.4 29.0 %all_to_all.21 = f16[8,32,1536]{2,1,0:T(8,128)(2,1)S(1)} all-to-all(f16[8,32,1536]{2,1,0:T(8,128)(2,1)S(1)} %maximum_maximum_fusion), channel_id=1, replica_groups=mesh['zlo'=2,'x'=8,'core'=2,'y'=8,'zhi'=4] {'y'}, dimensions={0} | all-to-all | bytes 1572864 | tf_op jit(solution)/shard_map/all_to_all | solution.py:168
  90.3 0.1 convert_reduce_fusion
  90.5 0.1 multiply_convert_fusion.2
  90.5 0.8 broadcast_in_dim.2
  91.3 5.3 %all-to-all-start.3 = ((bf16[4,32,1536]{2,1,0:T(8,128)(2,1)}), bf16[4,32,1536]{2,1,0:T(8,128)(2,1)S(1)}, u32[]{:S(2)}, u32[]{:S(2)}) async-start(bf16[4,32,1536]{2,1,0:T(8,128)(2,1)} %broadcast_in_dim.2), calls=%async_computation.3 | async-start | bytes 786432 | tf_op jit(solution)/shard_map/all_to_all | solution.py:136
  96.6 1.9 %collective-permute-start = (bf16[4,128,512]{2,1,0:T(8,128)(2,1)S(1)}, bf16[4,128,512]{2,1,0:T(8,128)(2,1)S(1)}, u32[]{:S(2)}, u32[]{:S(2)}) collective-permute-start(bf16[4,128,512]{2,1,0:T(8,128)(2,1)S(1)} %all-to-all-done.1.own_ref), channel_id=1, source_target_pairs={{0,32},{32,0},{1,33},{33,1},{2,34},{34,2},{3,35},{35,3},{4,36},{36... | collective-permute-start | bytes 1572872 | tf_op jit(solution)/shard_map/ppermute | solution.py:25
  98.5 9.0 %all-to-all-done.3 = bf16[4,32,1536]{2,1,0:T(8,128)(2,1)S(1)} async-done(((bf16[4,32,1536]{2,1,0:T(8,128)(2,1)}), bf16[4,32,1536]{2,1,0:T(8,128)(2,1)S(1)}, u32[]{:S(2)}, u32[]{:S(2)}) %all-to-all-start.3) | async-done | bytes 393248 | tf_op jit(solution)/shard_map/all_to_all | solution.py:136
  107.5 1.9 %collective-permute-start.2 = (bf16[128,1536]{1,0:T(8,128)(2,1)S(1)}, bf16[128,1536]{1,0:T(8,128)(2,1)}, u32[]{:S(2)}, u32[]{:S(2)}) collective-permute-start(bf16[128,1536]{1,0:T(8,128)(2,1)S(1)} %bitcast.21), channel_id=1, source_target_pairs={{0,4},{4,8},{8,12},{12,16},{16,20},{20,24},{24,28},{28,0},{1,5},{5... | collective-permute-start | bytes 1179656 | tf_op jit(solution)/shard_map/ppermute | solution.py:25
  109.4 5.1 %collective-permute-start.4 = (bf16[128,1536]{1,0:T(8,128)(2,1)S(1)}, bf16[128,1536]{1,0:T(8,128)(2,1)S(1)}, u32[]{:S(2)}, u32[]{:S(2)}) collective-permute-start(bf16[128,1536]{1,0:T(8,128)(2,1)S(1)} %bitcast.22), channel_id=1, source_target_pairs={{0,28},{4,0},{8,4},{12,8},{16,12},{20,16},{24,20},{28,24},{1,29},{... | collective-permute-start | bytes 1179656 | tf_op jit(solution)/shard_map/ppermute | solution.py:25
  114.6 3.9 %collective-permute-done.2 = bf16[128,1536]{1,0:T(8,128)(2,1)} collective-permute-done((bf16[128,1536]{1,0:T(8,128)(2,1)S(1)}, bf16[128,1536]{1,0:T(8,128)(2,1)}, u32[]{:S(2)}, u32[]{:S(2)}) %collective-permute-start.2) | collective-permute-done | bytes 393248 | tf_op jit(solution)/shard_map/ppermute | solution.py:25
  118.5 1.9 %collective-permute-start.3 = (bf16[128,1536]{1,0:T(8,128)(2,1)}, bf16[128,1536]{1,0:T(8,128)(2,1)S(1)}, u32[]{:S(2)}, u32[]{:S(2)}) collective-permute-start(bf16[128,1536]{1,0:T(8,128)(2,1)} %collective-permute-done.2), channel_id=1, source_target_pairs={{0,4},{4,8},{8,12},{12,16},{16,20},{20,24},{24,28},{28,0},{1,5},{5... | collective-permute-start | bytes 1179656 | tf_op jit(solution)/shard_map/ppermute | solution.py:25
  120.4 0.0 collective-permute-done.other_ref
  120.4 0.1 shard_map.105
  120.6 0.0 collective-permute-done.4
  120.6 5.1 %collective-permute-start.6 = (bf16[128,1536]{1,0:T(8,128)(2,1)S(1)}, bf16[128,1536]{1,0:T(8,128)(2,1)S(1)}, u32[]{:S(2)}, u32[]{:S(2)}) collective-permute-start(bf16[128,1536]{1,0:T(8,128)(2,1)S(1)} %collective-permute-done.4), channel_id=1, source_target_pairs={{0,28},{4,0},{8,4},{12,8},{16,12},{20,16},{24,20},{28,24},{1,29},{... | collective-permute-start | bytes 1179656 | tf_op jit(solution)/shard_map/ppermute | solution.py:25
  125.7 3.8 %collective-permute-done.3 = bf16[128,1536]{1,0:T(8,128)(2,1)S(1)} collective-permute-done((bf16[128,1536]{1,0:T(8,128)(2,1)}, bf16[128,1536]{1,0:T(8,128)(2,1)S(1)}, u32[]{:S(2)}, u32[]{:S(2)}) %collective-permute-start.3) | collective-permute-done | bytes 393248 | tf_op jit(solution)/shard_map/ppermute | solution.py:25
  129.6 1.0 constant_dynamic-update-slice_fusion.3
  130.6 1.9 %collective-permute-start.5 = (bf16[128,1536]{1,0:T(8,128)(2,1)S(1)}, bf16[128,1536]{1,0:T(8,128)(2,1)S(1)}, u32[]{:S(2)}, u32[]{:S(2)}) collective-permute-start(bf16[128,1536]{1,0:T(8,128)(2,1)S(1)} %collective-permute-done.3), channel_id=1, source_target_pairs={{0,4},{4,8},{8,12},{12,16},{16,20},{20,24},{24,28},{28,0},{1,5},{5... | collective-permute-start | bytes 1179656 | tf_op jit(solution)/shard_map/ppermute | solution.py:25
  132.5 0.3 fusion.17
  132.8 0.0 collective-permute-done.6
  132.8 5.1 %collective-permute-start.7 = (bf16[128,1536]{1,0:T(8,128)(2,1)S(1)}, bf16[128,1536]{1,0:T(8,128)(2,1)S(1)}, u32[]{:S(2)}, u32[]{:S(2)}) collective-permute-start(bf16[128,1536]{1,0:T(8,128)(2,1)S(1)} %collective-permute-done.6), channel_id=1, source_target_pairs={{0,28},{4,0},{8,4},{12,8},{16,12},{20,16},{24,20},{28,24},{1,29},{... | collective-permute-start | bytes 1179656 | tf_op jit(solution)/shard_map/ppermute | solution.py:25
  138.0 0.2 fusion.21
  138.2 0.2 fusion.25
  138.5 4.3 %collective-permute-done.5 = bf16[128,1536]{1,0:T(8,128)(2,1)S(1)} collective-permute-done((bf16[128,1536]{1,0:T(8,128)(2,1)S(1)}, bf16[128,1536]{1,0:T(8,128)(2,1)S(1)}, u32[]{:S(2)}, u32[]{:S(2)}) %collective-permute-start.5) | collective-permute-done | bytes 393248 | tf_op jit(solution)/shard_map/ppermute | solution.py:25
  142.8 1.9 %collective-permute-start.8 = (bf16[64,1536]{1,0:T(8,128)(2,1)S(1)}, bf16[64,1536]{1,0:T(8,128)(2,1)S(1)}, u32[]{:S(2)}, u32[]{:S(2)}) collective-permute-start(bf16[64,1536]{1,0:T(8,128)(2,1)S(1)} %slice.177), channel_id=1, source_target_pairs={{0,4},{4,8},{8,12},{12,16},{16,20},{20,24},{24,28},{28,0},{1,5},{5... | collective-permute-start | bytes 589832 | tf_op jit(solution)/shard_map/ppermute | solution.py:25
  144.8 0.3 fusion.15
  145.0 0.2 fusion.19
  145.3 0.2 fusion.23
  145.5 0.0 collective-permute-done.7
  145.6 5.1 %collective-permute-start.9 = (bf16[64,1536]{1,0:T(8,128)(2,1)S(1)}, bf16[64,1536]{1,0:T(8,128)(2,1)S(1)}, u32[]{:S(2)}, u32[]{:S(2)}) collective-permute-start(bf16[64,1536]{1,0:T(8,128)(2,1)S(1)} %slice.178), channel_id=1, source_target_pairs={{0,28},{4,0},{8,4},{12,8},{16,12},{20,16},{24,20},{28,24},{1,29},{... | collective-permute-start | bytes 589832 | tf_op jit(solution)/shard_map/ppermute | solution.py:25
  150.7 0.3 fusion.6
  151.0 0.3 fusion.3
  151.2 0.2 fusion
  151.5 0.2 fusion.35
  151.7 0.2 fusion.42
  152.0 0.2 fusion.47
  152.2 0.0 collective-permute-done.8
  152.3 1.6 %collective-permute-done.9 = bf16[64,1536]{1,0:T(8,128)(2,1)S(1)} collective-permute-done((bf16[64,1536]{1,0:T(8,128)(2,1)S(1)}, bf16[64,1536]{1,0:T(8,128)(2,1)S(1)}, u32[]{:S(2)}, u32[]{:S(2)}) %collective-permute-start.9) | collective-permute-done | bytes 196640 | tf_op jit(solution)/shard_map/ppermute | solution.py:25
  153.9 0.2 fusion.33
  154.1 0.2 fusion.40
  154.4 0.2 fusion.45
  154.7 1.1 fusion.8
  155.7 1.0 fusion.5
  156.7 1.0 fusion.2
  (11 shorter events, 0.2 us)
Async XLA Ops:
  0.6 30.9 %copy-start = (bf16[1024,512]{1,0:T(8,128)(2,1)S(1)}, bf16[1024,512]{1,0:T(8,128)(2,1)}, u32[]{:S(2)}) copy-start(bf16[1024,512]{1,0:T(8,128)(2,1)} %param.13) | copy-start | bytes 3145732
  29.6 17.5 %collective-permute-start.1 = (bf16[16,8,2048]{2,1,0:T(8,128)(2,1)S(1)}, bf16[16,8,2048]{2,1,0:T(8,128)(2,1)}, u32[]{:S(2)}, u32[]{:S(2)}) collective-permute-start(bf16[16,8,2048]{2,1,0:T(8,128)(2,1)S(1)} %all_to_all.20), channel_id=1, source_target_pairs={{0,32},{32,0},{1,33},{33,1},{2,34},{34,2},{3,35},{35,3},{4,36},{36... | collective-permute-start | bytes 1572872 | tf_op jit(solution)/shard_map/ppermute | solution.py:25
  31.9 13.5 %copy-start.1 = (bf16[1024,512]{1,0:T(8,128)(2,1)S(1)}, bf16[1024,512]{1,0:T(8,128)(2,1)}, u32[]{:S(2)}) copy-start(bf16[1024,512]{1,0:T(8,128)(2,1)} %param.14) | copy-start | bytes 3145732
  32.7 28.6 %all-to-all-start.1 = ((bf16[4,128,512]{2,1,0:T(8,128)(2,1)}), bf16[4,128,512]{2,1,0:T(8,128)(2,1)S(1)}, u32[]{:S(2)}, u32[]{:S(2)}) async-start(bf16[4,128,512]{2,1,0:T(8,128)(2,1)} %shard_map.104), calls=%async_computation.1 | async-start | bytes 1048576 | tf_op jit(solution)/shard_map/all_to_all | solution.py:156
  45.4 1.2 copy-start.2
  91.3 16.2 %all-to-all-start.3 = ((bf16[4,32,1536]{2,1,0:T(8,128)(2,1)}), bf16[4,32,1536]{2,1,0:T(8,128)(2,1)S(1)}, u32[]{:S(2)}, u32[]{:S(2)}) async-start(bf16[4,32,1536]{2,1,0:T(8,128)(2,1)} %broadcast_in_dim.2), calls=%async_computation.3 | async-start | bytes 786432 | tf_op jit(solution)/shard_map/all_to_all | solution.py:136
  96.6 23.8 %collective-permute-start = (bf16[4,128,512]{2,1,0:T(8,128)(2,1)S(1)}, bf16[4,128,512]{2,1,0:T(8,128)(2,1)S(1)}, u32[]{:S(2)}, u32[]{:S(2)}) collective-permute-start(bf16[4,128,512]{2,1,0:T(8,128)(2,1)S(1)} %all-to-all-done.1.own_ref), channel_id=1, source_target_pairs={{0,32},{32,0},{1,33},{33,1},{2,34},{34,2},{3,35},{35,3},{4,36},{36... | collective-permute-start | bytes 1572872 | tf_op jit(solution)/shard_map/ppermute | solution.py:25
  107.5 11.0 %collective-permute-start.2 = (bf16[128,1536]{1,0:T(8,128)(2,1)S(1)}, bf16[128,1536]{1,0:T(8,128)(2,1)}, u32[]{:S(2)}, u32[]{:S(2)}) collective-permute-start(bf16[128,1536]{1,0:T(8,128)(2,1)S(1)} %bitcast.21), channel_id=1, source_target_pairs={{0,4},{4,8},{8,12},{12,16},{16,20},{20,24},{24,28},{28,0},{1,5},{5... | collective-permute-start | bytes 1179656 | tf_op jit(solution)/shard_map/ppermute | solution.py:25
  109.4 11.1 %collective-permute-start.4 = (bf16[128,1536]{1,0:T(8,128)(2,1)S(1)}, bf16[128,1536]{1,0:T(8,128)(2,1)S(1)}, u32[]{:S(2)}, u32[]{:S(2)}) collective-permute-start(bf16[128,1536]{1,0:T(8,128)(2,1)S(1)} %bitcast.22), channel_id=1, source_target_pairs={{0,28},{4,0},{8,4},{12,8},{16,12},{20,16},{24,20},{28,24},{1,29},{... | collective-permute-start | bytes 1179656 | tf_op jit(solution)/shard_map/ppermute | solution.py:25
  118.5 11.1 %collective-permute-start.3 = (bf16[128,1536]{1,0:T(8,128)(2,1)}, bf16[128,1536]{1,0:T(8,128)(2,1)S(1)}, u32[]{:S(2)}, u32[]{:S(2)}) collective-permute-start(bf16[128,1536]{1,0:T(8,128)(2,1)} %collective-permute-done.2), channel_id=1, source_target_pairs={{0,4},{4,8},{8,12},{12,16},{16,20},{20,24},{24,28},{28,0},{1,5},{5... | collective-permute-start | bytes 1179656 | tf_op jit(solution)/shard_map/ppermute | solution.py:25
  120.6 12.2 %collective-permute-start.6 = (bf16[128,1536]{1,0:T(8,128)(2,1)S(1)}, bf16[128,1536]{1,0:T(8,128)(2,1)S(1)}, u32[]{:S(2)}, u32[]{:S(2)}) collective-permute-start(bf16[128,1536]{1,0:T(8,128)(2,1)S(1)} %collective-permute-done.4), channel_id=1, source_target_pairs={{0,28},{4,0},{8,4},{12,8},{16,12},{20,16},{24,20},{28,24},{1,29},{... | collective-permute-start | bytes 1179656 | tf_op jit(solution)/shard_map/ppermute | solution.py:25
  130.6 12.2 %collective-permute-start.5 = (bf16[128,1536]{1,0:T(8,128)(2,1)S(1)}, bf16[128,1536]{1,0:T(8,128)(2,1)S(1)}, u32[]{:S(2)}, u32[]{:S(2)}) collective-permute-start(bf16[128,1536]{1,0:T(8,128)(2,1)S(1)} %collective-permute-done.3), channel_id=1, source_target_pairs={{0,4},{4,8},{8,12},{12,16},{16,20},{20,24},{24,28},{28,0},{1,5},{5... | collective-permute-start | bytes 1179656 | tf_op jit(solution)/shard_map/ppermute | solution.py:25
  132.8 12.7 %collective-permute-start.7 = (bf16[128,1536]{1,0:T(8,128)(2,1)S(1)}, bf16[128,1536]{1,0:T(8,128)(2,1)S(1)}, u32[]{:S(2)}, u32[]{:S(2)}) collective-permute-start(bf16[128,1536]{1,0:T(8,128)(2,1)S(1)} %collective-permute-done.6), channel_id=1, source_target_pairs={{0,28},{4,0},{8,4},{12,8},{16,12},{20,16},{24,20},{28,24},{1,29},{... | collective-permute-start | bytes 1179656 | tf_op jit(solution)/shard_map/ppermute | solution.py:25
  142.8 9.4 %collective-permute-start.8 = (bf16[64,1536]{1,0:T(8,128)(2,1)S(1)}, bf16[64,1536]{1,0:T(8,128)(2,1)S(1)}, u32[]{:S(2)}, u32[]{:S(2)}) collective-permute-start(bf16[64,1536]{1,0:T(8,128)(2,1)S(1)} %slice.177), channel_id=1, source_target_pairs={{0,4},{4,8},{8,12},{12,16},{16,20},{20,24},{24,28},{28,0},{1,5},{5... | collective-permute-start | bytes 589832 | tf_op jit(solution)/shard_map/ppermute | solution.py:25
  145.6 8.3 %collective-permute-start.9 = (bf16[64,1536]{1,0:T(8,128)(2,1)S(1)}, bf16[64,1536]{1,0:T(8,128)(2,1)S(1)}, u32[]{:S(2)}, u32[]{:S(2)}) collective-permute-start(bf16[64,1536]{1,0:T(8,128)(2,1)S(1)} %slice.178), channel_id=1, source_target_pairs={{0,28},{4,0},{8,4},{12,8},{16,12},{20,16},{24,20},{28,24},{1,29},{... | collective-permute-start | bytes 589832 | tf_op jit(solution)/shard_map/ppermute | solution.py:25

commit v7 on v6

--- a/solution.py
+++ b/solution.py
@@ -23,6 +23,12 @@
 def shift(value, axis, step):
     n = lax.axis_size(axis)
     return lax.ppermute(value, axis, [(i, (i + step) % n) for i in range(n)])
+
+
+def ring_step(value):
+    n = lax.axis_size("y")
+    pairs = [(core * n + i, core * n + (i + 1 - 2 * core) % n) for core in range(CORES) for i in range(n)]
+    return lax.ppermute(value, ("core", "y"), pairs)
 
 
 def prepare_kernel(block_ref, rewards_ref, selected_ref, pad_ref, tokens_ref, cotangent_ref, all_ref):
@@ -84,12 +90,12 @@
     )(rows)
 
 
-def order_kernel(order, y_ref, own_ref, other_ref, *out_refs):
+def order_kernel(place_ref, own_ref, other_ref, *out_refs):
     n_k, rows, _ = own_ref.shape
-    n_y = len(order)
+    n_y = len(out_refs)
     part = rows // n_y
-    for r, out_ref in zip(order, out_refs):
-        share = lax.rem(y_ref[0] + r, n_y)
+    for s, out_ref in enumerate(out_refs):
+        share = lax.rem(place_ref[0] + n_y + s * place_ref[1], n_y)
         spot = pl.ds(pl.multiple_of(share * part, part), part)
         at = 0
         for t in range(n_k):
@@ -98,18 +104,16 @@
                 at += part
 
 
-def put_in_order(order, y, own, other):
+def put_in_order(n_y, place, own, other):
     n_k, rows, both = own.shape
-    n_y = len(order)
     out = jax.ShapeDtypeStruct((2 * n_k * rows // n_y, both), bf16)
-    pieces = pl.pallas_call(
-        functools.partial(order_kernel, order),
+    return pl.pallas_call(
+        order_kernel,
         out_shape=(out,) * n_y,
         in_specs=[in_smem(), in_vmem(), in_vmem()],
         out_specs=(in_vmem(),) * n_y,
         compiler_params=limit(8),
-    )(y.reshape(1), own, other)
-    return dict(zip(order, pieces))
+    )(place, own, other)
 
 
 def product(a, b):
@@ -139,7 +143,6 @@
 def body(tokens, cotangent, pad_mask, rewards, selected, gate_weight, up_weight, down_weight):
     n_y = lax.axis_size("y")
     n_k = lax.axis_size("zhi")
-    y = lax.axis_index("y")
     rows, width = tokens.shape
     units = gate_weight.shape[1]
     block = lax.axis_index(ROW) * n_k + lax.axis_index("zhi")
@@ -165,7 +168,9 @@
         whole = jnp.concatenate([gate, up, back], axis=1).astype(f16)
         pieces.append(whole.reshape(n_y, part, 3 * units))
     partial_sums = after(jnp.concatenate(pieces, axis=1), own_cuts)
-    sums = jnp.sum(lax.all_to_all(partial_sums, "y", 0, 0).astype(f32), axis=0)
+    other_cuts = shift(own_cuts, "core", 1)
+    sums = after(lax.all_to_all(partial_sums, "y", 0, 0), other_cuts)
+    sums = jnp.sum(sums.astype(f32), axis=0)
 
     gate_value = sums[:, :units] * (1.0 / SCALE_UP)
     up_value = sums[:, units : 2 * units] * (1.0 / SCALE_UP)
@@ -180,27 +185,15 @@
     values = jnp.concatenate([hidden, gate_back, up_back], axis=1)
     near = copies_to(values, "zhi").reshape(n_k * share, 3 * units)
 
-    order = [0]
-    for s in range(1, n_y // 2):
-        order += [s, n_y - s]
-    order.append(n_y // 2)
-    inputs = put_in_order(order, y, own_cuts, shift(own_cuts, "core", 1))
-    right = left = near
+    place = jnp.stack([lax.axis_index("y"), 2 * lax.axis_index("core") - 1])
+    inputs = put_in_order(n_y, place, own_cuts, other_cuts)
     sums = None
-    waiting = [(inputs[0], near)]
-    for s in range(1, n_y // 2):
-        right = shift(right, "y", 1)
-        left = shift(left, "y", -1)
-        rows_in, blocks = zip(*waiting)
-        blocks = jnp.concatenate([after(v, right) for v in blocks], axis=0)
-        sums = add_products(sums, jnp.concatenate(rows_in, axis=0), blocks)
-        waiting = [(inputs[n_y - s], right), (inputs[s], left)]
-    middle = near.shape[0] // 2
-    top = shift(right[:middle], "y", 1)
-    low = shift(left[middle:], "y", -1)
-    for rows_in, block_in in waiting:
-        sums = add_products(sums, rows_in, block_in)
-    return add_products(sums, inputs[n_y // 2], jnp.concatenate([top, low], axis=0))
+    held = near
+    for s in range(n_y - 1):
+        arrived = ring_step(held)
+        sums = lax.optimization_barrier(add_products(sums, inputs[s], held))
+        held = arrived
+    return add_products(sums, inputs[n_y - 1], held)
 
 
 def solution(mesh):

time: 160 us -> 190 us (1.19)
  waiting for transfers between devices: 32.7 us -> 97.8 us
  blocking collectives: 56.2 us -> 27.2 us
  starting transfers between devices: 49.9 us -> 42.6 us
  matrix products: 11.9 us -> 14.7 us
  local copies, waits for them, and re-layouts: 2.9 us -> 0.79 us
    ppermute x0 -> x7, waiting for transfers between devices: none -> 57.3 us  [ring_step(): return lax.ppermute(value, ('core', 'y'), pairs)]
    all_to_all x1 -> x0, blocking collectives: 29 us -> none  [body(): sums = jnp.sum(lax.all_to_all(partial_sums, 'y', 0, 0).astype(f32), axis=0)]
    ppermute x10 -> x2, starting transfers between devices: 32 us -> 3.82 us  [shift(): return lax.ppermute(value, axis, [(i, (i + step) % n) for i in range(n)])]
    all_to_all x0 -> x1, waiting for transfers between devices: none -> 17.9 us  [body(): sums = after(lax.all_to_all(partial_sums, 'y', 0, 0), other_cuts)]
    ppermute x0 -> x7, starting transfers between devices: none -> 13.4 us  [ring_step(): return lax.ppermute(value, ('core', 'y'), pairs)]
    ppermute x10 -> x2, waiting for transfers between devices: 13.7 us -> 1.88 us  [shift(): return lax.ppermute(value, axis, [(i, (i + step) % n) for i in range(n)])]
    all_to_all x0 -> x1, starting transfers between devices: none -> 7.53 us  [body(): sums = after(lax.all_to_all(partial_sums, 'y', 0, 0), other_cuts)]
    all_to_all x1, waiting for transfers between devices: 9.01 us -> 12 us  [copies_to(): return lax.all_to_all(spread, axis, 0, 0)]
  transfers between devices with their start and end apart: 12 -> 12, of which waited for: 6 -> 11; matrix products, arithmetic and copies ran while one was open for 6% -> 7% of each run, Pallas kernels for 1% -> 1%
where the time goes in v7:
time: 190 us; the launch traced here: 189 us
  waiting for transfers between devices  97.8 us (51%)
  starting transfers between devices  42.6 us (22%)
  blocking collectives  27.2 us (14%)
  matrix products  14.7 us (8%)
  Pallas kernels  3.19 us (2%)
    ppermute x7, waiting for transfers between devices, ring_step(): return lax.ppermute(value, ('core', 'y'), pairs)  57.3 us
    all_to_all x1, blocking collectives, body(): mine = lax.all_to_all(spread, ('zlo', 'x'), 0, 0)  27.2 us
    all_to_all x1, waiting for transfers between devices, body(): sums = after(lax.all_to_all(partial_sums, 'y', 0, 0), other_cuts)  17.9 us
    ppermute x7, starting transfers between devices, ring_step(): return lax.ppermute(value, ('core', 'y'), pairs)  13.4 us
    all_to_all x1, starting transfers between devices, body(): own_cuts = lax.all_to_all(cut_quarters(n_k, mine), 'zhi', 0, 0)  12.7 us
    all_to_all x1, waiting for transfers between devices, copies_to(): return lax.all_to_all(spread, axis, 0, 0)  12 us
    all_to_all x1, waiting for transfers between devices, body(): own_cuts = lax.all_to_all(cut_quarters(n_k, mine), 'zhi', 0, 0)  8.65 us
    dot_general x24, matrix products, product(): lax.dot_general(a, b, (((0,), (0,)), ((), ())), preferred_element_type=f32)  8.32 us
  transfers between devices with their start and end apart: 12, of which 11 were waited for; matrix products, arithmetic and copies ran while one was open for 7% of the time, Pallas kernels for 1%

profile of v7, /device:TPU:14, one launch (start us, length us, event | category | flops | bytes accessed | tf_op | source)
XLA Modules:
  0.0 188.8 jit_solution(3425581259629842354)
XLA Ops:
  0.6 0.0 copy-start
  0.7 1.7 shard_map.103
  2.4 27.2 %all_to_all.20 = bf16[16,8,2048]{2,1,0:T(8,128)(2,1)S(1)} all-to-all(bf16[16,8,2048]{2,1,0:T(8,128)(2,1)} %shard_map.103), channel_id=1, replica_groups=mesh['zlo'=2,'x'=8,'core'=2,'y'=8,'zhi'=4] {'zlo','x'}, dimensions={0} | all-to-all | bytes 1048576 | tf_op jit(solution)/shard_map/all_to_all | solution.py:156
  29.7 1.9 %collective-permute-start.1 = (bf16[16,8,2048]{2,1,0:T(8,128)(2,1)S(1)}, bf16[16,8,2048]{2,1,0:T(8,128)(2,1)}, u32[]{:S(2)}, u32[]{:S(2)}) collective-permute-start(bf16[16,8,2048]{2,1,0:T(8,128)(2,1)S(1)} %all_to_all.20), channel_id=1, source_target_pairs={{0,32},{32,0},{1,33},{33,1},{2,34},{34,2},{3,35},{35,3},{4,36},{36... | collective-permute-start | bytes 1572872 | tf_op jit(solution)/shard_map/ppermute | solution.py:25
  31.6 0.3 fusion
  31.9 0.8 shard_map.104
  32.7 12.7 %all-to-all-start.1 = ((bf16[4,128,512]{2,1,0:T(8,128)(2,1)}), bf16[4,128,512]{2,1,0:T(8,128)(2,1)S(1)}, u32[]{:S(2)}, u32[]{:S(2)}) async-start(bf16[4,128,512]{2,1,0:T(8,128)(2,1)} %shard_map.104), calls=%async_computation.1 | async-start | bytes 1048576 | tf_op jit(solution)/shard_map/all_to_all | solution.py:159
  45.4 1.5 fusion.1
  46.9 0.5 fusion.2
  47.5 1.4 fusion.5
  48.9 0.0 copy-start.2
  48.9 1.3 fusion.3
  50.3 1.3 fusion.4
  51.6 1.2 maximum_maximum_fusion
  52.7 8.6 %all-to-all-done.1.own_ref = bf16[4,128,512]{2,1,0:T(8,128)(2,1)S(1)} async-done(((bf16[4,128,512]{2,1,0:T(8,128)(2,1)}), bf16[4,128,512]{2,1,0:T(8,128)(2,1)S(1)}, u32[]{:S(2)}, u32[]{:S(2)}) %all-to-all-start.1) | async-done | bytes 524320 | tf_op jit(solution)/shard_map/all_to_all | solution.py:159
  61.4 7.5 %all-to-all-start.2 = ((f16[8,32,1536]{2,1,0:T(8,128)(2,1)}), f16[8,32,1536]{2,1,0:T(8,128)(2,1)S(1)}, u32[]{:S(2)}, u32[]{:S(2)}) async-start(f16[8,32,1536]{2,1,0:T(8,128)(2,1)} %maximum_maximum_fusion), calls=%async_computation.2 | async-start | bytes 1572864 | tf_op jit(solution)/shard_map/all_to_all | solution.py:172
  68.9 1.9 %collective-permute-start = (bf16[4,128,512]{2,1,0:T(8,128)(2,1)S(1)}, bf16[4,128,512]{2,1,0:T(8,128)(2,1)S(1)}, u32[]{:S(2)}, u32[]{:S(2)}) collective-permute-start(bf16[4,128,512]{2,1,0:T(8,128)(2,1)S(1)} %all-to-all-done.1.own_ref), channel_id=1, source_target_pairs={{0,32},{32,0},{1,33},{33,1},{2,34},{34,2},{3,35},{35,3},{4,36},{36... | collective-permute-start | bytes 1572872 | tf_op jit(solution)/shard_map/ppermute | solution.py:25
  70.8 1.9 collective-permute-done.other_ref
  72.7 17.9 %all-to-all-done.2 = f16[8,32,1536]{2,1,0:T(8,128)(2,1)S(1)} async-done(((f16[8,32,1536]{2,1,0:T(8,128)(2,1)}), f16[8,32,1536]{2,1,0:T(8,128)(2,1)S(1)}, u32[]{:S(2)}, u32[]{:S(2)}) %all-to-all-start.2) | async-done | bytes 786464 | tf_op jit(solution)/shard_map/all_to_all | solution.py:172
  90.6 0.1 convert_reduce_fusion
  90.7 0.1 multiply_convert_fusion.2
  90.8 0.8 broadcast_in_dim.2
  91.6 5.2 %all-to-all-start.3 = ((bf16[4,32,1536]{2,1,0:T(8,128)(2,1)}), bf16[4,32,1536]{2,1,0:T(8,128)(2,1)S(1)}, u32[]{:S(2)}, u32[]{:S(2)}) async-start(bf16[4,32,1536]{2,1,0:T(8,128)(2,1)} %broadcast_in_dim.2), calls=%async_computation.3 | async-start | bytes 786432 | tf_op jit(solution)/shard_map/all_to_all | solution.py:140
  96.8 0.1 pad_add_fusion.place_ref
  96.9 0.6 shard_map.105
  97.5 12.0 %all-to-all-done.3 = bf16[4,32,1536]{2,1,0:T(8,128)(2,1)S(1)} async-done(((bf16[4,32,1536]{2,1,0:T(8,128)(2,1)}), bf16[4,32,1536]{2,1,0:T(8,128)(2,1)S(1)}, u32[]{:S(2)}, u32[]{:S(2)}) %all-to-all-start.3) | async-done | bytes 393248 | tf_op jit(solution)/shard_map/all_to_all | solution.py:140
  109.5 1.9 %collective-permute-start.2 = (bf16[128,1536]{1,0:T(8,128)(2,1)S(1)}, bf16[128,1536]{1,0:T(8,128)(2,1)S(1)}, u32[]{:S(2)}, u32[]{:S(2)}) collective-permute-start(bf16[128,1536]{1,0:T(8,128)(2,1)S(1)} %bitcast.22), channel_id=1, source_target_pairs={{0,4},{4,8},{8,12},{12,16},{16,20},{20,24},{24,28},{28,0},{32,60},... | collective-permute-start | bytes 1179656 | tf_op jit(solution)/shard_map/ppermute | solution.py:31
  111.5 0.2 fusion.33
  111.7 0.2 fusion.35
  112.0 0.2 fusion.37
  112.2 8.2 %collective-permute-done.2 = bf16[128,1536]{1,0:T(8,128)(2,1)S(1)} collective-permute-done((bf16[128,1536]{1,0:T(8,128)(2,1)S(1)}, bf16[128,1536]{1,0:T(8,128)(2,1)S(1)}, u32[]{:S(2)}, u32[]{:S(2)}) %collective-permute-start.2) | collective-permute-done | bytes 393248 | tf_op jit(solution)/shard_map/ppermute | solution.py:31
  120.4 1.9 %collective-permute-start.3 = (bf16[128,1536]{1,0:T(8,128)(2,1)S(1)}, bf16[128,1536]{1,0:T(8,128)(2,1)S(1)}, u32[]{:S(2)}, u32[]{:S(2)}) collective-permute-start(bf16[128,1536]{1,0:T(8,128)(2,1)S(1)} %collective-permute-done.2), channel_id=1, source_target_pairs={{0,4},{4,8},{8,12},{12,16},{16,20},{20,24},{24,28},{28,0},{32,60},... | collective-permute-start | bytes 1179656 | tf_op jit(solution)/shard_map/ppermute | solution.py:31
  122.3 0.2 convolution_add_fusion.18
  122.6 0.2 convolution_add_fusion.19
  122.8 0.2 convolution_add_fusion.20
  123.1 8.2 %collective-permute-done.3 = bf16[128,1536]{1,0:T(8,128)(2,1)S(1)} collective-permute-done((bf16[128,1536]{1,0:T(8,128)(2,1)S(1)}, bf16[128,1536]{1,0:T(8,128)(2,1)S(1)}, u32[]{:S(2)}, u32[]{:S(2)}) %collective-permute-start.3) | collective-permute-done | bytes 393248 | tf_op jit(solution)/shard_map/ppermute | solution.py:31
  131.3 1.9 %collective-permute-start.4 = (bf16[128,1536]{1,0:T(8,128)(2,1)S(1)}, bf16[128,1536]{1,0:T(8,128)(2,1)S(1)}, u32[]{:S(2)}, u32[]{:S(2)}) collective-permute-start(bf16[128,1536]{1,0:T(8,128)(2,1)S(1)} %collective-permute-done.3), channel_id=1, source_target_pairs={{0,4},{4,8},{8,12},{12,16},{16,20},{20,24},{24,28},{28,0},{32,60},... | collective-permute-start | bytes 1179656 | tf_op jit(solution)/shard_map/ppermute | solution.py:31
  133.2 0.2 convolution_add_fusion.15
  133.5 0.2 convolution_add_fusion.16
  133.7 0.2 convolution_add_fusion.17
  134.0 8.2 %collective-permute-done.4 = bf16[128,1536]{1,0:T(8,128)(2,1)S(1)} collective-permute-done((bf16[128,1536]{1,0:T(8,128)(2,1)S(1)}, bf16[128,1536]{1,0:T(8,128)(2,1)S(1)}, u32[]{:S(2)}, u32[]{:S(2)}) %collective-permute-start.4) | collective-permute-done | bytes 393248 | tf_op jit(solution)/shard_map/ppermute | solution.py:31
  142.2 1.9 %collective-permute-start.5 = (bf16[128,1536]{1,0:T(8,128)(2,1)S(1)}, bf16[128,1536]{1,0:T(8,128)(2,1)S(1)}, u32[]{:S(2)}, u32[]{:S(2)}) collective-permute-start(bf16[128,1536]{1,0:T(8,128)(2,1)S(1)} %collective-permute-done.4), channel_id=1, source_target_pairs={{0,4},{4,8},{8,12},{12,16},{16,20},{20,24},{24,28},{28,0},{32,60},... | collective-permute-start | bytes 1179656 | tf_op jit(solution)/shard_map/ppermute | solution.py:31
  144.1 0.3 convolution_add_fusion.12
  144.3 0.3 convolution_add_fusion.13
  144.6 0.2 convolution_add_fusion.14
  144.9 8.2 %collective-permute-done.5 = bf16[128,1536]{1,0:T(8,128)(2,1)S(1)} collective-permute-done((bf16[128,1536]{1,0:T(8,128)(2,1)S(1)}, bf16[128,1536]{1,0:T(8,128)(2,1)S(1)}, u32[]{:S(2)}, u32[]{:S(2)}) %collective-permute-start.5) | collective-permute-done | bytes 393248 | tf_op jit(solution)/shard_map/ppermute | solution.py:31
  153.0 1.9 %collective-permute-start.6 = (bf16[128,1536]{1,0:T(8,128)(2,1)S(1)}, bf16[128,1536]{1,0:T(8,128)(2,1)S(1)}, u32[]{:S(2)}, u32[]{:S(2)}) collective-permute-start(bf16[128,1536]{1,0:T(8,128)(2,1)S(1)} %collective-permute-done.5), channel_id=1, source_target_pairs={{0,4},{4,8},{8,12},{12,16},{16,20},{20,24},{24,28},{28,0},{32,60},... | collective-permute-start | bytes 1179656 | tf_op jit(solution)/shard_map/ppermute | solution.py:31
  154.9 0.3 convolution_add_fusion.9
  155.2 0.2 convolution_add_fusion.10
  155.5 0.2 convolution_add_fusion.11
  155.7 8.2 %collective-permute-done.6 = bf16[128,1536]{1,0:T(8,128)(2,1)S(1)} collective-permute-done((bf16[128,1536]{1,0:T(8,128)(2,1)S(1)}, bf16[128,1536]{1,0:T(8,128)(2,1)S(1)}, u32[]{:S(2)}, u32[]{:S(2)}) %collective-permute-start.6) | collective-permute-done | bytes 393248 | tf_op jit(solution)/shard_map/ppermute | solution.py:31
  163.9 1.9 %collective-permute-start.7 = (bf16[128,1536]{1,0:T(8,128)(2,1)S(1)}, bf16[128,1536]{1,0:T(8,128)(2,1)S(1)}, u32[]{:S(2)}, u32[]{:S(2)}) collective-permute-start(bf16[128,1536]{1,0:T(8,128)(2,1)S(1)} %collective-permute-done.6), channel_id=1, source_target_pairs={{0,4},{4,8},{8,12},{12,16},{16,20},{20,24},{24,28},{28,0},{32,60},... | collective-permute-start | bytes 1179656 | tf_op jit(solution)/shard_map/ppermute | solution.py:31
  165.8 0.2 convolution_add_fusion.6
  166.1 0.2 convolution_add_fusion.7
  166.3 0.2 convolution_add_fusion.8
  166.6 8.2 %collective-permute-done.7 = bf16[128,1536]{1,0:T(8,128)(2,1)S(1)} collective-permute-done((bf16[128,1536]{1,0:T(8,128)(2,1)S(1)}, bf16[128,1536]{1,0:T(8,128)(2,1)S(1)}, u32[]{:S(2)}, u32[]{:S(2)}) %collective-permute-start.7) | collective-permute-done | bytes 393248 | tf_op jit(solution)/shard_map/ppermute | solution.py:31
  174.8 1.9 %collective-permute-start.8 = (bf16[128,1536]{1,0:T(8,128)(2,1)S(1)}, bf16[128,1536]{1,0:T(8,128)(2,1)S(1)}, u32[]{:S(2)}, u32[]{:S(2)}) collective-permute-start(bf16[128,1536]{1,0:T(8,128)(2,1)S(1)} %collective-permute-done.7), channel_id=1, source_target_pairs={{0,4},{4,8},{8,12},{12,16},{16,20},{20,24},{24,28},{28,0},{32,60},... | collective-permute-start | bytes 1179656 | tf_op jit(solution)/shard_map/ppermute | solution.py:31
  176.7 0.2 convolution_add_fusion.3
  176.9 0.2 convolution_add_fusion.4
  177.2 0.2 convolution_add_fusion.5
  177.4 8.2 %collective-permute-done.8 = bf16[128,1536]{1,0:T(8,128)(2,1)S(1)} collective-permute-done((bf16[128,1536]{1,0:T(8,128)(2,1)S(1)}, bf16[128,1536]{1,0:T(8,128)(2,1)S(1)}, u32[]{:S(2)}, u32[]{:S(2)}) %collective-permute-start.8) | collective-permute-done | bytes 393248 | tf_op jit(solution)/shard_map/ppermute | solution.py:31
  185.6 1.0 convolution_add_fusion
  186.7 1.0 convolution_add_fusion.1
  187.7 1.0 convolution_add_fusion.2
  (6 shorter events, 0.0 us)
Async XLA Ops:
  0.6 46.3 %copy-start = (bf16[512,1024]{1,0:T(8,128)(2,1)S(1)}, bf16[512,1024]{1,0:T(8,128)(2,1)}, u32[]{:S(2)}) copy-start(bf16[512,1024]{1,0:T(8,128)(2,1)} %param.15) | copy-start | bytes 3145732
  0.6 30.9 %copy-start.1 = (bf16[1024,512]{1,0:T(8,128)(2,1)S(1)}, bf16[1024,512]{1,0:T(8,128)(2,1)}, u32[]{:S(2)}) copy-start(bf16[1024,512]{1,0:T(8,128)(2,1)} %param.13) | copy-start | bytes 3145732
  29.7 17.8 %collective-permute-start.1 = (bf16[16,8,2048]{2,1,0:T(8,128)(2,1)S(1)}, bf16[16,8,2048]{2,1,0:T(8,128)(2,1)}, u32[]{:S(2)}, u32[]{:S(2)}) collective-permute-start(bf16[16,8,2048]{2,1,0:T(8,128)(2,1)S(1)} %all_to_all.20), channel_id=1, source_target_pairs={{0,32},{32,0},{1,33},{33,1},{2,34},{34,2},{3,35},{35,3},{4,36},{36... | collective-permute-start | bytes 1572872 | tf_op jit(solution)/shard_map/ppermute | solution.py:25
  32.7 28.6 %all-to-all-start.1 = ((bf16[4,128,512]{2,1,0:T(8,128)(2,1)}), bf16[4,128,512]{2,1,0:T(8,128)(2,1)S(1)}, u32[]{:S(2)}, u32[]{:S(2)}) async-start(bf16[4,128,512]{2,1,0:T(8,128)(2,1)} %shard_map.104), calls=%async_computation.1 | async-start | bytes 1048576 | tf_op jit(solution)/shard_map/all_to_all | solution.py:159
  48.9 1.4 copy-start.2
  61.4 29.2 %all-to-all-start.2 = ((f16[8,32,1536]{2,1,0:T(8,128)(2,1)}), f16[8,32,1536]{2,1,0:T(8,128)(2,1)S(1)}, u32[]{:S(2)}, u32[]{:S(2)}) async-start(f16[8,32,1536]{2,1,0:T(8,128)(2,1)} %maximum_maximum_fusion), calls=%async_computation.2 | async-start | bytes 1572864 | tf_op jit(solution)/shard_map/all_to_all | solution.py:172
  68.9 3.8 %collective-permute-start = (bf16[4,128,512]{2,1,0:T(8,128)(2,1)S(1)}, bf16[4,128,512]{2,1,0:T(8,128)(2,1)S(1)}, u32[]{:S(2)}, u32[]{:S(2)}) collective-permute-start(bf16[4,128,512]{2,1,0:T(8,128)(2,1)S(1)} %all-to-all-done.1.own_ref), channel_id=1, source_target_pairs={{0,32},{32,0},{1,33},{33,1},{2,34},{34,2},{3,35},{35,3},{4,36},{36... | collective-permute-start | bytes 1572872 | tf_op jit(solution)/shard_map/ppermute | solution.py:25
  91.6 18.0 %all-to-all-start.3 = ((bf16[4,32,1536]{2,1,0:T(8,128)(2,1)}), bf16[4,32,1536]{2,1,0:T(8,128)(2,1)S(1)}, u32[]{:S(2)}, u32[]{:S(2)}) async-start(bf16[4,32,1536]{2,1,0:T(8,128)(2,1)} %broadcast_in_dim.2), calls=%async_computation.3 | async-start | bytes 786432 | tf_op jit(solution)/shard_map/all_to_all | solution.py:140
  109.5 10.9 %collective-permute-start.2 = (bf16[128,1536]{1,0:T(8,128)(2,1)S(1)}, bf16[128,1536]{1,0:T(8,128)(2,1)S(1)}, u32[]{:S(2)}, u32[]{:S(2)}) collective-permute-start(bf16[128,1536]{1,0:T(8,128)(2,1)S(1)} %bitcast.22), channel_id=1, source_target_pairs={{0,4},{4,8},{8,12},{12,16},{16,20},{20,24},{24,28},{28,0},{32,60},... | collective-permute-start | bytes 1179656 | tf_op jit(solution)/shard_map/ppermute | solution.py:31
  120.4 10.9 %collective-permute-start.3 = (bf16[128,1536]{1,0:T(8,128)(2,1)S(1)}, bf16[128,1536]{1,0:T(8,128)(2,1)S(1)}, u32[]{:S(2)}, u32[]{:S(2)}) collective-permute-start(bf16[128,1536]{1,0:T(8,128)(2,1)S(1)} %collective-permute-done.2), channel_id=1, source_target_pairs={{0,4},{4,8},{8,12},{12,16},{16,20},{20,24},{24,28},{28,0},{32,60},... | collective-permute-start | bytes 1179656 | tf_op jit(solution)/shard_map/ppermute | solution.py:31
  131.3 10.9 %collective-permute-start.4 = (bf16[128,1536]{1,0:T(8,128)(2,1)S(1)}, bf16[128,1536]{1,0:T(8,128)(2,1)S(1)}, u32[]{:S(2)}, u32[]{:S(2)}) collective-permute-start(bf16[128,1536]{1,0:T(8,128)(2,1)S(1)} %collective-permute-done.3), channel_id=1, source_target_pairs={{0,4},{4,8},{8,12},{12,16},{16,20},{20,24},{24,28},{28,0},{32,60},... | collective-permute-start | bytes 1179656 | tf_op jit(solution)/shard_map/ppermute | solution.py:31
  142.2 10.9 %collective-permute-start.5 = (bf16[128,1536]{1,0:T(8,128)(2,1)S(1)}, bf16[128,1536]{1,0:T(8,128)(2,1)S(1)}, u32[]{:S(2)}, u32[]{:S(2)}) collective-permute-start(bf16[128,1536]{1,0:T(8,128)(2,1)S(1)} %collective-permute-done.4), channel_id=1, source_target_pairs={{0,4},{4,8},{8,12},{12,16},{16,20},{20,24},{24,28},{28,0},{32,60},... | collective-permute-start | bytes 1179656 | tf_op jit(solution)/shard_map/ppermute | solution.py:31
  153.0 10.9 %collective-permute-start.6 = (bf16[128,1536]{1,0:T(8,128)(2,1)S(1)}, bf16[128,1536]{1,0:T(8,128)(2,1)S(1)}, u32[]{:S(2)}, u32[]{:S(2)}) collective-permute-start(bf16[128,1536]{1,0:T(8,128)(2,1)S(1)} %collective-permute-done.5), channel_id=1, source_target_pairs={{0,4},{4,8},{8,12},{12,16},{16,20},{20,24},{24,28},{28,0},{32,60},... | collective-permute-start | bytes 1179656 | tf_op jit(solution)/shard_map/ppermute | solution.py:31
  163.9 10.9 %collective-permute-start.7 = (bf16[128,1536]{1,0:T(8,128)(2,1)S(1)}, bf16[128,1536]{1,0:T(8,128)(2,1)S(1)}, u32[]{:S(2)}, u32[]{:S(2)}) collective-permute-start(bf16[128,1536]{1,0:T(8,128)(2,1)S(1)} %collective-permute-done.6), channel_id=1, source_target_pairs={{0,4},{4,8},{8,12},{12,16},{16,20},{20,24},{24,28},{28,0},{32,60},... | collective-permute-start | bytes 1179656 | tf_op jit(solution)/shard_map/ppermute | solution.py:31
  174.8 10.9 %collective-permute-start.8 = (bf16[128,1536]{1,0:T(8,128)(2,1)S(1)}, bf16[128,1536]{1,0:T(8,128)(2,1)S(1)}, u32[]{:S(2)}, u32[]{:S(2)}) collective-permute-start(bf16[128,1536]{1,0:T(8,128)(2,1)S(1)} %collective-permute-done.7), channel_id=1, source_target_pairs={{0,4},{4,8},{8,12},{12,16},{16,20},{20,24},{24,28},{28,0},{32,60},... | collective-permute-start | bytes 1179656 | tf_op jit(solution)/shard_map/ppermute | solution.py:31

commit v8 on v6

--- a/solution.py
+++ b/solution.py
@@ -84,14 +84,14 @@
     )(rows)
 
 
-def order_kernel(order, y_ref, own_ref, other_ref, *out_refs):
+def order_kernel(order, y_ref, own_ref, other_ref, out_ref):
     n_k, rows, _ = own_ref.shape
     n_y = len(order)
     part = rows // n_y
-    for r, out_ref in zip(order, out_refs):
+    at = 0
+    for r in order:
         share = lax.rem(y_ref[0] + r, n_y)
         spot = pl.ds(pl.multiple_of(share * part, part), part)
-        at = 0
         for t in range(n_k):
             for ref in (own_ref, other_ref):
                 out_ref[at : at + part, :] = ref[t, spot, :]
@@ -100,31 +100,17 @@
 
 def put_in_order(order, y, own, other):
     n_k, rows, both = own.shape
-    n_y = len(order)
-    out = jax.ShapeDtypeStruct((2 * n_k * rows // n_y, both), bf16)
-    pieces = pl.pallas_call(
+    return pl.pallas_call(
         functools.partial(order_kernel, order),
-        out_shape=(out,) * n_y,
+        out_shape=jax.ShapeDtypeStruct((2 * n_k * rows, both), bf16),
         in_specs=[in_smem(), in_vmem(), in_vmem()],
-        out_specs=(in_vmem(),) * n_y,
+        out_specs=in_vmem(),
         compiler_params=limit(8),
     )(y.reshape(1), own, other)
-    return dict(zip(order, pieces))
 
 
 def product(a, b):
     return lax.dot_general(a, b, (((0,), (0,)), ((), ())), preferred_element_type=f32)
-
-
-def add_products(sums, inputs, values):
-    quarter = inputs.shape[1] // 2
-    units = values.shape[1] // 3
-    terms = (
-        product(inputs[:, :quarter], values[:, units : 2 * units]),
-        product(inputs[:, :quarter], values[:, 2 * units :]),
-        product(values[:, :units], inputs[:, quarter:]),
-    )
-    return terms if sums is None else tuple(a + b for a, b in zip(sums, terms))
 
 
 def after(value, *others):
@@ -165,7 +151,9 @@
         whole = jnp.concatenate([gate, up, back], axis=1).astype(f16)
         pieces.append(whole.reshape(n_y, part, 3 * units))
     partial_sums = after(jnp.concatenate(pieces, axis=1), own_cuts)
-    sums = jnp.sum(lax.all_to_all(partial_sums, "y", 0, 0).astype(f32), axis=0)
+    other_cuts = shift(own_cuts, "core", 1)
+    sums = after(lax.all_to_all(partial_sums, "y", 0, 0), other_cuts)
+    sums = jnp.sum(sums.astype(f32), axis=0)
 
     gate_value = sums[:, :units] * (1.0 / SCALE_UP)
     up_value = sums[:, units : 2 * units] * (1.0 / SCALE_UP)
@@ -184,23 +172,22 @@
     for s in range(1, n_y // 2):
         order += [s, n_y - s]
     order.append(n_y // 2)
-    inputs = put_in_order(order, y, own_cuts, shift(own_cuts, "core", 1))
+    inputs = put_in_order(order, y, own_cuts, other_cuts)
     right = left = near
-    sums = None
-    waiting = [(inputs[0], near)]
+    held = {0: near}
     for s in range(1, n_y // 2):
         right = shift(right, "y", 1)
         left = shift(left, "y", -1)
-        rows_in, blocks = zip(*waiting)
-        blocks = jnp.concatenate([after(v, right) for v in blocks], axis=0)
-        sums = add_products(sums, jnp.concatenate(rows_in, axis=0), blocks)
-        waiting = [(inputs[n_y - s], right), (inputs[s], left)]
+        held[n_y - s] = right
+        held[s] = left
     middle = near.shape[0] // 2
     top = shift(right[:middle], "y", 1)
     low = shift(left[middle:], "y", -1)
-    for rows_in, block_in in waiting:
-        sums = add_products(sums, rows_in, block_in)
-    return add_products(sums, inputs[n_y // 2], jnp.concatenate([top, low], axis=0))
+    every = jnp.concatenate([held[r] for r in order[:-1]] + [top, low], axis=0)
+    down_grad = product(every[:, :units], inputs[:, quarter:])
+    gate_grad = product(inputs[:, :quarter], every[:, units : 2 * units])
+    up_grad = product(inputs[:, :quarter], every[:, 2 * units :])
+    return (gate_grad, up_grad, down_grad)
 
 
 def solution(mesh):

time: 160 us -> 162 us (1.012)
  waiting for transfers between devices: 32.7 us -> 51.4 us
  blocking collectives: 56.2 us -> 45 us
  local copies, waits for them, and re-layouts: 2.9 us -> 0.3 us
  matrix products: 11.9 us -> 10.1 us
    all_to_all x1, blocking collectives: 29 us -> 17.8 us  [copies_to(): return lax.all_to_all(spread, axis, 0, 0)]
    ppermute x10, waiting for transfers between devices: 13.7 us -> 24.8 us  [shift(): return lax.ppermute(value, axis, [(i, (i + step) % n) for i in range(n)])]
    all_to_all x1, waiting for transfers between devices: 9.01 us -> 17.9 us  [body(): sums = after(lax.all_to_all(partial_sums, 'y', 0, 0), other_cuts)]
    dot_general x18 -> x3, matrix products: 6.86 us -> 3.77 us  [product(): lax.dot_general(a, b, (((0,), (0,)), ((), ())), preferred_element_type=f32)]
    ppermute x10, starting transfers between devices: 32 us -> 29.3 us  [shift(): return lax.ppermute(value, axis, [(i, (i + step) % n) for i in range(n)])]
    all_to_all x1, starting transfers between devices: 5.27 us -> 7.56 us  [body(): sums = after(lax.all_to_all(partial_sums, 'y', 0, 0), other_cuts)]
    unnamed x11 -> x14, local copies, waits for them, and re-layouts: 2.01 us -> 0.23 us
  transfers between devices with their start and end apart: 12 -> 12, of which waited for: 6 -> 8; matrix products, arithmetic and copies ran while one was open for 6% -> 5% of each run, Pallas kernels for 1% -> 1%
where the time goes in v8:
time: 162 us; the launch traced here: 161 us
  waiting for transfers between devices  51.4 us (32%)
  starting transfers between devices  49.6 us (31%)
  blocking collectives  45 us (28%)
  matrix products  10.1 us (6%)
  Pallas kernels  2.65 us (2%)
    ppermute x10, starting transfers between devices, shift(): return lax.ppermute(value, axis, [(i, (i + step) % n) for i in range(n)])  29.3 us
    all_to_all x1, blocking collectives, body(): mine = lax.all_to_all(spread, ('zlo', 'x'), 0, 0)  27.2 us
    ppermute x10, waiting for transfers between devices, shift(): return lax.ppermute(value, axis, [(i, (i + step) % n) for i in range(n)])  24.8 us
    all_to_all x1, waiting for transfers between devices, body(): sums = after(lax.all_to_all(partial_sums, 'y', 0, 0), other_cuts)  17.9 us
    all_to_all x1, blocking collectives, copies_to(): return lax.all_to_all(spread, axis, 0, 0)  17.8 us
    all_to_all x1, starting transfers between devices, body(): own_cuts = lax.all_to_all(cut_quarters(n_k, mine), 'zhi', 0, 0)  12.7 us
    all_to_all x1, waiting for transfers between devices, body(): own_cuts = lax.all_to_all(cut_quarters(n_k, mine), 'zhi', 0, 0)  8.75 us
    all_to_all x1, starting transfers between devices, body(): sums = after(lax.all_to_all(partial_sums, 'y', 0, 0), other_cuts)  7.56 us
  transfers between devices with their start and end apart: 12, of which 8 were waited for; matrix products, arithmetic and copies ran while one was open for 5% of the time, Pallas kernels for 1%

profile of v8, /device:TPU:14, one launch (start us, length us, event | category | flops | bytes accessed | tf_op | source)
XLA Modules:
  0.0 161.3 jit_solution(18005125118482045202)
XLA Ops:
  0.6 0.0 copy-start
  0.6 0.0 copy-start.1
  0.7 1.7 %shard_map.103 = bf16[16,8,2048]{2,1,0:T(8,128)(2,1)} custom-call(s32[1]{0:T(128)} %bitcast.1.block_ref, s32[8,8]{1,0:T(8,128)} %rewards_ref.1, s32[8]{0:T(128)} %selected_ref.1, s32[8]{0:T(128)} %pad_ref.1, bf16[8,1024]{1,0:T(8,128)(2,1)} %tokens_ref.1, bf16[8,1024]{1,0:T(8,128)(2,1)} %cotangent_ref.1), custom_call_target="tpu_custom_call" | custom-call | tf_op jit(solution)/shard_map/pallas_call | solution.py:60
  2.4 27.2 %all_to_all.20 = bf16[16,8,2048]{2,1,0:T(8,128)(2,1)S(1)} all-to-all(bf16[16,8,2048]{2,1,0:T(8,128)(2,1)} %shard_map.103), channel_id=1, replica_groups=mesh['zlo'=2,'x'=8,'core'=2,'y'=8,'zhi'=4] {'zlo','x'}, dimensions={0} | all-to-all | bytes 1048576 | tf_op jit(solution)/shard_map/all_to_all | solution.py:139
  29.7 1.9 %collective-permute-start.1 = (bf16[16,8,2048]{2,1,0:T(8,128)(2,1)S(1)}, bf16[16,8,2048]{2,1,0:T(8,128)(2,1)}, u32[]{:S(2)}, u32[]{:S(2)}) collective-permute-start(bf16[16,8,2048]{2,1,0:T(8,128)(2,1)S(1)} %all_to_all.20), channel_id=1, source_target_pairs={{0,32},{32,0},{1,33},{33,1},{2,34},{34,2},{3,35},{35,3},{4,36},{36... | collective-permute-start | bytes 1572872 | tf_op jit(solution)/shard_map/ppermute | solution.py:25
  31.6 0.0 copy-done
  31.6 0.3 fusion
  31.9 0.8 shard_map.104
  32.7 12.7 %all-to-all-start.1 = ((bf16[4,128,512]{2,1,0:T(8,128)(2,1)}), bf16[4,128,512]{2,1,0:T(8,128)(2,1)S(1)}, u32[]{:S(2)}, u32[]{:S(2)}) async-start(bf16[4,128,512]{2,1,0:T(8,128)(2,1)} %shard_map.104), calls=%async_computation.1 | async-start | bytes 1048576 | tf_op jit(solution)/shard_map/all_to_all | solution.py:142
  45.4 0.0 copy-done.1
  45.4 0.0 copy-start.2
  45.4 0.3 fusion.1
  45.7 1.7 %fusion.2 = f16[128,512]{1,0:T(8,128)(2,1)S(1)} fusion(bf16[512,1024]{1,0:T(8,128)(2,1)} %param.15, bf16[128,2048]{1,0:T(8,128)(2,1)S(1)} %bitcast.20), kind=kOutput, calls=%fused_computation.9 | convolution fusion | flops 134348800 | bytes 1441792 | tf_op jit(solution)/shard_map/dot_general | solution.py:148
  47.4 0.0 collective-permute-done.1
  47.5 1.3 fusion.3
  48.7 1.3 fusion.4
  50.0 0.0 copy-done.2
  50.0 1.4 fusion.5
  51.4 1.2 maximum_maximum_fusion
  52.6 8.7 %all-to-all-done.1.own_ref = bf16[4,128,512]{2,1,0:T(8,128)(2,1)S(1)} async-done(((bf16[4,128,512]{2,1,0:T(8,128)(2,1)}), bf16[4,128,512]{2,1,0:T(8,128)(2,1)S(1)}, u32[]{:S(2)}, u32[]{:S(2)}) %all-to-all-start.1) | async-done | bytes 524320 | tf_op jit(solution)/shard_map/all_to_all | solution.py:142
  61.4 7.6 %all-to-all-start.2 = ((f16[8,32,1536]{2,1,0:T(8,128)(2,1)}), f16[8,32,1536]{2,1,0:T(8,128)(2,1)S(1)}, u32[]{:S(2)}, u32[]{:S(2)}) async-start(f16[8,32,1536]{2,1,0:T(8,128)(2,1)} %maximum_maximum_fusion), calls=%async_computation.2 | async-start | bytes 1572864 | tf_op jit(solution)/shard_map/all_to_all | solution.py:155
  68.9 1.9 %collective-permute-start = (bf16[4,128,512]{2,1,0:T(8,128)(2,1)S(1)}, bf16[4,128,512]{2,1,0:T(8,128)(2,1)S(1)}, u32[]{:S(2)}, u32[]{:S(2)}) collective-permute-start(bf16[4,128,512]{2,1,0:T(8,128)(2,1)S(1)} %all-to-all-done.1.own_ref), channel_id=1, source_target_pairs={{0,32},{32,0},{1,33},{33,1},{2,34},{34,2},{3,35},{35,3},{4,36},{36... | collective-permute-start | bytes 1572872 | tf_op jit(solution)/shard_map/ppermute | solution.py:25
  70.8 1.9 %collective-permute-done.other_ref = bf16[4,128,512]{2,1,0:T(8,128)(2,1)S(1)} collective-permute-done((bf16[4,128,512]{2,1,0:T(8,128)(2,1)S(1)}, bf16[4,128,512]{2,1,0:T(8,128)(2,1)S(1)}, u32[]{:S(2)}, u32[]{:S(2)}) %collective-permute-start) | collective-permute-done | bytes 524320 | tf_op jit(solution)/shard_map/ppermute | solution.py:25
  72.7 17.9 %all-to-all-done.2 = f16[8,32,1536]{2,1,0:T(8,128)(2,1)S(1)} async-done(((f16[8,32,1536]{2,1,0:T(8,128)(2,1)}), f16[8,32,1536]{2,1,0:T(8,128)(2,1)S(1)}, u32[]{:S(2)}, u32[]{:S(2)}) %all-to-all-start.2) | async-done | bytes 786464 | tf_op jit(solution)/shard_map/all_to_all | solution.py:155
  90.6 0.1 convert_reduce_fusion
  90.7 0.1 multiply_convert_fusion.2
  90.8 17.8 %all_to_all.21 = bf16[4,32,1536]{2,1,0:T(8,128)(2,1)S(1)} all-to-all(bf16[4,32,1536]{2,1,0:T(8,128)(2,1)S(1)} %broadcast_in_dim.2), channel_id=1, replica_groups=mesh['zlo'=2,'x'=8,'core'=2,'y'=8,'zhi'=4] {'zhi'}, dimensions={0} | all-to-all | bytes 786432 | tf_op jit(solution)/shard_map/all_to_all | solution.py:122
  108.6 1.9 %collective-permute-start.2 = (bf16[128,1536]{1,0:T(8,128)(2,1)S(1)}, bf16[128,1536]{1,0:T(8,128)(2,1)S(1)}, u32[]{:S(2)}, u32[]{:S(2)}) collective-permute-start(bf16[128,1536]{1,0:T(8,128)(2,1)S(1)} %bitcast.21), channel_id=1, source_target_pairs={{0,28},{4,0},{8,4},{12,8},{16,12},{20,16},{24,20},{28,24},{1,29},{... | collective-permute-start | bytes 1179656 | tf_op jit(solution)/shard_map/ppermute | solution.py:25
  110.5 3.9 %collective-permute-start.3 = (bf16[128,1536]{1,0:T(8,128)(2,1)S(1)}, bf16[128,1536]{1,0:T(8,128)(2,1)S(1)}, u32[]{:S(2)}, u32[]{:S(2)}) collective-permute-start(bf16[128,1536]{1,0:T(8,128)(2,1)S(1)} %bitcast.22), channel_id=1, source_target_pairs={{0,4},{4,8},{8,12},{12,16},{16,20},{20,24},{24,28},{28,0},{1,5},{5... | collective-permute-start | bytes 1179656 | tf_op jit(solution)/shard_map/ppermute | solution.py:25
  114.5 0.1 shard_map.105
  114.6 5.8 %collective-permute-done.2 = bf16[128,1536]{1,0:T(8,128)(2,1)S(1)} collective-permute-done((bf16[128,1536]{1,0:T(8,128)(2,1)S(1)}, bf16[128,1536]{1,0:T(8,128)(2,1)S(1)}, u32[]{:S(2)}, u32[]{:S(2)}) %collective-permute-start.2) | collective-permute-done | bytes 393248 | tf_op jit(solution)/shard_map/ppermute | solution.py:25
  120.4 3.4 %collective-permute-start.4 = (bf16[128,1536]{1,0:T(8,128)(2,1)S(1)}, bf16[128,1536]{1,0:T(8,128)(2,1)S(1)}, u32[]{:S(2)}, u32[]{:S(2)}) collective-permute-start(bf16[128,1536]{1,0:T(8,128)(2,1)S(1)} %collective-permute-done.2), channel_id=1, source_target_pairs={{0,28},{4,0},{8,4},{12,8},{16,12},{20,16},{24,20},{28,24},{1,29},{... | collective-permute-start | bytes 1179656 | tf_op jit(solution)/shard_map/ppermute | solution.py:25
  123.8 0.0 collective-permute-done.3
  123.8 2.4 %collective-permute-start.5 = (bf16[128,1536]{1,0:T(8,128)(2,1)S(1)}, bf16[128,1536]{1,0:T(8,128)(2,1)S(1)}, u32[]{:S(2)}, u32[]{:S(2)}) collective-permute-start(bf16[128,1536]{1,0:T(8,128)(2,1)S(1)} %collective-permute-done.3), channel_id=1, source_target_pairs={{0,4},{4,8},{8,12},{12,16},{16,20},{20,24},{24,28},{28,0},{1,5},{5... | collective-permute-start | bytes 1179656 | tf_op jit(solution)/shard_map/ppermute | solution.py:25
  126.3 4.9 %collective-permute-done.4 = bf16[128,1536]{1,0:T(8,128)(2,1)S(1)} collective-permute-done((bf16[128,1536]{1,0:T(8,128)(2,1)S(1)}, bf16[128,1536]{1,0:T(8,128)(2,1)S(1)}, u32[]{:S(2)}, u32[]{:S(2)}) %collective-permute-start.4) | collective-permute-done | bytes 393248 | tf_op jit(solution)/shard_map/ppermute | solution.py:25
  131.2 4.9 %collective-permute-start.6 = (bf16[128,1536]{1,0:T(8,128)(2,1)S(1)}, bf16[128,1536]{1,0:T(8,128)(2,1)S(1)}, u32[]{:S(2)}, u32[]{:S(2)}) collective-permute-start(bf16[128,1536]{1,0:T(8,128)(2,1)S(1)} %collective-permute-done.4), channel_id=1, source_target_pairs={{0,28},{4,0},{8,4},{12,8},{16,12},{20,16},{24,20},{28,24},{1,29},{... | collective-permute-start | bytes 1179656 | tf_op jit(solution)/shard_map/ppermute | solution.py:25
  136.1 0.0 collective-permute-done.5
  136.1 1.9 %collective-permute-start.7 = (bf16[128,1536]{1,0:T(8,128)(2,1)S(1)}, bf16[128,1536]{1,0:T(8,128)(2,1)S(1)}, u32[]{:S(2)}, u32[]{:S(2)}) collective-permute-start(bf16[128,1536]{1,0:T(8,128)(2,1)S(1)} %collective-permute-done.5), channel_id=1, source_target_pairs={{0,4},{4,8},{8,12},{12,16},{16,20},{20,24},{24,28},{28,0},{1,5},{5... | collective-permute-start | bytes 1179656 | tf_op jit(solution)/shard_map/ppermute | solution.py:25
  138.1 9.1 %collective-permute-done.7 = bf16[128,1536]{1,0:T(8,128)(2,1)S(1)} collective-permute-done((bf16[128,1536]{1,0:T(8,128)(2,1)S(1)}, bf16[128,1536]{1,0:T(8,128)(2,1)S(1)}, u32[]{:S(2)}, u32[]{:S(2)}) %collective-permute-start.7) | collective-permute-done | bytes 393248 | tf_op jit(solution)/shard_map/ppermute | solution.py:25
  147.3 1.9 %collective-permute-start.8 = (bf16[64,1536]{1,0:T(8,128)(2,1)S(1)}, bf16[64,1536]{1,0:T(8,128)(2,1)S(1)}, u32[]{:S(2)}, u32[]{:S(2)}) collective-permute-start(bf16[64,1536]{1,0:T(8,128)(2,1)S(1)} %slice.67), channel_id=1, source_target_pairs={{0,4},{4,8},{8,12},{12,16},{16,20},{20,24},{24,28},{28,0},{1,5},{5... | collective-permute-start | bytes 589832 | tf_op jit(solution)/shard_map/ppermute | solution.py:25
  149.2 0.0 collective-permute-done.6
  149.2 5.1 %collective-permute-start.9 = (bf16[64,1536]{1,0:T(8,128)(2,1)S(1)}, bf16[64,1536]{1,0:T(8,128)(2,1)S(1)}, u32[]{:S(2)}, u32[]{:S(2)}) collective-permute-start(bf16[64,1536]{1,0:T(8,128)(2,1)S(1)} %slice.68), channel_id=1, source_target_pairs={{0,28},{4,0},{8,4},{12,8},{16,12},{20,16},{24,20},{28,24},{1,29},{... | collective-permute-start | bytes 589832 | tf_op jit(solution)/shard_map/ppermute | solution.py:25
  154.4 1.6 collective-permute-done.8
  156.1 1.5 collective-permute-done.9
  157.6 1.3 fusion.6
  158.8 1.2 fusion.8
  160.1 1.2 fusion.10
  (13 shorter events, 0.3 us)
Async XLA Ops:
  0.6 30.9 %copy-start = (bf16[1024,512]{1,0:T(8,128)(2,1)S(1)}, bf16[1024,512]{1,0:T(8,128)(2,1)}, u32[]{:S(2)}) copy-start(bf16[1024,512]{1,0:T(8,128)(2,1)} %param.13) | copy-start | bytes 3145732
  0.6 44.8 %copy-start.1 = (bf16[1024,512]{1,0:T(8,128)(2,1)S(1)}, bf16[1024,512]{1,0:T(8,128)(2,1)}, u32[]{:S(2)}) copy-start(bf16[1024,512]{1,0:T(8,128)(2,1)} %param.14) | copy-start | bytes 3145732
  29.7 17.8 %collective-permute-start.1 = (bf16[16,8,2048]{2,1,0:T(8,128)(2,1)S(1)}, bf16[16,8,2048]{2,1,0:T(8,128)(2,1)}, u32[]{:S(2)}, u32[]{:S(2)}) collective-permute-start(bf16[16,8,2048]{2,1,0:T(8,128)(2,1)S(1)} %all_to_all.20), channel_id=1, source_target_pairs={{0,32},{32,0},{1,33},{33,1},{2,34},{34,2},{3,35},{35,3},{4,36},{36... | collective-permute-start | bytes 1572872 | tf_op jit(solution)/shard_map/ppermute | solution.py:25
  32.7 28.6 %all-to-all-start.1 = ((bf16[4,128,512]{2,1,0:T(8,128)(2,1)}), bf16[4,128,512]{2,1,0:T(8,128)(2,1)S(1)}, u32[]{:S(2)}, u32[]{:S(2)}) async-start(bf16[4,128,512]{2,1,0:T(8,128)(2,1)} %shard_map.104), calls=%async_computation.1 | async-start | bytes 1048576 | tf_op jit(solution)/shard_map/all_to_all | solution.py:142
  45.4 4.6 %copy-start.2 = (bf16[512,1024]{1,0:T(8,128)(2,1)S(1)}, bf16[512,1024]{1,0:T(8,128)(2,1)}, u32[]{:S(2)}) copy-start(bf16[512,1024]{1,0:T(8,128)(2,1)} %param.15) | copy-start | bytes 3145732
  61.4 29.3 %all-to-all-start.2 = ((f16[8,32,1536]{2,1,0:T(8,128)(2,1)}), f16[8,32,1536]{2,1,0:T(8,128)(2,1)S(1)}, u32[]{:S(2)}, u32[]{:S(2)}) async-start(f16[8,32,1536]{2,1,0:T(8,128)(2,1)} %maximum_maximum_fusion), calls=%async_computation.2 | async-start | bytes 1572864 | tf_op jit(solution)/shard_map/all_to_all | solution.py:155
  68.9 3.8 %collective-permute-start = (bf16[4,128,512]{2,1,0:T(8,128)(2,1)S(1)}, bf16[4,128,512]{2,1,0:T(8,128)(2,1)S(1)}, u32[]{:S(2)}, u32[]{:S(2)}) collective-permute-start(bf16[4,128,512]{2,1,0:T(8,128)(2,1)S(1)} %all-to-all-done.1.own_ref), channel_id=1, source_target_pairs={{0,32},{32,0},{1,33},{33,1},{2,34},{34,2},{3,35},{35,3},{4,36},{36... | collective-permute-start | bytes 1572872 | tf_op jit(solution)/shard_map/ppermute | solution.py:25
  108.6 11.8 %collective-permute-start.2 = (bf16[128,1536]{1,0:T(8,128)(2,1)S(1)}, bf16[128,1536]{1,0:T(8,128)(2,1)S(1)}, u32[]{:S(2)}, u32[]{:S(2)}) collective-permute-start(bf16[128,1536]{1,0:T(8,128)(2,1)S(1)} %bitcast.21), channel_id=1, source_target_pairs={{0,28},{4,0},{8,4},{12,8},{16,12},{20,16},{24,20},{28,24},{1,29},{... | collective-permute-start | bytes 1179656 | tf_op jit(solution)/shard_map/ppermute | solution.py:25
  110.5 13.2 %collective-permute-start.3 = (bf16[128,1536]{1,0:T(8,128)(2,1)S(1)}, bf16[128,1536]{1,0:T(8,128)(2,1)S(1)}, u32[]{:S(2)}, u32[]{:S(2)}) collective-permute-start(bf16[128,1536]{1,0:T(8,128)(2,1)S(1)} %bitcast.22), channel_id=1, source_target_pairs={{0,4},{4,8},{8,12},{12,16},{16,20},{20,24},{24,28},{28,0},{1,5},{5... | collective-permute-start | bytes 1179656 | tf_op jit(solution)/shard_map/ppermute | solution.py:25
  120.4 10.8 %collective-permute-start.4 = (bf16[128,1536]{1,0:T(8,128)(2,1)S(1)}, bf16[128,1536]{1,0:T(8,128)(2,1)S(1)}, u32[]{:S(2)}, u32[]{:S(2)}) collective-permute-start(bf16[128,1536]{1,0:T(8,128)(2,1)S(1)} %collective-permute-done.2), channel_id=1, source_target_pairs={{0,28},{4,0},{8,4},{12,8},{16,12},{20,16},{24,20},{28,24},{1,29},{... | collective-permute-start | bytes 1179656 | tf_op jit(solution)/shard_map/ppermute | solution.py:25
  123.8 12.3 %collective-permute-start.5 = (bf16[128,1536]{1,0:T(8,128)(2,1)S(1)}, bf16[128,1536]{1,0:T(8,128)(2,1)S(1)}, u32[]{:S(2)}, u32[]{:S(2)}) collective-permute-start(bf16[128,1536]{1,0:T(8,128)(2,1)S(1)} %collective-permute-done.3), channel_id=1, source_target_pairs={{0,4},{4,8},{8,12},{12,16},{16,20},{20,24},{24,28},{28,0},{1,5},{5... | collective-permute-start | bytes 1179656 | tf_op jit(solution)/shard_map/ppermute | solution.py:25
  131.2 18.0 %collective-permute-start.6 = (bf16[128,1536]{1,0:T(8,128)(2,1)S(1)}, bf16[128,1536]{1,0:T(8,128)(2,1)S(1)}, u32[]{:S(2)}, u32[]{:S(2)}) collective-permute-start(bf16[128,1536]{1,0:T(8,128)(2,1)S(1)} %collective-permute-done.4), channel_id=1, source_target_pairs={{0,28},{4,0},{8,4},{12,8},{16,12},{20,16},{24,20},{28,24},{1,29},{... | collective-permute-start | bytes 1179656 | tf_op jit(solution)/shard_map/ppermute | solution.py:25
  136.1 11.1 %collective-permute-start.7 = (bf16[128,1536]{1,0:T(8,128)(2,1)S(1)}, bf16[128,1536]{1,0:T(8,128)(2,1)S(1)}, u32[]{:S(2)}, u32[]{:S(2)}) collective-permute-start(bf16[128,1536]{1,0:T(8,128)(2,1)S(1)} %collective-permute-done.5), channel_id=1, source_target_pairs={{0,4},{4,8},{8,12},{12,16},{16,20},{20,24},{24,28},{28,0},{1,5},{5... | collective-permute-start | bytes 1179656 | tf_op jit(solution)/shard_map/ppermute | solution.py:25
  147.3 8.8 %collective-permute-start.8 = (bf16[64,1536]{1,0:T(8,128)(2,1)S(1)}, bf16[64,1536]{1,0:T(8,128)(2,1)S(1)}, u32[]{:S(2)}, u32[]{:S(2)}) collective-permute-start(bf16[64,1536]{1,0:T(8,128)(2,1)S(1)} %slice.67), channel_id=1, source_target_pairs={{0,4},{4,8},{8,12},{12,16},{16,20},{20,24},{24,28},{28,0},{1,5},{5... | collective-permute-start | bytes 589832 | tf_op jit(solution)/shard_map/ppermute | solution.py:25
  149.2 8.3 %collective-permute-start.9 = (bf16[64,1536]{1,0:T(8,128)(2,1)S(1)}, bf16[64,1536]{1,0:T(8,128)(2,1)S(1)}, u32[]{:S(2)}, u32[]{:S(2)}) collective-permute-start(bf16[64,1536]{1,0:T(8,128)(2,1)S(1)} %slice.68), channel_id=1, source_target_pairs={{0,28},{4,0},{8,4},{12,8},{16,12},{20,16},{24,20},{28,24},{1,29},{... | collective-permute-start | bytes 589832 | tf_op jit(solution)/shard_map/ppermute | solution.py:25

commit v9 on v8

--- a/solution.py
+++ b/solution.py
@@ -65,40 +65,44 @@
     )(block.reshape(1), rewards, selected, pad_mask, tokens, cotangent)
 
 
-def cut_kernel(rows_ref, out_ref):
-    n_k = out_ref.shape[0]
+def cut_kernel(k_ref, rows_ref, *out_refs):
+    n_k = len(out_refs)
     width = rows_ref.shape[1] // 2
     quarter = width // n_k
-    for t in range(n_k):
-        out_ref[t, :, :quarter] = rows_ref[:, t * quarter : (t + 1) * quarter]
-        out_ref[t, :, quarter:] = rows_ref[:, width + t * quarter : width + (t + 1) * quarter]
-
-
-def cut_quarters(n_k, rows):
+    for t, out_ref in enumerate(out_refs):
+        owner = lax.rem(k_ref[0] + n_k - t, n_k)
+        at = pl.multiple_of(owner * quarter, quarter)
+        out_ref[:, :quarter] = rows_ref[:, pl.ds(at, quarter)]
+        out_ref[:, quarter:] = rows_ref[:, pl.ds(width + at, quarter)]
+
+
+def cut_quarters(n_k, k, rows):
+    out = jax.ShapeDtypeStruct((rows.shape[0], rows.shape[1] // n_k), bf16)
     return pl.pallas_call(
         cut_kernel,
-        out_shape=jax.ShapeDtypeStruct((n_k, rows.shape[0], rows.shape[1] // n_k), bf16),
-        in_specs=[in_vmem()],
-        out_specs=in_vmem(),
+        out_shape=(out,) * n_k,
+        in_specs=[in_smem(), in_vmem()],
+        out_specs=(in_vmem(),) * n_k,
         compiler_params=limit(4),
-    )(rows)
-
-
-def order_kernel(order, y_ref, own_ref, other_ref, out_ref):
+    )(k.reshape(1), rows)
+
+
+def order_kernel(order, place_ref, own_ref, other_ref, out_ref):
     n_k, rows, _ = own_ref.shape
     n_y = len(order)
     part = rows // n_y
     at = 0
     for r in order:
-        share = lax.rem(y_ref[0] + r, n_y)
+        share = lax.rem(place_ref[0] + r, n_y)
         spot = pl.ds(pl.multiple_of(share * part, part), part)
         for t in range(n_k):
+            source = lax.rem(t + n_k - place_ref[1], n_k)
             for ref in (own_ref, other_ref):
-                out_ref[at : at + part, :] = ref[t, spot, :]
+                out_ref[at : at + part, :] = ref[source, spot, :]
                 at += part
 
 
-def put_in_order(order, y, own, other):
+def put_in_order(order, place, own, other):
     n_k, rows, both = own.shape
     return pl.pallas_call(
         functools.partial(order_kernel, order),
@@ -106,7 +110,7 @@
         in_specs=[in_smem(), in_vmem(), in_vmem()],
         out_specs=in_vmem(),
         compiler_params=limit(8),
-    )(y.reshape(1), own, other)
+    )(place, own, other)
 
 
 def product(a, b):
@@ -128,7 +132,8 @@
     y = lax.axis_index("y")
     rows, width = tokens.shape
     units = gate_weight.shape[1]
-    block = lax.axis_index(ROW) * n_k + lax.axis_index("zhi")
+    k = lax.axis_index("zhi")
+    block = lax.axis_index(ROW) * n_k + k
     copies = lax.axis_size(("zlo", "x"))
     half = copies * rows
     part = half // n_y
@@ -139,7 +144,6 @@
     mine = lax.all_to_all(spread, ("zlo", "x"), 0, 0)
     other = shift(mine, "core", 1).reshape(half, 2 * width)
     mine = mine.reshape(half, 2 * width)
-    own_cuts = lax.all_to_all(cut_quarters(n_k, mine), "zhi", 0, 0)
 
     pieces = []
     for rows_in in (mine, other):
@@ -150,9 +154,13 @@
         )
         whole = jnp.concatenate([gate, up, back], axis=1).astype(f16)
         pieces.append(whole.reshape(n_y, part, 3 * units))
-    partial_sums = after(jnp.concatenate(pieces, axis=1), own_cuts)
+    partial_sums = jnp.concatenate(pieces, axis=1)
+    cuts = cut_quarters(n_k, k, mine)
+    cuts = lax.optimization_barrier(tuple(cuts) + (partial_sums,))[:n_k]
+    own_cuts = [cuts[0]] + [shift(cuts[t], "zhi", -t) for t in range(1, n_k)]
+    sums = after(lax.all_to_all(partial_sums, "y", 0, 0), *own_cuts)
+    own_cuts = jnp.stack(own_cuts, axis=0)
     other_cuts = shift(own_cuts, "core", 1)
-    sums = after(lax.all_to_all(partial_sums, "y", 0, 0), other_cuts)
     sums = jnp.sum(sums.astype(f32), axis=0)
 
     gate_value = sums[:, :units] * (1.0 / SCALE_UP)
@@ -166,13 +174,13 @@
     ).astype(bf16)
     up_back = (back_value * active).astype(bf16)
     values = jnp.concatenate([hidden, gate_back, up_back], axis=1)
-    near = copies_to(values, "zhi").reshape(n_k * share, 3 * units)
+    near = after(copies_to(values, "zhi"), other_cuts).reshape(n_k * share, 3 * units)
 
     order = [0]
     for s in range(1, n_y // 2):
         order += [s, n_y - s]
     order.append(n_y // 2)
-    inputs = put_in_order(order, y, own_cuts, other_cuts)
+    inputs = put_in_order(order, jnp.stack([y, k]), own_cuts, other_cuts)
     right = left = near
     held = {0: near}
     for s in range(1, n_y // 2):

time: 162 us -> 149 us (0.920); the launches traced: 161 us -> 146 us
  blocking collectives: 45 us -> 27.2 us
  starting transfers between devices: 49.6 us -> 64.6 us
  waiting for transfers between devices: 51.4 us -> 41.2 us
  matrix products: 10.1 us -> 7.22 us
    ppermute x10 -> x13, starting transfers between devices: 29.3 us -> 51 us  [shift(): return lax.ppermute(value, axis, [(i, (i + step) % n) for i in range(n)])]
    all_to_all x1 -> x0, blocking collectives: 17.8 us -> none  [copies_to(): return lax.all_to_all(spread, axis, 0, 0)]
    all_to_all x2, waiting for transfers between devices: 26.7 us -> 9.18 us  [the longest x1 9.18 us: copies_to(): return lax.all_to_all(spread, axis, 0, 0)]
    ppermute x10 -> x13, waiting for transfers between devices: 24.8 us -> 32 us  [shift(): return lax.ppermute(value, axis, [(i, (i + step) % n) for i in range(n)])]
    all_to_all x2, starting transfers between devices: 20.2 us -> 13.6 us  [the longest x1 8.26 us: copies_to(): return lax.all_to_all(spread, axis, 0, 0)]
    dot_general x2, matrix products: 3.15 us -> 0.98 us  [body(): lax.dot_general(rows_in[:, width:], down_weight, (((1,), (1,)), ((), ()))...]
  transfers between devices with their start and end apart: 12 -> 15, of which waited for: 8 -> 11; matrix products, arithmetic and copies ran while one was open for 5% -> 2% of each run, Pallas kernels for 1% -> 0%
where the time goes in v9:
time: 149 us; the launch traced here: 146 us
  starting transfers between devices  64.6 us (43%)
  waiting for transfers between devices  41.2 us (28%)
  blocking collectives  27.2 us (18%)
  matrix products  7.22 us (5%)
  Pallas kernels  2.43 us (2%)
    ppermute x13, starting transfers between devices, shift(): return lax.ppermute(value, axis, [(i, (i + step) % n) for i in range(n)])  51 us
    ppermute x13, waiting for transfers between devices, shift(): return lax.ppermute(value, axis, [(i, (i + step) % n) for i in range(n)])  32 us
    all_to_all x1, blocking collectives, body(): mine = lax.all_to_all(spread, ('zlo', 'x'), 0, 0)  27.2 us
    all_to_all x1, waiting for transfers between devices, copies_to(): return lax.all_to_all(spread, axis, 0, 0)  9.18 us
    all_to_all x1, starting transfers between devices, copies_to(): return lax.all_to_all(spread, axis, 0, 0)  8.26 us
    all_to_all x1, starting transfers between devices, body(): sums = after(lax.all_to_all(partial_sums, 'y', 0, 0), *own_cuts)  5.36 us
    dot_general x3, matrix products, product(): lax.dot_general(a, b, (((0,), (0,)), ((), ())), preferred_element_type=f32)  3.77 us
  transfers between devices with their start and end apart: 15, of which 11 were waited for; matrix products, arithmetic and copies ran while one was open for 2% of the time, Pallas kernels for 0%

profile of v9, /device:TPU:14, one launch (start us, length us, event | category | flops | bytes accessed | tf_op | source)
XLA Modules:
  0.0 146.1 jit_solution(10639130509019707265)
XLA Ops:
  0.6 0.0 copy-start
  0.6 0.0 copy-start.2
  0.7 1.7 %shard_map.103 = bf16[16,8,2048]{2,1,0:T(8,128)(2,1)} custom-call(s32[1]{0:T(128)} %bitcast.2.block_ref, s32[8,8]{1,0:T(8,128)} %rewards_ref.1, s32[8]{0:T(128)} %selected_ref.1, s32[8]{0:T(128)} %pad_ref.1, bf16[8,1024]{1,0:T(8,128)(2,1)} %tokens_ref.1, bf16[8,1024]{1,0:T(8,128)(2,1)} %cotangent_ref.1), custom_call_target="tpu_custom_call" | custom-call | tf_op jit(solution)/shard_map/pallas_call | solution.py:60
  2.4 27.2 %all_to_all.15 = bf16[16,8,2048]{2,1,0:T(8,128)(2,1)S(1)} all-to-all(bf16[16,8,2048]{2,1,0:T(8,128)(2,1)} %shard_map.103), channel_id=1, replica_groups=mesh['zlo'=2,'x'=8,'core'=2,'y'=8,'zhi'=4] {'zlo','x'}, dimensions={0} | all-to-all | bytes 1048576 | tf_op jit(solution)/shard_map/all_to_all | solution.py:144
  29.7 0.0 copy-start.1
  29.7 2.0 %collective-permute-start = (bf16[16,8,2048]{2,1,0:T(8,128)(2,1)S(1)}, bf16[16,8,2048]{2,1,0:T(8,128)(2,1)S(1)}, u32[]{:S(2)}, u32[]{:S(2)}) collective-permute-start(bf16[16,8,2048]{2,1,0:T(8,128)(2,1)S(1)} %all_to_all.15), channel_id=1, source_target_pairs={{0,32},{32,0},{1,33},{33,1},{2,34},{34,2},{3,35},{35,3},{4,36},{36... | collective-permute-start | bytes 1572872 | tf_op jit(solution)/shard_map/ppermute | solution.py:25
  31.7 1.5 %fusion = f16[128,512]{1,0:T(8,128)(2,1)S(1)} fusion(bf16[1024,512]{1,0:T(8,128)(2,1)} %param.13, bf16[128,2048]{1,0:T(8,128)(2,1)S(1)} %bitcast.22), kind=kOutput, calls=%fused_computation.7 | convolution fusion | flops 134348800 | bytes 1441792 | tf_op jit(solution)/shard_map/dot_general | solution.py:150
  33.2 0.0 copy-done.2
  33.3 0.3 fusion.1
  33.6 0.0 copy-done
  33.6 0.5 fusion.2
  34.1 0.0 collective-permute-done
  34.1 0.5 fusion.5
  34.6 0.0 copy-done.1
  34.6 0.3 fusion.3
  34.9 0.3 fusion.4
  35.2 1.2 maximum_maximum_fusion
  36.4 5.4 %all-to-all-start.1 = ((f16[8,32,1536]{2,1,0:T(8,128)(2,1)}), f16[8,32,1536]{2,1,0:T(8,128)(2,1)S(1)}, u32[]{:S(2)}, u32[]{:S(2)}) async-start(f16[8,32,1536]{2,1,0:T(8,128)(2,1)} %maximum_maximum_fusion), calls=%async_computation.1 | async-start | bytes 1572864 | tf_op jit(solution)/shard_map/all_to_all | solution.py:161
  41.8 0.1 shard_map.104
  41.8 15.5 %collective-permute-start.1 = (bf16[128,512]{1,0:T(8,128)(2,1)S(1)}, bf16[128,512]{1,0:T(8,128)(2,1)S(1)}, u32[]{:S(2)}, u32[]{:S(2)}) collective-permute-start(bf16[128,512]{1,0:T(8,128)(2,1)S(1)} %get-tuple-element.18), channel_id=1, source_target_pairs={{0,3},{1,0},{2,1},{3,2},{4,7},{5,4},{6,5},{7,6},{8,11},{9,8},{10,9... | collective-permute-start | bytes 393224 | tf_op jit(solution)/shard_map/ppermute | solution.py:25
  57.3 1.9 %collective-permute-start.2 = (bf16[128,512]{1,0:T(8,128)(2,1)S(1)}, bf16[128,512]{1,0:T(8,128)(2,1)S(1)}, u32[]{:S(2)}, u32[]{:S(2)}) collective-permute-start(bf16[128,512]{1,0:T(8,128)(2,1)S(1)} %get-tuple-element.19), channel_id=1, source_target_pairs={{0,2},{1,3},{2,0},{3,1},{4,6},{5,7},{6,4},{7,5},{8,10},{9,11},{10,... | collective-permute-start | bytes 393224 | tf_op jit(solution)/shard_map/ppermute | solution.py:25
  59.3 4.3 %collective-permute-start.3 = (bf16[128,512]{1,0:T(8,128)(2,1)S(1)}, bf16[128,512]{1,0:T(8,128)(2,1)S(1)}, u32[]{:S(2)}, u32[]{:S(2)}) collective-permute-start(bf16[128,512]{1,0:T(8,128)(2,1)S(1)} %get-tuple-element.20), channel_id=1, source_target_pairs={{0,1},{1,2},{2,3},{3,0},{4,5},{5,6},{6,7},{7,4},{8,9},{9,10},{10,1... | collective-permute-start | bytes 393224 | tf_op jit(solution)/shard_map/ppermute | solution.py:25
  63.5 5.3 %collective-permute-done.1 = bf16[128,512]{1,0:T(8,128)(2,1)S(1)} collective-permute-done((bf16[128,512]{1,0:T(8,128)(2,1)S(1)}, bf16[128,512]{1,0:T(8,128)(2,1)S(1)}, u32[]{:S(2)}, u32[]{:S(2)}) %collective-permute-start.1) | collective-permute-done | bytes 131104 | tf_op jit(solution)/shard_map/ppermute | solution.py:25
  68.9 3.1 %collective-permute-done.2 = bf16[128,512]{1,0:T(8,128)(2,1)S(1)} collective-permute-done((bf16[128,512]{1,0:T(8,128)(2,1)S(1)}, bf16[128,512]{1,0:T(8,128)(2,1)S(1)}, u32[]{:S(2)}, u32[]{:S(2)}) %collective-permute-start.2) | collective-permute-done | bytes 131104 | tf_op jit(solution)/shard_map/ppermute | solution.py:25
  72.0 0.2 collective-permute-done.3
  72.2 0.0 all-to-all-done.1
  72.2 0.1 convert_reduce_fusion
  72.3 0.1 multiply_convert_fusion.2
  72.4 0.8 broadcast_in_dim.2
  73.1 8.3 %all-to-all-start.2 = ((bf16[4,32,1536]{2,1,0:T(8,128)(2,1)}), bf16[4,32,1536]{2,1,0:T(8,128)(2,1)S(1)}, u32[]{:S(2)}, u32[]{:S(2)}) async-start(bf16[4,32,1536]{2,1,0:T(8,128)(2,1)} %broadcast_in_dim.2), calls=%async_computation.2 | async-start | bytes 786432 | tf_op jit(solution)/shard_map/all_to_all | solution.py:126
  81.4 0.1 pad_maximum_fusion.own_ref
  81.5 1.9 %collective-permute-start.4 = (bf16[4,128,512]{2,1,0:T(8,128)(2,1)S(1)}, bf16[4,128,512]{2,1,0:T(8,128)(2,1)S(1)}, u32[]{:S(2)}, u32[]{:S(2)}) collective-permute-start(bf16[4,128,512]{2,1,0:T(8,128)(2,1)S(1)} %pad_maximum_fusion.own_ref), channel_id=1, source_target_pairs={{0,32},{32,0},{1,33},{33,1},{2,34},{34,2},{3,35},{35,3},{4,36},{36... | collective-permute-start | bytes 1572872 | tf_op jit(solution)/shard_map/ppermute | solution.py:25
  83.4 1.9 %collective-permute-done.4.other_ref = bf16[4,128,512]{2,1,0:T(8,128)(2,1)S(1)} collective-permute-done((bf16[4,128,512]{2,1,0:T(8,128)(2,1)S(1)}, bf16[4,128,512]{2,1,0:T(8,128)(2,1)S(1)}, u32[]{:S(2)}, u32[]{:S(2)}) %collective-permute-start.4) | collective-permute-done | bytes 524320 | tf_op jit(solution)/shard_map/ppermute | solution.py:25
  85.3 9.2 %all-to-all-done.2 = bf16[4,32,1536]{2,1,0:T(8,128)(2,1)S(1)} async-done(((bf16[4,32,1536]{2,1,0:T(8,128)(2,1)}), bf16[4,32,1536]{2,1,0:T(8,128)(2,1)S(1)}, u32[]{:S(2)}, u32[]{:S(2)}) %all-to-all-start.2) | async-done | bytes 393248 | tf_op jit(solution)/shard_map/all_to_all | solution.py:126
  94.4 3.5 %collective-permute-start.5 = (bf16[128,1536]{1,0:T(8,128)(2,1)S(1)}, bf16[128,1536]{1,0:T(8,128)(2,1)S(1)}, u32[]{:S(2)}, u32[]{:S(2)}) collective-permute-start(bf16[128,1536]{1,0:T(8,128)(2,1)S(1)} %bitcast.27), channel_id=1, source_target_pairs={{0,28},{4,0},{8,4},{12,8},{16,12},{20,16},{24,20},{28,24},{1,29},{... | collective-permute-start | bytes 1179656 | tf_op jit(solution)/shard_map/ppermute | solution.py:25
  97.9 2.4 %collective-permute-start.6 = (bf16[128,1536]{1,0:T(8,128)(2,1)S(1)}, bf16[128,1536]{1,0:T(8,128)(2,1)S(1)}, u32[]{:S(2)}, u32[]{:S(2)}) collective-permute-start(bf16[128,1536]{1,0:T(8,128)(2,1)S(1)} %bitcast.28), channel_id=1, source_target_pairs={{0,4},{4,8},{8,12},{12,16},{16,20},{20,24},{24,28},{28,0},{1,5},{5... | collective-permute-start | bytes 1179656 | tf_op jit(solution)/shard_map/ppermute | solution.py:25
  100.3 0.1 pad_add_fusion.place_ref
  100.4 0.6 shard_map.105
  101.0 4.1 %collective-permute-done.5 = bf16[128,1536]{1,0:T(8,128)(2,1)S(1)} collective-permute-done((bf16[128,1536]{1,0:T(8,128)(2,1)S(1)}, bf16[128,1536]{1,0:T(8,128)(2,1)S(1)}, u32[]{:S(2)}, u32[]{:S(2)}) %collective-permute-start.5) | collective-permute-done | bytes 393248 | tf_op jit(solution)/shard_map/ppermute | solution.py:25
  105.2 3.6 %collective-permute-start.7 = (bf16[128,1536]{1,0:T(8,128)(2,1)S(1)}, bf16[128,1536]{1,0:T(8,128)(2,1)S(1)}, u32[]{:S(2)}, u32[]{:S(2)}) collective-permute-start(bf16[128,1536]{1,0:T(8,128)(2,1)S(1)} %collective-permute-done.5), channel_id=1, source_target_pairs={{0,28},{4,0},{8,4},{12,8},{16,12},{20,16},{24,20},{28,24},{1,29},{... | collective-permute-start | bytes 1179656 | tf_op jit(solution)/shard_map/ppermute | solution.py:25
  108.8 0.0 collective-permute-done.6
  108.8 2.2 %collective-permute-start.8 = (bf16[128,1536]{1,0:T(8,128)(2,1)S(1)}, bf16[128,1536]{1,0:T(8,128)(2,1)S(1)}, u32[]{:S(2)}, u32[]{:S(2)}) collective-permute-start(bf16[128,1536]{1,0:T(8,128)(2,1)S(1)} %collective-permute-done.6), channel_id=1, source_target_pairs={{0,4},{4,8},{8,12},{12,16},{16,20},{20,24},{24,28},{28,0},{1,5},{5... | collective-permute-start | bytes 1179656 | tf_op jit(solution)/shard_map/ppermute | solution.py:25
  111.1 3.9 %collective-permute-done.7 = bf16[128,1536]{1,0:T(8,128)(2,1)S(1)} collective-permute-done((bf16[128,1536]{1,0:T(8,128)(2,1)S(1)}, bf16[128,1536]{1,0:T(8,128)(2,1)S(1)}, u32[]{:S(2)}, u32[]{:S(2)}) %collective-permute-start.7) | collective-permute-done | bytes 393248 | tf_op jit(solution)/shard_map/ppermute | solution.py:25
  114.9 4.7 %collective-permute-start.9 = (bf16[128,1536]{1,0:T(8,128)(2,1)S(1)}, bf16[128,1536]{1,0:T(8,128)(2,1)S(1)}, u32[]{:S(2)}, u32[]{:S(2)}) collective-permute-start(bf16[128,1536]{1,0:T(8,128)(2,1)S(1)} %collective-permute-done.7), channel_id=1, source_target_pairs={{0,28},{4,0},{8,4},{12,8},{16,12},{20,16},{24,20},{28,24},{1,29},{... | collective-permute-start | bytes 1179656 | tf_op jit(solution)/shard_map/ppermute | solution.py:25
  119.7 0.2 collective-permute-done.8
  119.9 1.9 %collective-permute-start.10 = (bf16[128,1536]{1,0:T(8,128)(2,1)S(1)}, bf16[128,1536]{1,0:T(8,128)(2,1)S(1)}, u32[]{:S(2)}, u32[]{:S(2)}) collective-permute-start(bf16[128,1536]{1,0:T(8,128)(2,1)S(1)} %collective-permute-done.8), channel_id=1, source_target_pairs={{0,4},{4,8},{8,12},{12,16},{16,20},{20,24},{24,28},{28,0},{1,5},{5... | collective-permute-start | bytes 1179656 | tf_op jit(solution)/shard_map/ppermute | solution.py:25
  121.9 10.2 %collective-permute-done.10 = bf16[128,1536]{1,0:T(8,128)(2,1)S(1)} collective-permute-done((bf16[128,1536]{1,0:T(8,128)(2,1)S(1)}, bf16[128,1536]{1,0:T(8,128)(2,1)S(1)}, u32[]{:S(2)}, u32[]{:S(2)}) %collective-permute-start.10) | collective-permute-done | bytes 393248 | tf_op jit(solution)/shard_map/ppermute | solution.py:25
  132.1 1.9 %collective-permute-start.11 = (bf16[64,1536]{1,0:T(8,128)(2,1)S(1)}, bf16[64,1536]{1,0:T(8,128)(2,1)S(1)}, u32[]{:S(2)}, u32[]{:S(2)}) collective-permute-start(bf16[64,1536]{1,0:T(8,128)(2,1)S(1)} %slice.67), channel_id=1, source_target_pairs={{0,4},{4,8},{8,12},{12,16},{16,20},{20,24},{24,28},{28,0},{1,5},{5... | collective-permute-start | bytes 589832 | tf_op jit(solution)/shard_map/ppermute | solution.py:25
  134.0 0.0 collective-permute-done.9
  134.0 5.1 %collective-permute-start.12 = (bf16[64,1536]{1,0:T(8,128)(2,1)S(1)}, bf16[64,1536]{1,0:T(8,128)(2,1)S(1)}, u32[]{:S(2)}, u32[]{:S(2)}) collective-permute-start(bf16[64,1536]{1,0:T(8,128)(2,1)S(1)} %slice.68), channel_id=1, source_target_pairs={{0,28},{4,0},{8,4},{12,8},{16,12},{20,16},{24,20},{28,24},{1,29},{... | collective-permute-start | bytes 589832 | tf_op jit(solution)/shard_map/ppermute | solution.py:25
  139.3 1.6 %collective-permute-done.11 = bf16[64,1536]{1,0:T(8,128)(2,1)S(1)} collective-permute-done((bf16[64,1536]{1,0:T(8,128)(2,1)S(1)}, bf16[64,1536]{1,0:T(8,128)(2,1)S(1)}, u32[]{:S(2)}, u32[]{:S(2)}) %collective-permute-start.11) | collective-permute-done | bytes 196640 | tf_op jit(solution)/shard_map/ppermute | solution.py:25
  140.9 1.5 %collective-permute-done.12 = bf16[64,1536]{1,0:T(8,128)(2,1)S(1)} collective-permute-done((bf16[64,1536]{1,0:T(8,128)(2,1)S(1)}, bf16[64,1536]{1,0:T(8,128)(2,1)S(1)}, u32[]{:S(2)}, u32[]{:S(2)}) %collective-permute-start.12) | collective-permute-done | bytes 196640 | tf_op jit(solution)/shard_map/ppermute | solution.py:25
  142.4 1.3 fusion.6
  143.6 1.2 fusion.8
  144.9 1.2 fusion.10
  (12 shorter events, 0.3 us)
Async XLA Ops:
  0.6 32.9 %copy-start = (bf16[512,1024]{1,0:T(8,128)(2,1)S(1)}, bf16[512,1024]{1,0:T(8,128)(2,1)}, u32[]{:S(2)}) copy-start(bf16[512,1024]{1,0:T(8,128)(2,1)} %param.15) | copy-start | bytes 3145732
  0.6 32.6 %copy-start.2 = (bf16[1024,512]{1,0:T(8,128)(2,1)S(1)}, bf16[1024,512]{1,0:T(8,128)(2,1)}, u32[]{:S(2)}) copy-start(bf16[1024,512]{1,0:T(8,128)(2,1)} %param.14) | copy-start | bytes 3145732
  29.7 4.9 %copy-start.1 = (bf16[1024,512]{1,0:T(8,128)(2,1)S(1)}, bf16[1024,512]{1,0:T(8,128)(2,1)}, u32[]{:S(2)}) copy-start(bf16[1024,512]{1,0:T(8,128)(2,1)} %param.13) | copy-start | bytes 3145732
  29.7 4.4 %collective-permute-start = (bf16[16,8,2048]{2,1,0:T(8,128)(2,1)S(1)}, bf16[16,8,2048]{2,1,0:T(8,128)(2,1)S(1)}, u32[]{:S(2)}, u32[]{:S(2)}) collective-permute-start(bf16[16,8,2048]{2,1,0:T(8,128)(2,1)S(1)} %all_to_all.15), channel_id=1, source_target_pairs={{0,32},{32,0},{1,33},{33,1},{2,34},{34,2},{3,35},{35,3},{4,36},{36... | collective-permute-start | bytes 1572872 | tf_op jit(solution)/shard_map/ppermute | solution.py:25
  36.4 35.8 %all-to-all-start.1 = ((f16[8,32,1536]{2,1,0:T(8,128)(2,1)}), f16[8,32,1536]{2,1,0:T(8,128)(2,1)S(1)}, u32[]{:S(2)}, u32[]{:S(2)}) async-start(f16[8,32,1536]{2,1,0:T(8,128)(2,1)} %maximum_maximum_fusion), calls=%async_computation.1 | async-start | bytes 1572864 | tf_op jit(solution)/shard_map/all_to_all | solution.py:161
  41.8 27.1 %collective-permute-start.1 = (bf16[128,512]{1,0:T(8,128)(2,1)S(1)}, bf16[128,512]{1,0:T(8,128)(2,1)S(1)}, u32[]{:S(2)}, u32[]{:S(2)}) collective-permute-start(bf16[128,512]{1,0:T(8,128)(2,1)S(1)} %get-tuple-element.18), channel_id=1, source_target_pairs={{0,3},{1,0},{2,1},{3,2},{4,7},{5,4},{6,5},{7,6},{8,11},{9,8},{10,9... | collective-permute-start | bytes 393224 | tf_op jit(solution)/shard_map/ppermute | solution.py:25
  57.3 14.7 %collective-permute-start.2 = (bf16[128,512]{1,0:T(8,128)(2,1)S(1)}, bf16[128,512]{1,0:T(8,128)(2,1)S(1)}, u32[]{:S(2)}, u32[]{:S(2)}) collective-permute-start(bf16[128,512]{1,0:T(8,128)(2,1)S(1)} %get-tuple-element.19), channel_id=1, source_target_pairs={{0,2},{1,3},{2,0},{3,1},{4,6},{5,7},{6,4},{7,5},{8,10},{9,11},{10,... | collective-permute-start | bytes 393224 | tf_op jit(solution)/shard_map/ppermute | solution.py:25
  59.3 12.9 %collective-permute-start.3 = (bf16[128,512]{1,0:T(8,128)(2,1)S(1)}, bf16[128,512]{1,0:T(8,128)(2,1)S(1)}, u32[]{:S(2)}, u32[]{:S(2)}) collective-permute-start(bf16[128,512]{1,0:T(8,128)(2,1)S(1)} %get-tuple-element.20), channel_id=1, source_target_pairs={{0,1},{1,2},{2,3},{3,0},{4,5},{5,6},{6,7},{7,4},{8,9},{9,10},{10,1... | collective-permute-start | bytes 393224 | tf_op jit(solution)/shard_map/ppermute | solution.py:25
  73.1 21.3 %all-to-all-start.2 = ((bf16[4,32,1536]{2,1,0:T(8,128)(2,1)}), bf16[4,32,1536]{2,1,0:T(8,128)(2,1)S(1)}, u32[]{:S(2)}, u32[]{:S(2)}) async-start(bf16[4,32,1536]{2,1,0:T(8,128)(2,1)} %broadcast_in_dim.2), calls=%async_computation.2 | async-start | bytes 786432 | tf_op jit(solution)/shard_map/all_to_all | solution.py:126
  81.5 3.8 %collective-permute-start.4 = (bf16[4,128,512]{2,1,0:T(8,128)(2,1)S(1)}, bf16[4,128,512]{2,1,0:T(8,128)(2,1)S(1)}, u32[]{:S(2)}, u32[]{:S(2)}) collective-permute-start(bf16[4,128,512]{2,1,0:T(8,128)(2,1)S(1)} %pad_maximum_fusion.own_ref), channel_id=1, source_target_pairs={{0,32},{32,0},{1,33},{33,1},{2,34},{34,2},{3,35},{35,3},{4,36},{36... | collective-permute-start | bytes 1572872 | tf_op jit(solution)/shard_map/ppermute | solution.py:25
  94.4 10.7 %collective-permute-start.5 = (bf16[128,1536]{1,0:T(8,128)(2,1)S(1)}, bf16[128,1536]{1,0:T(8,128)(2,1)S(1)}, u32[]{:S(2)}, u32[]{:S(2)}) collective-permute-start(bf16[128,1536]{1,0:T(8,128)(2,1)S(1)} %bitcast.27), channel_id=1, source_target_pairs={{0,28},{4,0},{8,4},{12,8},{16,12},{20,16},{24,20},{28,24},{1,29},{... | collective-permute-start | bytes 1179656 | tf_op jit(solution)/shard_map/ppermute | solution.py:25
  97.9 10.9 %collective-permute-start.6 = (bf16[128,1536]{1,0:T(8,128)(2,1)S(1)}, bf16[128,1536]{1,0:T(8,128)(2,1)S(1)}, u32[]{:S(2)}, u32[]{:S(2)}) collective-permute-start(bf16[128,1536]{1,0:T(8,128)(2,1)S(1)} %bitcast.28), channel_id=1, source_target_pairs={{0,4},{4,8},{8,12},{12,16},{16,20},{20,24},{24,28},{28,0},{1,5},{5... | collective-permute-start | bytes 1179656 | tf_op jit(solution)/shard_map/ppermute | solution.py:25
  105.2 9.8 %collective-permute-start.7 = (bf16[128,1536]{1,0:T(8,128)(2,1)S(1)}, bf16[128,1536]{1,0:T(8,128)(2,1)S(1)}, u32[]{:S(2)}, u32[]{:S(2)}) collective-permute-start(bf16[128,1536]{1,0:T(8,128)(2,1)S(1)} %collective-permute-done.5), channel_id=1, source_target_pairs={{0,28},{4,0},{8,4},{12,8},{16,12},{20,16},{24,20},{28,24},{1,29},{... | collective-permute-start | bytes 1179656 | tf_op jit(solution)/shard_map/ppermute | solution.py:25
  108.8 11.1 %collective-permute-start.8 = (bf16[128,1536]{1,0:T(8,128)(2,1)S(1)}, bf16[128,1536]{1,0:T(8,128)(2,1)S(1)}, u32[]{:S(2)}, u32[]{:S(2)}) collective-permute-start(bf16[128,1536]{1,0:T(8,128)(2,1)S(1)} %collective-permute-done.6), channel_id=1, source_target_pairs={{0,4},{4,8},{8,12},{12,16},{16,20},{20,24},{24,28},{28,0},{1,5},{5... | collective-permute-start | bytes 1179656 | tf_op jit(solution)/shard_map/ppermute | solution.py:25
  114.9 19.1 %collective-permute-start.9 = (bf16[128,1536]{1,0:T(8,128)(2,1)S(1)}, bf16[128,1536]{1,0:T(8,128)(2,1)S(1)}, u32[]{:S(2)}, u32[]{:S(2)}) collective-permute-start(bf16[128,1536]{1,0:T(8,128)(2,1)S(1)} %collective-permute-done.7), channel_id=1, source_target_pairs={{0,28},{4,0},{8,4},{12,8},{16,12},{20,16},{24,20},{28,24},{1,29},{... | collective-permute-start | bytes 1179656 | tf_op jit(solution)/shard_map/ppermute | solution.py:25
  119.9 12.1 %collective-permute-start.10 = (bf16[128,1536]{1,0:T(8,128)(2,1)S(1)}, bf16[128,1536]{1,0:T(8,128)(2,1)S(1)}, u32[]{:S(2)}, u32[]{:S(2)}) collective-permute-start(bf16[128,1536]{1,0:T(8,128)(2,1)S(1)} %collective-permute-done.8), channel_id=1, source_target_pairs={{0,4},{4,8},{8,12},{12,16},{16,20},{20,24},{24,28},{28,0},{1,5},{5... | collective-permute-start | bytes 1179656 | tf_op jit(solution)/shard_map/ppermute | solution.py:25
  132.1 8.8 %collective-permute-start.11 = (bf16[64,1536]{1,0:T(8,128)(2,1)S(1)}, bf16[64,1536]{1,0:T(8,128)(2,1)S(1)}, u32[]{:S(2)}, u32[]{:S(2)}) collective-permute-start(bf16[64,1536]{1,0:T(8,128)(2,1)S(1)} %slice.67), channel_id=1, source_target_pairs={{0,4},{4,8},{8,12},{12,16},{16,20},{20,24},{24,28},{28,0},{1,5},{5... | collective-permute-start | bytes 589832 | tf_op jit(solution)/shard_map/ppermute | solution.py:25
  134.0 8.3 %collective-permute-start.12 = (bf16[64,1536]{1,0:T(8,128)(2,1)S(1)}, bf16[64,1536]{1,0:T(8,128)(2,1)S(1)}, u32[]{:S(2)}, u32[]{:S(2)}) collective-permute-start(bf16[64,1536]{1,0:T(8,128)(2,1)S(1)} %slice.68), channel_id=1, source_target_pairs={{0,28},{4,0},{8,4},{12,8},{16,12},{20,16},{24,20},{28,24},{1,29},{... | collective-permute-start | bytes 589832 | tf_op jit(solution)/shard_map/ppermute | solution.py:25

commit v10 on v9

--- a/solution.py
+++ b/solution.py
@@ -96,9 +96,8 @@
         share = lax.rem(place_ref[0] + r, n_y)
         spot = pl.ds(pl.multiple_of(share * part, part), part)
         for t in range(n_k):
-            source = lax.rem(t + n_k - place_ref[1], n_k)
             for ref in (own_ref, other_ref):
-                out_ref[at : at + part, :] = ref[source, spot, :]
+                out_ref[at : at + part, :] = ref[t, spot, :]
                 at += part
 
 
@@ -174,24 +173,42 @@
     ).astype(bf16)
     up_back = (back_value * active).astype(bf16)
     values = jnp.concatenate([hidden, gate_back, up_back], axis=1)
-    near = after(copies_to(values, "zhi"), other_cuts).reshape(n_k * share, 3 * units)
+    replicas = after(copies_to(values, "zhi"), other_cuts)
+    turned = jnp.concatenate([replicas, replicas[:-1]], axis=0)
+    near = lax.dynamic_slice_in_dim(turned, k + 1, n_k - 1, axis=0)
+    near = near.reshape((n_k - 1) * share, 3 * units)
 
     order = [0]
     for s in range(1, n_y // 2):
         order += [s, n_y - s]
     order.append(n_y // 2)
-    inputs = put_in_order(order, jnp.stack([y, k]), own_cuts, other_cuts)
-    right = left = near
-    held = {0: near}
-    for s in range(1, n_y // 2):
-        right = shift(right, "y", 1)
-        left = shift(left, "y", -1)
-        held[n_y - s] = right
-        held[s] = left
-    middle = near.shape[0] // 2
+    inputs = put_in_order(order, y.reshape(1), own_cuts, other_cuts)
+    rest = near.shape[0]
+    right_1 = shift(values, "y", 1)
+    left_1 = shift(values, "y", -1)
+    right_2 = shift(right_1, "y", 1)
+    left_2 = shift(left_1, "y", -1)
+    own = {0: values, n_y - 1: right_1, 1: left_1, n_y - 2: right_2, 2: left_2}
+    right = shift(jnp.concatenate([near, right_2], axis=0), "y", 1)
+    left = shift(jnp.concatenate([near, left_2[part:], left_2[:part]], axis=0), "y", -1)
+    own = {r: after(block, right) for r, block in own.items()}
+    own[n_y - 3] = right[rest:]
+    own[3] = jnp.concatenate([left[rest + part :], left[rest : rest + part]], axis=0)
+    far = {0: near, n_y - 1: right[:rest], 1: left[:rest]}
+    right = shift(right[: rest + part], "y", 1)
+    left = shift(left[: rest + part], "y", -1)
+    own[n_y // 2] = jnp.concatenate([right[rest:], left[rest:]], axis=0)
+    far[n_y - 2] = right[:rest]
+    far[2] = left[:rest]
+    right = shift(right[:rest], "y", 1)
+    left = shift(left[:rest], "y", -1)
+    far[n_y - 3] = right
+    far[3] = left
+    middle = rest // 2
     top = shift(right[:middle], "y", 1)
     low = shift(left[middle:], "y", -1)
-    every = jnp.concatenate([held[r] for r in order[:-1]] + [top, low], axis=0)
+    blocks = [block for r in order[:-1] for block in (own[r], far[r])]
+    every = jnp.concatenate(blocks + [own[n_y // 2], top, low], axis=0)
     down_grad = product(every[:, :units], inputs[:, quarter:])
     gate_grad = product(inputs[:, :quarter], every[:, units : 2 * units])
     up_grad = product(inputs[:, :quarter], every[:, 2 * units :])

time: 149 us -> 160 us (1.074); the launches traced: 146 us -> 159 us
  starting transfers between devices: 64.6 us -> 80.3 us
  waiting for transfers between devices: 41.2 us -> 36.7 us
    ppermute x13 -> x17, starting transfers between devices: 51 us -> 67.6 us  [shift(): return lax.ppermute(value, axis, [(i, (i + step) % n) for i in range(n)])]
    all_to_all x1, waiting for transfers between devices: 9.18 us -> 4.25 us  [copies_to(): return lax.all_to_all(spread, axis, 0, 0)]
    ppermute x13 -> x17, waiting for transfers between devices: 32 us -> 32.4 us  [shift(): return lax.ppermute(value, axis, [(i, (i + step) % n) for i in range(n)])]
  transfers between devices with their start and end apart: 15 -> 19, of which waited for: 11 -> 11; matrix products, arithmetic and copies ran while one was open for 2% -> 3% of each run, Pallas kernels for 0% -> 0%
where the time goes in v10:
time: 160 us; the launch traced here: 159 us
  starting transfers between devices  80.3 us (50%)
  waiting for transfers between devices  36.7 us (23%)
  blocking collectives  27.2 us (17%)
  matrix products  7.22 us (5%)
  other arithmetic  2.45 us (2%)
  local copies, waits for them, and re-layouts  2.07 us (1%)
  Pallas kernels  1.88 us (1%)
    ppermute x17, starting transfers between devices, shift(): return lax.ppermute(value, axis, [(i, (i + step) % n) for i in range(n)])  67.6 us
    ppermute x17, waiting for transfers between devices, shift(): return lax.ppermute(value, axis, [(i, (i + step) % n) for i in range(n)])  32.4 us
    all_to_all x1, blocking collectives, body(): mine = lax.all_to_all(spread, ('zlo', 'x'), 0, 0)  27.2 us
    all_to_all x1, starting transfers between devices, copies_to(): return lax.all_to_all(spread, axis, 0, 0)  7.32 us
    all_to_all x1, starting transfers between devices, body(): sums = after(lax.all_to_all(partial_sums, 'y', 0, 0), *own_cuts)  5.36 us
    all_to_all x1, waiting for transfers between devices, copies_to(): return lax.all_to_all(spread, axis, 0, 0)  4.25 us
    dot_general x3, matrix products, product(): lax.dot_general(a, b, (((0,), (0,)), ((), ())), preferred_element_type=f32)  3.77 us
  transfers between devices with their start and end apart: 19, of which 11 were waited for; matrix products, arithmetic and copies ran while one was open for 3% of the time, Pallas kernels for 0%

profile of v10, /device:TPU:14, one launch (start us, length us, event | category | flops | bytes accessed | tf_op | source)
XLA Modules:
  0.0 159.0 jit_solution(407080288313230776)
XLA Ops:
  0.6 0.0 copy-start
  0.6 0.0 copy-start.2
  0.7 1.7 %shard_map.103 = bf16[16,8,2048]{2,1,0:T(8,128)(2,1)} custom-call(s32[1]{0:T(128)} %bitcast.2.block_ref, s32[8,8]{1,0:T(8,128)} %rewards_ref.1, s32[8]{0:T(128)} %selected_ref.1, s32[8]{0:T(128)} %pad_ref.1, bf16[8,1024]{1,0:T(8,128)(2,1)} %tokens_ref.1, bf16[8,1024]{1,0:T(8,128)(2,1)} %cotangent_ref.1), custom_call_target="tpu_custom_call" | custom-call | tf_op jit(solution)/shard_map/pallas_call | solution.py:60
  2.4 27.2 %all_to_all.15 = bf16[16,8,2048]{2,1,0:T(8,128)(2,1)S(1)} all-to-all(bf16[16,8,2048]{2,1,0:T(8,128)(2,1)} %shard_map.103), channel_id=1, replica_groups=mesh['zlo'=2,'x'=8,'core'=2,'y'=8,'zhi'=4] {'zlo','x'}, dimensions={0} | all-to-all | bytes 1048576 | tf_op jit(solution)/shard_map/all_to_all | solution.py:143
  29.7 2.0 %collective-permute-start = (bf16[16,8,2048]{2,1,0:T(8,128)(2,1)S(1)}, bf16[16,8,2048]{2,1,0:T(8,128)(2,1)S(1)}, u32[]{:S(2)}, u32[]{:S(2)}) collective-permute-start(bf16[16,8,2048]{2,1,0:T(8,128)(2,1)S(1)} %all_to_all.15), channel_id=1, source_target_pairs={{0,32},{32,0},{1,33},{33,1},{2,34},{34,2},{3,35},{35,3},{4,36},{36... | collective-permute-start | bytes 1572872 | tf_op jit(solution)/shard_map/ppermute | solution.py:25
  31.7 1.5 fusion
  33.2 0.0 copy-done.2
  33.3 0.3 fusion.1
  33.6 0.0 copy-done
  33.6 0.5 fusion.2
  34.1 0.0 collective-permute-done
  34.1 0.5 fusion.5
  34.6 0.3 fusion.3
  34.9 0.3 fusion.4
  35.2 1.2 maximum_maximum_fusion
  36.4 5.4 %all-to-all-start.1 = ((f16[8,32,1536]{2,1,0:T(8,128)(2,1)}), f16[8,32,1536]{2,1,0:T(8,128)(2,1)S(1)}, u32[]{:S(2)}, u32[]{:S(2)}) async-start(f16[8,32,1536]{2,1,0:T(8,128)(2,1)} %maximum_maximum_fusion), calls=%async_computation.1 | async-start | bytes 1572864 | tf_op jit(solution)/shard_map/all_to_all | solution.py:160
  41.8 0.1 shard_map.104
  41.8 15.5 %collective-permute-start.1 = (bf16[128,512]{1,0:T(8,128)(2,1)S(1)}, bf16[128,512]{1,0:T(8,128)(2,1)S(1)}, u32[]{:S(2)}, u32[]{:S(2)}) collective-permute-start(bf16[128,512]{1,0:T(8,128)(2,1)S(1)} %get-tuple-element.23), channel_id=1, source_target_pairs={{0,3},{1,0},{2,1},{3,2},{4,7},{5,4},{6,5},{7,6},{8,11},{9,8},{10,9... | collective-permute-start | bytes 393224 | tf_op jit(solution)/shard_map/ppermute | solution.py:25
  57.3 1.9 %collective-permute-start.2 = (bf16[128,512]{1,0:T(8,128)(2,1)S(1)}, bf16[128,512]{1,0:T(8,128)(2,1)S(1)}, u32[]{:S(2)}, u32[]{:S(2)}) collective-permute-start(bf16[128,512]{1,0:T(8,128)(2,1)S(1)} %get-tuple-element.24), channel_id=1, source_target_pairs={{0,2},{1,3},{2,0},{3,1},{4,6},{5,7},{6,4},{7,5},{8,10},{9,11},{10,... | collective-permute-start | bytes 393224 | tf_op jit(solution)/shard_map/ppermute | solution.py:25
  59.3 4.3 %collective-permute-start.3 = (bf16[128,512]{1,0:T(8,128)(2,1)S(1)}, bf16[128,512]{1,0:T(8,128)(2,1)S(1)}, u32[]{:S(2)}, u32[]{:S(2)}) collective-permute-start(bf16[128,512]{1,0:T(8,128)(2,1)S(1)} %get-tuple-element.25), channel_id=1, source_target_pairs={{0,1},{1,2},{2,3},{3,0},{4,5},{5,6},{6,7},{7,4},{8,9},{9,10},{10,1... | collective-permute-start | bytes 393224 | tf_op jit(solution)/shard_map/ppermute | solution.py:25
  63.5 5.3 %collective-permute-done.1 = bf16[128,512]{1,0:T(8,128)(2,1)S(1)} collective-permute-done((bf16[128,512]{1,0:T(8,128)(2,1)S(1)}, bf16[128,512]{1,0:T(8,128)(2,1)S(1)}, u32[]{:S(2)}, u32[]{:S(2)}) %collective-permute-start.1) | collective-permute-done | bytes 131104 | tf_op jit(solution)/shard_map/ppermute | solution.py:25
  68.9 3.1 %collective-permute-done.2 = bf16[128,512]{1,0:T(8,128)(2,1)S(1)} collective-permute-done((bf16[128,512]{1,0:T(8,128)(2,1)S(1)}, bf16[128,512]{1,0:T(8,128)(2,1)S(1)}, u32[]{:S(2)}, u32[]{:S(2)}) %collective-permute-start.2) | collective-permute-done | bytes 131104 | tf_op jit(solution)/shard_map/ppermute | solution.py:25
  72.0 0.2 collective-permute-done.3
  72.2 0.0 all-to-all-done.1
  72.2 0.1 convert_reduce_fusion
  72.3 0.1 multiply_convert_fusion.2
  72.4 4.9 %collective-permute-start.8 = (bf16[32,1536]{1,0:T(8,128)(2,1)S(1)}, bf16[32,1536]{1,0:T(8,128)(2,1)S(1)}, u32[]{:S(2)}, u32[]{:S(2)}) collective-permute-start(bf16[32,1536]{1,0:T(8,128)(2,1)S(1)} %pad_maximum_fusion.3), channel_id=1, source_target_pairs={{0,28},{4,0},{8,4},{12,8},{16,12},{20,16},{24,20},{28,24},{1,29},{... | collective-permute-start | bytes 294920 | tf_op jit(solution)/shard_map/ppermute | solution.py:25
  77.2 1.9 %collective-permute-start.5 = (bf16[32,1536]{1,0:T(8,128)(2,1)S(1)}, bf16[32,1536]{1,0:T(8,128)(2,1)}, u32[]{:S(2)}, u32[]{:S(2)}) collective-permute-start(bf16[32,1536]{1,0:T(8,128)(2,1)S(1)} %pad_maximum_fusion.3), channel_id=1, source_target_pairs={{0,4},{4,8},{8,12},{12,16},{16,20},{20,24},{24,28},{28,0},{1,5},{5... | collective-permute-start | bytes 294920 | tf_op jit(solution)/shard_map/ppermute | solution.py:25
  79.2 0.8 broadcast_in_dim.2
  79.9 7.3 %all-to-all-start.2 = ((bf16[4,32,1536]{2,1,0:T(8,128)(2,1)}), bf16[4,32,1536]{2,1,0:T(8,128)(2,1)S(1)}, u32[]{:S(2)}, u32[]{:S(2)}) async-start(bf16[4,32,1536]{2,1,0:T(8,128)(2,1)} %broadcast_in_dim.2), calls=%async_computation.2 | async-start | bytes 786432 | tf_op jit(solution)/shard_map/all_to_all | solution.py:125
  87.2 0.0 collective-permute-done.8
  87.3 4.3 %collective-permute-start.9 = (bf16[32,1536]{1,0:T(8,128)(2,1)S(1)}, bf16[32,1536]{1,0:T(8,128)(2,1)S(1)}, u32[]{:S(2)}, u32[]{:S(2)}) collective-permute-start(bf16[32,1536]{1,0:T(8,128)(2,1)S(1)} %collective-permute-done.8), channel_id=1, source_target_pairs={{0,28},{4,0},{8,4},{12,8},{16,12},{20,16},{24,20},{28,24},{1,29},{... | collective-permute-start | bytes 294920 | tf_op jit(solution)/shard_map/ppermute | solution.py:25
  91.5 0.1 pad_maximum_fusion.own_ref
  91.6 1.9 %collective-permute-start.4 = (bf16[4,128,512]{2,1,0:T(8,128)(2,1)S(1)}, bf16[4,128,512]{2,1,0:T(8,128)(2,1)S(1)}, u32[]{:S(2)}, u32[]{:S(2)}) collective-permute-start(bf16[4,128,512]{2,1,0:T(8,128)(2,1)S(1)} %pad_maximum_fusion.own_ref), channel_id=1, source_target_pairs={{0,32},{32,0},{1,33},{33,1},{2,34},{34,2},{3,35},{35,3},{4,36},{36... | collective-permute-start | bytes 1572872 | tf_op jit(solution)/shard_map/ppermute | solution.py:25
  93.5 0.0 collective-permute-done.5
  93.5 1.9 %collective-permute-start.6 = (bf16[32,1536]{1,0:T(8,128)(2,1)}, bf16[32,1536]{1,0:T(8,128)(2,1)S(1)}, u32[]{:S(2)}, u32[]{:S(2)}) collective-permute-start(bf16[32,1536]{1,0:T(8,128)(2,1)} %collective-permute-done.5), channel_id=1, source_target_pairs={{0,4},{4,8},{8,12},{12,16},{16,20},{20,24},{24,28},{28,0},{1,5},{5... | collective-permute-start | bytes 294920 | tf_op jit(solution)/shard_map/ppermute | solution.py:25
  95.5 0.0 collective-permute-done.9
  95.5 0.0 collective-permute-done.4.other_ref
  95.5 4.2 %all-to-all-done.2 = bf16[4,32,1536]{2,1,0:T(8,128)(2,1)S(1)} async-done(((bf16[4,32,1536]{2,1,0:T(8,128)(2,1)}), bf16[4,32,1536]{2,1,0:T(8,128)(2,1)S(1)}, u32[]{:S(2)}, u32[]{:S(2)}) %all-to-all-start.2) | async-done | bytes 393248 | tf_op jit(solution)/shard_map/all_to_all | solution.py:125
  99.8 0.1 fusion.16
  99.9 0.0 copy-start.4
  99.9 2.1 %collective-permute-done.6 = bf16[32,1536]{1,0:T(8,128)(2,1)S(1)} collective-permute-done((bf16[32,1536]{1,0:T(8,128)(2,1)}, bf16[32,1536]{1,0:T(8,128)(2,1)S(1)}, u32[]{:S(2)}, u32[]{:S(2)}) %collective-permute-start.6) | collective-permute-done | bytes 98336 | tf_op jit(solution)/shard_map/ppermute | solution.py:25
  102.0 0.9 fusion.15
  103.0 1.9 %collective-permute-start.7 = (bf16[128,1536]{1,0:T(8,128)(2,1)}, bf16[128,1536]{1,0:T(8,128)(2,1)S(1)}, u32[]{:S(2)}, u32[]{:S(2)}) collective-permute-start(bf16[128,1536]{1,0:T(8,128)(2,1)} %get-tuple-element.38), channel_id=1, source_target_pairs={{0,4},{4,8},{8,12},{12,16},{16,20},{20,24},{24,28},{28,0},{1,5},{5... | collective-permute-start | bytes 1179656 | tf_op jit(solution)/shard_map/ppermute | solution.py:25
  104.9 0.1 shard_map.105
  105.0 5.1 %collective-permute-start.10 = (bf16[128,1536]{1,0:T(8,128)(2,1)}, bf16[128,1536]{1,0:T(8,128)(2,1)S(1)}, u32[]{:S(2)}, u32[]{:S(2)}) collective-permute-start(bf16[128,1536]{1,0:T(8,128)(2,1)} %get-tuple-element.37), channel_id=1, source_target_pairs={{0,28},{4,0},{8,4},{12,8},{16,12},{20,16},{24,20},{28,24},{1,29},{... | collective-permute-start | bytes 1179656 | tf_op jit(solution)/shard_map/ppermute | solution.py:25
  110.1 6.9 %collective-permute-done.7 = bf16[128,1536]{1,0:T(8,128)(2,1)S(1)} collective-permute-done((bf16[128,1536]{1,0:T(8,128)(2,1)}, bf16[128,1536]{1,0:T(8,128)(2,1)S(1)}, u32[]{:S(2)}, u32[]{:S(2)}) %collective-permute-start.7) | collective-permute-done | bytes 393248 | tf_op jit(solution)/shard_map/ppermute | solution.py:25
  117.0 1.3 collective-permute-done.10
  118.4 5.5 %collective-permute-start.11 = (bf16[112,1536]{1,0:T(8,128)(2,1)S(1)}, bf16[112,1536]{1,0:T(8,128)(2,1)S(1)}, u32[]{:S(2)}, u32[]{:S(2)}) collective-permute-start(bf16[112,1536]{1,0:T(8,128)(2,1)S(1)} %slice.129), channel_id=1, source_target_pairs={{0,28},{4,0},{8,4},{12,8},{16,12},{20,16},{24,20},{28,24},{1,29},{... | collective-permute-start | bytes 1032200 | tf_op jit(solution)/shard_map/ppermute | solution.py:25
  123.9 1.9 %collective-permute-start.12 = (bf16[112,1536]{1,0:T(8,128)(2,1)S(1)}, bf16[112,1536]{1,0:T(8,128)(2,1)S(1)}, u32[]{:S(2)}, u32[]{:S(2)}) collective-permute-start(bf16[112,1536]{1,0:T(8,128)(2,1)S(1)} %slice.131), channel_id=1, source_target_pairs={{0,4},{4,8},{8,12},{12,16},{16,20},{20,24},{24,28},{28,0},{1,5},{5... | collective-permute-start | bytes 1032200 | tf_op jit(solution)/shard_map/ppermute | solution.py:25
  125.9 0.9 constant_dynamic-update-slice_fusion.8
  126.9 3.0 %collective-permute-done.11 = bf16[112,1536]{1,0:T(8,128)(2,1)S(1)} collective-permute-done((bf16[112,1536]{1,0:T(8,128)(2,1)S(1)}, bf16[112,1536]{1,0:T(8,128)(2,1)S(1)}, u32[]{:S(2)}, u32[]{:S(2)}) %collective-permute-start.11) | collective-permute-done | bytes 344096 | tf_op jit(solution)/shard_map/ppermute | solution.py:25
  129.9 5.6 %collective-permute-start.13 = (bf16[96,1536]{1,0:T(8,128)(2,1)S(1)}, bf16[96,1536]{1,0:T(8,128)(2,1)S(1)}, u32[]{:S(2)}, u32[]{:S(2)}) collective-permute-start(bf16[96,1536]{1,0:T(8,128)(2,1)S(1)} %get-tuple-element.35), channel_id=1, source_target_pairs={{0,28},{4,0},{8,4},{12,8},{16,12},{20,16},{24,20},{28,24},{1,29},{... | collective-permute-start | bytes 884744 | tf_op jit(solution)/shard_map/ppermute | solution.py:25
  135.6 0.0 collective-permute-done.12
  135.6 1.9 %collective-permute-start.14 = (bf16[96,1536]{1,0:T(8,128)(2,1)S(1)}, bf16[96,1536]{1,0:T(8,128)(2,1)S(1)}, u32[]{:S(2)}, u32[]{:S(2)}) collective-permute-start(bf16[96,1536]{1,0:T(8,128)(2,1)S(1)} %get-tuple-element.33), channel_id=1, source_target_pairs={{0,4},{4,8},{8,12},{12,16},{16,20},{20,24},{24,28},{28,0},{1,5},{5... | collective-permute-start | bytes 884744 | tf_op jit(solution)/shard_map/ppermute | solution.py:25
  137.6 7.9 %collective-permute-done.14 = bf16[96,1536]{1,0:T(8,128)(2,1)S(1)} collective-permute-done((bf16[96,1536]{1,0:T(8,128)(2,1)S(1)}, bf16[96,1536]{1,0:T(8,128)(2,1)S(1)}, u32[]{:S(2)}, u32[]{:S(2)}) %collective-permute-start.14) | collective-permute-done | bytes 294944 | tf_op jit(solution)/shard_map/ppermute | solution.py:25
  145.5 1.9 %collective-permute-start.15 = (bf16[48,1536]{1,0:T(8,128)(2,1)S(1)}, bf16[48,1536]{1,0:T(8,128)(2,1)S(1)}, u32[]{:S(2)}, u32[]{:S(2)}) collective-permute-start(bf16[48,1536]{1,0:T(8,128)(2,1)S(1)} %slice.138), channel_id=1, source_target_pairs={{0,4},{4,8},{8,12},{12,16},{16,20},{20,24},{24,28},{28,0},{1,5},{5... | collective-permute-start | bytes 442376 | tf_op jit(solution)/shard_map/ppermute | solution.py:25
  147.4 0.0 collective-permute-done.13
  147.4 5.1 %collective-permute-start.16 = (bf16[48,1536]{1,0:T(8,128)(2,1)S(1)}, bf16[48,1536]{1,0:T(8,128)(2,1)S(1)}, u32[]{:S(2)}, u32[]{:S(2)}) collective-permute-start(bf16[48,1536]{1,0:T(8,128)(2,1)S(1)} %slice.139), channel_id=1, source_target_pairs={{0,28},{4,0},{8,4},{12,8},{16,12},{20,16},{24,20},{28,24},{1,29},{... | collective-permute-start | bytes 442376 | tf_op jit(solution)/shard_map/ppermute | solution.py:25
  152.7 1.0 collective-permute-done.15
  153.7 1.5 collective-permute-done.16
  155.2 1.3 fusion.6
  156.5 1.2 fusion.8
  157.8 1.2 fusion.10
  (30 shorter events, 0.4 us)
Async XLA Ops:
  0.6 32.9 %copy-start = (bf16[512,1024]{1,0:T(8,128)(2,1)S(1)}, bf16[512,1024]{1,0:T(8,128)(2,1)}, u32[]{:S(2)}) copy-start(bf16[512,1024]{1,0:T(8,128)(2,1)} %param.15) | copy-start | bytes 3145732
  0.6 32.6 %copy-start.2 = (bf16[1024,512]{1,0:T(8,128)(2,1)S(1)}, bf16[1024,512]{1,0:T(8,128)(2,1)}, u32[]{:S(2)}) copy-start(bf16[1024,512]{1,0:T(8,128)(2,1)} %param.14) | copy-start | bytes 3145732
  29.7 4.9 %copy-start.1 = (bf16[1024,512]{1,0:T(8,128)(2,1)S(1)}, bf16[1024,512]{1,0:T(8,128)(2,1)}, u32[]{:S(2)}) copy-start(bf16[1024,512]{1,0:T(8,128)(2,1)} %param.13) | copy-start | bytes 3145732
  29.7 4.4 %collective-permute-start = (bf16[16,8,2048]{2,1,0:T(8,128)(2,1)S(1)}, bf16[16,8,2048]{2,1,0:T(8,128)(2,1)S(1)}, u32[]{:S(2)}, u32[]{:S(2)}) collective-permute-start(bf16[16,8,2048]{2,1,0:T(8,128)(2,1)S(1)} %all_to_all.15), channel_id=1, source_target_pairs={{0,32},{32,0},{1,33},{33,1},{2,34},{34,2},{3,35},{35,3},{4,36},{36... | collective-permute-start | bytes 1572872 | tf_op jit(solution)/shard_map/ppermute | solution.py:25
  36.4 35.8 %all-to-all-start.1 = ((f16[8,32,1536]{2,1,0:T(8,128)(2,1)}), f16[8,32,1536]{2,1,0:T(8,128)(2,1)S(1)}, u32[]{:S(2)}, u32[]{:S(2)}) async-start(f16[8,32,1536]{2,1,0:T(8,128)(2,1)} %maximum_maximum_fusion), calls=%async_computation.1 | async-start | bytes 1572864 | tf_op jit(solution)/shard_map/all_to_all | solution.py:160
  41.8 27.1 %collective-permute-start.1 = (bf16[128,512]{1,0:T(8,128)(2,1)S(1)}, bf16[128,512]{1,0:T(8,128)(2,1)S(1)}, u32[]{:S(2)}, u32[]{:S(2)}) collective-permute-start(bf16[128,512]{1,0:T(8,128)(2,1)S(1)} %get-tuple-element.23), channel_id=1, source_target_pairs={{0,3},{1,0},{2,1},{3,2},{4,7},{5,4},{6,5},{7,6},{8,11},{9,8},{10,9... | collective-permute-start | bytes 393224 | tf_op jit(solution)/shard_map/ppermute | solution.py:25
  57.3 14.7 %collective-permute-start.2 = (bf16[128,512]{1,0:T(8,128)(2,1)S(1)}, bf16[128,512]{1,0:T(8,128)(2,1)S(1)}, u32[]{:S(2)}, u32[]{:S(2)}) collective-permute-start(bf16[128,512]{1,0:T(8,128)(2,1)S(1)} %get-tuple-element.24), channel_id=1, source_target_pairs={{0,2},{1,3},{2,0},{3,1},{4,6},{5,7},{6,4},{7,5},{8,10},{9,11},{10,... | collective-permute-start | bytes 393224 | tf_op jit(solution)/shard_map/ppermute | solution.py:25
  59.3 12.9 %collective-permute-start.3 = (bf16[128,512]{1,0:T(8,128)(2,1)S(1)}, bf16[128,512]{1,0:T(8,128)(2,1)S(1)}, u32[]{:S(2)}, u32[]{:S(2)}) collective-permute-start(bf16[128,512]{1,0:T(8,128)(2,1)S(1)} %get-tuple-element.25), channel_id=1, source_target_pairs={{0,1},{1,2},{2,3},{3,0},{4,5},{5,6},{6,7},{7,4},{8,9},{9,10},{10,1... | collective-permute-start | bytes 393224 | tf_op jit(solution)/shard_map/ppermute | solution.py:25
  72.4 14.9 %collective-permute-start.8 = (bf16[32,1536]{1,0:T(8,128)(2,1)S(1)}, bf16[32,1536]{1,0:T(8,128)(2,1)S(1)}, u32[]{:S(2)}, u32[]{:S(2)}) collective-permute-start(bf16[32,1536]{1,0:T(8,128)(2,1)S(1)} %pad_maximum_fusion.3), channel_id=1, source_target_pairs={{0,28},{4,0},{8,4},{12,8},{16,12},{20,16},{24,20},{28,24},{1,29},{... | collective-permute-start | bytes 294920 | tf_op jit(solution)/shard_map/ppermute | solution.py:25
  77.2 16.3 %collective-permute-start.5 = (bf16[32,1536]{1,0:T(8,128)(2,1)S(1)}, bf16[32,1536]{1,0:T(8,128)(2,1)}, u32[]{:S(2)}, u32[]{:S(2)}) collective-permute-start(bf16[32,1536]{1,0:T(8,128)(2,1)S(1)} %pad_maximum_fusion.3), channel_id=1, source_target_pairs={{0,4},{4,8},{8,12},{12,16},{16,20},{20,24},{24,28},{28,0},{1,5},{5... | collective-permute-start | bytes 294920 | tf_op jit(solution)/shard_map/ppermute | solution.py:25
  79.9 19.8 %all-to-all-start.2 = ((bf16[4,32,1536]{2,1,0:T(8,128)(2,1)}), bf16[4,32,1536]{2,1,0:T(8,128)(2,1)S(1)}, u32[]{:S(2)}, u32[]{:S(2)}) async-start(bf16[4,32,1536]{2,1,0:T(8,128)(2,1)} %broadcast_in_dim.2), calls=%async_computation.2 | async-start | bytes 786432 | tf_op jit(solution)/shard_map/all_to_all | solution.py:125
  87.3 12.5 %copy-start.3 = (bf16[32,1536]{1,0:T(8,128)(2,1)}, bf16[32,1536]{1,0:T(8,128)(2,1)S(1)}, u32[]{:S(2)}) copy-start(bf16[32,1536]{1,0:T(8,128)(2,1)S(1)} %collective-permute-done.8) | copy-start | bytes 294916
  87.3 8.2 %collective-permute-start.9 = (bf16[32,1536]{1,0:T(8,128)(2,1)S(1)}, bf16[32,1536]{1,0:T(8,128)(2,1)S(1)}, u32[]{:S(2)}, u32[]{:S(2)}) collective-permute-start(bf16[32,1536]{1,0:T(8,128)(2,1)S(1)} %collective-permute-done.8), channel_id=1, source_target_pairs={{0,28},{4,0},{8,4},{12,8},{16,12},{20,16},{24,20},{28,24},{1,29},{... | collective-permute-start | bytes 294920 | tf_op jit(solution)/shard_map/ppermute | solution.py:25
  91.6 3.9 %collective-permute-start.4 = (bf16[4,128,512]{2,1,0:T(8,128)(2,1)S(1)}, bf16[4,128,512]{2,1,0:T(8,128)(2,1)S(1)}, u32[]{:S(2)}, u32[]{:S(2)}) collective-permute-start(bf16[4,128,512]{2,1,0:T(8,128)(2,1)S(1)} %pad_maximum_fusion.own_ref), channel_id=1, source_target_pairs={{0,32},{32,0},{1,33},{33,1},{2,34},{34,2},{3,35},{35,3},{4,36},{36... | collective-permute-start | bytes 1572872 | tf_op jit(solution)/shard_map/ppermute | solution.py:25
  93.5 8.5 %collective-permute-start.6 = (bf16[32,1536]{1,0:T(8,128)(2,1)}, bf16[32,1536]{1,0:T(8,128)(2,1)S(1)}, u32[]{:S(2)}, u32[]{:S(2)}) collective-permute-start(bf16[32,1536]{1,0:T(8,128)(2,1)} %collective-permute-done.5), channel_id=1, source_target_pairs={{0,4},{4,8},{8,12},{12,16},{16,20},{20,24},{24,28},{28,0},{1,5},{5... | collective-permute-start | bytes 294920 | tf_op jit(solution)/shard_map/ppermute | solution.py:25
  99.9 26.0 %copy-start.4 = (bf16[32,1536]{1,0:T(8,128)(2,1)S(1)}, bf16[32,1536]{1,0:T(8,128)(2,1)}, u32[]{:S(2)}) copy-start(bf16[32,1536]{1,0:T(8,128)(2,1)} %copy-done.3) | copy-start | bytes 294916
  103.0 14.0 %collective-permute-start.7 = (bf16[128,1536]{1,0:T(8,128)(2,1)}, bf16[128,1536]{1,0:T(8,128)(2,1)S(1)}, u32[]{:S(2)}, u32[]{:S(2)}) collective-permute-start(bf16[128,1536]{1,0:T(8,128)(2,1)} %get-tuple-element.38), channel_id=1, source_target_pairs={{0,4},{4,8},{8,12},{12,16},{16,20},{20,24},{24,28},{28,0},{1,5},{5... | collective-permute-start | bytes 1179656 | tf_op jit(solution)/shard_map/ppermute | solution.py:25
  105.0 13.4 %collective-permute-start.10 = (bf16[128,1536]{1,0:T(8,128)(2,1)}, bf16[128,1536]{1,0:T(8,128)(2,1)S(1)}, u32[]{:S(2)}, u32[]{:S(2)}) collective-permute-start(bf16[128,1536]{1,0:T(8,128)(2,1)} %get-tuple-element.37), channel_id=1, source_target_pairs={{0,28},{4,0},{8,4},{12,8},{16,12},{20,16},{24,20},{28,24},{1,29},{... | collective-permute-start | bytes 1179656 | tf_op jit(solution)/shard_map/ppermute | solution.py:25
  118.4 11.5 %collective-permute-start.11 = (bf16[112,1536]{1,0:T(8,128)(2,1)S(1)}, bf16[112,1536]{1,0:T(8,128)(2,1)S(1)}, u32[]{:S(2)}, u32[]{:S(2)}) collective-permute-start(bf16[112,1536]{1,0:T(8,128)(2,1)S(1)} %slice.129), channel_id=1, source_target_pairs={{0,28},{4,0},{8,4},{12,8},{16,12},{20,16},{24,20},{28,24},{1,29},{... | collective-permute-start | bytes 1032200 | tf_op jit(solution)/shard_map/ppermute | solution.py:25
  123.9 11.6 %collective-permute-start.12 = (bf16[112,1536]{1,0:T(8,128)(2,1)S(1)}, bf16[112,1536]{1,0:T(8,128)(2,1)S(1)}, u32[]{:S(2)}, u32[]{:S(2)}) collective-permute-start(bf16[112,1536]{1,0:T(8,128)(2,1)S(1)} %slice.131), channel_id=1, source_target_pairs={{0,4},{4,8},{8,12},{12,16},{16,20},{20,24},{24,28},{28,0},{1,5},{5... | collective-permute-start | bytes 1032200 | tf_op jit(solution)/shard_map/ppermute | solution.py:25
  129.9 17.5 %collective-permute-start.13 = (bf16[96,1536]{1,0:T(8,128)(2,1)S(1)}, bf16[96,1536]{1,0:T(8,128)(2,1)S(1)}, u32[]{:S(2)}, u32[]{:S(2)}) collective-permute-start(bf16[96,1536]{1,0:T(8,128)(2,1)S(1)} %get-tuple-element.35), channel_id=1, source_target_pairs={{0,28},{4,0},{8,4},{12,8},{16,12},{20,16},{24,20},{28,24},{1,29},{... | collective-permute-start | bytes 884744 | tf_op jit(solution)/shard_map/ppermute | solution.py:25
  135.6 9.8 %collective-permute-start.14 = (bf16[96,1536]{1,0:T(8,128)(2,1)S(1)}, bf16[96,1536]{1,0:T(8,128)(2,1)S(1)}, u32[]{:S(2)}, u32[]{:S(2)}) collective-permute-start(bf16[96,1536]{1,0:T(8,128)(2,1)S(1)} %get-tuple-element.33), channel_id=1, source_target_pairs={{0,4},{4,8},{8,12},{12,16},{16,20},{20,24},{24,28},{28,0},{1,5},{5... | collective-permute-start | bytes 884744 | tf_op jit(solution)/shard_map/ppermute | solution.py:25
  145.5 8.2 %collective-permute-start.15 = (bf16[48,1536]{1,0:T(8,128)(2,1)S(1)}, bf16[48,1536]{1,0:T(8,128)(2,1)S(1)}, u32[]{:S(2)}, u32[]{:S(2)}) collective-permute-start(bf16[48,1536]{1,0:T(8,128)(2,1)S(1)} %slice.138), channel_id=1, source_target_pairs={{0,4},{4,8},{8,12},{12,16},{16,20},{20,24},{24,28},{28,0},{1,5},{5... | collective-permute-start | bytes 442376 | tf_op jit(solution)/shard_map/ppermute | solution.py:25
  147.4 7.8 %collective-permute-start.16 = (bf16[48,1536]{1,0:T(8,128)(2,1)S(1)}, bf16[48,1536]{1,0:T(8,128)(2,1)S(1)}, u32[]{:S(2)}, u32[]{:S(2)}) collective-permute-start(bf16[48,1536]{1,0:T(8,128)(2,1)S(1)} %slice.139), channel_id=1, source_target_pairs={{0,28},{4,0},{8,4},{12,8},{16,12},{20,16},{24,20},{28,24},{1,29},{... | collective-permute-start | bytes 442376 | tf_op jit(solution)/shard_map/ppermute | solution.py:25

commit v11 on v9

--- a/solution.py
+++ b/solution.py
@@ -119,11 +119,6 @@
 
 def after(value, *others):
     return lax.optimization_barrier((value,) + others)[0]
-
-
-def copies_to(value, axis):
-    spread = jnp.broadcast_to(value[None], (lax.axis_size(axis),) + value.shape)
-    return lax.all_to_all(spread, axis, 0, 0)
 
 
 def body(tokens, cotangent, pad_mask, rewards, selected, gate_weight, up_weight, down_weight):
@@ -174,7 +169,7 @@
     ).astype(bf16)
     up_back = (back_value * active).astype(bf16)
     values = jnp.concatenate([hidden, gate_back, up_back], axis=1)
-    near = after(copies_to(values, "zhi"), other_cuts).reshape(n_k * share, 3 * units)
+    near = after(lax.all_gather(values, "zhi"), other_cuts).reshape(n_k * share, 3 * units)
 
     order = [0]
     for s in range(1, n_y // 2):

time: 149 us -> 146 us (0.980)
  blocking collectives: 27.2 us -> 44.7 us
  waiting for transfers between devices: 41.2 us -> 27.7 us
  starting transfers between devices: 64.6 us -> 59.8 us
    all_gather x0 -> x1, blocking collectives: none -> 17.4 us  [body(): lax.all_gather(values, 'zhi')]
    all_to_all x1 -> x0, waiting for transfers between devices: 9.18 us -> none  [copies_to(): return lax.all_to_all(spread, axis, 0, 0)]
    all_to_all x1 -> x0, starting transfers between devices: 8.26 us -> none  [copies_to(): return lax.all_to_all(spread, axis, 0, 0)]
    ppermute x13, waiting for transfers between devices: 32 us -> 27.7 us  [shift(): return lax.ppermute(value, axis, [(i, (i + step) % n) for i in range(n)])]
    ppermute x13, starting transfers between devices: 51 us -> 54.5 us  [shift(): return lax.ppermute(value, axis, [(i, (i + step) % n) for i in range(n)])]
  transfers between devices with their start and end apart: 15 -> 14, of which waited for: 11 -> 8; matrix products, arithmetic and copies ran while one was open for 2% -> 2% of each run, Pallas kernels for 0% -> 0%
where the time goes in v11:
time: 146 us; the launch traced here: 145 us
  starting transfers between devices  59.8 us (41%)
  blocking collectives  44.7 us (31%)
  waiting for transfers between devices  27.7 us (19%)
  matrix products  7.22 us (5%)
  Pallas kernels  2.43 us (2%)
  other arithmetic  1.48 us (1%)
    ppermute x13, starting transfers between devices, shift(): return lax.ppermute(value, axis, [(i, (i + step) % n) for i in range(n)])  54.5 us
    ppermute x13, waiting for transfers between devices, shift(): return lax.ppermute(value, axis, [(i, (i + step) % n) for i in range(n)])  27.7 us
    all_to_all x1, blocking collectives, body(): mine = lax.all_to_all(spread, ('zlo', 'x'), 0, 0)  27.2 us
    all_gather x1, blocking collectives, body(): lax.all_gather(values, 'zhi')  17.4 us
    all_to_all x1, starting transfers between devices, body(): sums = after(lax.all_to_all(partial_sums, 'y', 0, 0), *own_cuts)  5.36 us
    dot_general x3, matrix products, product(): lax.dot_general(a, b, (((0,), (0,)), ((), ())), preferred_element_type=f32)  3.77 us
  transfers between devices with their start and end apart: 14, of which 8 were waited for; matrix products, arithmetic and copies ran while one was open for 2% of the time, Pallas kernels for 0%

profile of v11, /device:TPU:14, one launch (start us, length us, event | category | flops | bytes accessed | tf_op | source)
XLA Modules:
  0.0 144.6 jit_solution(8076390103783645920)
XLA Ops:
  0.6 0.0 copy-start
  0.6 0.0 copy-start.2
  0.7 1.7 %shard_map.103 = bf16[16,8,2048]{2,1,0:T(8,128)(2,1)} custom-call(s32[1]{0:T(128)} %bitcast.2.block_ref, s32[8,8]{1,0:T(8,128)} %rewards_ref.1, s32[8]{0:T(128)} %selected_ref.1, s32[8]{0:T(128)} %pad_ref.1, bf16[8,1024]{1,0:T(8,128)(2,1)} %tokens_ref.1, bf16[8,1024]{1,0:T(8,128)(2,1)} %cotangent_ref.1), custom_call_target="tpu_custom_call" | custom-call | tf_op jit(solution)/shard_map/pallas_call | solution.py:60
  2.4 27.2 %all_to_all.10 = bf16[16,8,2048]{2,1,0:T(8,128)(2,1)S(1)} all-to-all(bf16[16,8,2048]{2,1,0:T(8,128)(2,1)} %shard_map.103), channel_id=1, replica_groups=mesh['zlo'=2,'x'=8,'core'=2,'y'=8,'zhi'=4] {'zlo','x'}, dimensions={0} | all-to-all | bytes 1048576 | tf_op jit(solution)/shard_map/all_to_all | solution.py:139
  29.7 0.0 copy-start.1
  29.7 2.0 %collective-permute-start = (bf16[16,8,2048]{2,1,0:T(8,128)(2,1)S(1)}, bf16[16,8,2048]{2,1,0:T(8,128)(2,1)S(1)}, u32[]{:S(2)}, u32[]{:S(2)}) collective-permute-start(bf16[16,8,2048]{2,1,0:T(8,128)(2,1)S(1)} %all_to_all.10), channel_id=1, source_target_pairs={{0,32},{32,0},{1,33},{33,1},{2,34},{34,2},{3,35},{35,3},{4,36},{36... | collective-permute-start | bytes 1572872 | tf_op jit(solution)/shard_map/ppermute | solution.py:25
  31.7 1.5 %fusion = f16[128,512]{1,0:T(8,128)(2,1)S(1)} fusion(bf16[1024,512]{1,0:T(8,128)(2,1)} %param.13, bf16[128,2048]{1,0:T(8,128)(2,1)S(1)} %bitcast.23), kind=kOutput, calls=%fused_computation.7 | convolution fusion | flops 134348800 | bytes 1441792 | tf_op jit(solution)/shard_map/dot_general | solution.py:145
  33.2 0.0 copy-done.2
  33.3 0.3 fusion.1
  33.6 0.0 copy-done
  33.6 0.5 fusion.2
  34.1 0.0 collective-permute-done
  34.1 0.5 fusion.5
  34.6 0.0 copy-done.1
  34.6 0.3 fusion.3
  34.9 0.3 fusion.4
  35.2 1.2 maximum_maximum_fusion
  36.4 5.4 %all-to-all-start.1 = ((f16[8,32,1536]{2,1,0:T(8,128)(2,1)}), f16[8,32,1536]{2,1,0:T(8,128)(2,1)S(1)}, u32[]{:S(2)}, u32[]{:S(2)}) async-start(f16[8,32,1536]{2,1,0:T(8,128)(2,1)} %maximum_maximum_fusion), calls=%async_computation.1 | async-start | bytes 1572864 | tf_op jit(solution)/shard_map/all_to_all | solution.py:156
  41.8 0.1 shard_map.104
  41.8 15.5 %collective-permute-start.1 = (bf16[128,512]{1,0:T(8,128)(2,1)S(1)}, bf16[128,512]{1,0:T(8,128)(2,1)S(1)}, u32[]{:S(2)}, u32[]{:S(2)}) collective-permute-start(bf16[128,512]{1,0:T(8,128)(2,1)S(1)} %get-tuple-element.18), channel_id=1, source_target_pairs={{0,3},{1,0},{2,1},{3,2},{4,7},{5,4},{6,5},{7,6},{8,11},{9,8},{10,9... | collective-permute-start | bytes 393224 | tf_op jit(solution)/shard_map/ppermute | solution.py:25
  57.3 1.9 %collective-permute-start.2 = (bf16[128,512]{1,0:T(8,128)(2,1)S(1)}, bf16[128,512]{1,0:T(8,128)(2,1)S(1)}, u32[]{:S(2)}, u32[]{:S(2)}) collective-permute-start(bf16[128,512]{1,0:T(8,128)(2,1)S(1)} %get-tuple-element.19), channel_id=1, source_target_pairs={{0,2},{1,3},{2,0},{3,1},{4,6},{5,7},{6,4},{7,5},{8,10},{9,11},{10,... | collective-permute-start | bytes 393224 | tf_op jit(solution)/shard_map/ppermute | solution.py:25
  59.3 4.3 %collective-permute-start.3 = (bf16[128,512]{1,0:T(8,128)(2,1)S(1)}, bf16[128,512]{1,0:T(8,128)(2,1)S(1)}, u32[]{:S(2)}, u32[]{:S(2)}) collective-permute-start(bf16[128,512]{1,0:T(8,128)(2,1)S(1)} %get-tuple-element.20), channel_id=1, source_target_pairs={{0,1},{1,2},{2,3},{3,0},{4,5},{5,6},{6,7},{7,4},{8,9},{9,10},{10,1... | collective-permute-start | bytes 393224 | tf_op jit(solution)/shard_map/ppermute | solution.py:25
  63.5 5.3 %collective-permute-done.1 = bf16[128,512]{1,0:T(8,128)(2,1)S(1)} collective-permute-done((bf16[128,512]{1,0:T(8,128)(2,1)S(1)}, bf16[128,512]{1,0:T(8,128)(2,1)S(1)}, u32[]{:S(2)}, u32[]{:S(2)}) %collective-permute-start.1) | collective-permute-done | bytes 131104 | tf_op jit(solution)/shard_map/ppermute | solution.py:25
  68.9 3.1 %collective-permute-done.2 = bf16[128,512]{1,0:T(8,128)(2,1)S(1)} collective-permute-done((bf16[128,512]{1,0:T(8,128)(2,1)S(1)}, bf16[128,512]{1,0:T(8,128)(2,1)S(1)}, u32[]{:S(2)}, u32[]{:S(2)}) %collective-permute-start.2) | collective-permute-done | bytes 131104 | tf_op jit(solution)/shard_map/ppermute | solution.py:25
  72.0 0.2 collective-permute-done.3
  72.2 0.1 pad_maximum_fusion.own_ref
  72.3 1.9 %collective-permute-start.4 = (bf16[4,128,512]{2,1,0:T(8,128)(2,1)S(1)}, bf16[4,128,512]{2,1,0:T(8,128)(2,1)S(1)}, u32[]{:S(2)}, u32[]{:S(2)}) collective-permute-start(bf16[4,128,512]{2,1,0:T(8,128)(2,1)S(1)} %pad_maximum_fusion.own_ref), channel_id=1, source_target_pairs={{0,32},{32,0},{1,33},{33,1},{2,34},{34,2},{3,35},{35,3},{4,36},{36... | collective-permute-start | bytes 1572872 | tf_op jit(solution)/shard_map/ppermute | solution.py:25
  74.2 0.0 all-to-all-done.1
  74.2 0.1 convert_reduce_fusion
  74.3 0.1 multiply_convert_fusion.2
  74.4 17.4 %all-gather = bf16[128,1536]{1,0:T(8,128)(2,1)S(1)} all-gather(bf16[32,1536]{1,0:T(8,128)(2,1)S(1)} %pad_maximum_fusion.1), channel_id=2, replica_groups=mesh['zlo'=2,'x'=8,'core'=2,'y'=8,'zhi'=4] {'zhi'}, dimensions={0}, use_global_device_ids=true | all-gather | bytes 491520 | tf_op jit(solution)/shard_map/all_gather | solution.py:172
  91.8 0.0 collective-permute-done.4.other_ref
  91.8 4.9 %collective-permute-start.5 = (bf16[128,1536]{1,0:T(8,128)(2,1)S(1)}, bf16[128,1536]{1,0:T(8,128)(2,1)S(1)}, u32[]{:S(2)}, u32[]{:S(2)}) collective-permute-start(bf16[128,1536]{1,0:T(8,128)(2,1)S(1)} %all-gather), channel_id=1, source_target_pairs={{0,28},{4,0},{8,4},{12,8},{16,12},{20,16},{24,20},{28,24},{1,29},{... | collective-permute-start | bytes 1179656 | tf_op jit(solution)/shard_map/ppermute | solution.py:25
  96.7 1.9 %collective-permute-start.6 = (bf16[128,1536]{1,0:T(8,128)(2,1)S(1)}, bf16[128,1536]{1,0:T(8,128)(2,1)S(1)}, u32[]{:S(2)}, u32[]{:S(2)}) collective-permute-start(bf16[128,1536]{1,0:T(8,128)(2,1)S(1)} %all-gather), channel_id=1, source_target_pairs={{0,4},{4,8},{8,12},{12,16},{16,20},{20,24},{24,28},{28,0},{1,5},{5... | collective-permute-start | bytes 1179656 | tf_op jit(solution)/shard_map/ppermute | solution.py:25
  98.6 0.1 pad_add_fusion.place_ref
  98.7 0.6 shard_map.105
  99.3 3.7 %collective-permute-done.5 = bf16[128,1536]{1,0:T(8,128)(2,1)S(1)} collective-permute-done((bf16[128,1536]{1,0:T(8,128)(2,1)S(1)}, bf16[128,1536]{1,0:T(8,128)(2,1)S(1)}, u32[]{:S(2)}, u32[]{:S(2)}) %collective-permute-start.5) | collective-permute-done | bytes 393248 | tf_op jit(solution)/shard_map/ppermute | solution.py:25
  103.0 5.6 %collective-permute-start.7 = (bf16[128,1536]{1,0:T(8,128)(2,1)S(1)}, bf16[128,1536]{1,0:T(8,128)(2,1)S(1)}, u32[]{:S(2)}, u32[]{:S(2)}) collective-permute-start(bf16[128,1536]{1,0:T(8,128)(2,1)S(1)} %collective-permute-done.5), channel_id=1, source_target_pairs={{0,28},{4,0},{8,4},{12,8},{16,12},{20,16},{24,20},{28,24},{1,29},{... | collective-permute-start | bytes 1179656 | tf_op jit(solution)/shard_map/ppermute | solution.py:25
  108.6 0.0 collective-permute-done.6
  108.6 1.9 %collective-permute-start.8 = (bf16[128,1536]{1,0:T(8,128)(2,1)S(1)}, bf16[128,1536]{1,0:T(8,128)(2,1)S(1)}, u32[]{:S(2)}, u32[]{:S(2)}) collective-permute-start(bf16[128,1536]{1,0:T(8,128)(2,1)S(1)} %collective-permute-done.6), channel_id=1, source_target_pairs={{0,4},{4,8},{8,12},{12,16},{16,20},{20,24},{24,28},{28,0},{1,5},{5... | collective-permute-start | bytes 1179656 | tf_op jit(solution)/shard_map/ppermute | solution.py:25
  110.6 3.4 %collective-permute-done.7 = bf16[128,1536]{1,0:T(8,128)(2,1)S(1)} collective-permute-done((bf16[128,1536]{1,0:T(8,128)(2,1)S(1)}, bf16[128,1536]{1,0:T(8,128)(2,1)S(1)}, u32[]{:S(2)}, u32[]{:S(2)}) %collective-permute-start.7) | collective-permute-done | bytes 393248 | tf_op jit(solution)/shard_map/ppermute | solution.py:25
  114.0 5.6 %collective-permute-start.9 = (bf16[128,1536]{1,0:T(8,128)(2,1)S(1)}, bf16[128,1536]{1,0:T(8,128)(2,1)S(1)}, u32[]{:S(2)}, u32[]{:S(2)}) collective-permute-start(bf16[128,1536]{1,0:T(8,128)(2,1)S(1)} %collective-permute-done.7), channel_id=1, source_target_pairs={{0,28},{4,0},{8,4},{12,8},{16,12},{20,16},{24,20},{28,24},{1,29},{... | collective-permute-start | bytes 1179656 | tf_op jit(solution)/shard_map/ppermute | solution.py:25
  119.6 0.0 collective-permute-done.8
  119.6 1.9 %collective-permute-start.10 = (bf16[128,1536]{1,0:T(8,128)(2,1)S(1)}, bf16[128,1536]{1,0:T(8,128)(2,1)S(1)}, u32[]{:S(2)}, u32[]{:S(2)}) collective-permute-start(bf16[128,1536]{1,0:T(8,128)(2,1)S(1)} %collective-permute-done.8), channel_id=1, source_target_pairs={{0,4},{4,8},{8,12},{12,16},{16,20},{20,24},{24,28},{28,0},{1,5},{5... | collective-permute-start | bytes 1179656 | tf_op jit(solution)/shard_map/ppermute | solution.py:25
  121.6 8.9 %collective-permute-done.10 = bf16[128,1536]{1,0:T(8,128)(2,1)S(1)} collective-permute-done((bf16[128,1536]{1,0:T(8,128)(2,1)S(1)}, bf16[128,1536]{1,0:T(8,128)(2,1)S(1)}, u32[]{:S(2)}, u32[]{:S(2)}) %collective-permute-start.10) | collective-permute-done | bytes 393248 | tf_op jit(solution)/shard_map/ppermute | solution.py:25
  130.5 1.9 %collective-permute-start.11 = (bf16[64,1536]{1,0:T(8,128)(2,1)S(1)}, bf16[64,1536]{1,0:T(8,128)(2,1)S(1)}, u32[]{:S(2)}, u32[]{:S(2)}) collective-permute-start(bf16[64,1536]{1,0:T(8,128)(2,1)S(1)} %slice.67), channel_id=1, source_target_pairs={{0,4},{4,8},{8,12},{12,16},{16,20},{20,24},{24,28},{28,0},{1,5},{5... | collective-permute-start | bytes 589832 | tf_op jit(solution)/shard_map/ppermute | solution.py:25
  132.5 0.0 collective-permute-done.9
  132.5 5.1 %collective-permute-start.12 = (bf16[64,1536]{1,0:T(8,128)(2,1)S(1)}, bf16[64,1536]{1,0:T(8,128)(2,1)S(1)}, u32[]{:S(2)}, u32[]{:S(2)}) collective-permute-start(bf16[64,1536]{1,0:T(8,128)(2,1)S(1)} %slice.68), channel_id=1, source_target_pairs={{0,28},{4,0},{8,4},{12,8},{16,12},{20,16},{24,20},{28,24},{1,29},{... | collective-permute-start | bytes 589832 | tf_op jit(solution)/shard_map/ppermute | solution.py:25
  137.7 1.6 %collective-permute-done.11 = bf16[64,1536]{1,0:T(8,128)(2,1)S(1)} collective-permute-done((bf16[64,1536]{1,0:T(8,128)(2,1)S(1)}, bf16[64,1536]{1,0:T(8,128)(2,1)S(1)}, u32[]{:S(2)}, u32[]{:S(2)}) %collective-permute-start.11) | collective-permute-done | bytes 196640 | tf_op jit(solution)/shard_map/ppermute | solution.py:25
  139.3 1.5 %collective-permute-done.12 = bf16[64,1536]{1,0:T(8,128)(2,1)S(1)} collective-permute-done((bf16[64,1536]{1,0:T(8,128)(2,1)S(1)}, bf16[64,1536]{1,0:T(8,128)(2,1)S(1)}, u32[]{:S(2)}, u32[]{:S(2)}) %collective-permute-start.12) | collective-permute-done | bytes 196640 | tf_op jit(solution)/shard_map/ppermute | solution.py:25
  140.8 1.3 fusion.6
  142.1 1.2 fusion.8
  143.3 1.2 fusion.10
  (12 shorter events, 0.3 us)
Async XLA Ops:
  0.6 32.9 %copy-start = (bf16[512,1024]{1,0:T(8,128)(2,1)S(1)}, bf16[512,1024]{1,0:T(8,128)(2,1)}, u32[]{:S(2)}) copy-start(bf16[512,1024]{1,0:T(8,128)(2,1)} %param.15) | copy-start | bytes 3145732
  0.6 32.6 %copy-start.2 = (bf16[1024,512]{1,0:T(8,128)(2,1)S(1)}, bf16[1024,512]{1,0:T(8,128)(2,1)}, u32[]{:S(2)}) copy-start(bf16[1024,512]{1,0:T(8,128)(2,1)} %param.14) | copy-start | bytes 3145732
  29.7 4.9 %copy-start.1 = (bf16[1024,512]{1,0:T(8,128)(2,1)S(1)}, bf16[1024,512]{1,0:T(8,128)(2,1)}, u32[]{:S(2)}) copy-start(bf16[1024,512]{1,0:T(8,128)(2,1)} %param.13) | copy-start | bytes 3145732
  29.7 4.4 %collective-permute-start = (bf16[16,8,2048]{2,1,0:T(8,128)(2,1)S(1)}, bf16[16,8,2048]{2,1,0:T(8,128)(2,1)S(1)}, u32[]{:S(2)}, u32[]{:S(2)}) collective-permute-start(bf16[16,8,2048]{2,1,0:T(8,128)(2,1)S(1)} %all_to_all.10), channel_id=1, source_target_pairs={{0,32},{32,0},{1,33},{33,1},{2,34},{34,2},{3,35},{35,3},{4,36},{36... | collective-permute-start | bytes 1572872 | tf_op jit(solution)/shard_map/ppermute | solution.py:25
  36.4 37.8 %all-to-all-start.1 = ((f16[8,32,1536]{2,1,0:T(8,128)(2,1)}), f16[8,32,1536]{2,1,0:T(8,128)(2,1)S(1)}, u32[]{:S(2)}, u32[]{:S(2)}) async-start(f16[8,32,1536]{2,1,0:T(8,128)(2,1)} %maximum_maximum_fusion), calls=%async_computation.1 | async-start | bytes 1572864 | tf_op jit(solution)/shard_map/all_to_all | solution.py:156
  41.8 27.1 %collective-permute-start.1 = (bf16[128,512]{1,0:T(8,128)(2,1)S(1)}, bf16[128,512]{1,0:T(8,128)(2,1)S(1)}, u32[]{:S(2)}, u32[]{:S(2)}) collective-permute-start(bf16[128,512]{1,0:T(8,128)(2,1)S(1)} %get-tuple-element.18), channel_id=1, source_target_pairs={{0,3},{1,0},{2,1},{3,2},{4,7},{5,4},{6,5},{7,6},{8,11},{9,8},{10,9... | collective-permute-start | bytes 393224 | tf_op jit(solution)/shard_map/ppermute | solution.py:25
  57.3 14.7 %collective-permute-start.2 = (bf16[128,512]{1,0:T(8,128)(2,1)S(1)}, bf16[128,512]{1,0:T(8,128)(2,1)S(1)}, u32[]{:S(2)}, u32[]{:S(2)}) collective-permute-start(bf16[128,512]{1,0:T(8,128)(2,1)S(1)} %get-tuple-element.19), channel_id=1, source_target_pairs={{0,2},{1,3},{2,0},{3,1},{4,6},{5,7},{6,4},{7,5},{8,10},{9,11},{10,... | collective-permute-start | bytes 393224 | tf_op jit(solution)/shard_map/ppermute | solution.py:25
  59.3 12.9 %collective-permute-start.3 = (bf16[128,512]{1,0:T(8,128)(2,1)S(1)}, bf16[128,512]{1,0:T(8,128)(2,1)S(1)}, u32[]{:S(2)}, u32[]{:S(2)}) collective-permute-start(bf16[128,512]{1,0:T(8,128)(2,1)S(1)} %get-tuple-element.20), channel_id=1, source_target_pairs={{0,1},{1,2},{2,3},{3,0},{4,5},{5,6},{6,7},{7,4},{8,9},{9,10},{10,1... | collective-permute-start | bytes 393224 | tf_op jit(solution)/shard_map/ppermute | solution.py:25
  72.3 19.5 %collective-permute-start.4 = (bf16[4,128,512]{2,1,0:T(8,128)(2,1)S(1)}, bf16[4,128,512]{2,1,0:T(8,128)(2,1)S(1)}, u32[]{:S(2)}, u32[]{:S(2)}) collective-permute-start(bf16[4,128,512]{2,1,0:T(8,128)(2,1)S(1)} %pad_maximum_fusion.own_ref), channel_id=1, source_target_pairs={{0,32},{32,0},{1,33},{33,1},{2,34},{34,2},{3,35},{35,3},{4,36},{36... | collective-permute-start | bytes 1572872 | tf_op jit(solution)/shard_map/ppermute | solution.py:25
  91.8 11.2 %collective-permute-start.5 = (bf16[128,1536]{1,0:T(8,128)(2,1)S(1)}, bf16[128,1536]{1,0:T(8,128)(2,1)S(1)}, u32[]{:S(2)}, u32[]{:S(2)}) collective-permute-start(bf16[128,1536]{1,0:T(8,128)(2,1)S(1)} %all-gather), channel_id=1, source_target_pairs={{0,28},{4,0},{8,4},{12,8},{16,12},{20,16},{24,20},{28,24},{1,29},{... | collective-permute-start | bytes 1179656 | tf_op jit(solution)/shard_map/ppermute | solution.py:25
  96.7 11.9 %collective-permute-start.6 = (bf16[128,1536]{1,0:T(8,128)(2,1)S(1)}, bf16[128,1536]{1,0:T(8,128)(2,1)S(1)}, u32[]{:S(2)}, u32[]{:S(2)}) collective-permute-start(bf16[128,1536]{1,0:T(8,128)(2,1)S(1)} %all-gather), channel_id=1, source_target_pairs={{0,4},{4,8},{8,12},{12,16},{16,20},{20,24},{24,28},{28,0},{1,5},{5... | collective-permute-start | bytes 1179656 | tf_op jit(solution)/shard_map/ppermute | solution.py:25
  103.0 11.0 %collective-permute-start.7 = (bf16[128,1536]{1,0:T(8,128)(2,1)S(1)}, bf16[128,1536]{1,0:T(8,128)(2,1)S(1)}, u32[]{:S(2)}, u32[]{:S(2)}) collective-permute-start(bf16[128,1536]{1,0:T(8,128)(2,1)S(1)} %collective-permute-done.5), channel_id=1, source_target_pairs={{0,28},{4,0},{8,4},{12,8},{16,12},{20,16},{24,20},{28,24},{1,29},{... | collective-permute-start | bytes 1179656 | tf_op jit(solution)/shard_map/ppermute | solution.py:25
  108.6 11.0 %collective-permute-start.8 = (bf16[128,1536]{1,0:T(8,128)(2,1)S(1)}, bf16[128,1536]{1,0:T(8,128)(2,1)S(1)}, u32[]{:S(2)}, u32[]{:S(2)}) collective-permute-start(bf16[128,1536]{1,0:T(8,128)(2,1)S(1)} %collective-permute-done.6), channel_id=1, source_target_pairs={{0,4},{4,8},{8,12},{12,16},{16,20},{20,24},{24,28},{28,0},{1,5},{5... | collective-permute-start | bytes 1179656 | tf_op jit(solution)/shard_map/ppermute | solution.py:25
  114.0 18.4 %collective-permute-start.9 = (bf16[128,1536]{1,0:T(8,128)(2,1)S(1)}, bf16[128,1536]{1,0:T(8,128)(2,1)S(1)}, u32[]{:S(2)}, u32[]{:S(2)}) collective-permute-start(bf16[128,1536]{1,0:T(8,128)(2,1)S(1)} %collective-permute-done.7), channel_id=1, source_target_pairs={{0,28},{4,0},{8,4},{12,8},{16,12},{20,16},{24,20},{28,24},{1,29},{... | collective-permute-start | bytes 1179656 | tf_op jit(solution)/shard_map/ppermute | solution.py:25
  119.6 10.9 %collective-permute-start.10 = (bf16[128,1536]{1,0:T(8,128)(2,1)S(1)}, bf16[128,1536]{1,0:T(8,128)(2,1)S(1)}, u32[]{:S(2)}, u32[]{:S(2)}) collective-permute-start(bf16[128,1536]{1,0:T(8,128)(2,1)S(1)} %collective-permute-done.8), channel_id=1, source_target_pairs={{0,4},{4,8},{8,12},{12,16},{16,20},{20,24},{24,28},{28,0},{1,5},{5... | collective-permute-start | bytes 1179656 | tf_op jit(solution)/shard_map/ppermute | solution.py:25
  130.5 8.8 %collective-permute-start.11 = (bf16[64,1536]{1,0:T(8,128)(2,1)S(1)}, bf16[64,1536]{1,0:T(8,128)(2,1)S(1)}, u32[]{:S(2)}, u32[]{:S(2)}) collective-permute-start(bf16[64,1536]{1,0:T(8,128)(2,1)S(1)} %slice.67), channel_id=1, source_target_pairs={{0,4},{4,8},{8,12},{12,16},{16,20},{20,24},{24,28},{28,0},{1,5},{5... | collective-permute-start | bytes 589832 | tf_op jit(solution)/shard_map/ppermute | solution.py:25
  132.5 8.3 %collective-permute-start.12 = (bf16[64,1536]{1,0:T(8,128)(2,1)S(1)}, bf16[64,1536]{1,0:T(8,128)(2,1)S(1)}, u32[]{:S(2)}, u32[]{:S(2)}) collective-permute-start(bf16[64,1536]{1,0:T(8,128)(2,1)S(1)} %slice.68), channel_id=1, source_target_pairs={{0,28},{4,0},{8,4},{12,8},{16,12},{20,16},{24,20},{28,24},{1,29},{... | collective-permute-start | bytes 589832 | tf_op jit(solution)/shard_map/ppermute | solution.py:25
